TPU v7x, 32 devices: a whole 2x2x4 slice. The times are simulated.
32 devices in a mesh: fsdp: 4 (over z), heads: 4 (over y, x), tensor: 2 (over core).
Axes of the slice: x: 2, y: 2, z: 4, core: 2. Of those that a mesh axis runs over, the one named last changes fastest.
Arguments:
- tokens: bfloat16 [4096, 2048], P('fsdp'), may hold values from -6 to 6
- segments: int32 [4, 1024], P('fsdp'), may hold values from 0 to 7, never falling along the last dimension, each value on 1 to 512 neighbouring positions
- ln1_gain: bfloat16 [2048], P('fsdp'), may hold values from 0.25 to 1.75
- w_query: bfloat16 [2048, 2048], P('fsdp', ('heads', 'tensor')), may hold values from -0.125 to 0.125
- w_key: bfloat16 [2048, 1024], P('fsdp', ('heads', 'tensor')), may hold values from -0.125 to 0.125
- w_value: bfloat16 [2048, 1024], P('fsdp', ('heads', 'tensor')), may hold values from -0.125 to 0.125
- query_gain: bfloat16 [128], P('fsdp'), may hold values from 0.25 to 1.75
- key_gain: bfloat16 [128], P('fsdp'), may hold values from 0.25 to 1.75
- w_out: bfloat16 [2048, 2048], P('fsdp', ('heads', 'tensor')), may hold values from -1 to 1
- ln2_gain: bfloat16 [2048], P('fsdp'), may hold values from 0.25 to 1.75
- w_gate: bfloat16 [2048, 6144], P('fsdp', ('heads', 'tensor')), may hold values from -0.125 to 0.125
- w_up: bfloat16 [2048, 6144], P('fsdp', ('heads', 'tensor')), may hold values from -0.125 to 0.125
- w_down: bfloat16 [2048, 6144], P('fsdp', ('heads', 'tensor')), may hold values from -0.078125 to 0.078125
- cotangent: bfloat16 [4096, 2048], P('fsdp'), may hold values from -6 to 6
Outputs:
- block_out: bfloat16 [4096, 2048], P(('fsdp', 'heads', 'tensor'))
- tokens_grad: bfloat16 [4096, 2048], P(('fsdp', 'heads', 'tensor'))
- ln1_grad: float32 [2048], P('fsdp')
- query_w_grad: float32 [2048, 2048], P('fsdp', ('heads', 'tensor'))
- key_w_grad: float32 [2048, 1024], P('fsdp', ('heads', 'tensor'))
- value_w_grad: float32 [2048, 1024], P('fsdp', ('heads', 'tensor'))
- query_gain_grad: float32 [128], P('fsdp')
- key_gain_grad: float32 [128], P('fsdp')
- out_w_grad: float32 [2048, 2048], P('fsdp', ('heads', 'tensor'))
- ln2_grad: float32 [2048], P('fsdp')
- gate_w_grad: float32 [2048, 6144], P('fsdp', ('heads', 'tensor'))
- up_w_grad: float32 [2048, 6144], P('fsdp', ('heads', 'tensor'))
- down_w_grad: float32 [2048, 6144], P('fsdp', ('heads', 'tensor'))
Inputs may be any that keep to these rules, and one draw needn't show every extreme that they name: `segments`: in each sequence the segment numbers never fall, and some segment holds exactly 512 tokens.
All inputs are finite; a program needn't handle non-finite values.
Results may differ from a plain program's by a relative error of at most 0.02.
Values may be sent and summed in bfloat16 or wider, within the bound.
No kernel may reach another device: no remote copies, remote signals or barrier semaphores. Data moves between devices by JAX's collectives and lax.ppermute only.
A program may use at most 256 MiB of HBM per device.

v0:
```python
import jax
import jax.numpy as jnp
from jax import lax
from jax.sharding import PartitionSpec as P

HD = 128


EPSILON = 1e-06
THETA = 1000000.0


def rms_parts(values):
    return lax.rsqrt(jnp.mean(values * values, axis=-1, keepdims=True) + EPSILON)


def norm_back(values, scale, upstream):
    return scale * upstream - values * scale**3 * jnp.mean(
        values * upstream, axis=-1, keepdims=True
    )


def contract(left, right, left_dim, right_dim):
    return lax.dot_general(
        left, right, (((left_dim,), (right_dim,)), ((), ())), preferred_element_type=jnp.float32
    )


def doc_positions(segment_row):
    places = jnp.arange(segment_row.shape[0], dtype=jnp.int32)
    previous = jnp.concatenate([segment_row[:1], segment_row[:-1]])
    starts = lax.cummax(jnp.where(segment_row != previous, places, 0), axis=0)
    return places - starts


def rope_tables(positions):
    frequency = THETA ** (-(jnp.arange(HD // 2, dtype=jnp.float32) * 2.0 / HD))
    angles = positions.astype(jnp.float32)[:, None] * frequency[None, :]
    return (jnp.cos(angles), jnp.sin(angles))


def rotate(values, cosine, sine):
    middle = values.shape[-1] // 2
    front_half = values[..., :middle]
    back_half = values[..., middle:]
    cosine = cosine[:, None, :]
    sine = sine[:, None, :]
    return jnp.concatenate(
        [front_half * cosine - back_half * sine, back_half * cosine + front_half * sine], axis=-1
    )


def per_device(
    tokens,
    segments,
    ln1_gain,
    w_query,
    w_key,
    w_value,
    query_gain,
    key_gain,
    w_out,
    ln2_gain,
    w_gate,
    w_up,
    w_down,
    cotangent,
):
    length = tokens.shape[0]
    query_heads = w_query.shape[1] // HD
    kv_local = w_key.shape[1] // HD
    group = query_heads // kv_local
    scale_factor = HD ** (-0.5)
    block = min(512, length)
    count = length // block
    group_size = lax.axis_size(("heads", "tensor"))
    share_rows = length // group_size
    share_start = lax.axis_index(("heads", "tensor")) * share_rows
    segment_row = segments[0]
    places = jnp.arange(length, dtype=jnp.int32)
    cosine, sine = rope_tables(doc_positions(segment_row))

    def share_of(array):
        return lax.dynamic_slice_in_dim(array, share_start, share_rows, 0)

    gain_attn, query_proj, key_proj, value_proj, query_norm, key_norm, output_proj = (
        lax.all_gather(ln1_gain, "fsdp", axis=0, tiled=True),
        lax.all_gather(w_query, "fsdp", axis=0, tiled=True),
        lax.all_gather(w_key, "fsdp", axis=0, tiled=True),
        lax.all_gather(w_value, "fsdp", axis=0, tiled=True),
        lax.all_gather(query_gain, "fsdp", axis=0, tiled=True),
        lax.all_gather(key_gain, "fsdp", axis=0, tiled=True),
        lax.all_gather(w_out, "fsdp", axis=0, tiled=True),
    )
    block_in = tokens.astype(jnp.float32)
    scale_one = rms_parts(block_in)
    normed = (block_in * scale_one * gain_attn.astype(jnp.float32)).astype(jnp.bfloat16)
    query_raw = jnp.dot(normed, query_proj, preferred_element_type=jnp.float32).reshape(
        length, query_heads, HD
    )
    key_raw = jnp.dot(normed, key_proj, preferred_element_type=jnp.float32).reshape(
        length, kv_local, HD
    )
    values = (
        jnp.dot(normed, value_proj, preferred_element_type=jnp.float32)
        .astype(jnp.bfloat16)
        .reshape(length, kv_local, HD)
    )
    query_scale = rms_parts(query_raw)
    key_scale = rms_parts(key_raw)
    query_rot = rotate(
        query_raw * query_scale * query_norm.astype(jnp.float32), cosine, sine
    ).astype(jnp.bfloat16)
    key_rot = rotate(key_raw * key_scale * key_norm.astype(jnp.float32), cosine, sine).astype(
        jnp.bfloat16
    )

    def scores_of(query_block, start):
        rows_at = start + jnp.arange(block, dtype=jnp.int32)
        seg_rows = lax.dynamic_slice_in_dim(segment_row, start, block)
        allowed = (rows_at[:, None] >= places[None, :]) & (
            seg_rows[:, None] == segment_row[None, :]
        )
        raw_scores = jnp.einsum(
            "qkgd,skd->kgqs", query_block, key_rot, preferred_element_type=jnp.float32
        )
        return jnp.where(allowed[None, None], raw_scores * scale_factor, -1e30)

    def forward_block(packed):
        query_block, start = packed
        scores = scores_of(query_block, start)
        peak = jnp.max(scores, axis=-1, keepdims=True)
        expo = jnp.exp(scores - peak)
        total = jnp.sum(expo, axis=-1, keepdims=True)
        probs_low = (expo / total).astype(jnp.bfloat16)
        mixed_block = jnp.einsum(
            "kgqs,skd->qkgd", probs_low, values, preferred_element_type=jnp.float32
        )
        return (mixed_block, peak + jnp.log(total))

    grouped_query = query_rot.reshape(count, block, kv_local, group, HD)
    starts = jnp.arange(count, dtype=jnp.int32) * block
    mixed, log_total = lax.map(forward_block, (grouped_query, starts))
    mixed_low = mixed.reshape(length, query_heads * HD).astype(jnp.bfloat16)
    gain_ffn, gate_proj, up_proj, down_proj = (
        lax.all_gather(ln2_gain, "fsdp", axis=0, tiled=True),
        lax.all_gather(w_gate, "fsdp", axis=0, tiled=True),
        lax.all_gather(w_up, "fsdp", axis=0, tiled=True),
        lax.all_gather(w_down, "fsdp", axis=0, tiled=True),
    )
    block_share = share_of(block_in)
    hidden_one = block_in + lax.psum(contract(mixed_low, output_proj, 1, 1), ("heads", "tensor"))
    scale_two = rms_parts(hidden_one)
    normed_two = (hidden_one * scale_two * gain_ffn.astype(jnp.float32)).astype(jnp.bfloat16)
    hidden_share = share_of(hidden_one)
    scale_share = share_of(scale_two)
    gate_value = jnp.dot(normed_two, gate_proj, preferred_element_type=jnp.float32)
    up_value = jnp.dot(normed_two, up_proj, preferred_element_type=jnp.float32)
    sigmoid_gate = jax.nn.sigmoid(gate_value)
    silu_gate = gate_value * sigmoid_gate
    activated = (silu_gate * up_value).astype(jnp.bfloat16)
    block_out = (
        hidden_share
        + lax.psum_scatter(
            contract(activated, down_proj, 1, 1).astype(jnp.bfloat16),
            ("heads", "tensor"),
            scatter_dimension=0,
            tiled=True,
        ).astype(jnp.float32)
    ).astype(jnp.bfloat16)
    gain_ffn, gate_proj, up_proj, down_proj = (
        lax.all_gather(ln2_gain, "fsdp", axis=0, tiled=True),
        lax.all_gather(w_gate, "fsdp", axis=0, tiled=True),
        lax.all_gather(w_up, "fsdp", axis=0, tiled=True),
        lax.all_gather(w_down, "fsdp", axis=0, tiled=True),
    )
    act_grad = jnp.dot(cotangent, down_proj, preferred_element_type=jnp.float32)
    down_grad = contract(cotangent, activated, 0, 0)
    gate_grad = (
        act_grad * up_value * sigmoid_gate * (1.0 + gate_value * (1.0 - sigmoid_gate))
    ).astype(jnp.bfloat16)
    up_grad = (act_grad * silu_gate).astype(jnp.bfloat16)
    gate_w_part = contract(normed_two, gate_grad, 0, 0)
    up_w_part = contract(normed_two, up_grad, 0, 0)
    normed_two_grad = lax.psum(
        (contract(gate_grad, gate_proj, 1, 1) + contract(up_grad, up_proj, 1, 1)).astype(
            jnp.bfloat16
        ),
        ("heads", "tensor"),
    ).astype(jnp.float32)
    hidden_grad = cotangent.astype(jnp.float32) + norm_back(
        hidden_one, scale_two, normed_two_grad * gain_ffn.astype(jnp.float32)
    )
    attn_out_grad = hidden_grad.astype(jnp.bfloat16)
    grad_share = share_of(normed_two_grad)
    hidden_grad_share = share_of(hidden_grad)
    ffn_gain_part = jnp.sum(grad_share * hidden_share * scale_share, axis=0)
    gate_w_grad, up_w_grad, down_w_grad = (
        lax.psum_scatter(
            gate_w_part.astype(jnp.bfloat16), "fsdp", scatter_dimension=0, tiled=True
        ).astype(jnp.float32),
        lax.psum_scatter(
            up_w_part.astype(jnp.bfloat16), "fsdp", scatter_dimension=0, tiled=True
        ).astype(jnp.float32),
        lax.psum_scatter(
            down_grad.astype(jnp.bfloat16), "fsdp", scatter_dimension=0, tiled=True
        ).astype(jnp.float32),
    )
    gain_attn, query_proj, key_proj, value_proj, query_norm, key_norm, output_proj = (
        lax.all_gather(ln1_gain, "fsdp", axis=0, tiled=True),
        lax.all_gather(w_query, "fsdp", axis=0, tiled=True),
        lax.all_gather(w_key, "fsdp", axis=0, tiled=True),
        lax.all_gather(w_value, "fsdp", axis=0, tiled=True),
        lax.all_gather(query_gain, "fsdp", axis=0, tiled=True),
        lax.all_gather(key_gain, "fsdp", axis=0, tiled=True),
        lax.all_gather(w_out, "fsdp", axis=0, tiled=True),
    )
    out_w_part = contract(attn_out_grad, mixed_low, 0, 0)
    mixed_grad = jnp.dot(attn_out_grad, output_proj, preferred_element_type=jnp.float32).astype(
        jnp.bfloat16
    )

    def backward_block(carry, packed):
        key_sum, value_sum = carry
        query_block, grad_block, log_block, start = packed
        probs = jnp.exp(scores_of(query_block, start) - log_block)
        probs_low = probs.astype(jnp.bfloat16)
        prob_grad = jnp.einsum(
            "qkgd,skd->kgqs", grad_block, values, preferred_element_type=jnp.float32
        )
        row_inner = jnp.sum(probs * prob_grad, axis=-1, keepdims=True)
        score_grad = (scale_factor * probs * (prob_grad - row_inner)).astype(jnp.bfloat16)
        query_block_grad = jnp.einsum(
            "kgqs,skd->qkgd", score_grad, key_rot, preferred_element_type=jnp.float32
        )
        key_sum = key_sum + jnp.einsum(
            "kgqs,qkgd->skd", score_grad, query_block, preferred_element_type=jnp.float32
        )
        value_sum = value_sum + jnp.einsum(
            "kgqs,qkgd->skd", probs_low, grad_block, preferred_element_type=jnp.float32
        )
        return ((key_sum, value_sum), query_block_grad)

    zero_heads = jnp.zeros((length, kv_local, HD), jnp.float32)
    grouped_grad = mixed_grad.reshape(count, block, kv_local, group, HD)
    (key_rot_grad, value_grad), query_rot_grad = lax.scan(
        backward_block, (zero_heads, zero_heads), (grouped_query, grouped_grad, log_total, starts)
    )
    query_rot_grad = query_rot_grad.reshape(length, query_heads, HD)

    def head_back(rot_grad, raw_values, raw_scale, gain):
        turned = rotate(rot_grad, cosine, -sine)
        gain_part = jnp.sum(turned * raw_values * raw_scale, axis=(0, 1))
        raw_grad = norm_back(raw_values, raw_scale, turned * gain.astype(jnp.float32))
        return (raw_grad.reshape(length, -1).astype(jnp.bfloat16), gain_part)

    query_low_grad, query_gain_part = head_back(query_rot_grad, query_raw, query_scale, query_norm)
    key_low_grad, key_gain_part = head_back(key_rot_grad, key_raw, key_scale, key_norm)
    value_low_grad = value_grad.reshape(length, -1).astype(jnp.bfloat16)
    query_w_part = contract(normed, query_low_grad, 0, 0)
    key_w_part = contract(normed, key_low_grad, 0, 0)
    value_w_part = contract(normed, value_low_grad, 0, 0)
    normed_part = (
        contract(query_low_grad, query_proj, 1, 1)
        + contract(key_low_grad, key_proj, 1, 1)
        + contract(value_low_grad, value_proj, 1, 1)
    )
    normed_grad, query_gain_sum, key_gain_sum, ffn_gain_sum = (
        lax.psum(normed_part.astype(jnp.bfloat16), ("heads", "tensor")).astype(jnp.float32),
        lax.psum(query_gain_part.astype(jnp.bfloat16), ("heads", "tensor")).astype(jnp.float32),
        lax.psum(key_gain_part.astype(jnp.bfloat16), ("heads", "tensor")).astype(jnp.float32),
        lax.psum(ffn_gain_part.astype(jnp.bfloat16), ("heads", "tensor")).astype(jnp.float32),
    )
    attn_gain_part = jnp.sum(normed_grad * block_in * scale_one, axis=0)
    tokens_grad = (
        hidden_grad_share
        + norm_back(
            block_share, share_of(scale_one), share_of(normed_grad) * gain_attn.astype(jnp.float32)
        )
    ).astype(jnp.bfloat16)
    (
        ln1_grad,
        query_w_grad,
        key_w_grad,
        value_w_grad,
        query_gain_grad,
        key_gain_grad,
        out_w_grad,
        ln2_grad,
    ) = (
        lax.psum_scatter(
            attn_gain_part.astype(jnp.bfloat16), "fsdp", scatter_dimension=0, tiled=True
        ).astype(jnp.float32),
        lax.psum_scatter(
            query_w_part.astype(jnp.bfloat16), "fsdp", scatter_dimension=0, tiled=True
        ).astype(jnp.float32),
        lax.psum_scatter(
            key_w_part.astype(jnp.bfloat16), "fsdp", scatter_dimension=0, tiled=True
        ).astype(jnp.float32),
        lax.psum_scatter(
            value_w_part.astype(jnp.bfloat16), "fsdp", scatter_dimension=0, tiled=True
        ).astype(jnp.float32),
        lax.psum_scatter(
            query_gain_sum.astype(jnp.bfloat16), "fsdp", scatter_dimension=0, tiled=True
        ).astype(jnp.float32),
        lax.psum_scatter(
            key_gain_sum.astype(jnp.bfloat16), "fsdp", scatter_dimension=0, tiled=True
        ).astype(jnp.float32),
        lax.psum_scatter(
            out_w_part.astype(jnp.bfloat16), "fsdp", scatter_dimension=0, tiled=True
        ).astype(jnp.float32),
        lax.psum_scatter(
            ffn_gain_sum.astype(jnp.bfloat16), "fsdp", scatter_dimension=0, tiled=True
        ).astype(jnp.float32),
    )
    return (
        block_out,
        tokens_grad,
        ln1_grad,
        query_w_grad,
        key_w_grad,
        value_w_grad,
        query_gain_grad,
        key_gain_grad,
        out_w_grad,
        ln2_grad,
        gate_w_grad,
        up_w_grad,
        down_w_grad,
    )


def solution(mesh):
    in_specs = (
        P("fsdp", None),
        P("fsdp", None),
        P("fsdp"),
        P("fsdp", ("heads", "tensor")),
        P("fsdp", ("heads", "tensor")),
        P("fsdp", ("heads", "tensor")),
        P("fsdp"),
        P("fsdp"),
        P("fsdp", ("heads", "tensor")),
        P("fsdp"),
        P("fsdp", ("heads", "tensor")),
        P("fsdp", ("heads", "tensor")),
        P("fsdp", ("heads", "tensor")),
        P("fsdp", None),
    )
    out_specs = (
        P(("fsdp", "heads", "tensor"), None),
        P(("fsdp", "heads", "tensor"), None),
        P("fsdp"),
        P("fsdp", ("heads", "tensor")),
        P("fsdp", ("heads", "tensor")),
        P("fsdp", ("heads", "tensor")),
        P("fsdp"),
        P("fsdp"),
        P("fsdp", ("heads", "tensor")),
        P("fsdp"),
        P("fsdp", ("heads", "tensor")),
        P("fsdp", ("heads", "tensor")),
        P("fsdp", ("heads", "tensor")),
    )
    return jax.shard_map(
        per_device, mesh=mesh, in_specs=in_specs, out_specs=out_specs, check_vma=False
    )
```

profile of v0, /device:TPU:0, one launch (start us, length us, event | category | flops | bytes accessed | tf_op | source)
XLA Modules:
  0.0 1051.8 jit_solution(1030262262164979271)
XLA Ops:
  9.5 13.5 %all-gather = bf16[4,1,512]{2,1,0:T(2,128)(2,1)S(1)} all-gather(bf16[1,1,512]{2,1,0:T(2,128)(2,1)S(1)} %reshape.650), channel_id=1, replica_groups=mesh['fsdp'=4,'heads'=4,'tensor'=2] {'fsdp'}, dimensions={0}, use_global_device_ids=true | all-gather | bytes 5120 | tf_op jit(solution)/shard_map/all_gather | solution.py:87
  28.0 10.8 %all-reduce.8 = (bf16[128]{0:T(256)(128)(2,1)S(1)}, bf16[128]{0:T(256)(128)(2,1)S(1)}) all-reduce(bf16[128]{0:T(256)(128)(2,1)S(1)} %dynamic-update-slice, bf16[128]{0:T(256)(128)(2,1)S(1)} %dynamic-update-slice.1), channel_id=1, replica_groups=mesh['fsdp'=4,'heads'=4,'tensor'=2] {'fsdp'}, use_global_device_ids=true, to_apply=%add | all-reduce | flops 256 | bytes 1024
  40.6 16.2 %all_gather.47 = bf16[2048,128]{1,0:T(8,128)(2,1)S(1)} all-gather(bf16[512,128]{1,0:T(8,128)(2,1)S(1)} %copy-done.31), channel_id=1, replica_groups=mesh['fsdp'=4,'heads'=4,'tensor'=2] {'fsdp'}, dimensions={0}, use_global_device_ids=true | all-gather | bytes 655360 | tf_op jit(solution)/shard_map/all_gather | solution.py:89
  67.1 17.8 %all_gather.49 = bf16[2048,128]{1,0:T(8,128)(2,1)S(1)} all-gather(bf16[512,128]{1,0:T(8,128)(2,1)S(1)} %copy-done.32), channel_id=1, replica_groups=mesh['fsdp'=4,'heads'=4,'tensor'=2] {'fsdp'}, dimensions={0}, use_global_device_ids=true | all-gather | bytes 655360 | tf_op jit(solution)/shard_map/all_gather | solution.py:90
  89.2 3.8 multiply_reduce_fusion.7
  101.2 19.1 %while.28 = (s32[]{:T(128)}, bf16[2,512,1,2,128]{4,1,3,2,0:T(8,128)(2,1)}, f32[2,1,2,512,1]{3,2,4,1,0:T(2,128)S(1)}, s32[2]{0:T(128)S(1)}, s32[1024]{0:T(1024)S(...) while((s32[]{:T(128)}, ...), condition=%wide.region_8.9_spmd.clone, body=%wide.region_5.8_spmd.clone.sunk | while | flops 551026176 | bytes 20232440 | solution.py:143
  121.9 5.9 fusion.69
  129.6 12.5 %all-gather.1 = bf16[4,1,512]{2,1,0:T(2,128)(2,1)S(1)} all-gather(bf16[1,1,512]{2,1,0:T(2,128)(2,1)S(1)} %reshape.652), channel_id=1, replica_groups=mesh['fsdp'=4,'heads'=4,'tensor'=2] {'fsdp'}, dimensions={0}, use_global_device_ids=true | all-gather | bytes 5120 | tf_op jit(solution)/shard_map/all_gather | solution.py:146
  142.1 110.9 %all-reduce.13.cloned.1.call-done = f32[1024,2048]{1,0:T(8,128)} async-done(((f32[1024,2048]{1,0:T(8,128)}), f32[1024,2048]{1,0:T(8,128)}) %all-reduce.13.cloned.1.call-update) | async-done | bytes 8388624 | tf_op jit(solution)/shard_map/psum | solution.py:152
  252.9 5.7 multiply_reduce_fusion.2
  264.7 53.5 %all-gather.12.cloned.1.call-done = bf16[2048,768]{1,0:T(8,128)(2,1)} async-done(((bf16[512,768]{1,0:T(8,128)(2,1)}), bf16[2048,768]{1,0:T(8,128)(2,1)}) %all-gather.12.cloned.1.call-update) | async-done | bytes 3145744 | tf_op jit(solution)/shard_map/all_gather | solution.py:147
  318.2 8.2 fusion.100
  326.4 55.5 %all-gather.14.cloned.1.call-done = bf16[2048,768]{1,0:T(8,128)(2,1)} async-done(((bf16[512,768]{1,0:T(8,128)(2,1)}), bf16[2048,768]{1,0:T(8,128)(2,1)}) %all-gather.14.cloned.1.call-update) | async-done | bytes 3145744 | tf_op jit(solution)/shard_map/all_gather | solution.py:148
  381.8 8.3 fusion.101
  390.1 55.4 %all-gather.16.cloned.1.call-done = bf16[2048,768]{1,0:T(8,128)(2,1)} async-done(((bf16[512,768]{1,0:T(8,128)(2,1)}), bf16[2048,768]{1,0:T(8,128)(2,1)}) %all-gather.16.cloned.1.call-update) | async-done | bytes 3145744 | tf_op jit(solution)/shard_map/all_gather | solution.py:149
  445.5 10.6 %multiply_convert_fusion.2 = (bf16[1024,768]{1,0:T(8,128)(2,1)S(1)}, bf16[1024,768]{1,0:T(8,128)(2,1)S(1)}, bf16[1024,768]{1,0:T(8,128)(2,1)}) fusion(f32[1024,768]{1,0:T(8,128)} %fusion.100, f32[1024,768]{1,0:T(8,128)} %fusion.101, bf16[1024,2048]{1,0:T(8,128)(2,1)} %param.31, bf16[2048,768]{1,0:T(8,128)(2,1)} %all-gather.16.cloned.1.call-done), kind=kOutput, calls=%fused_computation.75 | convolution fusion | flops 3233021952 | bytes 18350080 | tf_op jit(solution)/shard_map/dot_general | solution.py:177
  459.8 5.1 add_convert_fusion.1
  465.0 79.7 %all-reduce.15.cloned.1.call-done = bf16[1024,2048]{1,0:T(8,128)(2,1)} async-done(((bf16[1024,2048]{1,0:T(8,128)(2,1)}), bf16[1024,2048]{1,0:T(8,128)(2,1)}) %all-reduce.15.cloned.1.call-update) | async-done | bytes 4194320 | tf_op jit(solution)/shard_map/psum | solution.py:185
  544.7 5.9 multiply_reduce_fusion.1
  551.7 5.0 subtract_add_fusion
  562.1 45.1 %while.29 = (s32[]{:T(128)}, f32[1024,1,128]{0,2,1:T(8,128)}, f32[1024,1,128]{0,2,1:T(8,128)}, f32[2,512,1,2,128]{4,1,0,3,2:T(8,128)}, bf16[2,512,1,2,128]{4,1,3...) while((s32[]{:T(128)}, f32[1024,1,128]{0,2,1:T(8,128)}, ...), condition=%wide.region_16.17_spmd.clone, body=%wide.region_14.16_spmd.clone.sunk | while | flops 1361051136 | bytes 63744312 | solution.py:246
  570.6 4.0 fusion.177
  578.3 4.5 fusion.180
  593.0 4.0 fusion.177
  600.9 4.6 fusion.180
  611.8 4.3 convolution_convert_fusion.7
  616.4 4.5 convolution_convert_fusion.6
  624.4 4.6 fusion.103
  628.9 4.5 fusion.91
  633.9 9.5 add_convert_fusion
  643.5 4.7 convolution_convert_fusion.5
  648.3 6.9 convolution_convert_fusion
  656.2 5.7 convolution_convert_fusion.4
  662.4 7.8 convolution_convert_fusion.3
  670.3 7.9 convolution_convert_fusion.2
  678.5 7.1 fusion.57
  685.7 6.6 convert_element_type.196
  693.7 6.5 convert_element_type.215
  703.6 39.8 %all-reduce.17.cloned.1.call-done = bf16[1024,2048]{1,0:T(8,128)(2,1)} async-done(((bf16[1024,2048]{1,0:T(8,128)(2,1)}), bf16[1024,2048]{1,0:T(8,128)(2,1)}) %all-reduce.17.cloned.1.call-update) | async-done | bytes 4194320 | tf_op jit(solution)/shard_map/psum | solution.py:269
  743.3 6.5 convert_element_type.223
  749.8 23.1 %reduce-scatter.11.cloned.1.call-done = bf16[512,256]{1,0:T(8,128)(2,1)} async-done(((bf16[2048,256]{1,0:T(8,128)(2,1)}), bf16[512,256]{1,0:T(8,128)(2,1)}) %reduce-scatter.11.cloned.1.call-update) | async-done | bytes 262160 | tf_op jit(solution)/shard_map/reduce_scatter | solution.py:294
  783.4 42.8 %reduce-scatter.9.cloned.1.call-done = bf16[128,2048]{1,0:T(8,128)(2,1)} async-done(((bf16[1024,2048]{1,0:T(8,128)(2,1)}), bf16[128,2048]{1,0:T(8,128)(2,1)}) %reduce-scatter.9.cloned.1.call-update) | async-done | bytes 524304 | tf_op jit(solution)/shard_map/reduce_scatter | solution.py:164
  828.9 12.2 %all-reduce.7 = (bf16[2048]{0:T(1024)(128)(2,1)S(1)}, bf16[128]{0:T(256)(128)(2,1)S(1)}, bf16[128]{0:T(256)(128)(2,1)S(1)}, bf16[2048]{0:T(1024)(128)(2,1)S(1)}) all-reduce(bf16[2048]{0:T(1024)(128)(2,1)S(1)} %multiply_reduce_fusion, ...), channel_id=3, replica_groups=mesh['fsdp'=4,'heads'=4,'tensor'=2] {'fsdp'}, use_global_device_ids=true, to_apply=%region_22.23.clone | all-reduce | flops 4352 | bytes 17408
  841.3 15.1 %reduce-scatter.17.cloned.1.call-done = bf16[512,256]{1,0:T(8,128)(2,1)} async-done(((bf16[2048,256]{1,0:T(8,128)(2,1)}), bf16[512,256]{1,0:T(8,128)(2,1)}) %reduce-scatter.17.cloned.1.call-update) | async-done | bytes 262160 | tf_op jit(solution)/shard_map/reduce_scatter | solution.py:309
  858.2 13.8 %all-reduce.6 = (bf16[32]{0:T(256)(128)(2,1)S(1)}, bf16[32]{0:T(256)(128)(2,1)S(1)}, bf16[512]{0:T(512)(128)(2,1)S(1)}) all-reduce(bf16[32]{0:T(256)(128)(2,1)S(1)} %dynamic-slice.13, bf16[32]{0:T(256)(128)(2,1)S(1)} %dynamic-slice.15, ...), channel_id=1, replica_groups=mesh['fsdp'=4,'heads'=4,'tensor'=2] {'heads','tensor'}, use_global_device_ids=true, to_apply=%region_28.29 | all-reduce | flops 576 | bytes 2304 | tf_op jit(solution)/shard_map/psum | solution.py:270
  873.7 43.9 %reduce-scatter.19.cloned.1.call-done = bf16[512,768]{1,0:T(8,128)(2,1)} async-done(((bf16[2048,768]{1,0:T(8,128)(2,1)}), bf16[512,768]{1,0:T(8,128)(2,1)}) %reduce-scatter.19.cloned.1.call-update) | async-done | bytes 786448 | tf_op jit(solution)/shard_map/reduce_scatter | solution.py:199
  919.9 60.1 %reduce-scatter.21.cloned.1.call-done = bf16[512,768]{1,0:T(8,128)(2,1)} async-done(((bf16[2048,768]{1,0:T(8,128)(2,1)}), bf16[512,768]{1,0:T(8,128)(2,1)}) %reduce-scatter.21.cloned.1.call-update) | async-done | bytes 786448 | tf_op jit(solution)/shard_map/reduce_scatter | solution.py:202
  983.0 59.4 %reduce-scatter.23.cloned.1.call-done = bf16[512,768]{0,1:T(8,128)(2,1)} async-done(((bf16[2048,768]{0,1:T(8,128)(2,1)}), bf16[512,768]{0,1:T(8,128)(2,1)}) %reduce-scatter.23.cloned.1.call-update) | async-done | bytes 786448 | tf_op jit(solution)/shard_map/reduce_scatter | solution.py:205
  (277 shorter events, 128.5 us)
Async XLA Ops:
  7.2 19.0 %copy-start.47 = (u32[32]{0:T(128)S(1)}, u32[32]{0:T(128)}, u32[]{:S(2)}) copy-start(u32[32]{0:T(128)} %constant.98) | copy-start | bytes 388
  7.2 20.3 %copy-start.51 = (bf16[32]{0:T(256)(128)(2,1)S(1)}, bf16[32]{0:T(256)(128)(2,1)}, u32[]{:S(2)}) copy-start(bf16[32]{0:T(256)(128)(2,1)} %param.24) | copy-start | bytes 196
  7.2 20.5 %copy-start.52 = (bf16[32]{0:T(256)(128)(2,1)S(1)}, bf16[32]{0:T(256)(128)(2,1)}, u32[]{:S(2)}) copy-start(bf16[32]{0:T(256)(128)(2,1)} %param.25) | copy-start | bytes 196
  7.2 31.6 %copy-start.26 = (s32[1,1024]{1,0:T(1,128)S(1)}, s32[1,1024]{1,0:T(1,128)}, u32[]{:S(2)}) copy-start(s32[1,1024]{1,0:T(1,128)} %param.19) | copy-start | bytes 12292
  7.2 33.4 %copy-start.31 = (bf16[512,128]{1,0:T(8,128)(2,1)S(1)}, bf16[512,128]{1,0:T(8,128)(2,1)}, u32[]{:S(2)}) copy-start(bf16[512,128]{1,0:T(8,128)(2,1)} %param.22) | copy-start | bytes 393220
  7.2 81.9 %all-gather.8.cloned.1.call-start = ((), (), s32[]{:S(2)}) async-start(), calls=%async_computation.8 | async-start | bytes 1310720 | tf_op jit(solution)/shard_map/all_gather | solution.py:88
  8.0 113.9 %all-gather.10.cloned.1.call-start = ((), (), s32[]{:S(2)}) async-start(), calls=%async_computation.9 | async-start | bytes 1310720 | tf_op jit(solution)/shard_map/all_gather | solution.py:93
  8.7 244.2 %all-reduce.13.cloned.1.call-start = ((), (), s32[]{:S(2)}) async-start(), calls=%async_computation.10 | async-start | bytes 16777216 | tf_op jit(solution)/shard_map/psum | solution.py:152
  8.8 56.9 %copy-start.45 = (f32[64]{0:T(128)}, f32[64]{0:T(128)S(1)}, u32[]{:S(2)}) copy-start(f32[64]{0:T(128)S(1)} %negate_power_fusion) | copy-start | bytes 772
  23.1 37.2 %copy-start.29 = (f32[4,1,512]{2,1,0:T(1,128)}, f32[4,1,512]{2,1,0:T(1,128)S(1)}, u32[]{:S(2)}) copy-start(f32[4,1,512]{2,1,0:T(1,128)S(1)} %convert_element_type.248) | copy-start | bytes 24580
  26.2 34.1 %copy-start.39 = (f32[1024]{0:T(1024)}, f32[1024]{0:T(1024)S(1)}, u32[]{:S(2)}) copy-start(f32[1024]{0:T(1024)S(1)} %add_rsqrt_fusion.3) | copy-start | bytes 12292
  40.6 25.1 %copy-start.37 = (f32[1024]{0:T(1024)}, f32[1024]{0:T(1024)S(1)}, u32[]{:S(2)}) copy-start(f32[1024]{0:T(1024)S(1)} %fusion.97) | copy-start | bytes 12292
  56.9 8.7 copy-start.43
  60.3 6.6 copy-start.4
  60.3 6.8 copy-start.32
  61.9 5.0 copy-start.8
  65.6 28.8 %copy-start.13 = (f32[1024,64]{1,0:T(8,128)}, f32[1024,64]{1,0:T(8,128)S(1)}, u32[]{:S(2)}) copy-start(f32[1024,64]{1,0:T(8,128)S(1)} %get-tuple-element.419) | copy-start | bytes 786436
  93.3 6.7 copy-start.6
  121.8 5.9 copy-start.9
  127.8 190.4 %all-gather.12.cloned.1.call-start = ((), (), s32[]{:S(2)}) async-start(), calls=%async_computation.11 | async-start | bytes 3932160 | tf_op jit(solution)/shard_map/all_gather | solution.py:147
  128.4 253.5 %all-gather.14.cloned.1.call-start = ((), (), s32[]{:S(2)}) async-start(), calls=%async_computation.12 | async-start | bytes 3932160 | tf_op jit(solution)/shard_map/all_gather | solution.py:148
  129.0 316.6 %all-gather.16.cloned.1.call-start = ((), (), s32[]{:S(2)}) async-start(), calls=%async_computation.13 | async-start | bytes 3932160 | tf_op jit(solution)/shard_map/all_gather | solution.py:149
  129.5 415.1 %all-reduce.15.cloned.1.call-start = ((), (), s32[]{:S(2)}) async-start(), calls=%async_computation.15 | async-start | bytes 8388608 | tf_op jit(solution)/shard_map/psum | solution.py:185
  445.5 10.6 %copy-start.49 = (bf16[2048,768]{1,0:T(8,128)(2,1)S(1)}, bf16[2048,768]{1,0:T(8,128)(2,1)}, u32[]{:S(2)}) copy-start(bf16[2048,768]{1,0:T(8,128)(2,1)} %all-gather.12.cloned.1.call-done) | copy-start | bytes 9437188
  464.9 235.4 %reduce-scatter.13.cloned.1.call-start = ((), (), s32[]{:S(2)}) async-start(), calls=%async_computation.18 | async-start | bytes 655360 | tf_op jit(solution)/shard_map/reduce_scatter | solution.py:297
  544.7 5.9 copy-start.5
  544.7 7.0 copy-start.22
  551.7 8.2 copy-start.15
  562.1 45.1 %copy-start.38 = (f32[1024]{0:T(1024)S(1)}, f32[1024]{0:T(1024)}, u32[]{:S(2)}) copy-start(f32[1024]{0:T(1024)} %copy-done.37) | copy-start | bytes 12292
  562.1 45.1 %copy-start.46 = (f32[64]{0:T(128)S(1)}, f32[64]{0:T(128)}, u32[]{:S(2)}) copy-start(f32[64]{0:T(128)} %copy-done.45) | copy-start | bytes 772
  562.1 47.2 %copy-start.36 = (f32[1024]{0:T(1024)S(1)}, f32[1024]{0:T(1024)}, u32[]{:S(2)}) copy-start(f32[1024]{0:T(1024)} %copy-done.35) | copy-start | bytes 12292
  562.1 47.2 %copy-start.44 = (f32[128]{0:T(128)S(1)}, f32[128]{0:T(128)}, u32[]{:S(2)}) copy-start(f32[128]{0:T(128)} %copy-done.43) | copy-start | bytes 1540
  562.1 48.5 %copy-start.42 = (f32[1024]{0:T(1024)S(1)}, f32[1024]{0:T(1024)}, u32[]{:S(2)}) copy-start(f32[1024]{0:T(1024)} %get-tuple-element.420) | copy-start | bytes 12292
  609.4 7.0 copy-start.23
  616.1 4.8 copy-start.20
  616.1 85.8 %reduce-scatter.15.cloned.1.call-start = ((), (), s32[]{:S(2)}) async-start(), calls=%async_computation.19 | async-start | bytes 655360 | tf_op jit(solution)/shard_map/reduce_scatter | solution.py:300
  616.4 5.9 copy-start.7
  633.5 109.8 %all-reduce.17.cloned.1.call-start = ((), (), s32[]{:S(2)}) async-start(), calls=%async_computation.16 | async-start | bytes 8388608 | tf_op jit(solution)/shard_map/psum | solution.py:269
  643.4 4.8 copy-start.53
  643.4 129.6 %reduce-scatter.11.cloned.1.call-start = ((), (), s32[]{:S(2)}) async-start(), calls=%async_computation.17 | async-start | bytes 1310720 | tf_op jit(solution)/shard_map/reduce_scatter | solution.py:294
  648.2 178.0 %reduce-scatter.9.cloned.1.call-start = ((), (), s32[]{:S(2)}) async-start(), calls=%async_computation.14 | async-start | bytes 4718592 | tf_op jit(solution)/shard_map/reduce_scatter | solution.py:164
  655.2 201.2 %reduce-scatter.17.cloned.1.call-start = ((), (), s32[]{:S(2)}) async-start(), calls=%async_computation.20 | async-start | bytes 1310720 | tf_op jit(solution)/shard_map/reduce_scatter | solution.py:309
  662.0 255.6 %reduce-scatter.19.cloned.1.call-start = ((), (), s32[]{:S(2)}) async-start(), calls=%async_computation.21 | async-start | bytes 3932160 | tf_op jit(solution)/shard_map/reduce_scatter | solution.py:199
  670.3 309.7 %reduce-scatter.21.cloned.1.call-start = ((), (), s32[]{:S(2)}) async-start(), calls=%async_computation.22 | async-start | bytes 3932160 | tf_op jit(solution)/shard_map/reduce_scatter | solution.py:202
  678.3 364.2 %reduce-scatter.23.cloned.1.call-start = ((), (), s32[]{:S(2)}) async-start(), calls=%async_computation.23 | async-start | bytes 3932160 | tf_op jit(solution)/shard_map/reduce_scatter | solution.py:205
  685.7 7.9 copy-start.40
  703.6 71.3 %copy-start.30 = (f32[4,1,512]{2,1,0:T(1,128)S(1)}, f32[4,1,512]{2,1,0:T(1,128)}, u32[]{:S(2)}) copy-start(f32[4,1,512]{2,1,0:T(1,128)} %copy-done.29) | copy-start | bytes 24580
  773.0 6.7 copy-start.3
  (29 other events, 90.2 us)
Sparse Core Ops, SparseCore 0:
  9.6 31.9 all-gather.7
  43.2 32.9 all-gather.9
  127.9 124.9 all-reduce.12
  254.4 63.6 all-gather.11
  319.7 62.1 all-gather.13
  383.3 62.1 all-gather.15
  465.0 79.6 all-reduce.14
  616.3 21.6 reduce-scatter.12
  640.9 19.9 reduce-scatter.14
  664.0 79.3 all-reduce.16
  745.7 27.2 reduce-scatter.10
  776.2 49.9 reduce-scatter.8
  829.2 27.2 reduce-scatter.16
  858.6 58.8 reduce-scatter.18
  919.7 60.2 reduce-scatter.20
  982.2 60.2 reduce-scatter.22
where the time goes:
time: 1060 us; the launch traced here: 1050 us
  waiting for transfers between devices  642 us (61%)
  matrix products  157 us (15%)
  other arithmetic  98.1 us (9%)
  blocking collectives  96.9 us (9%)
  local copies, waits for them, and re-layouts  31.4 us (3%)
  between operations  16.9 us (2%)
    psum x1, waiting for transfers between devices, per_device(): lax.psum(contract(mixed_low, output_proj, 1, 1), ('heads', 'tensor'))  111 us
    dot_general x14, matrix products, contract(): lax.dot_general(left, right, (((left_dim,), (right_dim,)), ((), ())), pre...  82.1 us
    psum x1, waiting for transfers between devices, per_device(): lax.psum((contract(gate_grad, gate_proj, 1, 1) + contract(up_grad, up_pro...  79.7 us
    reduce_scatter x1, waiting for transfers between devices, per_device(): lax.psum_scatter(up_w_part.astype(jnp.bfloat16), 'fsdp', scatter_dimensio...  60.1 us
    reduce_scatter x1, waiting for transfers between devices, per_device(): lax.psum_scatter(down_grad.astype(jnp.bfloat16), 'fsdp', scatter_dimensio...  59.4 us
    all_gather x1, waiting for transfers between devices, per_device(): lax.all_gather(w_up, 'fsdp', axis=0, tiled=True)  55.5 us
    all_gather x1, waiting for transfers between devices, per_device(): lax.all_gather(w_down, 'fsdp', axis=0, tiled=True)  55.4 us
    all_gather x1, waiting for transfers between devices, per_device(): lax.all_gather(w_gate, 'fsdp', axis=0, tiled=True)  53.5 us
  transfers between devices with their start and end apart: 16, of which 12 were waited for; matrix products, arithmetic and copies ran while one was open for 18% of the time, Pallas kernels for 0%

commit v1 on v0

v1 whole, which is shorter than its diff:
```python
import functools

import jax
import jax.numpy as jnp
from jax import lax
from jax.experimental import pallas as pl
from jax.experimental.pallas import tpu as pltpu
from jax.sharding import PartitionSpec as P

HD = 128


EPSILON = 1e-06
THETA = 1000000.0
ROWS = 256
BAND = 512
PLANE = ("heads", "tensor")
SWAP = ((0, 1), (1, 0))
NEAR = ((0, 1), (1, 0), (2, 3), (3, 2))
FAR = ((0, 2), (2, 0), (1, 3), (3, 1))


def rms_parts(values):
    return lax.rsqrt(jnp.mean(values * values, axis=-1, keepdims=True) + EPSILON)


def norm_back(values, scale, upstream):
    return scale * upstream - values * scale**3 * jnp.mean(
        values * upstream, axis=-1, keepdims=True
    )


def contract(left, right, left_dim, right_dim):
    return lax.dot_general(
        left, right, (((left_dim,), (right_dim,)), ((), ())), preferred_element_type=jnp.float32
    )


def doc_positions(segment_row):
    places = jnp.arange(segment_row.shape[0], dtype=jnp.int32)
    previous = jnp.concatenate([segment_row[:1], segment_row[:-1]])
    starts = lax.cummax(jnp.where(segment_row != previous, places, 0), axis=0)
    return places - starts


def rope_tables(positions):
    frequency = THETA ** (-(jnp.arange(HD // 2, dtype=jnp.float32) * 2.0 / HD))
    angles = positions.astype(jnp.float32)[:, None] * frequency[None, :]
    cosine, sine = jnp.cos(angles), jnp.sin(angles)
    return (
        jnp.concatenate([cosine, cosine], axis=1),
        jnp.concatenate([-sine, sine], axis=1),
    )


def low(values):
    return values.astype(jnp.bfloat16)


def wide(values):
    return values.astype(jnp.float32)


def flip(axis, stride):
    return [(k, k ^ stride) for k in range(lax.axis_size(axis))]


class Job:
    def __init__(self, steps):
        self.steps, self.moves, self.value = steps, (), None
        self.resume(None)

    def resume(self, got):
        try:
            self.moves = self.steps.send(got)
        except StopIteration as end:
            self.moves, self.value = (), end.value


def beside(*jobs, kernels=()):
    jobs = [job for job in jobs if job.moves]
    given = [[move[0] for move in job.moves] for job in jobs], [args for _, args in kernels]
    arrays, args = lax.optimization_barrier(given)
    got = [
        [lax.ppermute(array, *move[1:]) for array, move in zip(held, job.moves)]
        for held, job in zip(arrays, jobs)
    ]
    results = [kernel[0](*own) for own, kernel in zip(args, kernels)]
    got, results = lax.optimization_barrier((got, results))
    for job, arrived in zip(jobs, got):
        job.resume(arrived)
    return results


def finish(*jobs):
    while any(job.moves for job in jobs):
        beside(*jobs)


def bits(axis):
    size = lax.axis_size(axis)
    return [1 << k for k in range(size.bit_length() - 1)]


def swap(array, axis, stride):
    return lax.ppermute(array, axis, flip(axis, stride))


def bit(axis, stride):
    return (lax.axis_index(axis) // stride) % 2


def line_gather(block, strides):
    block = block[None]
    for stride in strides:
        block = both(block, swap(block, "fsdp", stride), bit("fsdp", stride), 0)
        block = block.reshape(-1, *block.shape[2:])
    return block


def sum_small(values, axis):
    for stride in bits(axis):
        values = values + swap(values, axis, stride)
    return values


def pick(array, index, axis):
    return lax.dynamic_index_in_dim(array, index, axis, keepdims=False)


def both(mine, got, index, axis):
    lower = jnp.where(index == 0, mine, got)
    upper = jnp.where(index == 0, got, mine)
    return jnp.stack([lower, upper], axis=axis)


def plane_scatter(part):
    rows, width = part.shape
    heads = lax.axis_index("heads")
    x, y, core = heads % 2, heads // 2, lax.axis_index("tensor")
    cut = part.reshape(2, 2, 2, rows // 8, width)
    (got,) = yield [(pick(cut, 1 - core, 2), "tensor", SWAP)]
    chip = low(wide(pick(cut, core, 2)) + wide(got))
    first, second = chip[..., : width // 2], chip[..., width // 2 :]
    got = yield [(pick(first, 1 - x, 1), "heads", NEAR), (pick(second, 1 - y, 0), "heads", FAR)]
    first = low(wide(pick(first, x, 1)) + wide(got[0]))
    second = low(wide(pick(second, y, 0)) + wide(got[1]))
    got = yield [(pick(first, 1 - y, 0), "heads", FAR), (pick(second, 1 - x, 0), "heads", NEAR)]
    first = wide(pick(first, y, 0)) + wide(got[0])
    second = wide(pick(second, x, 0)) + wide(got[1])
    return jnp.concatenate([first, second], axis=-1)


def plane_gather(share):
    lead, rows, width = share.shape
    heads = lax.axis_index("heads")
    x, y, core = heads % 2, heads // 2, lax.axis_index("tensor")
    first, second = share[..., : width // 2], share[..., width // 2 :]
    got = yield [(first, "heads", FAR), (second, "heads", NEAR)]
    first = both(first, got[0], y, 1)
    second = both(second, got[1], x, 1)
    got = yield [(first, "heads", NEAR), (second, "heads", FAR)]
    first = both(first, got[0], x, 2)
    second = both(second, got[1], y, 1)
    chip = jnp.concatenate([first, second], axis=-1)
    (got,) = yield [(chip, "tensor", SWAP)]
    return both(chip, got, core, 3).reshape(lead, rows * 8, width)


def pair_swap(array):
    (got,) = yield [(array, "fsdp", flip("fsdp", 1))]
    return got


def pair_cot(cotangent):
    core = lax.axis_index("tensor")
    rows, width = cotangent.shape
    half = lax.dynamic_slice_in_dim(cotangent, core * (rows // 2), rows // 2, 0)
    got = []
    for cut in range(0, rows // 2, rows // 8):
        (arrived,) = yield [(half[cut : cut + rows // 8], "fsdp", flip("fsdp", 1))]
        got.append(arrived)
    got = jnp.concatenate(got, axis=0)
    (other,) = yield [(got, "tensor", SWAP)]
    return both(got, other, core, 0).reshape(rows, width)


def weights_gather(mine, given):
    size, rows = lax.axis_size("fsdp"), mine.shape[0]
    pair = flip("fsdp", 1)
    slots = [[] for _ in range(size)]
    slots[0] = [mine]
    if size == 4:
        far = flip("fsdp", 2)
        plan = [(0, 96, 0, 256), (96, 64), (160, 144, 256, 256), (304, 96), (400, 112)]
        unit = rows // 32
        for start, count, *near in plan:
            start, count = start * unit // 16, count * unit // 16
            moves = [(mine[start : start + count], "fsdp", far)]
            if near:
                at, span = near[0] * unit // 16, near[1] * unit // 16
                moves.append((given[at : at + span], "fsdp", pair))
            got = yield moves
            slots[2].append(got[0])
            slots[1] += got[1:]
        for steps in ([(0, 144)], [(144, 112), (256, 128)], [(384, 128)]):
            moves = []
            for start, count in steps:
                held = slots[1][start // 256]
                start, count = (start % 256) * unit // 16, count * unit // 16
                moves.append((held[start : start + count], "fsdp", far))
            slots[3] += yield moves
        return slots
    slots[1] = yield [(given, "fsdp", pair)]
    stride = 2
    while stride < size:
        for slot in range(stride):
            slots[stride + slot] = yield [(slots[slot][0], "fsdp", flip("fsdp", stride))]
        stride *= 2
    return slots


def weights_scatter(near, far):
    size, rows = lax.axis_size("fsdp"), near.shape[1]
    pair = flip("fsdp", 1)
    if size == 4:
        cross = flip("fsdp", 2)
        own, other = [], []
        unit = rows // 32
        first = []
        waiting = []
        plan = [(3, 0, 160), (3, 160, 128), (3, 288, 96), (3, 384, 128), (2, 0, 96), (2, 96, 176), (2, 272, 128), (2, 400, 112)]
        for slot, start, count in plan:
            here = slice(start * unit // 16, (start + count) * unit // 16)
            moves = [(far[slot - 2, here], "fsdp", cross)]
            if slot == 2 and waiting:
                moves.append((waiting.pop(0), "fsdp", pair))
            got = yield moves
            summed = wide(near[slot - 2, here]) + wide(got[0])
            if slot == 3:
                waiting.append(low(summed))
            else:
                own.append(summed)
            other += got[1:]
        return own, other
    sums = [near[k] for k in range(size // 2)] + [far[k] for k in range(size // 2)]
    stride = size // 2
    while stride > 1:
        for slot in range(stride):
            (got,) = yield [(low(sums[stride + slot]), "fsdp", flip("fsdp", stride))]
            sums[slot] = wide(sums[slot]) + wide(got)
        stride //= 2
    (got,) = yield [(low(sums[1]), "fsdp", pair)]
    return [wide(sums[0])], [got]


def rotate(values, cosine, sine):
    return values * cosine + pltpu.roll(values, HD // 2, 1) * sine


def call_params(megabytes):
    return pltpu.CompilerParams(vmem_limit_bytes=megabytes << 20)


def cheap():
    return pl.CostEstimate(flops=1000, bytes_accessed=1000, transcendentals=0)


def key_blocks(at, count):
    return max(0, at - BAND // ROWS), at + 1


def masked_probs(query, keys, seg_rows, seg_keys, first_row, first_key):
    scores = contract(query, keys, 1, 1) * HD**-0.5
    rows = first_row + lax.broadcasted_iota(jnp.int32, scores.shape, 0)
    cols = first_key + lax.broadcasted_iota(jnp.int32, scores.shape, 1)
    scores = jnp.where((rows >= cols) & (seg_rows == seg_keys), scores, -1e30)
    expo = jnp.exp(scores - jnp.max(scores, axis=-1, keepdims=True))
    return expo / jnp.sum(expo, axis=-1, keepdims=True)


def attend_kernel(
    group,
    normed_ref,
    proj_ref,
    cosine_ref,
    sine_ref,
    query_gain_ref,
    key_gain_ref,
    seg_rows_ref,
    seg_keys_ref,
    raw_ref,
    query_ref,
    key_ref,
    value_ref,
    mixed_ref,
    part_ref,
    keys,
    values,
):
    length, kv_cols = keys.shape
    kv_local = kv_cols // HD
    query_cols = kv_cols * group
    count = length // ROWS
    step = pl.program_id(0)
    split = query_cols + 2 * kv_cols
    raw = jnp.dot(normed_ref[...], proj_ref[:, :split], preferred_element_type=jnp.float32)
    raw_ref[...] = raw[:, : query_cols + kv_cols]
    cosine, sine = cosine_ref[...], sine_ref[...]
    here = pl.ds(pl.multiple_of(step * ROWS, ROWS), ROWS)

    def turned(head, gain_ref):
        one = raw[:, head * HD : (head + 1) * HD]
        return low(rotate(one * rms_parts(one) * gain_ref[...], cosine, sine))

    for kv in range(kv_local):
        at = slice(kv * HD, (kv + 1) * HD)
        new_keys = turned(query_cols // HD + kv, key_gain_ref)
        new_values = low(raw[:, query_cols + kv_cols + kv * HD : query_cols + kv_cols + (kv + 1) * HD])
        key_ref[:, at] = new_keys
        value_ref[:, at] = new_values
        keys[here, at] = new_keys
        values[here, at] = new_values
    for head in range(query_cols // HD):
        query_ref[:, head * HD : (head + 1) * HD] = turned(head, query_gain_ref)

    for at in range(count):

        @pl.when(step == at)
        def _():
            lower, upper = key_blocks(at, count)
            span = slice(lower * ROWS, upper * ROWS)
            for head in range(query_cols // HD):
                cols = slice(head * HD, (head + 1) * HD)
                kv = slice((head // group) * HD, (head // group + 1) * HD)
                probs = masked_probs(
                    query_ref[:, cols],
                    keys[span, kv],
                    seg_rows_ref[...],
                    seg_keys_ref[:, span],
                    at * ROWS,
                    lower * ROWS,
                )
                mixed_ref[:, cols] = low(
                    jnp.dot(low(probs), values[span, kv], preferred_element_type=jnp.float32)
                )

    part_ref[...] = low(contract(mixed_ref[...], proj_ref[:, split:], 1, 1))


def attend(group, normed, proj, cosine, sine, query_gain, key_gain, segment_row):
    length, model = normed.shape
    kv_cols = proj.shape[1] // (2 * group + 2)
    query_cols = kv_cols * group

    def rows(width):
        return pl.BlockSpec((ROWS, width), lambda i: (i, 0))

    def whole(array):
        return pl.BlockSpec(array.shape, lambda i: (0, 0))

    seg_rows, seg_keys = segment_row[:, None], segment_row[None, :]
    args = (normed, proj, cosine, sine, query_gain[None], key_gain[None], seg_rows, seg_keys)
    outs = [
        (query_cols + kv_cols, jnp.float32),
        (query_cols, jnp.bfloat16),
        (kv_cols, jnp.bfloat16),
        (kv_cols, jnp.bfloat16),
        (query_cols, jnp.bfloat16),
        (model, jnp.bfloat16),
    ]
    return pl.pallas_call(
        functools.partial(attend_kernel, group),
        grid=(length // ROWS,),
        in_specs=[
            rows(model),
            whole(proj),
            rows(HD),
            rows(HD),
            whole(args[4]),
            whole(args[5]),
            rows(1),
            whole(seg_keys),
        ],
        out_specs=[rows(width) for width, _ in outs],
        out_shape=[jax.ShapeDtypeStruct((length, width), kind) for width, kind in outs],
        scratch_shapes=[
            pltpu.VMEM((length, kv_cols), jnp.bfloat16),
            pltpu.VMEM((length, kv_cols), jnp.bfloat16),
        ],
        compiler_params=call_params(40),
        cost_estimate=cheap(),
        name="attend",
    )(*args)


def attend_back_kernel(
    group,
    grad_ref,
    proj_ref,
    cosine_ref,
    sine_ref,
    query_gain_ref,
    key_gain_ref,
    seg_rows_ref,
    seg_keys_ref,
    raw_ref,
    query_ref,
    key_ref,
    value_ref,
    tokens_ref,
    scale_ref,
    low_ref,
    part_ref,
    gain_ref,
    head_gain_ref,
    mixed_grad,
    query_sum,
    key_sum,
    value_sum,
):
    length, kv_cols = key_sum.shape
    query_cols = kv_cols * group
    count = length // ROWS
    split = query_cols + 2 * kv_cols
    for at in range(count):
        here = slice(at * ROWS, (at + 1) * ROWS)
        mixed_grad[here, :] = low(
            jnp.dot(grad_ref[here, :], proj_ref[:, split:], preferred_element_type=jnp.float32)
        )
    key_sum[...] = jnp.zeros_like(key_sum)
    value_sum[...] = jnp.zeros_like(value_sum)
    for at in range(count):
        here = slice(at * ROWS, (at + 1) * ROWS)
        lower, upper = key_blocks(at, count)
        span = slice(lower * ROWS, upper * ROWS)
        for head in range(query_cols // HD):
            cols = slice(head * HD, (head + 1) * HD)
            kv = slice((head // group) * HD, (head // group + 1) * HD)
            query = query_ref[here, cols]
            grad = mixed_grad[here, cols]
            probs = masked_probs(
                query,
                key_ref[span, kv],
                seg_rows_ref[here, :],
                seg_keys_ref[:, span],
                at * ROWS,
                lower * ROWS,
            )
            prob_grad = contract(grad, value_ref[span, kv], 1, 1)
            row_inner = jnp.sum(probs * prob_grad, axis=-1, keepdims=True)
            score_grad = low(HD**-0.5 * probs * (prob_grad - row_inner))
            query_sum[here, cols] = jnp.dot(
                score_grad, key_ref[span, kv], preferred_element_type=jnp.float32
            )
            key_sum[span, kv] += contract(score_grad, query, 0, 0)
            value_sum[span, kv] += contract(low(probs), grad, 0, 0)

    gain_ref[...] = jnp.zeros_like(gain_ref)
    head_gain_ref[...] = jnp.zeros_like(head_gain_ref)
    for at in range(count):
        here = slice(at * ROWS, (at + 1) * ROWS)
        cosine, sine = cosine_ref[here, :], -sine_ref[here, :]
        for head in range((query_cols + kv_cols) // HD):
            cols = slice(head * HD, (head + 1) * HD)
            own = slice(head * HD - query_cols, (head + 1) * HD - query_cols)
            is_query = head * HD < query_cols
            turned = rotate(query_sum[here, cols] if is_query else key_sum[here, own], cosine, sine)
            raw = raw_ref[here, cols]
            scale = rms_parts(raw)
            row = 0 if is_query else 1
            head_gain_ref[row : row + 1, :] += jnp.sum(turned * raw * scale, axis=0, keepdims=True)
            gain = query_gain_ref[...] if is_query else key_gain_ref[...]
            low_ref[here, cols] = low(norm_back(raw, scale, turned * gain))
        low_ref[here, query_cols + kv_cols :] = low(value_sum[here, :])
        part = contract(low_ref[here, :], proj_ref[:, :split], 1, 1)
        part_ref[here, :] = low(part)
        gain_ref[...] += jnp.sum(part * wide(tokens_ref[here, :]) * scale_ref[here, :], axis=0, keepdims=True)


def attend_back(
    group, grad, proj, cosine, sine, query_gain, key_gain, segment_row, raw, query, key, value, tokens, scale
):
    length, model = grad.shape
    query_cols, kv_cols = query.shape[1], key.shape[1]
    args = (
        grad, proj, cosine, sine, query_gain[None], key_gain[None],
        segment_row[:, None], segment_row[None, :], raw, query, key, value, tokens, scale,
    )
    return pl.pallas_call(
        functools.partial(attend_back_kernel, group),
        in_specs=[pl.BlockSpec(memory_space=pltpu.VMEM)] * len(args),
        out_specs=[pl.BlockSpec(memory_space=pltpu.VMEM)] * 4,
        out_shape=[
            jax.ShapeDtypeStruct((length, query_cols + 2 * kv_cols), jnp.bfloat16),
            jax.ShapeDtypeStruct((length, model), jnp.bfloat16),
            jax.ShapeDtypeStruct((1, model), jnp.float32),
            jax.ShapeDtypeStruct((2, HD), jnp.float32),
        ],
        scratch_shapes=[
            pltpu.VMEM((length, query_cols), jnp.bfloat16),
            pltpu.VMEM((length, query_cols), jnp.float32),
            pltpu.VMEM((length, kv_cols), jnp.float32),
            pltpu.VMEM((length, kv_cols), jnp.float32),
        ],
        compiler_params=call_params(48),
        cost_estimate=cheap(),
        name="attend_back",
    )(*args)


def feed_kernel(layout, shard, place_ref, normed_ref, cotangent_ref, *refs):
    parts, (act_ref, gate_up_grad_ref, normed_grad_ref, proj_ref) = refs[:-4], refs[-4:]
    half = act_ref.shape[1]
    if layout:

        @pl.when(pl.program_id(0) == 0)
        def _():
            for part, (slot, first) in zip(parts, layout):
                owner = lax.bitwise_xor(place_ref[0], slot)
                start = pl.multiple_of(owner * shard + first, 16)
                proj_ref[pl.ds(start, part.shape[0]), :] = part[...]

        proj = proj_ref
    else:
        proj = parts[0]
    gate_up = jnp.dot(normed_ref[...], proj[:, : 2 * half], preferred_element_type=jnp.float32)
    gate, up = gate_up[:, :half], gate_up[:, half:]
    act_grad = jnp.dot(cotangent_ref[...], proj[:, 2 * half :], preferred_element_type=jnp.float32)
    sigmoid = jax.nn.sigmoid(gate)
    silu = gate * sigmoid
    act_ref[...] = low(silu * up)
    gate_up_grad_ref[:, :half] = low(act_grad * up * sigmoid * (1.0 + gate * (1.0 - sigmoid)))
    gate_up_grad_ref[:, half:] = low(act_grad * silu)
    normed_grad_ref[...] = low(contract(gate_up_grad_ref[...], proj[:, : 2 * half], 1, 1))


def feed(place, normed, cotangent, *slots):
    tokens, model = normed.shape
    layout, parts = [], []
    if len(slots) == 1:
        parts = slots
    else:
        for slot, held in enumerate(slots):
            first = 0
            for part in held:
                layout.append((slot, first))
                parts.append(part)
                first += part.shape[0]
    width = parts[0].shape[1]
    half = width // 3
    shard = model // len(slots)

    def rows(width):
        return pl.BlockSpec((ROWS, width), lambda i, place: (i, 0))

    def whole(shape):
        return pl.BlockSpec(shape, lambda i, place: (0, 0), pipeline_mode=pl.Buffered(1))

    widths = [half, 2 * half, model]
    out_shape = [jax.ShapeDtypeStruct((tokens, w), jnp.bfloat16) for w in widths]
    proj_shape = (model, width) if layout else (16, 128)
    return pl.pallas_call(
        functools.partial(feed_kernel, layout, shard),
        grid_spec=pltpu.PrefetchScalarGridSpec(
            num_scalar_prefetch=1,
            grid=(tokens // ROWS,),
            in_specs=[rows(model), rows(model)] + [whole(p.shape) for p in parts],
            out_specs=[rows(w) for w in widths] + [whole(proj_shape)],
        ),
        out_shape=out_shape + [jax.ShapeDtypeStruct(proj_shape, jnp.bfloat16)],
        compiler_params=call_params(40),
        cost_estimate=cheap(),
        name="feed",
    )(place, normed, cotangent, *parts)


def feed_weights_kernel(
    slots, place_ref, normed_own, normed_pair, cot_own, cot_pair, grad_own, grad_pair, act_own, act_pair, out_ref
):
    wide_cols = grad_own.shape[1]
    out_ref[0, :, :wide_cols] = low(
        contract(normed_own[...], grad_own[...], 0, 0) + contract(normed_pair[...], grad_pair[...], 0, 0)
    )
    out_ref[0, :, wide_cols:] = low(
        contract(cot_own[...], act_own[...], 0, 0) + contract(cot_pair[...], act_pair[...], 0, 0)
    )


def feed_weights(size, slots, place, normed, cotangent, grad, act):
    length, model = normed[0].shape
    shard = model // size
    width = grad[0].shape[1] + act[0].shape[1]
    first, count = slots

    def columns():
        return pl.BlockSpec((length, shard), lambda i, place: (0, lax.bitwise_xor(place[0], first + i)))

    def whole(array):
        return pl.BlockSpec(array.shape, lambda i, place: (0, 0), pipeline_mode=pl.Buffered(1))

    return pl.pallas_call(
        functools.partial(feed_weights_kernel, slots),
        grid_spec=pltpu.PrefetchScalarGridSpec(
            num_scalar_prefetch=1,
            grid=(count,),
            in_specs=[columns()] * 4 + [whole(a) for a in (*grad, *act)],
            out_specs=pl.BlockSpec((1, shard, width), lambda i, place: (i, 0, 0)),
        ),
        out_shape=jax.ShapeDtypeStruct((count, shard, width), jnp.bfloat16),
        compiler_params=call_params(48),
        cost_estimate=cheap(),
        name="feed_weights",
    )(place, *normed, *cotangent, *grad, *act)


def feed_sums_kernel(count, side_ref, *refs):
    own, other, outs = refs[:count], refs[count:-3], refs[-3:]
    half = outs[0].shape[1]
    mine = pl.program_id(0) == side_ref[0]
    for held, keep in ((own, mine), (other, jnp.logical_not(mine))):

        @pl.when(keep)
        def _():
            first = 0
            for part in held:
                for k, out in enumerate(outs):
                    out[first : first + part.shape[0], :] = wide(part[:, k * half : (k + 1) * half])
                first += part.shape[0]


def feed_sums(side, own, other):
    rows, width = sum(part.shape[0] for part in own), own[0].shape[1]
    half = width // 3
    parts = (*own, *other)
    return pl.pallas_call(
        functools.partial(feed_sums_kernel, len(own)),
        grid_spec=pltpu.PrefetchScalarGridSpec(
            num_scalar_prefetch=1,
            grid=(2,),
            in_specs=[
                pl.BlockSpec(p.shape, lambda i, side: (0, 0), pipeline_mode=pl.Buffered(1)) for p in parts
            ],
            out_specs=[pl.BlockSpec((rows, half), lambda i, side: (0, i))] * 3,
        ),
        out_shape=[jax.ShapeDtypeStruct((rows, 2 * half), jnp.float32)] * 3,
        compiler_params=call_params(32),
        cost_estimate=cheap(),
        name="feed_sums",
    )(side, *parts)


def per_device(
    tokens,
    segments,
    ln1_gain,
    w_query,
    w_key,
    w_value,
    query_gain,
    key_gain,
    w_out,
    ln2_gain,
    w_gate,
    w_up,
    w_down,
    cotangent,
):
    length, model = tokens.shape
    query_cols, key_cols = w_query.shape[1], w_key.shape[1]
    query_heads = query_cols // HD
    kv_local = key_cols // HD
    group = query_heads // kv_local
    size = lax.axis_size("fsdp")
    shard = model // size
    hidden = w_gate.shape[1]
    half = hidden // 2
    strides = bits("fsdp")
    group_size = lax.axis_size(PLANE)
    share_rows = length // group_size
    share_start = lax.axis_index(PLANE) * share_rows
    segment_row = segments[0]

    def share_of(array):
        return lax.dynamic_slice_in_dim(array, share_start, share_rows, 0)

    proj = lax.all_gather(
        jnp.concatenate([w_query, w_key, w_value, w_out], axis=1), "fsdp", axis=0, tiled=True
    )
    side = bit("fsdp", 1)
    place = lax.axis_index("fsdp")[None]

    def half_of(which):
        return jnp.concatenate(
            [lax.dynamic_slice_in_dim(w, which * half, half, 1) for w in (w_gate, w_up, w_down)], axis=1
        )

    mine, given = half_of(side), half_of(1 - side)

    gains = line_gather(jnp.concatenate([ln1_gain, ln2_gain, query_gain, key_gain]), strides)
    gain_attn = gains[:, :shard].reshape(model)
    gain_ffn = gains[:, shard : 2 * shard].reshape(model)
    head_part = HD // size
    query_norm = gains[:, 2 * shard : 2 * shard + head_part].reshape(HD)
    key_norm = gains[:, 2 * shard + head_part :].reshape(HD)

    cosine, sine = rope_tables(doc_positions(segment_row))
    block_in = tokens.astype(jnp.float32)
    scale_one = rms_parts(block_in)
    normed = (block_in * scale_one * gain_attn.astype(jnp.float32)).astype(jnp.bfloat16)
    query_gain_wide, key_gain_wide = wide(query_norm), wide(key_norm)
    weights = Job(weights_gather(mine, given))
    cot = Job(pair_cot(cotangent))
    attend_args = (normed, proj, cosine, sine, query_gain_wide, key_gain_wide, segment_row)
    ((raw, query_rot, key_rot, values, mixed_low, out_part),) = beside(
        weights, kernels=[(functools.partial(attend, group), attend_args)]
    )
    out_sum = Job(plane_scatter(out_part))
    beside(out_sum, weights)
    beside(out_sum, weights)
    beside(out_sum, weights, cot)
    hidden_share = wide(share_of(tokens)) + out_sum.value
    scale_share = rms_parts(hidden_share)
    normed_share = low(hidden_share * scale_share * wide(gain_ffn))
    pair_share = Job(pair_swap(normed_share))
    beside(pair_share, weights)
    gather = Job(plane_gather(jnp.stack([normed_share, pair_share.value])))
    beside(gather, weights, cot)
    beside(gather, weights, cot)
    beside(gather, weights, cot)
    finish(gather, weights, cot)
    normed_two, pair_normed_two = gather.value
    pair_cotangent = cot.value

    pair_act, pair_grad, pair_normed_grad, feed_proj = feed(
        place, pair_normed_two, pair_cotangent, *weights.value
    )
    pair_sum = Job(plane_scatter(pair_normed_grad))
    ((act, grad, normed_grad, _),) = beside(
        pair_sum, kernels=[(feed, (place, normed_two, cotangent, feed_proj))]
    )
    own_sum = Job(plane_scatter(normed_grad))
    weight_args = (
        place, (normed_two, pair_normed_two), (cotangent, pair_cotangent), (grad, pair_grad), (act, pair_act)
    )
    (far,) = beside(
        pair_sum,
        own_sum,
        kernels=[(functools.partial(feed_weights, size, (size // 2, size // 2)), weight_args)],
    )
    near = feed_weights(size, (0, size // 2), *weight_args)
    weight_sums = Job(weights_scatter(near, far))
    beside(pair_sum, own_sum, weight_sums)
    pair_share = Job(pair_swap(low(pair_sum.value)))
    beside(pair_share, own_sum, weight_sums)
    grad_share = own_sum.value + wide(pair_share.value)
    hidden_grad_share = wide(share_of(cotangent)) + norm_back(
        hidden_share, scale_share, grad_share * wide(gain_ffn)
    )
    ffn_gain_part = jnp.sum(grad_share * hidden_share * scale_share, axis=0)
    gather = Job(plane_gather(low(hidden_grad_share)[None]))
    beside(gather, weight_sums)
    beside(gather, weight_sums)
    beside(gather, weight_sums)
    attn_out_grad = gather.value[0]
    down_proj = feed_proj[:, 2 * half :]
    out_sum = Job(plane_scatter(low(contract(act, down_proj, 1, 1))))
    pair_out_sum = Job(plane_scatter(low(contract(pair_act, down_proj, 1, 1))))

    out_w_part = low(contract(attn_out_grad, mixed_low, 0, 0))
    out_w_grad = wide(lax.psum_scatter(out_w_part, "fsdp", scatter_dimension=0, tiled=True))

    back_args = (
        attn_out_grad, proj, cosine, sine, query_gain_wide, key_gain_wide, segment_row,
        raw, query_rot, key_rot, values, tokens, scale_one,
    )
    ((low_grad, normed_part, attn_gain_part, head_gain_part),) = beside(
        weight_sums, pair_out_sum, kernels=[(functools.partial(attend_back, group), back_args)]
    )
    query_gain_part, key_gain_part = head_gain_part[0], head_gain_part[1]
    attn_w_part = low(contract(normed, low_grad, 0, 0))
    attn_w_grad = wide(lax.psum_scatter(attn_w_part, "fsdp", scatter_dimension=0, tiled=True))
    normed_sum = Job(plane_scatter(normed_part))
    beside(normed_sum, weight_sums, pair_out_sum, out_sum)
    beside(normed_sum, weight_sums, pair_out_sum, out_sum)
    pair_out = Job(pair_swap(low(pair_out_sum.value)))
    beside(normed_sum, weight_sums, pair_out, out_sum)
    finish(weight_sums, pair_out, out_sum)
    normed_share = normed_sum.value
    block_out = low(hidden_share + out_sum.value + wide(pair_out.value))
    gate_w_grad, up_w_grad, down_w_grad = feed_sums(side[None], *weight_sums.value)

    token_share = wide(share_of(tokens))
    scale_one_share = share_of(scale_one)
    tokens_grad = (
        hidden_grad_share + norm_back(token_share, scale_one_share, normed_share * wide(gain_attn))
    ).astype(jnp.bfloat16)

    gain_sums = jnp.concatenate(
        [
            attn_gain_part.reshape(size, shard),
            ffn_gain_part.reshape(size, shard),
            query_gain_part.reshape(size, head_part),
            key_gain_part.reshape(size, head_part),
        ],
        axis=1,
    )
    gain_sums = sum_small(sum_small(sum_small(gain_sums, "tensor"), "heads"), "fsdp")
    gain_sums = pick(gain_sums, lax.axis_index("fsdp"), 0)
    ln1_grad = gain_sums[:shard]
    ln2_grad = gain_sums[shard : 2 * shard]
    query_gain_grad = gain_sums[2 * shard : 2 * shard + head_part]
    key_gain_grad = gain_sums[2 * shard + head_part :]

    return (
        block_out,
        tokens_grad,
        ln1_grad,
        attn_w_grad[:, :query_cols],
        attn_w_grad[:, query_cols : query_cols + key_cols],
        attn_w_grad[:, query_cols + key_cols :],
        query_gain_grad,
        key_gain_grad,
        out_w_grad,
        ln2_grad,
        gate_w_grad,
        up_w_grad,
        down_w_grad,
    )


def solution(mesh):
    in_specs = (
        P("fsdp", None),
        P("fsdp", None),
        P("fsdp"),
        P("fsdp", ("heads", "tensor")),
        P("fsdp", ("heads", "tensor")),
        P("fsdp", ("heads", "tensor")),
        P("fsdp"),
        P("fsdp"),
        P("fsdp", ("heads", "tensor")),
        P("fsdp"),
        P("fsdp", ("heads", "tensor")),
        P("fsdp", ("heads", "tensor")),
        P("fsdp", ("heads", "tensor")),
        P("fsdp", None),
    )
    out_specs = (
        P(("fsdp", "heads", "tensor"), None),
        P(("fsdp", "heads", "tensor"), None),
        P("fsdp"),
        P("fsdp", ("heads", "tensor")),
        P("fsdp", ("heads", "tensor")),
        P("fsdp", ("heads", "tensor")),
        P("fsdp"),
        P("fsdp"),
        P("fsdp", ("heads", "tensor")),
        P("fsdp"),
        P("fsdp", ("heads", "tensor")),
        P("fsdp", ("heads", "tensor")),
        P("fsdp", ("heads", "tensor")),
    )
    return jax.shard_map(
        per_device, mesh=mesh, in_specs=in_specs, out_specs=out_specs, check_vma=False
    )
```

time: 1060 us -> 620 us (0.58)
  waiting for transfers between devices: 642 us -> 268 us
  matrix products: 157 us -> 15.9 us
  blocking collectives: 96.9 us -> 0 us
  starting transfers between devices: 1.44 us -> 83.3 us
  Pallas kernels: 0 us -> 76.7 us
  local copies, waits for them, and re-layouts: 31.4 us -> 68.4 us
  other arithmetic: 98.1 us -> 84.2 us
    reduce_scatter x8 -> x2, waiting for transfers between devices: 244 us -> 0.02 us  [the longest x1 0.02 us: per_device(): lax.psum_scatter(out_w_part, 'fsdp', scatter_dimension=0, tiled=True)]
    psum x3 -> x0, waiting for transfers between devices: 230 us -> none  [the longest x1 111 us: per_device(): lax.psum(contract(mixed_low, output_proj, 1, 1), ('heads', 'tensor'))]
    ppermute x0 -> x78, waiting for transfers between devices: none -> 222 us  [the longest x71 214 us: beside(): lax.ppermute(array, *move[1:])]
    all_gather x5 -> x1, waiting for transfers between devices: 164 us -> 45.4 us  [per_device(): lax.all_gather(jnp.concatenate([w_query, w_key, w_value, w_out], axis=1),...]
    ppermute x0 -> x78, starting transfers between devices: none -> 83.2 us  [the longest x71 75.1 us: beside(): lax.ppermute(array, *move[1:])]
    pallas_call x0 -> x7, Pallas kernels: none -> 76.7 us  [the longest x2 25.6 us: feed(): pl.pallas_call(functools.partial(feed_kernel, layout, shard), grid_spec=p...]
    dot_general x21 -> x0, matrix products: 74.8 us -> none  [the longest x4 11.4 us: scores_of(): jnp.einsum('qkgd,skd->kgqs', query_block, key_rot, preferred_element_type...]
    dot_general x14 -> x4, matrix products: 82.1 us -> 15.9 us  [contract(): lax.dot_general(left, right, (((left_dim,), (right_dim,)), ((), ())), pre...]
  transfers between devices with their start and end apart: 16 -> 81, of which waited for: 12 -> 38; matrix products, arithmetic and copies ran while one was open for 18% -> 16% of each run, Pallas kernels for 0% -> 10%
where the time goes in v1:
time: 620 us; the launch traced here: 612 us
  waiting for transfers between devices  268 us (43%)
  other arithmetic  84.2 us (14%)
  starting transfers between devices  83.3 us (13%)
  Pallas kernels  76.7 us (12%)
  local copies, waits for them, and re-layouts  68.4 us (11%)
  matrix products  15.9 us (3%)
  between operations  15.8 us (3%)
    ppermute x71, waiting for transfers between devices, beside(): lax.ppermute(array, *move[1:])  214 us
    ppermute x71, starting transfers between devices, beside(): lax.ppermute(array, *move[1:])  75.1 us
    all_gather x1, waiting for transfers between devices, per_device(): lax.all_gather(jnp.concatenate([w_query, w_key, w_value, w_out], axis=1),...  45.4 us
    convert_element_type x22, other arithmetic, low(): return values.astype(jnp.bfloat16)  30.3 us
    pallas_call x2, Pallas kernels, feed(): pl.pallas_call(functools.partial(feed_kernel, layout, shard), grid_spec=p...  25.6 us
    squeeze x30, local copies, waits for them, and re-layouts, pick(): return lax.dynamic_index_in_dim(array, index, axis, keepdims=False)  20.5 us
    unnamed x185, local copies, waits for them, and re-layouts  18.7 us
    pallas_call x2, Pallas kernels, feed_weights(): pl.pallas_call(functools.partial(feed_weights_kernel, slots), grid_spec=p...  18.4 us
  transfers between devices with their start and end apart: 81, of which 38 were waited for; matrix products, arithmetic and copies ran while one was open for 16% of the time, Pallas kernels for 10%

profile of v1, /device:TPU:0, one launch (start us, length us, event | category | flops | bytes accessed | tf_op | source)
XLA Modules:
  0.0 611.9 jit_solution(12937457901309241823)
XLA Ops:
  7.3 2.9 concatenate.57
  10.2 3.0 collective-permute-start
  17.8 3.0 fusion.40
  23.7 2.7 collective-permute-start.1
  28.7 5.3 fusion.2.normed_ref
  34.0 45.4 %all-gather.2.cloned.1.call-done.proj_ref = bf16[2048,768]{1,0:T(8,128)(2,1)} async-done(((bf16[512,768]{1,0:T(8,128)(2,1)}), bf16[2048,768]{1,0:T(8,128)(2,1)}) %all-gather.2.cloned.1.call-update) | async-done | bytes 3145744 | tf_op jit(solution)/shard_map/all_gather | solution.py:687
  82.9 12.1 %attend.1 = (f32[1024,384]{1,0:T(8,128)S(1)}, bf16[1024,256]{1,0:T(8,128)(2,1)S(1)}, bf16[1024,128]{1,0:T(8,128)(2,1)S(1)}, bf16[1024,128]{1,0:T(8,128)(2,1)S(1)...) custom-call(bf16[1024,2048]{1,0:T(8,128)(2,1)} %fusion.2.normed_ref, bf16[2048,768]{1,0:T(8,128)(2,1)S(1)} %copy-done.1, ...), custom_call_target="tpu_custom_call" | custom-call | flops 1000 | bytes 1000 | tf_op jit(solution)/shard_map/attend/pallas_call | solution.py:372
  103.1 8.3 %collective-permute-done.5.refs_4_ = bf16[64,1152]{1,0:T(8,128)(2,1)S(1)} collective-permute-done((bf16[64,1152]{1,0:T(8,128)(2,1)S(1)}, bf16[64,1152]{1,0:T(8,128)(2,1)S(1)}, u32[]{:S(2)}, u32[]{:S(2)}) %collective-permute-start.5) | collective-permute-done | bytes 147488 | tf_op jit(solution)/shard_map/ppermute | solution.py:85
  111.4 3.1 fusion.9
  121.2 3.0 constant_dynamic-slice_fusion.5
  124.2 12.3 %collective-permute-done.8.refs_5_ = bf16[144,1152]{1,0:T(8,128)(2,1)} collective-permute-done((bf16[144,1152]{1,0:T(8,128)(2,1)}, bf16[144,1152]{1,0:T(8,128)(2,1)}, u32[]{:S(2)}, u32[]{:S(2)}) %collective-permute-start.8) | collective-permute-done | bytes 331808 | tf_op jit(solution)/shard_map/ppermute | solution.py:85
  148.3 10.0 %collective-permute-done.12.refs_6_ = bf16[96,1152]{1,0:T(8,128)(2,1)} collective-permute-done((bf16[96,1152]{1,0:T(8,128)(2,1)}, bf16[96,1152]{1,0:T(8,128)(2,1)}, u32[]{:S(2)}, u32[]{:S(2)}) %collective-permute-start.12) | collective-permute-done | bytes 221216 | tf_op jit(solution)/shard_map/ppermute | solution.py:85
  167.1 13.9 %collective-permute-done.15.refs_7_ = bf16[112,1152]{1,0:T(8,128)(2,1)S(1)} collective-permute-done((bf16[112,1152]{1,0:T(8,128)(2,1)S(1)}, bf16[112,1152]{1,0:T(8,128)(2,1)S(1)}, u32[]{:S(2)}, u32[]{:S(2)}) %collective-permute-start.15) | collective-permute-done | bytes 258080 | tf_op jit(solution)/shard_map/ppermute | solution.py:85
  189.3 13.9 %collective-permute-done.18.refs_8_ = bf16[144,1152]{1,0:T(8,128)(2,1)S(1)} collective-permute-done((bf16[144,1152]{1,0:T(8,128)(2,1)}, bf16[144,1152]{1,0:T(8,128)(2,1)S(1)}, u32[]{:S(2)}, u32[]{:S(2)}) %collective-permute-start.18) | collective-permute-done | bytes 331808 | tf_op jit(solution)/shard_map/ppermute | solution.py:85
  208.1 3.3 collective-permute-start.24
  211.4 2.9 collective-permute-start.22
  214.3 18.7 %collective-permute-done.22.refs_9_ = bf16[112,1152]{1,0:T(8,128)(2,1)S(1)} collective-permute-done((bf16[112,1152]{1,0:T(8,128)(2,1)S(1)}, bf16[112,1152]{1,0:T(8,128)(2,1)S(1)}, u32[]{:S(2)}, u32[]{:S(2)}) %collective-permute-start.22) | collective-permute-done | bytes 258080 | tf_op jit(solution)/shard_map/ppermute | solution.py:85
  243.4 11.7 %collective-permute-done.26.refs_11_ = bf16[128,1152]{1,0:T(8,128)(2,1)S(1)} collective-permute-done((bf16[128,1152]{1,0:T(8,128)(2,1)S(1)}, bf16[128,1152]{1,0:T(8,128)(2,1)S(1)}, u32[]{:S(2)}, u32[]{:S(2)}) %collective-permute-start.26) | collective-permute-done | bytes 294944 | tf_op jit(solution)/shard_map/ppermute | solution.py:85
  258.2 4.5 select_bitcast_fusion
  266.2 4.0 select_bitcast_fusion.5
  272.6 12.9 %feed.2 = (bf16[1024,384]{1,0:T(8,128)(2,1)S(1)}, bf16[1024,768]{1,0:T(8,128)(2,1)S(1)}, bf16[1024,2048]{1,0:T(8,128)(2,1)S(1)}, bf16[2048,1152]{1,0:T(8,128)(2,1)}) custom-call(s32[1]{0:T(128)} %bitcast.26.place_ref, bf16[1024,2048]{1,0:T(8,128)(2,1)} %bitcast.358, bf16[1024,2048]{1,0:T(8,128)(2,1)} %bitcast.361, ...), custom_call_target="tpu_custom_call" | custom-call | flops 1000 | bytes 1000 | tf_op jit(solution)/shard_map/feed/pallas_call | solution.py:563
  286.4 12.6 %feed.3 = (bf16[1024,384]{1,0:T(8,128)(2,1)S(1)}, bf16[1024,768]{1,0:T(8,128)(2,1)S(1)}, bf16[1024,2048]{1,0:T(8,128)(2,1)S(1)}, bf16[16,128]{1,0:T(8,128)(2,1)}) custom-call(s32[1]{0:T(128)} %bitcast.26.place_ref, bf16[1024,2048]{1,0:T(8,128)(2,1)S(1)} %bitcast.341, bf16[1024,2048]{1,0:T(8,128)(2,1)} %cot_own.2, bf16[2048,1152]{1,0:T(8,128)(2,1)} %get-tuple-element.292.refs_0_), custom_call_target="tpu_custom_call" | custom-call | flops 1000 | bytes 1000 | tf_op jit(solution)/shard_map/feed/pallas_call | solution.py:563
  305.4 9.2 %feed_weights.2 = bf16[2,512,1152]{2,1,0:T(8,128)(2,1)} custom-call(s32[1]{0:T(128)} %bitcast.26.place_ref, bf16[1024,2048]{1,0:T(8,128)(2,1)} %bitcast.342, bf16[1024,2048]{1,0:T(8,128)(2,1)} %bitcast.359, bf16[1024,2048]{1,0:T(8,128)(2,1)} %cot_own.2, bf16[1024,2048]{1,0:T(8,128)(2,1)} %bitcast.362, bf16[1024,768]{1,0:T(8,128)(2,1)S(1)} %get-tuple-element.310.grad_own, ...), custom_call_target="tpu_custom_call" | custom-call | flops 1000 | bytes 1000 | tf_op jit(solution)/shard_map/feed_weights/pallas_call | solution.py:602
  329.9 12.4 %collective-permute-done.33 = bf16[128,1024]{1,0:T(8,128)(2,1)S(1)} collective-permute-done((bf16[128,1024]{1,0:T(8,128)(2,1)S(1)}, bf16[128,1024]{1,0:T(8,128)(2,1)S(1)}, u32[]{:S(2)}, u32[]{:S(2)}) %collective-permute-start.33) | collective-permute-done | bytes 262176 | tf_op jit(solution)/shard_map/ppermute | solution.py:85
  349.8 3.4 collective-permute-done.39
  354.7 8.1 %collective-permute-done.41 = bf16[128,1152]{1,0:T(8,128)(2,1)S(1)} collective-permute-done((bf16[128,1152]{1,0:T(8,128)(2,1)S(1)}, bf16[128,1152]{1,0:T(8,128)(2,1)S(1)}, u32[]{:S(2)}, u32[]{:S(2)}) %collective-permute-start.41) | collective-permute-done | bytes 294944 | tf_op jit(solution)/shard_map/ppermute | solution.py:85
  372.3 8.8 %collective-permute-done.44 = bf16[96,1152]{1,0:T(8,128)(2,1)S(1)} collective-permute-done((bf16[96,1152]{1,0:T(8,128)(2,1)S(1)}, bf16[96,1152]{1,0:T(8,128)(2,1)S(1)}, u32[]{:S(2)}, u32[]{:S(2)}) %collective-permute-start.44) | collective-permute-done | bytes 221216 | tf_op jit(solution)/shard_map/ppermute | solution.py:85
  383.8 9.2 %feed_weights.3 = bf16[2,512,1152]{2,1,0:T(8,128)(2,1)} custom-call(s32[1]{0:T(128)} %bitcast.26.place_ref, bf16[1024,2048]{1,0:T(8,128)(2,1)} %bitcast.343, bf16[1024,2048]{1,0:T(8,128)(2,1)} %bitcast.360, bf16[1024,2048]{1,0:T(8,128)(2,1)} %cot_own.2, bf16[1024,2048]{1,0:T(8,128)(2,1)} %bitcast.363, bf16[1024,768]{1,0:T(8,128)(2,1)S(1)} %get-tuple-element.310.grad_own, ...), custom_call_target="tpu_custom_call" | custom-call | flops 1000 | bytes 1000 | tf_op jit(solution)/shard_map/feed_weights/pallas_call | solution.py:602
  394.1 10.6 %collective-permute-done.47 = bf16[128,1152]{1,0:T(8,128)(2,1)S(1)} collective-permute-done((bf16[128,1152]{1,0:T(8,128)(2,1)S(1)}, bf16[128,1152]{1,0:T(8,128)(2,1)S(1)}, u32[]{:S(2)}, u32[]{:S(2)}) %collective-permute-start.47) | collective-permute-done | bytes 294944 | tf_op jit(solution)/shard_map/ppermute | solution.py:85
  405.5 3.8 convolution_convert_fusion
  415.8 8.6 %collective-permute-done.49 = bf16[96,1152]{1,0:T(8,128)(2,1)S(1)} collective-permute-done((bf16[96,1152]{1,0:T(8,128)(2,1)S(1)}, bf16[96,1152]{1,0:T(8,128)(2,1)S(1)}, u32[]{:S(2)}, u32[]{:S(2)}) %collective-permute-start.49) | collective-permute-done | bytes 221216 | tf_op jit(solution)/shard_map/ppermute | solution.py:85
  424.4 3.4 collective-permute-done.50.refs_4_
  429.7 2.7 copy.47
  432.4 3.8 convolution_convert_fusion.1
  438.2 2.5 collective-permute-start.52
  444.9 18.3 %attend_back.1 = (bf16[1024,512]{1,0:T(8,128)(2,1)S(1)}, bf16[1024,2048]{1,0:T(8,128)(2,1)}, f32[1,2048]{1,0:T(1,128)S(1)}, f32[2,128]{1,0:T(2,128)S(1)}) custom-call(bf16[1024,2048]{1,0:T(8,128)(2,1)} %bitcast.364, bf16[2048,768]{1,0:T(8,128)(2,1)} %all-gather.2.cloned.1.call-done.proj_ref, f32[1024,128]{1,0:T(8,128)S(1)} %get-tuple-element.359.cosine_ref, ...), custom_call_target="tpu_custom_call" | custom-call | flops 1000 | bytes 1000 | tf_op jit(solution)/shard_map/attend_back/pallas_call | solution.py:490
  464.8 3.3 dynamic-slice_bitcast_fusion.1
  478.1 3.1 collective-permute-done.74
  493.7 4.5 convolution_convert_fusion.3
  498.3 6.5 %collective-permute-done.55 = bf16[128,1152]{1,0:T(8,128)(2,1)} collective-permute-done((bf16[128,1152]{1,0:T(8,128)(2,1)S(1)}, bf16[128,1152]{1,0:T(8,128)(2,1)}, u32[]{:S(2)}, u32[]{:S(2)}) %collective-permute-start.55) | collective-permute-done | bytes 294944 | tf_op jit(solution)/shard_map/ppermute | solution.py:85
  504.8 3.0 fusion.4
  513.4 2.6 fusion.8
  520.8 3.0 collective-permute-start.62
  525.3 3.8 convolution_convert_fusion.2
  531.7 3.9 collective-permute-done.62
  541.6 8.3 %collective-permute-done.65 = bf16[128,1024]{1,0:T(8,128)(2,1)} collective-permute-done((bf16[128,1024]{1,0:T(8,128)(2,1)}, bf16[128,1024]{1,0:T(8,128)(2,1)}, u32[]{:S(2)}, u32[]{:S(2)}) %collective-permute-start.65) | collective-permute-done | bytes 262176 | tf_op jit(solution)/shard_map/ppermute | solution.py:85
  550.5 19.7 %collective-permute-done.63.refs_7_ = bf16[128,1152]{1,0:T(8,128)(2,1)S(1)} collective-permute-done((bf16[128,1152]{1,0:T(8,128)(2,1)S(1)}, bf16[128,1152]{1,0:T(8,128)(2,1)S(1)}, u32[]{:S(2)}, u32[]{:S(2)}) %collective-permute-start.63) | collective-permute-done | bytes 294944 | tf_op jit(solution)/shard_map/ppermute | solution.py:85
  587.8 8.6 %collective-permute-done.70 = bf16[128,2048]{1,0:T(8,128)(2,1)S(1)} collective-permute-done((bf16[128,2048]{1,0:T(8,128)(2,1)S(1)}, bf16[128,2048]{1,0:T(8,128)(2,1)S(1)}, u32[]{:S(2)}, u32[]{:S(2)}) %collective-permute-start.70) | collective-permute-done | bytes 524320 | tf_op jit(solution)/shard_map/ppermute | solution.py:85
  (488 shorter events, 211.5 us)
Async XLA Ops:
  7.2 72.1 %all-gather.2.cloned.1.call-start = ((), (), s32[]{:S(2)}) async-start(), calls=%async_computation.2 | async-start | bytes 3932160 | tf_op jit(solution)/shard_map/all_gather | solution.py:687
  15.4 524.3 %reduce-scatter.5.cloned.1.call-start = ((), (), s32[]{:S(2)}) async-start(), calls=%async_computation.4 | async-start | bytes 1310720 | tf_op jit(solution)/shard_map/reduce_scatter | solution.py:771
  79.3 20.0 %collective-permute-start.3 = (bf16[256,1152]{1,0:T(8,128)(2,1)}, bf16[256,1152]{1,0:T(8,128)(2,1)S(1)}, u32[]{:S(2)}, u32[]{:S(2)}) collective-permute-start(bf16[256,1152]{1,0:T(8,128)(2,1)} %get-tuple-element.221), channel_id=1, source_target_pairs={{0,8},{8,0},{16,24},{24,16},{1,9},{9,1},{17,25},{25,17},{2,10},{10... | collective-permute-start | bytes 1769480 | tf_op jit(solution)/shard_map/ppermute | solution.py:85
  79.4 17.9 %collective-permute-start.2 = (bf16[96,1152]{1,0:T(8,128)(2,1)}, bf16[96,1152]{1,0:T(8,128)(2,1)}, u32[]{:S(2)}, u32[]{:S(2)}) collective-permute-start(bf16[96,1152]{1,0:T(8,128)(2,1)} %get-tuple-element.220), channel_id=1, source_target_pairs={{0,16},{8,24},{16,0},{24,8},{1,17},{9,25},{17,1},{25,9},{2,18},{10... | collective-permute-start | bytes 663560 | tf_op jit(solution)/shard_map/ppermute | solution.py:85
  116.4 22.3 %collective-permute-start.9 = (bf16[256,1152]{1,0:T(8,128)(2,1)}, bf16[256,1152]{1,0:T(8,128)(2,1)S(1)}, u32[]{:S(2)}, u32[]{:S(2)}) collective-permute-start(bf16[256,1152]{1,0:T(8,128)(2,1)} %get-tuple-element.242), channel_id=1, source_target_pairs={{0,8},{8,0},{16,24},{24,16},{1,9},{9,1},{17,25},{25,17},{2,10},{10... | collective-permute-start | bytes 1769480 | tf_op jit(solution)/shard_map/ppermute | solution.py:85
  116.4 20.2 %collective-permute-start.6 = (bf16[2,128,1024]{2,1,0:T(8,128)(2,1)}, bf16[2,128,1024]{2,1,0:T(8,128)(2,1)}, u32[]{:S(2)}, u32[]{:S(2)}) collective-permute-start(bf16[2,128,1024]{2,1,0:T(8,128)(2,1)} %dynamic-slice_bitcast_fusion.17), channel_id=1, source_target_pairs={{0,2},{2,0},{4,6},{6,4},{1,3},{3,1},{5,7},{7,5},{8,10},{10,8},{12,... | collective-permute-start | bytes 1572872 | tf_op jit(solution)/shard_map/ppermute | solution.py:85
  118.0 18.5 %collective-permute-start.7 = (bf16[2,128,1024]{2,1,0:T(8,128)(2,1)}, bf16[2,128,1024]{2,1,0:T(8,128)(2,1)}, u32[]{:S(2)}, u32[]{:S(2)}) collective-permute-start(bf16[2,128,1024]{2,1,0:T(8,128)(2,1)} %dynamic-slice_bitcast_fusion.16), channel_id=1, source_target_pairs={{0,4},{4,0},{2,6},{6,2},{1,5},{5,1},{3,7},{7,3},{8,12},{12,8},{10,... | collective-permute-start | bytes 1572872 | tf_op jit(solution)/shard_map/ppermute | solution.py:85
  119.5 17.1 %collective-permute-start.8 = (bf16[144,1152]{1,0:T(8,128)(2,1)}, bf16[144,1152]{1,0:T(8,128)(2,1)}, u32[]{:S(2)}, u32[]{:S(2)}) collective-permute-start(bf16[144,1152]{1,0:T(8,128)(2,1)} %slice.296), channel_id=1, source_target_pairs={{0,16},{8,24},{16,0},{24,8},{1,17},{9,25},{17,1},{25,9},{2,18},{10... | collective-permute-start | bytes 995336 | tf_op jit(solution)/shard_map/ppermute | solution.py:85
  142.8 17.7 %collective-permute-start.13 = (bf16[128,2048]{1,0:T(8,128)(2,1)}, bf16[128,2048]{1,0:T(8,128)(2,1)}, u32[]{:S(2)}, u32[]{:S(2)}) collective-permute-start(bf16[128,2048]{1,0:T(8,128)(2,1)} %get-tuple-element.248), channel_id=1, source_target_pairs={{0,8},{8,0},{16,24},{24,16},{1,9},{9,1},{17,25},{25,17},{2,10},{10... | collective-permute-start | bytes 1572872 | tf_op jit(solution)/shard_map/ppermute | solution.py:85
  164.2 17.5 %collective-permute-start.14 = (bf16[128,2048]{1,0:T(8,128)(2,1)S(1)}, bf16[128,2048]{1,0:T(8,128)(2,1)S(1)}, u32[]{:S(2)}, u32[]{:S(2)}) collective-permute-start(bf16[128,2048]{1,0:T(8,128)(2,1)S(1)} %multiply_convert_fusion), channel_id=1, source_target_pairs={{0,8},{8,0},{16,24},{24,16},{1,9},{9,1},{17,25},{25,17},{2,10},{10... | collective-permute-start | bytes 1572872 | tf_op jit(solution)/shard_map/ppermute | solution.py:85
  182.8 21.1 %collective-permute-start.16 = (bf16[2,128,1024]{2,1,0:T(8,128)(2,1)}, bf16[2,128,1024]{2,1,0:T(8,128)(2,1)}, u32[]{:S(2)}, u32[]{:S(2)}) collective-permute-start(bf16[2,128,1024]{2,1,0:T(8,128)(2,1)} %get-tuple-element.255), channel_id=1, source_target_pairs={{0,4},{4,0},{2,6},{6,2},{1,5},{5,1},{3,7},{7,3},{8,12},{12,8},{10,... | collective-permute-start | bytes 1572872 | tf_op jit(solution)/shard_map/ppermute | solution.py:85
  184.4 19.6 %collective-permute-start.17 = (bf16[2,128,1024]{2,1,0:T(8,128)(2,1)}, bf16[2,128,1024]{2,1,0:T(8,128)(2,1)}, u32[]{:S(2)}, u32[]{:S(2)}) collective-permute-start(bf16[2,128,1024]{2,1,0:T(8,128)(2,1)} %get-tuple-element.256), channel_id=1, source_target_pairs={{0,2},{2,0},{4,6},{6,4},{1,3},{3,1},{5,7},{7,5},{8,10},{10,8},{12,... | collective-permute-start | bytes 1572872 | tf_op jit(solution)/shard_map/ppermute | solution.py:85
  186.2 18.3 %collective-permute-start.19 = (bf16[128,2048]{1,0:T(8,128)(2,1)}, bf16[128,2048]{1,0:T(8,128)(2,1)}, u32[]{:S(2)}, u32[]{:S(2)}) collective-permute-start(bf16[128,2048]{1,0:T(8,128)(2,1)} %get-tuple-element.258), channel_id=1, source_target_pairs={{0,8},{8,0},{16,24},{24,16},{1,9},{9,1},{17,25},{25,17},{2,10},{10... | collective-permute-start | bytes 1572872 | tf_op jit(solution)/shard_map/ppermute | solution.py:85
  207.4 27.1 %collective-permute-start.20 = (bf16[2,2,128,1024]{3,2,0,1:T(8,128)(2,1)S(1)}, bf16[2,2,128,1024]{3,2,0,1:T(8,128)(2,1)S(1)}, u32[]{:S(2)}, u32[]{:S(2)}) collective-permute-start(bf16[2,2,128,1024]{3,2,0,1:T(8,128)(2,1)S(1)} %pad_maximum_fusion.5), channel_id=1, source_target_pairs={{0,2},{2,0},{4,6},{6,4},{1,3},{3,1},{5,7},{7,5},{8,10},{10,8},{12,... | collective-permute-start | bytes 3145736 | tf_op jit(solution)/shard_map/ppermute | solution.py:85
  207.7 26.7 %collective-permute-start.21 = (bf16[2,2,128,1024]{3,2,0,1:T(8,128)(2,1)S(1)}, bf16[2,2,128,1024]{3,2,0,1:T(8,128)(2,1)S(1)}, u32[]{:S(2)}, u32[]{:S(2)}) collective-permute-start(bf16[2,2,128,1024]{3,2,0,1:T(8,128)(2,1)S(1)} %pad_maximum_fusion.6), channel_id=1, source_target_pairs={{0,4},{4,0},{2,6},{6,2},{1,5},{5,1},{3,7},{7,3},{8,12},{12,8},{10,... | collective-permute-start | bytes 3145736 | tf_op jit(solution)/shard_map/ppermute | solution.py:85
  208.1 26.4 %collective-permute-start.24 = (bf16[128,2048]{1,0:T(8,128)(2,1)S(1)}, bf16[128,2048]{1,0:T(8,128)(2,1)S(1)}, u32[]{:S(2)}, u32[]{:S(2)}) collective-permute-start(bf16[128,2048]{1,0:T(8,128)(2,1)S(1)} %copy-done.72), channel_id=1, source_target_pairs={{0,8},{8,0},{16,24},{24,16},{1,9},{9,1},{17,25},{25,17},{2,10},{10... | collective-permute-start | bytes 1572872 | tf_op jit(solution)/shard_map/ppermute | solution.py:85
  211.4 22.3 %collective-permute-start.23 = (bf16[128,1152]{1,0:T(8,128)(2,1)S(1)}, bf16[128,1152]{1,0:T(8,128)(2,1)S(1)}, u32[]{:S(2)}, u32[]{:S(2)}) collective-permute-start(bf16[128,1152]{1,0:T(8,128)(2,1)S(1)} %get-tuple-element.265), channel_id=1, source_target_pairs={{0,16},{8,24},{16,0},{24,8},{1,17},{9,25},{17,1},{25,9},{2,18},{10... | collective-permute-start | bytes 884744 | tf_op jit(solution)/shard_map/ppermute | solution.py:85
  211.4 21.6 %collective-permute-start.22 = (bf16[112,1152]{1,0:T(8,128)(2,1)S(1)}, bf16[112,1152]{1,0:T(8,128)(2,1)S(1)}, u32[]{:S(2)}, u32[]{:S(2)}) collective-permute-start(bf16[112,1152]{1,0:T(8,128)(2,1)S(1)} %slice.240), channel_id=1, source_target_pairs={{0,16},{8,24},{16,0},{24,8},{1,17},{9,25},{17,1},{25,9},{2,18},{10... | collective-permute-start | bytes 774152 | tf_op jit(solution)/shard_map/ppermute | solution.py:85
  236.6 20.7 %collective-permute-start.25 = (bf16[2,2,2,128,2048]{4,3,0,2,1:T(8,128)(2,1)S(1)}, bf16[2,2,2,128,2048]{4,3,0,2,1:T(8,128)(2,1)}, u32[]{:S(2)}, u32[]{:S(2)}) collective-permute-start(bf16[2,2,2,128,2048]{4,3,0,2,1:T(8,128)(2,1)S(1)} %maximum_maximum_fusion), channel_id=1, source_target_pairs={{0,1},{1,0},{2,3},{3,2},{4,5},{5,4},{6,7},{7,6},{8,9},{9,8},{10,11... | collective-permute-start | bytes 12582920 | tf_op jit(solution)/shard_map/ppermute | solution.py:85
  236.6 20.7 %collective-permute-start.27 = (bf16[128,2048]{1,0:T(8,128)(2,1)S(1)}, bf16[128,2048]{1,0:T(8,128)(2,1)S(1)}, u32[]{:S(2)}, u32[]{:S(2)}) collective-permute-start(bf16[128,2048]{1,0:T(8,128)(2,1)S(1)} %copy-done.71), channel_id=1, source_target_pairs={{0,8},{8,0},{16,24},{24,16},{1,9},{9,1},{17,25},{25,17},{2,10},{10... | collective-permute-start | bytes 1572872 | tf_op jit(solution)/shard_map/ppermute | solution.py:85
  238.5 16.6 %collective-permute-start.26 = (bf16[128,1152]{1,0:T(8,128)(2,1)S(1)}, bf16[128,1152]{1,0:T(8,128)(2,1)S(1)}, u32[]{:S(2)}, u32[]{:S(2)}) collective-permute-start(bf16[128,1152]{1,0:T(8,128)(2,1)S(1)} %get-tuple-element.270), channel_id=1, source_target_pairs={{0,16},{8,24},{16,0},{24,8},{1,17},{9,25},{17,1},{25,9},{2,18},{10... | collective-permute-start | bytes 884744 | tf_op jit(solution)/shard_map/ppermute | solution.py:85
  302.0 16.1 %collective-permute-start.32 = (bf16[2,2,128,2048]{3,2,1,0:T(8,128)(2,1)S(1)}, bf16[2,2,128,2048]{3,2,1,0:T(8,128)(2,1)S(1)}, u32[]{:S(2)}, u32[]{:S(2)}) collective-permute-start(bf16[2,2,128,2048]{3,2,1,0:T(8,128)(2,1)S(1)} %dynamic-slice_bitcast_fusion.3), channel_id=1, source_target_pairs={{0,1},{1,0},{2,3},{3,2},{4,5},{5,4},{6,7},{7,6},{8,9},{9,8},{10,11... | collective-permute-start | bytes 6291464 | tf_op jit(solution)/shard_map/ppermute | solution.py:85
  323.1 21.6 %collective-permute-start.35 = (bf16[2,128,1024]{2,1,0:T(8,128)(2,1)S(1)}, bf16[2,128,1024]{2,1,0:T(8,128)(2,1)S(1)}, u32[]{:S(2)}, u32[]{:S(2)}) collective-permute-start(bf16[2,128,1024]{2,1,0:T(8,128)(2,1)S(1)} %dynamic-slice_bitcast_fusion.13), channel_id=1, source_target_pairs={{0,2},{2,0},{4,6},{6,4},{1,3},{3,1},{5,7},{7,5},{8,10},{10,8},{12,... | collective-permute-start | bytes 1572872 | tf_op jit(solution)/shard_map/ppermute | solution.py:85
  323.6 21.1 %collective-permute-start.36 = (bf16[2,128,1024]{2,1,0:T(8,128)(2,1)S(1)}, bf16[2,128,1024]{2,1,0:T(8,128)(2,1)S(1)}, u32[]{:S(2)}, u32[]{:S(2)}) collective-permute-start(bf16[2,128,1024]{2,1,0:T(8,128)(2,1)S(1)} %dynamic-slice_bitcast_fusion.12), channel_id=1, source_target_pairs={{0,4},{4,0},{2,6},{6,2},{1,5},{5,1},{3,7},{7,3},{8,12},{12,8},{10,... | collective-permute-start | bytes 1572872 | tf_op jit(solution)/shard_map/ppermute | solution.py:85
  325.2 17.1 %collective-permute-start.33 = (bf16[128,1024]{1,0:T(8,128)(2,1)S(1)}, bf16[128,1024]{1,0:T(8,128)(2,1)S(1)}, u32[]{:S(2)}, u32[]{:S(2)}) collective-permute-start(bf16[128,1024]{1,0:T(8,128)(2,1)S(1)} %dynamic-slice_bitcast_fusion.27), channel_id=1, source_target_pairs={{0,4},{4,0},{2,6},{6,2},{1,5},{5,1},{3,7},{7,3},{8,12},{12,8},{10,... | collective-permute-start | bytes 786440 | tf_op jit(solution)/shard_map/ppermute | solution.py:85
  325.6 16.7 %collective-permute-start.34 = (bf16[128,1024]{1,0:T(8,128)(2,1)S(1)}, bf16[128,1024]{1,0:T(8,128)(2,1)S(1)}, u32[]{:S(2)}, u32[]{:S(2)}) collective-permute-start(bf16[128,1024]{1,0:T(8,128)(2,1)S(1)} %dynamic-slice_bitcast_fusion.26), channel_id=1, source_target_pairs={{0,2},{2,0},{4,6},{6,4},{1,3},{3,1},{5,7},{7,5},{8,10},{10,8},{12,... | collective-permute-start | bytes 786440 | tf_op jit(solution)/shard_map/ppermute | solution.py:85
  327.2 17.5 %collective-permute-start.37 = (bf16[160,1152]{1,0:T(8,128)(2,1)S(1)}, bf16[160,1152]{1,0:T(8,128)(2,1)S(1)}, u32[]{:S(2)}, u32[]{:S(2)}) collective-permute-start(bf16[160,1152]{1,0:T(8,128)(2,1)S(1)} %slice_bitcast_fusion.3), channel_id=1, source_target_pairs={{0,16},{8,24},{16,0},{24,8},{1,17},{9,25},{17,1},{25,9},{2,18},{10... | collective-permute-start | bytes 1105928 | tf_op jit(solution)/shard_map/ppermute | solution.py:85
  345.4 19.6 %collective-permute-start.38 = (bf16[128,2048]{1,0:T(8,128)(2,1)S(1)}, bf16[128,2048]{1,0:T(8,128)(2,1)S(1)}, u32[]{:S(2)}, u32[]{:S(2)}) collective-permute-start(bf16[128,2048]{1,0:T(8,128)(2,1)S(1)} %pad_maximum_fusion.11), channel_id=1, source_target_pairs={{0,8},{8,0},{16,24},{24,16},{1,9},{9,1},{17,25},{25,17},{2,10},{10... | collective-permute-start | bytes 1572872 | tf_op jit(solution)/shard_map/ppermute | solution.py:85
  381.9 22.8 %collective-permute-start.45 = (bf16[1,2,128,1024]{3,2,1,0:T(8,128)(2,1)S(1)}, bf16[1,2,128,1024]{3,2,1,0:T(8,128)(2,1)S(1)}, u32[]{:S(2)}, u32[]{:S(2)}) collective-permute-start(bf16[1,2,128,1024]{3,2,1,0:T(8,128)(2,1)S(1)} %pad_maximum_fusion.12), channel_id=1, source_target_pairs={{0,2},{2,0},{4,6},{6,4},{1,3},{3,1},{5,7},{7,5},{8,10},{10,8},{12,... | collective-permute-start | bytes 1572872 | tf_op jit(solution)/shard_map/ppermute | solution.py:85
  383.5 21.3 %collective-permute-start.46 = (bf16[1,2,128,1024]{3,2,1,0:T(8,128)(2,1)S(1)}, bf16[1,2,128,1024]{3,2,1,0:T(8,128)(2,1)S(1)}, u32[]{:S(2)}, u32[]{:S(2)}) collective-permute-start(bf16[1,2,128,1024]{3,2,1,0:T(8,128)(2,1)S(1)} %pad_maximum_fusion.13), channel_id=1, source_target_pairs={{0,4},{4,0},{2,6},{6,2},{1,5},{5,1},{3,7},{7,3},{8,12},{12,8},{10,... | collective-permute-start | bytes 1572872 | tf_op jit(solution)/shard_map/ppermute | solution.py:85
  405.5 22.3 %collective-permute-start.48 = (bf16[1,2,2,128,2048]{4,3,2,1,0:T(8,128)(2,1)S(1)}, bf16[1,2,2,128,2048]{4,3,2,1,0:T(8,128)(2,1)S(1)}, u32[]{:S(2)}, u32[]{:S(2)}) collective-permute-start(bf16[1,2,2,128,2048]{4,3,2,1,0:T(8,128)(2,1)S(1)} %maximum_maximum_fusion.1), channel_id=1, source_target_pairs={{0,1},{1,0},{2,3},{3,2},{4,5},{5,4},{6,7},{7,6},{8,9},{9,8},{10,11... | collective-permute-start | bytes 6291464 | tf_op jit(solution)/shard_map/ppermute | solution.py:85
  412.1 15.7 %collective-permute-start.50 = (bf16[160,1152]{1,0:T(8,128)(2,1)S(1)}, bf16[160,1152]{1,0:T(8,128)(2,1)S(1)}, u32[]{:S(2)}, u32[]{:S(2)}) collective-permute-start(bf16[160,1152]{1,0:T(8,128)(2,1)S(1)} %fusion.31), channel_id=1, source_target_pairs={{0,8},{8,0},{16,24},{24,16},{1,9},{9,1},{17,25},{25,17},{2,10},{10... | collective-permute-start | bytes 1105928 | tf_op jit(solution)/shard_map/ppermute | solution.py:85
  432.4 32.4 %collective-permute-start.53 = (bf16[2,2,128,2048]{3,2,1,0:T(8,128)(2,1)}, bf16[2,2,128,2048]{3,2,1,0:T(8,128)(2,1)}, u32[]{:S(2)}, u32[]{:S(2)}) collective-permute-start(bf16[2,2,128,2048]{3,2,1,0:T(8,128)(2,1)} %dynamic-slice_bitcast_fusion.2), channel_id=1, source_target_pairs={{0,1},{1,0},{2,3},{3,2},{4,5},{5,4},{6,7},{7,6},{8,9},{9,8},{10,11... | collective-permute-start | bytes 6291464 | tf_op jit(solution)/shard_map/ppermute | solution.py:85
  437.8 26.9 %collective-permute-start.51 = (bf16[176,1152]{1,0:T(8,128)(2,1)}, bf16[176,1152]{1,0:T(8,128)(2,1)}, u32[]{:S(2)}, u32[]{:S(2)}) collective-permute-start(bf16[176,1152]{1,0:T(8,128)(2,1)} %slice_bitcast_fusion.1), channel_id=1, source_target_pairs={{0,16},{8,24},{16,0},{24,8},{1,17},{9,25},{17,1},{25,9},{2,18},{10... | collective-permute-start | bytes 1216520 | tf_op jit(solution)/shard_map/ppermute | solution.py:85
  438.2 26.5 %collective-permute-start.52 = (bf16[128,1152]{1,0:T(8,128)(2,1)}, bf16[128,1152]{1,0:T(8,128)(2,1)S(1)}, u32[]{:S(2)}, u32[]{:S(2)}) collective-permute-start(bf16[128,1152]{1,0:T(8,128)(2,1)} %fusion.33), channel_id=1, source_target_pairs={{0,8},{8,0},{16,24},{24,16},{1,9},{9,1},{17,25},{25,17},{2,10},{10... | collective-permute-start | bytes 884744 | tf_op jit(solution)/shard_map/ppermute | solution.py:85
  473.2 31.6 %collective-permute-start.54 = (bf16[2,2,128,2048]{3,2,1,0:T(8,128)(2,1)}, bf16[2,2,128,2048]{3,2,1,0:T(8,128)(2,1)}, u32[]{:S(2)}, u32[]{:S(2)}) collective-permute-start(bf16[2,2,128,2048]{3,2,1,0:T(8,128)(2,1)} %dynamic-slice_bitcast_fusion.1), channel_id=1, source_target_pairs={{0,1},{1,0},{2,3},{3,2},{4,5},{5,4},{6,7},{7,6},{8,9},{9,8},{10,11... | collective-permute-start | bytes 6291464 | tf_op jit(solution)/shard_map/ppermute | solution.py:85
  473.2 31.6 %collective-permute-start.59 = (bf16[2,2,128,2048]{3,2,1,0:T(8,128)(2,1)}, bf16[2,2,128,2048]{3,2,1,0:T(8,128)(2,1)}, u32[]{:S(2)}, u32[]{:S(2)}) collective-permute-start(bf16[2,2,128,2048]{3,2,1,0:T(8,128)(2,1)} %dynamic-slice_bitcast_fusion), channel_id=1, source_target_pairs={{0,1},{1,0},{2,3},{3,2},{4,5},{5,4},{6,7},{7,6},{8,9},{9,8},{10,11... | collective-permute-start | bytes 6291464 | tf_op jit(solution)/shard_map/ppermute | solution.py:85
  487.7 17.1 %collective-permute-start.57 = (bf16[2,128,1024]{2,1,0:T(8,128)(2,1)}, bf16[2,128,1024]{2,1,0:T(8,128)(2,1)}, u32[]{:S(2)}, u32[]{:S(2)}) collective-permute-start(bf16[2,128,1024]{2,1,0:T(8,128)(2,1)} %dynamic-slice_bitcast_fusion.11), channel_id=1, source_target_pairs={{0,2},{2,0},{4,6},{6,4},{1,3},{3,1},{5,7},{7,5},{8,10},{10,8},{12,... | collective-permute-start | bytes 1572872 | tf_op jit(solution)/shard_map/ppermute | solution.py:85
  488.7 16.1 %collective-permute-start.58 = (bf16[2,128,1024]{2,1,0:T(8,128)(2,1)}, bf16[2,128,1024]{2,1,0:T(8,128)(2,1)}, u32[]{:S(2)}, u32[]{:S(2)}) collective-permute-start(bf16[2,128,1024]{2,1,0:T(8,128)(2,1)} %dynamic-slice_bitcast_fusion.10), channel_id=1, source_target_pairs={{0,4},{4,0},{2,6},{6,2},{1,5},{5,1},{3,7},{7,3},{8,12},{12,8},{10,... | collective-permute-start | bytes 1572872 | tf_op jit(solution)/shard_map/ppermute | solution.py:85
  498.2 103.4 %reduce-scatter.3.cloned.1.call-start = ((), (), s32[]{:S(2)}) async-start(), calls=%async_computation.3 | async-start | bytes 2621440 | tf_op jit(solution)/shard_map/reduce_scatter | solution.py:782
  504.8 26.2 %collective-permute-start.77 = (f32[4,1088]{1,0:T(4,128)S(1)}, f32[4,1088]{1,0:T(4,128)S(1)}, u32[]{:S(2)}, u32[]{:S(2)}) collective-permute-start(f32[4,1088]{1,0:T(4,128)S(1)} %add.369), channel_id=1, source_target_pairs={{0,16},{8,24},{16,0},{24,8},{1,17},{9,25},{17,1},{25,9},{2,18},{10... | collective-permute-start | bytes 52232 | tf_op jit(solution)/shard_map/ppermute | solution.py:106
  529.1 41.1 %collective-permute-start.60 = (bf16[2,128,1024]{2,1,0:T(8,128)(2,1)}, bf16[2,128,1024]{2,1,0:T(8,128)(2,1)}, u32[]{:S(2)}, u32[]{:S(2)}) collective-permute-start(bf16[2,128,1024]{2,1,0:T(8,128)(2,1)} %dynamic-slice_bitcast_fusion.9), channel_id=1, source_target_pairs={{0,2},{2,0},{4,6},{6,4},{1,3},{3,1},{5,7},{7,5},{8,10},{10,8},{12,... | collective-permute-start | bytes 1572872 | tf_op jit(solution)/shard_map/ppermute | solution.py:85
  529.7 40.5 %collective-permute-start.61 = (bf16[2,128,1024]{2,1,0:T(8,128)(2,1)}, bf16[2,128,1024]{2,1,0:T(8,128)(2,1)}, u32[]{:S(2)}, u32[]{:S(2)}) collective-permute-start(bf16[2,128,1024]{2,1,0:T(8,128)(2,1)} %dynamic-slice_bitcast_fusion.8), channel_id=1, source_target_pairs={{0,4},{4,0},{2,6},{6,2},{1,5},{5,1},{3,7},{7,3},{8,12},{12,8},{10,... | collective-permute-start | bytes 1572872 | tf_op jit(solution)/shard_map/ppermute | solution.py:85
  531.0 18.9 %collective-permute-start.65 = (bf16[128,1024]{1,0:T(8,128)(2,1)}, bf16[128,1024]{1,0:T(8,128)(2,1)}, u32[]{:S(2)}, u32[]{:S(2)}) collective-permute-start(bf16[128,1024]{1,0:T(8,128)(2,1)} %dynamic-slice_bitcast_fusion.22), channel_id=1, source_target_pairs={{0,2},{2,0},{4,6},{6,4},{1,3},{3,1},{5,7},{7,5},{8,10},{10,8},{12,... | collective-permute-start | bytes 786440 | tf_op jit(solution)/shard_map/ppermute | solution.py:85
  535.6 34.7 %collective-permute-start.66 = (bf16[2,128,1024]{2,1,0:T(8,128)(2,1)}, bf16[2,128,1024]{2,1,0:T(8,128)(2,1)}, u32[]{:S(2)}, u32[]{:S(2)}) collective-permute-start(bf16[2,128,1024]{2,1,0:T(8,128)(2,1)} %dynamic-slice_bitcast_fusion.7), channel_id=1, source_target_pairs={{0,2},{2,0},{4,6},{6,4},{1,3},{3,1},{5,7},{7,5},{8,10},{10,8},{12,... | collective-permute-start | bytes 1572872 | tf_op jit(solution)/shard_map/ppermute | solution.py:85
  537.0 33.2 %collective-permute-start.67 = (bf16[2,128,1024]{2,1,0:T(8,128)(2,1)}, bf16[2,128,1024]{2,1,0:T(8,128)(2,1)}, u32[]{:S(2)}, u32[]{:S(2)}) collective-permute-start(bf16[2,128,1024]{2,1,0:T(8,128)(2,1)} %dynamic-slice_bitcast_fusion.6), channel_id=1, source_target_pairs={{0,4},{4,0},{2,6},{6,2},{1,5},{5,1},{3,7},{7,3},{8,12},{12,8},{10,... | collective-permute-start | bytes 1572872 | tf_op jit(solution)/shard_map/ppermute | solution.py:85
  549.9 20.3 %collective-permute-start.63 = (bf16[128,1152]{1,0:T(8,128)(2,1)S(1)}, bf16[128,1152]{1,0:T(8,128)(2,1)S(1)}, u32[]{:S(2)}, u32[]{:S(2)}) collective-permute-start(bf16[128,1152]{1,0:T(8,128)(2,1)S(1)} %get-tuple-element.391), channel_id=1, source_target_pairs={{0,8},{8,0},{16,24},{24,16},{1,9},{9,1},{17,25},{25,17},{2,10},{10... | collective-permute-start | bytes 884744 | tf_op jit(solution)/shard_map/ppermute | solution.py:85
  577.0 19.5 %collective-permute-start.70 = (bf16[128,2048]{1,0:T(8,128)(2,1)S(1)}, bf16[128,2048]{1,0:T(8,128)(2,1)S(1)}, u32[]{:S(2)}, u32[]{:S(2)}) collective-permute-start(bf16[128,2048]{1,0:T(8,128)(2,1)S(1)} %pad_maximum_fusion.14), channel_id=1, source_target_pairs={{0,8},{8,0},{16,24},{24,16},{1,9},{9,1},{17,25},{25,17},{2,10},{10... | collective-permute-start | bytes 1572872 | tf_op jit(solution)/shard_map/ppermute | solution.py:85
  (123 other events, 933.2 us)
Sparse Core Ops, SparseCore 0:
  15.5 63.7 all-gather.1
  498.4 27.4 reduce-scatter.4
  539.8 56.8 reduce-scatter.2

commit v2 on v1

v2 whole, which is shorter than its diff:
```python
import functools

import jax
import jax.numpy as jnp
from jax import lax
from jax.experimental import pallas as pl
from jax.experimental.pallas import tpu as pltpu
from jax.sharding import PartitionSpec as P

HD = 128


EPSILON = 1e-06
THETA = 1000000.0
ROWS = 256
BAND = 512
PLANE = ("heads", "tensor")
SWAP = ((0, 1), (1, 0))
NEAR = ((0, 1), (1, 0), (2, 3), (3, 2))
FAR = ((0, 2), (2, 0), (1, 3), (3, 1))


def rms_parts(values):
    return lax.rsqrt(jnp.mean(values * values, axis=-1, keepdims=True) + EPSILON)


def norm_back(values, scale, upstream):
    return scale * upstream - values * scale**3 * jnp.mean(
        values * upstream, axis=-1, keepdims=True
    )


def contract(left, right, left_dim, right_dim):
    return lax.dot_general(
        left, right, (((left_dim,), (right_dim,)), ((), ())), preferred_element_type=jnp.float32
    )


def doc_positions(segment_row):
    places = jnp.arange(segment_row.shape[0], dtype=jnp.int32)
    previous = jnp.concatenate([segment_row[:1], segment_row[:-1]])
    starts = lax.cummax(jnp.where(segment_row != previous, places, 0), axis=0)
    return places - starts


def rope_tables(positions):
    frequency = THETA ** (-(jnp.arange(HD // 2, dtype=jnp.float32) * 2.0 / HD))
    angles = positions.astype(jnp.float32)[:, None] * frequency[None, :]
    cosine, sine = jnp.cos(angles), jnp.sin(angles)
    return (
        jnp.concatenate([cosine, cosine], axis=1),
        jnp.concatenate([-sine, sine], axis=1),
    )


def low(values):
    return values.astype(jnp.bfloat16)


def wide(values):
    return values.astype(jnp.float32)


def flip(axis, stride):
    return [(k, k ^ stride) for k in range(lax.axis_size(axis))]


def after(value, *others):
    return lax.optimization_barrier((value, *others))[0]


def apart(work, *args):
    zeros = [jnp.zeros(out.shape, out.dtype) for out in jax.eval_shape(work, *args)]
    return lax.cond(
        lax.axis_index("fsdp") < lax.axis_size("fsdp"), work, lambda *_: tuple(zeros), *args
    )


class Job:
    def __init__(self, steps):
        self.steps, self.moves, self.keep, self.value = steps, (), (), None
        self.resume(None)

    def resume(self, got):
        try:
            given = self.steps.send(got)
            self.moves, self.keep = given if isinstance(given, tuple) else (given, ())
        except StopIteration as end:
            self.moves, self.keep, self.value = (), (), end.value


def beside(*jobs, kernels=()):
    jobs = [job for job in jobs if job.moves]
    given = [[move[0] for move in job.moves] for job in jobs], [args for _, args in kernels]
    arrays, args = lax.optimization_barrier(given)
    got = [
        [lax.ppermute(array, *move[1:]) for array, move in zip(held, job.moves)]
        for held, job in zip(arrays, jobs)
    ]
    results = [kernel[0](*own) for own, kernel in zip(args, kernels)]
    got, results = lax.optimization_barrier((got, results))
    for job, arrived in zip(jobs, got):
        job.resume(arrived)
    return results


def finish(*jobs):
    while any(job.moves for job in jobs):
        beside(*jobs)


def bits(axis):
    size = lax.axis_size(axis)
    return [1 << k for k in range(size.bit_length() - 1)]


def swap(array, axis, stride):
    return lax.ppermute(array, axis, flip(axis, stride))


def bit(axis, stride):
    return (lax.axis_index(axis) // stride) % 2


def line_gather(block, strides):
    block = block[None]
    for stride in strides:
        block = both(block, swap(block, "fsdp", stride), bit("fsdp", stride), 0)
        block = block.reshape(-1, *block.shape[2:])
    return block


def pick(array, index, axis):
    return lax.dynamic_index_in_dim(array, index, axis, keepdims=False)


def both(mine, got, index, axis):
    lower = jnp.where(index == 0, mine, got)
    upper = jnp.where(index == 0, got, mine)
    return jnp.stack([lower, upper], axis=axis)


def position():
    heads = lax.axis_index("heads")
    return jnp.stack([lax.axis_index("tensor"), heads % 2, heads // 2]).astype(jnp.int32)


def vmem_call(kernel, name, megabytes, out_shape, *args):
    return pl.pallas_call(
        kernel,
        in_specs=[pl.BlockSpec(memory_space=pltpu.SMEM)]
        + [pl.BlockSpec(memory_space=pltpu.VMEM)] * len(args),
        out_specs=[pl.BlockSpec(memory_space=pltpu.VMEM)] * len(out_shape),
        out_shape=[jax.ShapeDtypeStruct(shape, jnp.bfloat16) for shape in out_shape],
        compiler_params=call_params(megabytes),
        cost_estimate=cheap(),
        name=name,
    )(position(), *args)


def fold_chip_kernel(position_ref, keep_ref, got_ref, give_first, keep_first, give_second, keep_second):
    x, y = position_ref[1], position_ref[2]
    middle = keep_ref.shape[-1] // 2
    first, second = slice(0, middle), slice(middle, 2 * middle)

    def summed(row, column, cols):
        return low(wide(keep_ref[row, column, :, cols]) + wide(got_ref[row, column, :, cols]))

    for k in range(2):
        give_first[k] = summed(k, 1 - x, first)
        keep_first[k] = summed(k, x, first)
        give_second[k] = summed(1 - y, k, second)
        keep_second[k] = summed(y, k, second)


def fold_chip(keep, got):
    rows, width = keep.shape
    shape = (2, 2, rows // 4, width)
    return vmem_call(
        fold_chip_kernel, "fold_chip", 24, [(2, rows // 4, width // 2)] * 4, keep.reshape(shape), got.reshape(shape)
    )


def fold_line_kernel(
    position_ref, keep_first_ref, got_first_ref, keep_second_ref, got_second_ref, give_first, keep_first, give_second, keep_second
):
    x, y = position_ref[1], position_ref[2]
    for at, keep_ref, got_ref, give, keep in (
        (y, keep_first_ref, got_first_ref, give_first, keep_first),
        (x, keep_second_ref, got_second_ref, give_second, keep_second),
    ):
        give[...] = low(wide(keep_ref[1 - at]) + wide(got_ref[1 - at]))
        keep[...] = low(wide(keep_ref[at]) + wide(got_ref[at]))


def fold_line(keep_first, got_first, keep_second, got_second):
    shape = keep_first.shape[1:]
    return vmem_call(
        fold_line_kernel, "fold_line", 16, [shape] * 4, keep_first, got_first, keep_second, got_second
    )


def plane_scatter(keep, give):
    (got,) = yield [(give, "tensor", SWAP)]
    folded = fold_chip(keep, got)
    return (yield from chip_scatter(*folded))


def chip_scatter(give_first, keep_first, give_second, keep_second):
    held = (give_first, keep_first, give_second, keep_second)
    got = yield [(give_first, "heads", NEAR), (give_second, "heads", FAR)], held
    return (yield from line_scatter(*fold_line(keep_first, got[0], keep_second, got[1])))


def line_scatter(give_first, keep_first, give_second, keep_second):
    held = (give_first, keep_first, give_second, keep_second)
    got = yield [(give_first, "heads", FAR), (give_second, "heads", NEAR)], held
    first = wide(keep_first) + wide(got[0])
    second = wide(keep_second) + wide(got[1])
    return jnp.concatenate([first, second], axis=-1)


def open_line_kernel(position_ref, first_ref, got_first_ref, second_ref, got_second_ref, first, second):
    x, y = position_ref[1], position_ref[2]
    first[y] = first_ref[...]
    first[1 - y] = got_first_ref[...]
    second[x] = second_ref[...]
    second[1 - x] = got_second_ref[...]


def open_chip_kernel(position_ref, first_ref, got_first_ref, second_ref, got_second_ref, out_ref):
    x, y = position_ref[1], position_ref[2]
    lead, middle = first_ref.shape[1], first_ref.shape[-1]
    for k in range(lead):
        for j in range(2):
            out_ref[k, j, x, :, :middle] = first_ref[j, k]
            out_ref[k, j, 1 - x, :, :middle] = got_first_ref[j, k]
            out_ref[k, y, j, :, middle:] = second_ref[j, k]
            out_ref[k, 1 - y, j, :, middle:] = got_second_ref[j, k]


def plane_gather(share):
    lead, rows, width = share.shape
    first, second = share[..., : width // 2], share[..., width // 2 :]
    got = yield [(first, "heads", FAR), (second, "heads", NEAR)]
    first, second = vmem_call(
        open_line_kernel, "open_line", 16, [(2, lead, rows, width // 2)] * 2, first, got[0], second, got[1]
    )
    got = yield [(first, "heads", NEAR), (second, "heads", FAR)]
    (mine,) = vmem_call(
        open_chip_kernel, "open_chip", 24, [(lead, 2, 2, rows, width)], first, got[0], second, got[1]
    )
    mine = mine.reshape(lead, 4 * rows, width)
    (other,) = yield [(mine, "tensor", SWAP)]
    return mine, other


def pair_swap(array, pieces=1):
    rows = array.shape[0] // pieces
    got = []
    for k in range(pieces):
        got += yield [(array[k * rows : (k + 1) * rows], "fsdp", flip("fsdp", 1))]
    return jnp.concatenate(got, axis=0) if pieces > 1 else got[0]


def pair_gather(share, pieces):
    got = yield from pair_swap(share, pieces)
    return (yield from plane_gather(got[None]))


def sum_all(values):
    for axis in ("tensor", "heads", "fsdp"):
        for stride in bits(axis):
            (got,) = yield [(values, axis, flip(axis, stride))]
            values = values + got
    return values


def alike():
    return [list(range(k, lax.axis_size("fsdp"), 2)) for k in range(2)]


def rotate(values, cosine, sine):
    return values * cosine + pltpu.roll(values, HD // 2, 1) * sine


def call_params(megabytes):
    return pltpu.CompilerParams(vmem_limit_bytes=megabytes << 20)


def cheap():
    return pl.CostEstimate(flops=1000, bytes_accessed=1000, transcendentals=0)


def key_blocks(at, count):
    return max(0, at - BAND // ROWS), at + 1


def masked_probs(query, keys, seg_rows, seg_keys, first_row, first_key):
    scores = contract(query, keys, 1, 1) * HD**-0.5
    rows = first_row + lax.broadcasted_iota(jnp.int32, scores.shape, 0)
    cols = first_key + lax.broadcasted_iota(jnp.int32, scores.shape, 1)
    scores = jnp.where((rows >= cols) & (seg_rows == seg_keys), scores, -1e30)
    expo = jnp.exp(scores - jnp.max(scores, axis=-1, keepdims=True))
    return expo / jnp.sum(expo, axis=-1, keepdims=True)


def by_core(core, block):
    middle = block.shape[0] // 2
    lower, upper = block[:middle], block[middle:]
    first = core == 0
    return jnp.where(first, lower, upper), jnp.where(first, upper, lower)


def joined(core, mine, other):
    first = core == 0
    return jnp.concatenate([jnp.where(first, mine, other), jnp.where(first, other, mine)], axis=0)


def attend_kernel(
    group,
    normed_ref,
    proj_ref,
    cosine_ref,
    sine_ref,
    query_gain_ref,
    key_gain_ref,
    seg_rows_ref,
    seg_keys_ref,
    position_ref,
    raw_ref,
    query_ref,
    key_ref,
    value_ref,
    mixed_ref,
    keep_ref,
    give_ref,
    keys,
    values,
):
    length, kv_cols = keys.shape
    kv_local = kv_cols // HD
    query_cols = kv_cols * group
    count = length // ROWS
    step = pl.program_id(0)
    split = query_cols + 2 * kv_cols
    raw = jnp.dot(normed_ref[...], proj_ref[:, :split], preferred_element_type=jnp.float32)
    raw_ref[...] = raw[:, : query_cols + kv_cols]
    cosine, sine = cosine_ref[...], sine_ref[...]
    here = pl.ds(pl.multiple_of(step * ROWS, ROWS), ROWS)

    def turned(head, gain_ref):
        one = raw[:, head * HD : (head + 1) * HD]
        return low(rotate(one * rms_parts(one) * gain_ref[...], cosine, sine))

    for kv in range(kv_local):
        at = slice(kv * HD, (kv + 1) * HD)
        new_keys = turned(query_cols // HD + kv, key_gain_ref)
        new_values = low(raw[:, query_cols + kv_cols + kv * HD : query_cols + kv_cols + (kv + 1) * HD])
        key_ref[:, at] = new_keys
        value_ref[:, at] = new_values
        keys[here, at] = new_keys
        values[here, at] = new_values
    for head in range(query_cols // HD):
        query_ref[:, head * HD : (head + 1) * HD] = turned(head, query_gain_ref)

    for at in range(count):

        @pl.when(step == at)
        def _():
            lower, upper = key_blocks(at, count)
            span = slice(lower * ROWS, upper * ROWS)
            for head in range(query_cols // HD):
                cols = slice(head * HD, (head + 1) * HD)
                kv = slice((head // group) * HD, (head // group + 1) * HD)
                probs = masked_probs(
                    query_ref[:, cols],
                    keys[span, kv],
                    seg_rows_ref[...],
                    seg_keys_ref[:, span],
                    at * ROWS,
                    lower * ROWS,
                )
                mixed_ref[:, cols] = low(
                    jnp.dot(low(probs), values[span, kv], preferred_element_type=jnp.float32)
                )

    keep_ref[...], give_ref[...] = by_core(
        position_ref[0], low(contract(mixed_ref[...], proj_ref[:, split:], 1, 1))
    )


def attend(group, normed, proj, cosine, sine, query_gain, key_gain, segment_row):
    length, model = normed.shape
    kv_cols = proj.shape[1] // (2 * group + 2)
    query_cols = kv_cols * group

    def rows(width):
        return pl.BlockSpec((ROWS, width), lambda i: (i, 0))

    def whole(array):
        return pl.BlockSpec(array.shape, lambda i: (0, 0))

    seg_rows, seg_keys = segment_row[:, None], segment_row[None, :]
    args = (normed, proj, cosine, sine, query_gain[None], key_gain[None], seg_rows, seg_keys, position())
    outs = [
        (query_cols + kv_cols, jnp.float32),
        (query_cols, jnp.bfloat16),
        (kv_cols, jnp.bfloat16),
        (kv_cols, jnp.bfloat16),
        (query_cols, jnp.bfloat16),
    ]
    halves = (length // 2, model)
    return pl.pallas_call(
        functools.partial(attend_kernel, group),
        grid=(length // ROWS,),
        in_specs=[
            rows(model),
            whole(proj),
            rows(HD),
            rows(HD),
            whole(args[4]),
            whole(args[5]),
            rows(1),
            whole(seg_keys),
            pl.BlockSpec(memory_space=pltpu.SMEM),
        ],
        out_specs=[rows(width) for width, _ in outs]
        + [pl.BlockSpec((ROWS // 2, model), lambda i: (i, 0))] * 2,
        out_shape=[jax.ShapeDtypeStruct((length, width), kind) for width, kind in outs]
        + [jax.ShapeDtypeStruct(halves, jnp.bfloat16)] * 2,
        scratch_shapes=[
            pltpu.VMEM((length, kv_cols), jnp.bfloat16),
            pltpu.VMEM((length, kv_cols), jnp.bfloat16),
        ],
        compiler_params=call_params(40),
        cost_estimate=cheap(),
        name="attend",
    )(*args)


def attend_back_kernel(
    group,
    grad_mine_ref,
    grad_other_ref,
    proj_ref,
    cosine_ref,
    sine_ref,
    query_gain_ref,
    key_gain_ref,
    seg_rows_ref,
    seg_keys_ref,
    raw_ref,
    query_ref,
    key_ref,
    value_ref,
    tokens_ref,
    scale_ref,
    normed_ref,
    mixed_ref,
    position_ref,
    weight_ref,
    keep_ref,
    give_ref,
    gain_ref,
    head_gain_ref,
    grad_ref,
    low_ref,
    mixed_grad,
    query_sum,
    key_sum,
    value_sum,
):
    length, kv_cols = key_sum.shape
    query_cols = kv_cols * group
    count = length // ROWS
    split = query_cols + 2 * kv_cols
    for at in range(count):
        here = slice(at * ROWS, (at + 1) * ROWS)
        rows = slice(at * ROWS // 2, (at + 1) * ROWS // 2)
        grad_ref[here, :] = joined(position_ref[0], grad_mine_ref[rows, :], grad_other_ref[rows, :])
        mixed_grad[here, :] = low(
            jnp.dot(grad_ref[here, :], proj_ref[:, split:], preferred_element_type=jnp.float32)
        )
    key_sum[...] = jnp.zeros_like(key_sum)
    value_sum[...] = jnp.zeros_like(value_sum)
    for at in range(count):
        here = slice(at * ROWS, (at + 1) * ROWS)
        lower, upper = key_blocks(at, count)
        span = slice(lower * ROWS, upper * ROWS)
        for head in range(query_cols // HD):
            cols = slice(head * HD, (head + 1) * HD)
            kv = slice((head // group) * HD, (head // group + 1) * HD)
            query = query_ref[here, cols]
            grad = mixed_grad[here, cols]
            probs = masked_probs(
                query,
                key_ref[span, kv],
                seg_rows_ref[here, :],
                seg_keys_ref[:, span],
                at * ROWS,
                lower * ROWS,
            )
            prob_grad = contract(grad, value_ref[span, kv], 1, 1)
            row_inner = jnp.sum(probs * prob_grad, axis=-1, keepdims=True)
            score_grad = low(HD**-0.5 * probs * (prob_grad - row_inner))
            query_sum[here, cols] = jnp.dot(
                score_grad, key_ref[span, kv], preferred_element_type=jnp.float32
            )
            key_sum[span, kv] += contract(score_grad, query, 0, 0)
            value_sum[span, kv] += contract(low(probs), grad, 0, 0)

    gain_ref[...] = jnp.zeros_like(gain_ref)
    head_gain_ref[...] = jnp.zeros_like(head_gain_ref)
    for at in range(count):
        here = slice(at * ROWS, (at + 1) * ROWS)
        cosine, sine = cosine_ref[here, :], -sine_ref[here, :]
        for head in range((query_cols + kv_cols) // HD):
            cols = slice(head * HD, (head + 1) * HD)
            own = slice(head * HD - query_cols, (head + 1) * HD - query_cols)
            is_query = head * HD < query_cols
            turned = rotate(query_sum[here, cols] if is_query else key_sum[here, own], cosine, sine)
            raw = raw_ref[here, cols]
            scale = rms_parts(raw)
            row = 0 if is_query else 1
            head_gain_ref[row : row + 1, :] += jnp.sum(turned * raw * scale, axis=0, keepdims=True)
            gain = query_gain_ref[...] if is_query else key_gain_ref[...]
            low_ref[here, cols] = low(norm_back(raw, scale, turned * gain))
        low_ref[here, query_cols + kv_cols :] = low(value_sum[here, :])
        part = contract(low_ref[here, :], proj_ref[:, :split], 1, 1)
        rows = slice(at * ROWS // 2, (at + 1) * ROWS // 2)
        keep_ref[rows, :], give_ref[rows, :] = by_core(position_ref[0], low(part))
        gain_ref[...] += jnp.sum(part * wide(tokens_ref[here, :]) * scale_ref[here, :], axis=0, keepdims=True)
    cols = 512
    for at in range(0, normed_ref.shape[1], cols):
        here = slice(at, at + cols)
        weight_ref[here, :split] = low(contract(normed_ref[:, here], low_ref[...], 0, 0))
        weight_ref[here, split:] = low(contract(grad_ref[:, here], mixed_ref[...], 0, 0))


def attend_back(
    group, grad_mine, grad_other, proj, cosine, sine, query_gain, key_gain, segment_row, raw, query, key, value, tokens, scale,
    normed, mixed,
):
    length, model = tokens.shape
    query_cols, kv_cols = query.shape[1], key.shape[1]
    args = (
        grad_mine, grad_other, proj, cosine, sine, query_gain[None], key_gain[None],
        segment_row[:, None], segment_row[None, :], raw, query, key, value, tokens, scale, normed, mixed, position(),
    )
    return pl.pallas_call(
        functools.partial(attend_back_kernel, group),
        in_specs=[pl.BlockSpec(memory_space=pltpu.VMEM)] * (len(args) - 1)
        + [pl.BlockSpec(memory_space=pltpu.SMEM)],
        out_specs=[pl.BlockSpec(memory_space=pltpu.VMEM)] * 5,
        out_shape=[
            jax.ShapeDtypeStruct(proj.shape, jnp.bfloat16),
            jax.ShapeDtypeStruct((length // 2, model), jnp.bfloat16),
            jax.ShapeDtypeStruct((length // 2, model), jnp.bfloat16),
            jax.ShapeDtypeStruct((1, model), jnp.float32),
            jax.ShapeDtypeStruct((2, HD), jnp.float32),
        ],
        scratch_shapes=[
            pltpu.VMEM((length, model), jnp.bfloat16),
            pltpu.VMEM((length, query_cols + 2 * kv_cols), jnp.bfloat16),
            pltpu.VMEM((length, query_cols), jnp.bfloat16),
            pltpu.VMEM((length, query_cols), jnp.float32),
            pltpu.VMEM((length, kv_cols), jnp.float32),
            pltpu.VMEM((length, kv_cols), jnp.float32),
        ],
        compiler_params=call_params(56),
        cost_estimate=cheap(),
        name="attend_back",
    )(*args)


def feed_kernel(own, position_ref, *refs):
    count = 3 if own else 4
    proj_ref = refs[count]
    act_ref, gate_up_grad_ref, keep_ref, give_ref, normed, cotangent = refs[count + 1 :]
    core = position_ref[0]
    half = act_ref.shape[-1]
    middle = normed.shape[0] // 2
    normed[:middle, :], normed[middle:, :] = refs[0][...], refs[1][...]
    if own:
        cotangent[:middle, :], cotangent[middle:, :] = by_core(core, refs[2][...])
    else:
        cotangent[:middle, :], cotangent[middle:, :] = refs[2][...], refs[3][...]
    gate_up = jnp.dot(normed[...], proj_ref[:, : 2 * half], preferred_element_type=jnp.float32)
    gate, up = gate_up[:, :half], gate_up[:, half:]
    act_grad = jnp.dot(cotangent[...], proj_ref[:, 2 * half :], preferred_element_type=jnp.float32)
    sigmoid = jax.nn.sigmoid(gate)
    silu = gate * sigmoid
    activated = low(silu * up)
    gate_grad = low(act_grad * up * sigmoid * (1.0 + gate * (1.0 - sigmoid)))
    up_grad = low(act_grad * silu)
    for k in range(2):
        here = slice(k * middle, (k + 1) * middle)
        act_ref[k] = activated[here]
        gate_up_grad_ref[k, :, :half] = gate_grad[here]
        gate_up_grad_ref[k, :, half:] = up_grad[here]
    normed_grad = contract(gate_grad, proj_ref[:, :half], 1, 1) + contract(
        up_grad, proj_ref[:, half : 2 * half], 1, 1
    )
    keep_ref[...], give_ref[...] = low(normed_grad[:middle]), low(normed_grad[middle:])


def feed(which, mine, other, cotangent, proj):
    _, rows, model = mine.shape
    half = proj.shape[1] // 3
    own = len(cotangent) == 1
    tile = ROWS // 2

    def halves(index):
        return pl.BlockSpec((None, tile, model), lambda i: (index, i, 0))

    return pl.pallas_call(
        functools.partial(feed_kernel, own),
        grid=(rows // tile,),
        in_specs=[pl.BlockSpec(memory_space=pltpu.SMEM), halves(which), halves(which)]
        + ([pl.BlockSpec((ROWS, model), lambda i: (i, 0))] if own else [halves(0), halves(0)])
        + [pl.BlockSpec(proj.shape, lambda i: (0, 0), pipeline_mode=pl.Buffered(1))],
        out_specs=[pl.BlockSpec((2, tile, w), lambda i: (0, i, 0)) for w in (half, 2 * half)]
        + [pl.BlockSpec((tile, model), lambda i: (i, 0))] * 2,
        out_shape=[jax.ShapeDtypeStruct((2, rows, w), jnp.bfloat16) for w in (half, 2 * half)]
        + [jax.ShapeDtypeStruct((rows, model), jnp.bfloat16)] * 2,
        scratch_shapes=[pltpu.VMEM((ROWS, model), jnp.bfloat16)] * 2,
        compiler_params=call_params(48),
        cost_estimate=cheap(),
        name="feed",
    )(position(), mine, other, *cotangent, proj)


def feed_out_kernel(act_ref, proj_ref, keep_ref, give_ref):
    half = act_ref.shape[-1]
    for k, out_ref in enumerate((keep_ref, give_ref)):
        out_ref[...] = low(contract(act_ref[k], proj_ref[:, 2 * half :], 1, 1))


def feed_out(act, proj):
    _, rows, half = act.shape
    model = proj.shape[0]
    tile = ROWS
    return pl.pallas_call(
        feed_out_kernel,
        grid=(rows // tile,),
        in_specs=[
            pl.BlockSpec((2, tile, half), lambda i: (0, i, 0)),
            pl.BlockSpec(proj.shape, lambda i: (0, 0), pipeline_mode=pl.Buffered(1)),
        ],
        out_specs=[pl.BlockSpec((tile, model), lambda i: (i, 0))] * 2,
        out_shape=[jax.ShapeDtypeStruct((rows, model), jnp.bfloat16)] * 2,
        compiler_params=call_params(32),
        cost_estimate=cheap(),
        name="feed_out",
    )(act, proj)


def feed_weights_kernel(
    position_ref, mine_own, mine_pair, other_own, other_pair, cot_own, cot_mine, cot_other, grad_own, grad_pair, act_own, act_pair,
    out_ref,
):
    wide_cols = grad_own.shape[-1]
    core = position_ref[0]
    rows, cols = mine_own.shape
    out_ref[:, :wide_cols] = low(
        contract(mine_own[...], grad_own[0], 0, 0)
        + contract(other_own[...], grad_own[1], 0, 0)
        + contract(mine_pair[...], grad_pair[0], 0, 0)
        + contract(other_pair[...], grad_pair[1], 0, 0)
    )
    out_ref[:, wide_cols:] = low(
        contract(cot_own[:, core].reshape(rows, cols), act_own[0], 0, 0)
        + contract(cot_own[:, 1 - core].reshape(rows, cols), act_own[1], 0, 0)
        + contract(cot_mine[...], act_pair[0], 0, 0)
        + contract(cot_other[...], act_pair[1], 0, 0)
    )


def feed_weights(mine, other, cotangent, cot_mine, cot_other, grad, act):
    _, rows, model = mine.shape
    width = grad[0].shape[-1] + act[0].shape[-1]
    cols = min(512, model)
    cotangent = cotangent.reshape(-1, 2, ROWS // 2, model)

    def whole(array):
        return pl.BlockSpec(array.shape, lambda i: (0, 0, 0), pipeline_mode=pl.Buffered(1))

    def part(index):
        return pl.BlockSpec((None, rows, cols), lambda i: (index, 0, i))

    return pl.pallas_call(
        feed_weights_kernel,
        grid=(model // cols,),
        in_specs=[
            pl.BlockSpec(memory_space=pltpu.SMEM),
            part(0),
            part(1),
            part(0),
            part(1),
            pl.BlockSpec((*cotangent.shape[:3], cols), lambda i: (0, 0, 0, i)),
            part(0),
            part(0),
        ]
        + [whole(a) for a in (*grad, *act)],
        out_specs=pl.BlockSpec((cols, width), lambda i: (i, 0)),
        out_shape=jax.ShapeDtypeStruct((model, width), jnp.bfloat16),
        compiler_params=call_params(48),
        cost_estimate=cheap(),
        name="feed_weights",
    )(position(), mine, mine, other, other, cotangent, cot_mine, cot_other, *grad, *act)


def feed_sums_kernel(count, side_ref, *refs):
    own, other, outs = refs[:count], refs[count:-3], refs[-3:]
    half = outs[0].shape[1]
    mine = pl.program_id(0) == side_ref[0]
    for held, keep in ((own, mine), (other, jnp.logical_not(mine))):

        @pl.when(keep)
        def _():
            first = 0
            for part in held:
                for k, out in enumerate(outs):
                    out[first : first + part.shape[0], :] = wide(part[:, k * half : (k + 1) * half])
                first += part.shape[0]


def feed_sums(side, own, other):
    rows, width = sum(part.shape[0] for part in own), own[0].shape[1]
    half = width // 3
    parts = (*own, *other)
    return pl.pallas_call(
        functools.partial(feed_sums_kernel, len(own)),
        grid_spec=pltpu.PrefetchScalarGridSpec(
            num_scalar_prefetch=1,
            grid=(2,),
            in_specs=[
                pl.BlockSpec(p.shape, lambda i, side: (0, 0), pipeline_mode=pl.Buffered(1)) for p in parts
            ],
            out_specs=[pl.BlockSpec((rows, half), lambda i, side: (0, i))] * 3,
        ),
        out_shape=[jax.ShapeDtypeStruct((rows, 2 * half), jnp.float32)] * 3,
        compiler_params=call_params(32),
        cost_estimate=cheap(),
        name="feed_sums",
    )(side, *parts)


def per_device(
    tokens,
    segments,
    ln1_gain,
    w_query,
    w_key,
    w_value,
    query_gain,
    key_gain,
    w_out,
    ln2_gain,
    w_gate,
    w_up,
    w_down,
    cotangent,
):
    length, model = tokens.shape
    query_cols, key_cols = w_query.shape[1], w_key.shape[1]
    query_heads = query_cols // HD
    kv_local = key_cols // HD
    group = query_heads // kv_local
    size = lax.axis_size("fsdp")
    shard = model // size
    hidden = w_gate.shape[1]
    half = hidden // 2
    strides = bits("fsdp")
    group_size = lax.axis_size(PLANE)
    share_rows = length // group_size
    share_start = lax.axis_index(PLANE) * share_rows
    segment_row = segments[0]

    def share_of(array):
        return lax.dynamic_slice_in_dim(array, share_start, share_rows, 0)

    proj = lax.all_gather(
        jnp.concatenate([w_query, w_key, w_value, w_out], axis=1), "fsdp", axis=0, tiled=True
    )
    side = bit("fsdp", 1)

    def half_of(which):
        return jnp.concatenate(
            [lax.dynamic_slice_in_dim(w, which * half, half, 1) for w in (w_gate, w_up, w_down)], axis=1
        )

    got = swap(after(half_of(1 - side), proj), "fsdp", 1)
    feed_block = both(half_of(side), got, side, 0)

    gains = line_gather(jnp.concatenate([ln1_gain, ln2_gain, query_gain, key_gain]), strides)
    gain_attn = gains[:, :shard].reshape(model)
    gain_ffn = gains[:, shard : 2 * shard].reshape(model)
    head_part = HD // size
    query_norm = gains[:, 2 * shard : 2 * shard + head_part].reshape(HD)
    key_norm = gains[:, 2 * shard + head_part :].reshape(HD)

    cosine, sine = rope_tables(doc_positions(segment_row))
    block_in = tokens.astype(jnp.float32)
    scale_one = rms_parts(block_in)
    normed = (block_in * scale_one * gain_attn.astype(jnp.float32)).astype(jnp.bfloat16)
    query_gain_wide, key_gain_wide = wide(query_norm), wide(key_norm)
    raw, query_rot, key_rot, values, mixed_low, out_keep, out_give = attend(
        group, normed, proj, cosine, sine, query_gain_wide, key_gain_wide, segment_row
    )
    out_give, feed_block = lax.optimization_barrier((out_give, feed_block))
    feed_proj = lax.all_gather(
        feed_block, "fsdp", axis=0, tiled=True, axis_index_groups=alike()
    ).reshape(model, -1)

    def middle(out_keep, out_give, tokens, cotangent):
        cot = Job(pair_gather(share_of(cotangent), 2))
        out_sum = Job(plane_scatter(out_keep, out_give))
        beside(out_sum)
        beside(out_sum, cot)
        beside(out_sum, cot)
        hidden_share = wide(share_of(tokens)) + out_sum.value
        scale_share = rms_parts(hidden_share)
        normed_share = low(hidden_share * scale_share * wide(gain_ffn))
        pair_share = Job(pair_swap(normed_share))
        beside(pair_share, cot)
        gather = Job(plane_gather(jnp.stack([normed_share, pair_share.value])))
        beside(gather, cot)
        beside(gather, cot)
        finish(gather)
        return hidden_share, scale_share, *gather.value, *cot.value

    hidden_share, scale_share, mine, other, cot_mine, cot_other = apart(
        middle, out_keep, out_give, tokens, cotangent
    )

    pair_act, pair_grad, *pair_parts = feed(1, mine, other, (cot_mine, cot_other), feed_proj)
    pair_sum = Job(plane_scatter(*pair_parts))
    ((act, grad, *own_parts),) = beside(
        pair_sum, kernels=[(functools.partial(feed, 0), (mine, other, (cotangent,), feed_proj))]
    )
    own_sum = Job(plane_scatter(*own_parts))
    weight_args = (mine, other, cotangent, cot_mine, cot_other, (grad, pair_grad), (act, pair_act))
    (feed_w_part,) = beside(pair_sum, own_sum, kernels=[(feed_weights, weight_args)])
    feed_w_sum = lax.psum_scatter(
        feed_w_part, "fsdp", scatter_dimension=0, tiled=True, axis_index_groups=alike()
    ).reshape(2, shard, -1)
    pair_held, own_held = (tuple(job.keep) for job in (pair_sum, own_sum))

    def back(hidden_share, scale_share, cotangent, act, pair_act, feed_proj, *kept):
        pair_sum = Job(line_scatter(*pair_held))
        own_sum = Job(chip_scatter(*own_held))
        out_parts, pair_out_parts = beside(
            pair_sum, own_sum, kernels=[(feed_out, (act, feed_proj)), (feed_out, (pair_act, feed_proj))]
        )
        out_sum = Job(plane_scatter(*out_parts))
        pair_out_sum = Job(plane_scatter(*pair_out_parts))
        pair_share = Job(pair_swap(low(pair_sum.value), 2))
        beside(pair_share, own_sum, pair_out_sum, out_sum)
        beside(pair_share, pair_out_sum)
        grad_share = own_sum.value + wide(pair_share.value)
        hidden_grad_share = wide(share_of(cotangent)) + norm_back(
            hidden_share, scale_share, grad_share * wide(gain_ffn)
        )
        ffn_gain_part = jnp.sum(grad_share * hidden_share * scale_share, axis=0)
        gather = Job(plane_gather(low(hidden_grad_share)[None]))
        beside(gather)
        beside(gather)
        beside(gather, pair_out_sum)
        pair_out = Job(pair_swap(low(pair_out_sum.value)))
        grad_mine, grad_other = gather.value
        ((attn_w_part, keep, give, attn_gain_part, head_gain_part),) = beside(
            pair_out,
            out_sum,
            kernels=[(functools.partial(attend_back, group), (grad_mine[0], grad_other[0], *kept))],
        )
        out_share = hidden_share + wide(pair_out.value)
        return (
            hidden_grad_share, attn_w_part, keep, give, attn_gain_part, head_gain_part, ffn_gain_part, out_share,
            *out_sum.keep,
        )

    hidden_grad_share, attn_w_part, keep, give, attn_gain_part, head_gain_part, ffn_gain_part, out_share, *held = apart(
        back, hidden_share, scale_share, cotangent, act, pair_act, feed_proj,
        proj, cosine, sine, query_gain_wide, key_gain_wide, segment_row, raw, query_rot, key_rot, values, tokens,
        scale_one, normed, mixed_low,
    )
    attn_w_part, feed_w_sum, give = lax.optimization_barrier((attn_w_part, feed_w_sum, give))
    attn_w_sum = lax.psum_scatter(attn_w_part, "fsdp", scatter_dimension=0, tiled=True)

    def last(feed_w_sum, keep, give, out_share, hidden_grad_share, tokens, scale_one, *rest):
        gain_parts, held = rest[:4], rest[4:]
        out_sum = Job(line_scatter(*held))
        feed_pair = Job(pair_swap(pick(feed_w_sum, 1 - side, 0), 4))
        normed_sum = Job(plane_scatter(keep, give))
        gains = Job(sum_all(jnp.concatenate([part.reshape(size, -1) for part in gain_parts], axis=1)))
        beside(normed_sum, out_sum, gains)
        beside(normed_sum, feed_pair, gains)
        beside(normed_sum, feed_pair, gains)
        finish(feed_pair, gains)
        gate_w_grad, up_w_grad, down_w_grad = feed_sums(side[None], [pick(feed_w_sum, side, 0)], [feed_pair.value])
        block_out = low(out_share + out_sum.value)
        token_share = wide(share_of(tokens))
        scale_one_share = share_of(scale_one)
        tokens_grad = low(
            hidden_grad_share + norm_back(token_share, scale_one_share, normed_sum.value * wide(gain_attn))
        )
        gain_sums = pick(gains.value, lax.axis_index("fsdp"), 0)
        return block_out, tokens_grad, gate_w_grad, up_w_grad, down_w_grad, gain_sums

    block_out, tokens_grad, gate_w_grad, up_w_grad, down_w_grad, gain_sums = apart(
        last, feed_w_sum, keep, give, out_share, hidden_grad_share, tokens, scale_one,
        attn_gain_part, ffn_gain_part, head_gain_part[0], head_gain_part[1], *held,
    )
    attn_w_grad, gain_sums = lax.optimization_barrier((attn_w_sum, gain_sums))
    attn_w_grad = wide(attn_w_grad)
    out_w_grad = attn_w_grad[:, query_cols + 2 * key_cols :]
    ln1_grad = gain_sums[:shard]
    ln2_grad = gain_sums[shard : 2 * shard]
    query_gain_grad = gain_sums[2 * shard : 2 * shard + head_part]
    key_gain_grad = gain_sums[2 * shard + head_part :]

    return (
        block_out,
        tokens_grad,
        ln1_grad,
        attn_w_grad[:, :query_cols],
        attn_w_grad[:, query_cols : query_cols + key_cols],
        attn_w_grad[:, query_cols + key_cols : query_cols + 2 * key_cols],
        query_gain_grad,
        key_gain_grad,
        out_w_grad,
        ln2_grad,
        gate_w_grad,
        up_w_grad,
        down_w_grad,
    )


def solution(mesh):
    in_specs = (
        P("fsdp", None),
        P("fsdp", None),
        P("fsdp"),
        P("fsdp", ("heads", "tensor")),
        P("fsdp", ("heads", "tensor")),
        P("fsdp", ("heads", "tensor")),
        P("fsdp"),
        P("fsdp"),
        P("fsdp", ("heads", "tensor")),
        P("fsdp"),
        P("fsdp", ("heads", "tensor")),
        P("fsdp", ("heads", "tensor")),
        P("fsdp", ("heads", "tensor")),
        P("fsdp", None),
    )
    out_specs = (
        P(("fsdp", "heads", "tensor"), None),
        P(("fsdp", "heads", "tensor"), None),
        P("fsdp"),
        P("fsdp", ("heads", "tensor")),
        P("fsdp", ("heads", "tensor")),
        P("fsdp", ("heads", "tensor")),
        P("fsdp"),
        P("fsdp"),
        P("fsdp", ("heads", "tensor")),
        P("fsdp"),
        P("fsdp", ("heads", "tensor")),
        P("fsdp", ("heads", "tensor")),
        P("fsdp", ("heads", "tensor")),
    )
    return jax.shard_map(
        per_device, mesh=mesh, in_specs=in_specs, out_specs=out_specs, check_vma=False
    )
```

time: 620 us -> 540 us (0.87)
  Pallas kernels: 76.7 us -> 123 us
  other arithmetic: 84.2 us -> 39.3 us
  local copies, waits for them, and re-layouts: 68.4 us -> 28.6 us
  matrix products: 15.9 us -> 0 us
  waiting for transfers between devices: 268 us -> 257 us
  starting transfers between devices: 83.3 us -> 73.6 us
    pallas_call x4 -> x23, Pallas kernels: 44 us -> 84.2 us  [the longest x18 30.7 us: vmem_call(): pl.pallas_call(kernel, in_specs=[pl.BlockSpec(memory_space=pltpu.SMEM)] +...]
    convert_element_type x22 -> x2, other arithmetic: 30.3 us -> 3.52 us  [low(): return values.astype(jnp.bfloat16)]
    ppermute x71 -> x60, waiting for transfers between devices: 214 us -> 194 us  [beside(): lax.ppermute(array, *move[1:])]
    squeeze x30 -> x1, local copies, waits for them, and re-layouts: 20.5 us -> 0.09 us  [pick(): return lax.dynamic_index_in_dim(array, index, axis, keepdims=False)]
    ppermute x71 -> x60, starting transfers between devices: 75.1 us -> 57.1 us  [beside(): lax.ppermute(array, *move[1:])]
    unnamed x185 -> x40, local copies, waits for them, and re-layouts: 18.7 us -> 1.96 us
    dot_general x4 -> x0, matrix products: 15.9 us -> none  [contract(): lax.dot_general(left, right, (((left_dim,), (right_dim,)), ((), ())), pre...]
    another operation x20 -> x5, other arithmetic: 16.9 us -> 4.19 us  [both(): return jnp.stack([lower, upper], axis=axis)]
  transfers between devices with their start and end apart: 81 -> 67, of which waited for: 38 -> 36; matrix products, arithmetic and copies ran while one was open for 16% -> 8% of each run, Pallas kernels for 10% -> 20%
where the time goes in v2:
time: 540 us; the launch traced here: 536 us
  waiting for transfers between devices  257 us (48%)
  Pallas kernels  123 us (23%)
  starting transfers between devices  73.6 us (14%)
  other arithmetic  39.3 us (7%)
  local copies, waits for them, and re-layouts  28.6 us (5%)
  between operations  14.3 us (3%)
    ppermute x60, waiting for transfers between devices, beside(): lax.ppermute(array, *move[1:])  194 us
    ppermute x60, starting transfers between devices, beside(): lax.ppermute(array, *move[1:])  57.1 us
    all_gather x1, waiting for transfers between devices, per_device(): lax.all_gather(jnp.concatenate([w_query, w_key, w_value, w_out], axis=1),...  48.8 us
    pallas_call x18, Pallas kernels, vmem_call(): pl.pallas_call(kernel, in_specs=[pl.BlockSpec(memory_space=pltpu.SMEM)] +...  30.7 us
    pallas_call x2, Pallas kernels, feed(): pl.pallas_call(functools.partial(feed_kernel, own), grid=(rows // tile,),...  29.9 us
    pallas_call x1, Pallas kernels, attend_back(): pl.pallas_call(functools.partial(attend_back_kernel, group), in_specs=[pl...  24.1 us
    pallas_call x1, Pallas kernels, feed_weights(): pl.pallas_call(feed_weights_kernel, grid=(model // cols,), in_specs=[pl.B...  15.5 us
    ppermute x3, waiting for transfers between devices, swap(): return lax.ppermute(array, axis, flip(axis, stride))  14.7 us
  transfers between devices with their start and end apart: 67, of which 36 were waited for; matrix products, arithmetic and copies ran while one was open for 8% of the time, Pallas kernels for 20%

profile of v2, /device:TPU:0, one launch (start us, length us, event | category | flops | bytes accessed | tf_op | source)
XLA Modules:
  0.0 536.2 jit_solution(11076902957974423156)
XLA Ops:
  10.4 3.0 collective-permute-start.56
  22.5 2.7 collective-permute-start.57
  25.5 2.4 collective-permute-done.57
  27.9 48.8 %all-gather.3.cloned.1.call-done.proj_ref = bf16[2048,768]{1,0:T(8,128)(2,1)} async-done(((bf16[512,768]{1,0:T(8,128)(2,1)}), bf16[2048,768]{1,0:T(8,128)(2,1)}) %all-gather.3.cloned.1.call-update) | async-done | bytes 3145744 | tf_op jit(solution)/shard_map/all_gather | solution.py:784
  77.0 3.4 fusion.15.normed_ref
  80.4 11.9 %attend.1 = (f32[1024,384]{1,0:T(8,128)}, bf16[1024,256]{1,0:T(8,128)(2,1)}, bf16[1024,128]{1,0:T(8,128)(2,1)}, bf16[1024,128]{1,0:T(8,128)(2,1)}, bf16[1024,256...) custom-call(bf16[1024,2048]{1,0:T(8,128)(2,1)S(1)} %fusion.15.normed_ref, ...), custom_call_target="tpu_custom_call" | custom-call | flops 1000 | bytes 1000 | tf_op jit(solution)/shard_map/attend/pallas_call | solution.py:414
  92.3 12.3 %collective-permute-done.58 = bf16[512,1152]{1,0:T(8,128)(2,1)} collective-permute-done((bf16[512,1152]{1,0:T(8,128)(2,1)}, bf16[512,1152]{1,0:T(8,128)(2,1)}, u32[]{:S(2)}, u32[]{:S(2)}) %collective-permute-start.58) | collective-permute-done | bytes 1179680 | tf_op jit(solution)/shard_map/ppermute | solution.py:118
  108.1 10.7 %reduce-scatter.3.cloned.1.call-start = ((), (), s32[]{:S(2)}) async-start(), calls=%async_computation.4 | async-start | bytes 7077888 | tf_op jit(solution)/shard_map/reduce_scatter | solution.py:846
  118.8 127.6 %conditional.3 = (f32[128,2048]{1,0:T(8,128)S(1)}, f32[128,1]{0,1:T(1,128)S(1)}, bf16[2,512,2048]{2,1,0:T(8,128)(2,1)}, bf16[2,512,2048]{2,1,0:T(8,128)(2,1)}, b...) conditional(s32[]{:T(128)} %convert_element_type.182, () %tuple.77, (s32[]{:T(128)}, ...), branch_computations={%region_3.4_spmd, %region_4.6_spmd} | conditional | flops 6823954 | bytes 84449256 | solution.py:74
  120.3 3.0 collective-permute-done.38
  128.6 12.1 %collective-permute-done.41 = bf16[64,2048]{1,0:T(8,128)(2,1)S(1)} collective-permute-done((bf16[64,2048]{1,0:T(8,128)(2,1)S(1)}, bf16[64,2048]{1,0:T(8,128)(2,1)S(1)}, u32[]{:S(2)}, u32[]{:S(2)}) %collective-permute-start.41) | collective-permute-done | bytes 262176 | tf_op jit(solution)/shard_map/cond/branch_1_fun/ppermute | solution.py:97
  144.9 3.8 collective-permute-done.42
  149.9 6.4 %collective-permute-done.44 = bf16[64,2048]{1,0:T(8,128)(2,1)S(1)} collective-permute-done((bf16[64,2048]{1,0:T(8,128)(2,1)S(1)}, bf16[64,2048]{1,0:T(8,128)(2,1)S(1)}, u32[]{:S(2)}, u32[]{:S(2)}) %collective-permute-start.44) | collective-permute-done | bytes 262176 | tf_op jit(solution)/shard_map/cond/branch_1_fun/ppermute | solution.py:97
  158.1 2.5 collective-permute-start.45
  163.8 3.3 collective-permute-done.46.got_first_ref
  168.5 14.5 %collective-permute-done.45 = bf16[128,2048]{1,0:T(8,128)(2,1)S(1)} collective-permute-done((bf16[128,2048]{1,0:T(8,128)(2,1)S(1)}, bf16[128,2048]{1,0:T(8,128)(2,1)S(1)}, u32[]{:S(2)}, u32[]{:S(2)}) %collective-permute-start.45) | collective-permute-done | bytes 524320 | tf_op jit(solution)/shard_map/cond/branch_1_fun/ppermute | solution.py:97
  187.9 10.8 %collective-permute-done.48.got_first_ref = bf16[2,128,1024]{2,1,0:T(8,128)(2,1)S(1)} collective-permute-done((bf16[2,128,1024]{2,1,0:T(8,128)(2,1)S(1)}, bf16[2,128,1024]{2,1,0:T(8,128)(2,1)S(1)}, u32[]{:S(2)}, u32[]{:S(2)}) %collective-permute-start.48) | collective-permute-done | bytes 524320 | tf_op jit(solution)/shard_map/cond/branch_1_fun/ppermute | solution.py:97
  200.2 6.6 %collective-permute-done.50.got_first_ref = bf16[2,1,128,1024]{3,2,1,0:T(8,128)(2,1)S(1)} collective-permute-done((bf16[2,1,128,1024]{3,2,1,0:T(8,128)(2,1)S(1)}, bf16[2,1,128,1024]{3,2,1,0:T(8,128)(2,1)S(1)}, u32[]{:S(2)}, u32[]{:S(2)}) %collective-permute-start.50) | collective-permute-done | bytes 524320 | tf_op jit(solution)/shard_map/cond/branch_1_fun/ppermute | solution.py:97
  211.5 23.6 %collective-permute-done.52.got_first_ref = bf16[2,2,128,1024]{3,2,1,0:T(8,128)(2,1)S(1)} collective-permute-done((bf16[2,2,128,1024]{3,2,1,0:T(8,128)(2,1)S(1)}, bf16[2,2,128,1024]{3,2,1,0:T(8,128)(2,1)S(1)}, u32[]{:S(2)}, u32[]{:S(2)}) %collective-permute-start.52) | collective-permute-done | bytes 1048608 | tf_op jit(solution)/shard_map/cond/branch_1_fun/ppermute | solution.py:97
  236.2 2.8 open_chip.4
  238.9 7.5 %collective-permute-done.55 = bf16[2,512,2048]{2,1,0:T(8,128)(2,1)} collective-permute-done((bf16[2,512,2048]{2,1,0:T(8,128)(2,1)}, bf16[2,512,2048]{2,1,0:T(8,128)(2,1)}, u32[]{:S(2)}, u32[]{:S(2)}) %collective-permute-start.55) | collective-permute-done | bytes 4194336 | tf_op jit(solution)/shard_map/cond/branch_1_fun/ppermute | solution.py:97
  246.5 15.0 %feed.2 = (bf16[2,512,384]{2,1,0:T(8,128)(2,1)}, bf16[2,512,768]{2,1,0:T(8,128)(2,1)S(1)}, bf16[512,2048]{1,0:T(8,128)(2,1)S(1)}, bf16[512,2048]{1,0:T(8,128)(2,1)S(1)}) custom-call(s32[3]{0:T(128)S(1)} %pad_add_fusion.3.position_ref, bf16[2,512,2048]{2,1,0:T(8,128)(2,1)} %get-tuple-element.493.refs_0_.mine_own.mine_pair, ...), custom_call_target="tpu_custom_call" | custom-call | flops 1000 | bytes 1000 | tf_op jit(solution)/shard_map/feed/pallas_call | solution.py:617
  261.6 14.9 %feed.3 = (bf16[2,512,384]{2,1,0:T(8,128)(2,1)}, bf16[2,512,768]{2,1,0:T(8,128)(2,1)S(1)}, bf16[512,2048]{1,0:T(8,128)(2,1)S(1)}, bf16[512,2048]{1,0:T(8,128)(2,1)}) custom-call(s32[3]{0:T(128)S(1)} %pad_add_fusion.3.position_ref, bf16[2,512,2048]{2,1,0:T(8,128)(2,1)} %get-tuple-element.493.refs_0_.mine_own.mine_pair, ...), custom_call_target="tpu_custom_call" | custom-call | flops 1000 | bytes 1000 | tf_op jit(solution)/shard_map/feed/pallas_call | solution.py:617
  279.9 15.5 %feed_weights.1 = bf16[2048,1152]{1,0:T(8,128)(2,1)} custom-call(s32[3]{0:T(128)S(1)} %pad_add_fusion.3.position_ref, bf16[2,512,2048]{2,1,0:T(8,128)(2,1)} %get-tuple-element.493.refs_0_.mine_own.mine_pair, bf16[2,512,2048]{2,1,0:T(8,128)(2,1)} %get-tuple-element.493.refs_0_.mine_own.mine_pair, ...), custom_call_target="tpu_custom_call" | custom-call | flops 1000 | bytes 1000 | tf_op jit(solution)/shard_map/feed_weights/pallas_call | solution.py:692
  295.5 3.4 fold_chip.11
  301.2 134.4 %conditional.4 = (f32[128,2048]{1,0:T(8,128)}, bf16[2048,768]{1,0:T(8,128)(2,1)}, bf16[512,2048]{1,0:T(8,128)(2,1)}, bf16[512,2048]{1,0:T(8,128)(2,1)}, f32[1,20...) conditional(s32[]{:T(128)} %convert_element_type.182, () %tuple.76, ...), branch_computations={%region_6.7_spmd, %region_7.10_spmd} | conditional | flops 12331057 | bytes 185147088 | solution.py:74
  305.3 5.0 feed_out.2
  313.0 3.2 feed_out.3
  317.6 4.2 collective-permute-done.16
  326.5 2.6 collective-permute-start.20
  331.2 12.8 %collective-permute-done.20 = bf16[64,2048]{1,0:T(8,128)(2,1)S(1)} collective-permute-done((bf16[64,2048]{1,0:T(8,128)(2,1)S(1)}, bf16[64,2048]{1,0:T(8,128)(2,1)S(1)}, u32[]{:S(2)}, u32[]{:S(2)}) %collective-permute-start.20) | collective-permute-done | bytes 262176 | tf_op jit(solution)/shard_map/cond/branch_1_fun/ppermute | solution.py:97
  352.0 10.0 %collective-permute-done.25 = bf16[64,2048]{1,0:T(8,128)(2,1)S(1)} collective-permute-done((bf16[64,2048]{1,0:T(8,128)(2,1)}, bf16[64,2048]{1,0:T(8,128)(2,1)S(1)}, u32[]{:S(2)}, u32[]{:S(2)}) %collective-permute-start.25) | collective-permute-done | bytes 262176 | tf_op jit(solution)/shard_map/cond/branch_1_fun/ppermute | solution.py:97
  362.4 2.7 convert_bitcast_fusion
  365.2 2.8 collective-permute-start.28
  369.3 5.2 collective-permute-done.28.got_first_ref
  380.5 8.9 %collective-permute-done.30.got_first_ref = bf16[2,1,128,1024]{3,2,1,0:T(8,128)(2,1)S(1)} collective-permute-done((bf16[2,1,128,1024]{3,2,1,0:T(8,128)(2,1)S(1)}, bf16[2,1,128,1024]{3,2,1,0:T(8,128)(2,1)S(1)}, u32[]{:S(2)}, u32[]{:S(2)}) %collective-permute-start.30) | collective-permute-done | bytes 524320 | tf_op jit(solution)/shard_map/cond/branch_1_fun/ppermute | solution.py:97
  406.9 24.1 %attend_back.1 = (bf16[2048,768]{1,0:T(8,128)(2,1)}, bf16[512,2048]{1,0:T(8,128)(2,1)}, bf16[512,2048]{1,0:T(8,128)(2,1)}, f32[1,2048]{1,0:T(1,128)S(1)}, f32[2,128]{1,0:T(2,128)}) custom-call(bf16[512,2048]{1,0:T(8,128)(2,1)} %bitcast.106, bf16[512,2048]{1,0:T(8,128)(2,1)} %bitcast.23.grad_other_ref, bf16[2048,768]{1,0:T(8,128)(2,1)} %get-tuple-element.267.proj_ref, ...), custom_call_target="tpu_custom_call" | custom-call | flops 1000 | bytes 1000 | tf_op jit(solution)/shard_map/cond/branch_1_fun/attend_back/pallas_call | solution.py:551
  435.6 88.8 %conditional.5 = (bf16[128,2048]{1,0:T(8,128)(2,1)}, bf16[128,2048]{1,0:T(8,128)(2,1)}, f32[512,768]{1,0:T(8,128)}, f32[512,768]{1,0:T(8,128)}, f32[512,768]{1,0:T(8,128)}, /*index=5*/f32[1088]{0:T(1024)S(1)}) conditional(s32[]{:T(128)} %convert_element_type.182, () %tuple.75, (bf16[128,1024]{1,0:T(8,128)(2,1)}, f32[1,2048]{1,0:T(1,128)S(1)}, ...), branch_computations={%region_11.12_spmd, %region_12.14_spmd} | conditional | flops 10771753 | bytes 57990744 | solution.py:74
  443.1 4.3 collective-permute-done.1
  448.5 3.1 fold_chip.9
  457.2 7.9 %collective-permute-done.7 = f32[4,1088]{1,0:T(4,128)S(1)} collective-permute-done((f32[4,1088]{1,0:T(4,128)S(1)}, f32[4,1088]{1,0:T(4,128)S(1)}, u32[]{:S(2)}, u32[]{:S(2)}) %collective-permute-start.7) | collective-permute-done | bytes 17440 | tf_op jit(solution)/shard_map/cond/branch_1_fun/ppermute | solution.py:97
  465.2 10.8 %collective-permute-done.6 = bf16[128,1152]{1,0:T(8,128)(2,1)S(1)} collective-permute-done((bf16[128,1152]{1,0:T(8,128)(2,1)S(1)}, bf16[128,1152]{1,0:T(8,128)(2,1)S(1)}, u32[]{:S(2)}, u32[]{:S(2)}) %collective-permute-start.6) | collective-permute-done | bytes 294944 | tf_op jit(solution)/shard_map/cond/branch_1_fun/ppermute | solution.py:97
  484.7 17.6 %collective-permute-done.10 = bf16[128,1152]{1,0:T(8,128)(2,1)S(1)} collective-permute-done((bf16[128,1152]{1,0:T(8,128)(2,1)}, bf16[128,1152]{1,0:T(8,128)(2,1)S(1)}, u32[]{:S(2)}, u32[]{:S(2)}) %collective-permute-start.10) | collective-permute-done | bytes 294944 | tf_op jit(solution)/shard_map/cond/branch_1_fun/ppermute | solution.py:97
  506.9 5.6 %collective-permute-done.12 = bf16[128,1152]{1,0:T(8,128)(2,1)S(1)} collective-permute-done((bf16[128,1152]{1,0:T(8,128)(2,1)S(1)}, bf16[128,1152]{1,0:T(8,128)(2,1)S(1)}, u32[]{:S(2)}, u32[]{:S(2)}) %collective-permute-start.12) | collective-permute-done | bytes 294944 | tf_op jit(solution)/shard_map/cond/branch_1_fun/ppermute | solution.py:97
  512.5 2.7 collective-permute-start.15
  515.5 3.4 fusion.7
  518.8 3.2 collective-permute-done.14
  522.1 2.4 feed_sums.1
  (318 shorter events, 138.3 us)
Async XLA Ops:
  7.3 69.4 %all-gather.3.cloned.1.call-start = ((), (), s32[]{:S(2)}) async-start(), calls=%async_computation.2 | async-start | bytes 3932160 | tf_op jit(solution)/shard_map/all_gather | solution.py:784
  9.6 236.9 %all-gather.5.cloned.1.call-start = ((), (), s32[]{:S(2)}) async-start(), calls=%async_computation.3 | async-start | bytes 7077888 | tf_op jit(solution)/shard_map/all_gather | solution.py:813
  10.4 11.4 %collective-permute-start.56 = (bf16[1,1088]{1,0:T(2,128)(2,1)}, bf16[1,1088]{1,0:T(2,128)(2,1)}, u32[]{:S(2)}, u32[]{:S(2)}) collective-permute-start(bf16[1,1088]{1,0:T(2,128)(2,1)} %broadcast_in_dim.58), channel_id=1, source_target_pairs={{0,8},{8,0},{16,24},{24,16},{1,9},{9,1},{17,25},{25,17},{2,10},{10... | collective-permute-start | bytes 6536 | tf_op jit(solution)/shard_map/ppermute | solution.py:118
  76.7 28.0 %collective-permute-start.58 = (bf16[512,1152]{1,0:T(8,128)(2,1)}, bf16[512,1152]{1,0:T(8,128)(2,1)}, u32[]{:S(2)}, u32[]{:S(2)}) collective-permute-start(bf16[512,1152]{1,0:T(8,128)(2,1)} %pad_maximum_fusion.6), channel_id=1, source_target_pairs={{0,8},{8,0},{16,24},{24,16},{1,9},{9,1},{17,25},{25,17},{2,10},{10... | collective-permute-start | bytes 3538952 | tf_op jit(solution)/shard_map/ppermute | solution.py:118
  108.1 327.5 %reduce-scatter.3.cloned.1.call-start = ((), (), s32[]{:S(2)}) async-start(), calls=%async_computation.4 | async-start | bytes 7077888 | tf_op jit(solution)/shard_map/reduce_scatter | solution.py:846
  125.4 15.3 %collective-permute-start.39 = (bf16[2,128,1024]{2,1,0:T(8,128)(2,1)S(1)}, bf16[2,128,1024]{2,1,0:T(8,128)(2,1)S(1)}, u32[]{:S(2)}, u32[]{:S(2)}) collective-permute-start(bf16[2,128,1024]{2,1,0:T(8,128)(2,1)S(1)} %get-tuple-element.124), channel_id=1, source_target_pairs={{0,2},{2,0},{4,6},{6,4},{1,3},{3,1},{5,7},{7,5},{8,10},{10,8},{12,... | collective-permute-start | bytes 1572872 | tf_op jit(solution)/shard_map/cond/branch_1_fun/ppermute | solution.py:97
  126.9 13.8 %collective-permute-start.40 = (bf16[2,128,1024]{2,1,0:T(8,128)(2,1)S(1)}, bf16[2,128,1024]{2,1,0:T(8,128)(2,1)S(1)}, u32[]{:S(2)}, u32[]{:S(2)}) collective-permute-start(bf16[2,128,1024]{2,1,0:T(8,128)(2,1)S(1)} %get-tuple-element.125), channel_id=1, source_target_pairs={{0,4},{4,0},{2,6},{6,2},{1,5},{5,1},{3,7},{7,3},{8,12},{12,8},{10,... | collective-permute-start | bytes 1572872 | tf_op jit(solution)/shard_map/cond/branch_1_fun/ppermute | solution.py:97
  128.4 12.3 %collective-permute-start.41 = (bf16[64,2048]{1,0:T(8,128)(2,1)S(1)}, bf16[64,2048]{1,0:T(8,128)(2,1)S(1)}, u32[]{:S(2)}, u32[]{:S(2)}) collective-permute-start(bf16[64,2048]{1,0:T(8,128)(2,1)S(1)} %get-tuple-element.126), channel_id=1, source_target_pairs={{0,8},{8,0},{16,24},{24,16},{1,9},{9,1},{17,25},{25,17},{2,10},{10... | collective-permute-start | bytes 786440 | tf_op jit(solution)/shard_map/cond/branch_1_fun/ppermute | solution.py:97
  143.5 12.8 %collective-permute-start.44 = (bf16[64,2048]{1,0:T(8,128)(2,1)S(1)}, bf16[64,2048]{1,0:T(8,128)(2,1)S(1)}, u32[]{:S(2)}, u32[]{:S(2)}) collective-permute-start(bf16[64,2048]{1,0:T(8,128)(2,1)S(1)} %get-tuple-element.135), channel_id=1, source_target_pairs={{0,8},{8,0},{16,24},{24,16},{1,9},{9,1},{17,25},{25,17},{2,10},{10... | collective-permute-start | bytes 786440 | tf_op jit(solution)/shard_map/cond/branch_1_fun/ppermute | solution.py:97
  158.1 24.9 %collective-permute-start.45 = (bf16[128,2048]{1,0:T(8,128)(2,1)S(1)}, bf16[128,2048]{1,0:T(8,128)(2,1)S(1)}, u32[]{:S(2)}, u32[]{:S(2)}) collective-permute-start(bf16[128,2048]{1,0:T(8,128)(2,1)S(1)} %multiply_convert_fusion), channel_id=1, source_target_pairs={{0,8},{8,0},{16,24},{24,16},{1,9},{9,1},{17,25},{25,17},{2,10},{10... | collective-permute-start | bytes 1572872 | tf_op jit(solution)/shard_map/cond/branch_1_fun/ppermute | solution.py:97
  183.8 14.9 %collective-permute-start.48 = (bf16[2,128,1024]{2,1,0:T(8,128)(2,1)S(1)}, bf16[2,128,1024]{2,1,0:T(8,128)(2,1)S(1)}, u32[]{:S(2)}, u32[]{:S(2)}) collective-permute-start(bf16[2,128,1024]{2,1,0:T(8,128)(2,1)S(1)} %get-tuple-element.150.first_ref), channel_id=1, source_target_pairs={{0,4},{4,0},{2,6},{6,2},{1,5},{5,1},{3,7},{7,3},{8,12},{12,8},{10,... | collective-permute-start | bytes 1572872 | tf_op jit(solution)/shard_map/cond/branch_1_fun/ppermute | solution.py:97
  185.3 14.9 %collective-permute-start.49 = (bf16[2,128,1024]{2,1,0:T(8,128)(2,1)S(1)}, bf16[2,128,1024]{2,1,0:T(8,128)(2,1)S(1)}, u32[]{:S(2)}, u32[]{:S(2)}) collective-permute-start(bf16[2,128,1024]{2,1,0:T(8,128)(2,1)S(1)} %get-tuple-element.151.second_ref), channel_id=1, source_target_pairs={{0,2},{2,0},{4,6},{6,4},{1,3},{3,1},{5,7},{7,5},{8,10},{10,8},{12,... | collective-permute-start | bytes 1572872 | tf_op jit(solution)/shard_map/cond/branch_1_fun/ppermute | solution.py:97
  186.8 20.0 %collective-permute-start.50 = (bf16[2,1,128,1024]{3,2,1,0:T(8,128)(2,1)S(1)}, bf16[2,1,128,1024]{3,2,1,0:T(8,128)(2,1)S(1)}, u32[]{:S(2)}, u32[]{:S(2)}) collective-permute-start(bf16[2,1,128,1024]{3,2,1,0:T(8,128)(2,1)S(1)} %get-tuple-element.152.first_ref), channel_id=1, source_target_pairs={{0,2},{2,0},{4,6},{6,4},{1,3},{3,1},{5,7},{7,5},{8,10},{10,8},{12,... | collective-permute-start | bytes 1572872 | tf_op jit(solution)/shard_map/cond/branch_1_fun/ppermute | solution.py:97
  187.3 19.4 %collective-permute-start.51 = (bf16[2,1,128,1024]{3,2,1,0:T(8,128)(2,1)S(1)}, bf16[2,1,128,1024]{3,2,1,0:T(8,128)(2,1)S(1)}, u32[]{:S(2)}, u32[]{:S(2)}) collective-permute-start(bf16[2,1,128,1024]{3,2,1,0:T(8,128)(2,1)S(1)} %get-tuple-element.153.second_ref), channel_id=1, source_target_pairs={{0,4},{4,0},{2,6},{6,2},{1,5},{5,1},{3,7},{7,3},{8,12},{12,8},{10,... | collective-permute-start | bytes 1572872 | tf_op jit(solution)/shard_map/cond/branch_1_fun/ppermute | solution.py:97
  209.4 26.7 %collective-permute-start.54 = (bf16[1,512,2048]{2,1,0:T(8,128)(2,1)}, bf16[1,512,2048]{2,1,0:T(8,128)(2,1)}, u32[]{:S(2)}, u32[]{:S(2)}) collective-permute-start(bf16[1,512,2048]{2,1,0:T(8,128)(2,1)} %bitcast.9), channel_id=1, source_target_pairs={{0,1},{1,0},{2,3},{3,2},{4,5},{5,4},{6,7},{7,6},{8,9},{9,8},{10,11... | collective-permute-start | bytes 6291464 | tf_op jit(solution)/shard_map/cond/branch_1_fun/ppermute | solution.py:97
  209.4 25.6 %collective-permute-start.52 = (bf16[2,2,128,1024]{3,2,1,0:T(8,128)(2,1)S(1)}, bf16[2,2,128,1024]{3,2,1,0:T(8,128)(2,1)S(1)}, u32[]{:S(2)}, u32[]{:S(2)}) collective-permute-start(bf16[2,2,128,1024]{3,2,1,0:T(8,128)(2,1)S(1)} %get-tuple-element.160.first_ref), channel_id=1, source_target_pairs={{0,2},{2,0},{4,6},{6,4},{1,3},{3,1},{5,7},{7,5},{8,10},{10,8},{12,... | collective-permute-start | bytes 3145736 | tf_op jit(solution)/shard_map/cond/branch_1_fun/ppermute | solution.py:97
  210.9 25.3 %collective-permute-start.53 = (bf16[2,2,128,1024]{3,2,1,0:T(8,128)(2,1)S(1)}, bf16[2,2,128,1024]{3,2,1,0:T(8,128)(2,1)S(1)}, u32[]{:S(2)}, u32[]{:S(2)}) collective-permute-start(bf16[2,2,128,1024]{3,2,1,0:T(8,128)(2,1)S(1)} %get-tuple-element.161.second_ref), channel_id=1, source_target_pairs={{0,4},{4,0},{2,6},{6,2},{1,5},{5,1},{3,7},{7,3},{8,12},{12,8},{10,... | collective-permute-start | bytes 3145736 | tf_op jit(solution)/shard_map/cond/branch_1_fun/ppermute | solution.py:97
  261.5 15.0 %collective-permute-start.59 = (bf16[512,2048]{1,0:T(8,128)(2,1)S(1)}, bf16[512,2048]{1,0:T(8,128)(2,1)S(1)}, u32[]{:S(2)}, u32[]{:S(2)}) collective-permute-start(bf16[512,2048]{1,0:T(8,128)(2,1)S(1)} %get-tuple-element.472), channel_id=1, source_target_pairs={{0,1},{1,0},{2,3},{3,2},{4,5},{5,4},{6,7},{7,6},{8,9},{9,8},{10,11... | collective-permute-start | bytes 6291464 | tf_op jit(solution)/shard_map/ppermute | solution.py:97
  278.4 17.0 %collective-permute-start.62 = (bf16[512,2048]{1,0:T(8,128)(2,1)}, bf16[512,2048]{1,0:T(8,128)(2,1)}, u32[]{:S(2)}, u32[]{:S(2)}) collective-permute-start(bf16[512,2048]{1,0:T(8,128)(2,1)} %get-tuple-element.492), channel_id=1, source_target_pairs={{0,1},{1,0},{2,3},{3,2},{4,5},{5,4},{6,7},{7,6},{8,9},{9,8},{10,11... | collective-permute-start | bytes 6291464 | tf_op jit(solution)/shard_map/ppermute | solution.py:97
  278.8 16.6 %collective-permute-start.60 = (bf16[2,128,1024]{2,1,0:T(8,128)(2,1)}, bf16[2,128,1024]{2,1,0:T(8,128)(2,1)}, u32[]{:S(2)}, u32[]{:S(2)}) collective-permute-start(bf16[2,128,1024]{2,1,0:T(8,128)(2,1)} %get-tuple-element.490), channel_id=1, source_target_pairs={{0,2},{2,0},{4,6},{6,4},{1,3},{3,1},{5,7},{7,5},{8,10},{10,8},{12,... | collective-permute-start | bytes 1572872 | tf_op jit(solution)/shard_map/ppermute | solution.py:97
  279.3 16.0 %collective-permute-start.61 = (bf16[2,128,1024]{2,1,0:T(8,128)(2,1)}, bf16[2,128,1024]{2,1,0:T(8,128)(2,1)}, u32[]{:S(2)}, u32[]{:S(2)}) collective-permute-start(bf16[2,128,1024]{2,1,0:T(8,128)(2,1)} %get-tuple-element.491), channel_id=1, source_target_pairs={{0,4},{4,0},{2,6},{6,2},{1,5},{5,1},{3,7},{7,3},{8,12},{12,8},{10,... | collective-permute-start | bytes 1572872 | tf_op jit(solution)/shard_map/ppermute | solution.py:97
  295.4 229.1 %reduce-scatter.5.cloned.1.call-start = ((), (), s32[]{:S(2)}) async-start(), calls=%async_computation.5 | async-start | bytes 3932160 | tf_op jit(solution)/shard_map/reduce_scatter | solution.py:890
  301.2 20.6 %collective-permute-start.18 = (bf16[2,128,1024]{2,1,0:T(8,128)(2,1)}, bf16[2,128,1024]{2,1,0:T(8,128)(2,1)S(1)}, u32[]{:S(2)}, u32[]{:S(2)}) collective-permute-start(bf16[2,128,1024]{2,1,0:T(8,128)(2,1)} %get-tuple-element.179), channel_id=1, source_target_pairs={{0,2},{2,0},{4,6},{6,4},{1,3},{3,1},{5,7},{7,5},{8,10},{10,8},{12,... | collective-permute-start | bytes 1572872 | tf_op jit(solution)/shard_map/cond/branch_1_fun/ppermute | solution.py:97
  302.7 19.1 %collective-permute-start.19 = (bf16[2,128,1024]{2,1,0:T(8,128)(2,1)}, bf16[2,128,1024]{2,1,0:T(8,128)(2,1)S(1)}, u32[]{:S(2)}, u32[]{:S(2)}) collective-permute-start(bf16[2,128,1024]{2,1,0:T(8,128)(2,1)} %get-tuple-element.180), channel_id=1, source_target_pairs={{0,4},{4,0},{2,6},{6,2},{1,5},{5,1},{3,7},{7,3},{8,12},{12,8},{10,... | collective-permute-start | bytes 1572872 | tf_op jit(solution)/shard_map/cond/branch_1_fun/ppermute | solution.py:97
  304.2 17.6 %collective-permute-start.16 = (bf16[128,1024]{1,0:T(8,128)(2,1)}, bf16[128,1024]{1,0:T(8,128)(2,1)}, u32[]{:S(2)}, u32[]{:S(2)}) collective-permute-start(bf16[128,1024]{1,0:T(8,128)(2,1)} %get-tuple-element.177), channel_id=1, source_target_pairs={{0,4},{4,0},{2,6},{6,2},{1,5},{5,1},{3,7},{7,3},{8,12},{12,8},{10,... | collective-permute-start | bytes 786440 | tf_op jit(solution)/shard_map/cond/branch_1_fun/ppermute | solution.py:97
  304.8 17.0 %collective-permute-start.17 = (bf16[128,1024]{1,0:T(8,128)(2,1)}, bf16[128,1024]{1,0:T(8,128)(2,1)}, u32[]{:S(2)}, u32[]{:S(2)}) collective-permute-start(bf16[128,1024]{1,0:T(8,128)(2,1)} %get-tuple-element.178), channel_id=1, source_target_pairs={{0,2},{2,0},{4,6},{6,4},{1,3},{3,1},{5,7},{7,5},{8,10},{10,8},{12,... | collective-permute-start | bytes 786440 | tf_op jit(solution)/shard_map/cond/branch_1_fun/ppermute | solution.py:97
  326.0 17.9 %collective-permute-start.23 = (bf16[512,2048]{1,0:T(8,128)(2,1)S(1)}, bf16[512,2048]{1,0:T(8,128)(2,1)S(1)}, u32[]{:S(2)}, u32[]{:S(2)}) collective-permute-start(bf16[512,2048]{1,0:T(8,128)(2,1)S(1)} %copy-done.13), channel_id=1, source_target_pairs={{0,1},{1,0},{2,3},{3,2},{4,5},{5,4},{6,7},{7,6},{8,9},{9,8},{10,11... | collective-permute-start | bytes 6291464 | tf_op jit(solution)/shard_map/cond/branch_1_fun/ppermute | solution.py:97
  326.0 17.9 %collective-permute-start.24 = (bf16[512,2048]{1,0:T(8,128)(2,1)S(1)}, bf16[512,2048]{1,0:T(8,128)(2,1)S(1)}, u32[]{:S(2)}, u32[]{:S(2)}) collective-permute-start(bf16[512,2048]{1,0:T(8,128)(2,1)S(1)} %copy-done.11), channel_id=1, source_target_pairs={{0,1},{1,0},{2,3},{3,2},{4,5},{5,4},{6,7},{7,6},{8,9},{9,8},{10,11... | collective-permute-start | bytes 6291464 | tf_op jit(solution)/shard_map/cond/branch_1_fun/ppermute | solution.py:97
  326.5 17.4 %collective-permute-start.20 = (bf16[64,2048]{1,0:T(8,128)(2,1)S(1)}, bf16[64,2048]{1,0:T(8,128)(2,1)S(1)}, u32[]{:S(2)}, u32[]{:S(2)}) collective-permute-start(bf16[64,2048]{1,0:T(8,128)(2,1)S(1)} %get-tuple-element.201), channel_id=1, source_target_pairs={{0,8},{8,0},{16,24},{24,16},{1,9},{9,1},{17,25},{25,17},{2,10},{10... | collective-permute-start | bytes 786440 | tf_op jit(solution)/shard_map/cond/branch_1_fun/ppermute | solution.py:97
  329.2 14.8 %collective-permute-start.21 = (bf16[128,1024]{1,0:T(8,128)(2,1)S(1)}, bf16[128,1024]{1,0:T(8,128)(2,1)S(1)}, u32[]{:S(2)}, u32[]{:S(2)}) collective-permute-start(bf16[128,1024]{1,0:T(8,128)(2,1)S(1)} %get-tuple-element.202), channel_id=1, source_target_pairs={{0,4},{4,0},{2,6},{6,2},{1,5},{5,1},{3,7},{7,3},{8,12},{12,8},{10,... | collective-permute-start | bytes 786440 | tf_op jit(solution)/shard_map/cond/branch_1_fun/ppermute | solution.py:97
  330.6 13.3 %collective-permute-start.22 = (bf16[128,1024]{1,0:T(8,128)(2,1)S(1)}, bf16[128,1024]{1,0:T(8,128)(2,1)S(1)}, u32[]{:S(2)}, u32[]{:S(2)}) collective-permute-start(bf16[128,1024]{1,0:T(8,128)(2,1)S(1)} %get-tuple-element.203), channel_id=1, source_target_pairs={{0,2},{2,0},{4,6},{6,4},{1,3},{3,1},{5,7},{7,5},{8,10},{10,8},{12,... | collective-permute-start | bytes 786440 | tf_op jit(solution)/shard_map/cond/branch_1_fun/ppermute | solution.py:97
  347.5 14.6 %collective-permute-start.26 = (bf16[2,128,1024]{2,1,0:T(8,128)(2,1)}, bf16[2,128,1024]{2,1,0:T(8,128)(2,1)S(1)}, u32[]{:S(2)}, u32[]{:S(2)}) collective-permute-start(bf16[2,128,1024]{2,1,0:T(8,128)(2,1)} %get-tuple-element.215), channel_id=1, source_target_pairs={{0,2},{2,0},{4,6},{6,4},{1,3},{3,1},{5,7},{7,5},{8,10},{10,8},{12,... | collective-permute-start | bytes 1572872 | tf_op jit(solution)/shard_map/cond/branch_1_fun/ppermute | solution.py:97
  348.3 13.8 %collective-permute-start.27 = (bf16[2,128,1024]{2,1,0:T(8,128)(2,1)}, bf16[2,128,1024]{2,1,0:T(8,128)(2,1)S(1)}, u32[]{:S(2)}, u32[]{:S(2)}) collective-permute-start(bf16[2,128,1024]{2,1,0:T(8,128)(2,1)} %get-tuple-element.216), channel_id=1, source_target_pairs={{0,4},{4,0},{2,6},{6,2},{1,5},{5,1},{3,7},{7,3},{8,12},{12,8},{10,... | collective-permute-start | bytes 1572872 | tf_op jit(solution)/shard_map/cond/branch_1_fun/ppermute | solution.py:97
  349.7 12.3 %collective-permute-start.25 = (bf16[64,2048]{1,0:T(8,128)(2,1)}, bf16[64,2048]{1,0:T(8,128)(2,1)S(1)}, u32[]{:S(2)}, u32[]{:S(2)}) collective-permute-start(bf16[64,2048]{1,0:T(8,128)(2,1)} %get-tuple-element.214), channel_id=1, source_target_pairs={{0,8},{8,0},{16,24},{24,16},{1,9},{9,1},{17,25},{25,17},{2,10},{10... | collective-permute-start | bytes 786440 | tf_op jit(solution)/shard_map/cond/branch_1_fun/ppermute | solution.py:97
  365.2 9.3 %collective-permute-start.28 = (bf16[1,128,1024]{2,1,0:T(8,128)(2,1)S(1)}, bf16[1,128,1024]{2,1,0:T(8,128)(2,1)S(1)}, u32[]{:S(2)}, u32[]{:S(2)}) collective-permute-start(bf16[1,128,1024]{2,1,0:T(8,128)(2,1)S(1)} %get-tuple-element.225.first_ref), channel_id=1, source_target_pairs={{0,4},{4,0},{2,6},{6,2},{1,5},{5,1},{3,7},{7,3},{8,12},{12,8},{10,... | collective-permute-start | bytes 786440 | tf_op jit(solution)/shard_map/cond/branch_1_fun/ppermute | solution.py:97
  376.5 12.9 %collective-permute-start.30 = (bf16[2,1,128,1024]{3,2,1,0:T(8,128)(2,1)S(1)}, bf16[2,1,128,1024]{3,2,1,0:T(8,128)(2,1)S(1)}, u32[]{:S(2)}, u32[]{:S(2)}) collective-permute-start(bf16[2,1,128,1024]{3,2,1,0:T(8,128)(2,1)S(1)} %get-tuple-element.229.first_ref), channel_id=1, source_target_pairs={{0,2},{2,0},{4,6},{6,4},{1,3},{3,1},{5,7},{7,5},{8,10},{10,8},{12,... | collective-permute-start | bytes 1572872 | tf_op jit(solution)/shard_map/cond/branch_1_fun/ppermute | solution.py:97
  377.9 12.5 %collective-permute-start.31 = (bf16[2,1,128,1024]{3,2,1,0:T(8,128)(2,1)S(1)}, bf16[2,1,128,1024]{3,2,1,0:T(8,128)(2,1)S(1)}, u32[]{:S(2)}, u32[]{:S(2)}) collective-permute-start(bf16[2,1,128,1024]{3,2,1,0:T(8,128)(2,1)S(1)} %get-tuple-element.231), channel_id=1, source_target_pairs={{0,4},{4,0},{2,6},{6,2},{1,5},{5,1},{3,7},{7,3},{8,12},{12,8},{10,... | collective-permute-start | bytes 1572872 | tf_op jit(solution)/shard_map/cond/branch_1_fun/ppermute | solution.py:97
  391.1 9.5 %collective-permute-start.32 = (bf16[1,512,2048]{2,1,0:T(8,128)(2,1)S(1)}, bf16[1,512,2048]{2,1,0:T(8,128)(2,1)}, u32[]{:S(2)}, u32[]{:S(2)}) collective-permute-start(bf16[1,512,2048]{2,1,0:T(8,128)(2,1)S(1)} %bitcast.105), channel_id=1, source_target_pairs={{0,1},{1,0},{2,3},{3,2},{4,5},{5,4},{6,7},{7,6},{8,9},{9,8},{10,11... | collective-permute-start | bytes 6291464 | tf_op jit(solution)/shard_map/cond/branch_1_fun/ppermute | solution.py:97
  391.2 9.0 %collective-permute-start.33 = (bf16[128,1024]{1,0:T(8,128)(2,1)}, bf16[128,1024]{1,0:T(8,128)(2,1)}, u32[]{:S(2)}, u32[]{:S(2)}) collective-permute-start(bf16[128,1024]{1,0:T(8,128)(2,1)} %get-tuple-element.238), channel_id=1, source_target_pairs={{0,4},{4,0},{2,6},{6,2},{1,5},{5,1},{3,7},{7,3},{8,12},{12,8},{10,... | collective-permute-start | bytes 786440 | tf_op jit(solution)/shard_map/cond/branch_1_fun/ppermute | solution.py:97
  403.6 27.4 %collective-permute-start.35 = (bf16[128,2048]{1,0:T(8,128)(2,1)}, bf16[128,2048]{1,0:T(8,128)(2,1)}, u32[]{:S(2)}, u32[]{:S(2)}) collective-permute-start(bf16[128,2048]{1,0:T(8,128)(2,1)} %pad_maximum_fusion.1), channel_id=1, source_target_pairs={{0,8},{8,0},{16,24},{24,16},{1,9},{9,1},{17,25},{25,17},{2,10},{10... | collective-permute-start | bytes 1572872 | tf_op jit(solution)/shard_map/cond/branch_1_fun/ppermute | solution.py:97
  403.6 27.4 %collective-permute-start.36 = (bf16[2,128,1024]{2,1,0:T(8,128)(2,1)}, bf16[2,128,1024]{2,1,0:T(8,128)(2,1)S(1)}, u32[]{:S(2)}, u32[]{:S(2)}) collective-permute-start(bf16[2,128,1024]{2,1,0:T(8,128)(2,1)} %get-tuple-element.263), channel_id=1, source_target_pairs={{0,2},{2,0},{4,6},{6,4},{1,3},{3,1},{5,7},{7,5},{8,10},{10,8},{12,... | collective-permute-start | bytes 1572872 | tf_op jit(solution)/shard_map/cond/branch_1_fun/ppermute | solution.py:97
  404.5 26.5 %collective-permute-start.37 = (bf16[2,128,1024]{2,1,0:T(8,128)(2,1)}, bf16[2,128,1024]{2,1,0:T(8,128)(2,1)S(1)}, u32[]{:S(2)}, u32[]{:S(2)}) collective-permute-start(bf16[2,128,1024]{2,1,0:T(8,128)(2,1)} %get-tuple-element.264), channel_id=1, source_target_pairs={{0,4},{4,0},{2,6},{6,2},{1,5},{5,1},{3,7},{7,3},{8,12},{12,8},{10,... | collective-permute-start | bytes 1572872 | tf_op jit(solution)/shard_map/cond/branch_1_fun/ppermute | solution.py:97
  438.4 9.4 %collective-permute-start = (bf16[512,2048]{1,0:T(8,128)(2,1)}, bf16[512,2048]{1,0:T(8,128)(2,1)S(1)}, u32[]{:S(2)}, u32[]{:S(2)}) collective-permute-start(bf16[512,2048]{1,0:T(8,128)(2,1)} %get-tuple-element.309), channel_id=1, source_target_pairs={{0,1},{1,0},{2,3},{3,2},{4,5},{5,4},{6,7},{7,6},{8,9},{9,8},{10,11... | collective-permute-start | bytes 6291464 | tf_op jit(solution)/shard_map/cond/branch_1_fun/ppermute | solution.py:97
  451.7 24.3 %collective-permute-start.4 = (bf16[2,128,1024]{2,1,0:T(8,128)(2,1)}, bf16[2,128,1024]{2,1,0:T(8,128)(2,1)S(1)}, u32[]{:S(2)}, u32[]{:S(2)}) collective-permute-start(bf16[2,128,1024]{2,1,0:T(8,128)(2,1)} %get-tuple-element.327), channel_id=1, source_target_pairs={{0,2},{2,0},{4,6},{6,4},{1,3},{3,1},{5,7},{7,5},{8,10},{10,8},{12,... | collective-permute-start | bytes 1572872 | tf_op jit(solution)/shard_map/cond/branch_1_fun/ppermute | solution.py:97
  452.8 23.1 %collective-permute-start.5 = (bf16[2,128,1024]{2,1,0:T(8,128)(2,1)}, bf16[2,128,1024]{2,1,0:T(8,128)(2,1)}, u32[]{:S(2)}, u32[]{:S(2)}) collective-permute-start(bf16[2,128,1024]{2,1,0:T(8,128)(2,1)} %get-tuple-element.328), channel_id=1, source_target_pairs={{0,4},{4,0},{2,6},{6,2},{1,5},{5,1},{3,7},{7,3},{8,12},{12,8},{10,... | collective-permute-start | bytes 1572872 | tf_op jit(solution)/shard_map/cond/branch_1_fun/ppermute | solution.py:97
  454.3 21.7 %collective-permute-start.6 = (bf16[128,1152]{1,0:T(8,128)(2,1)S(1)}, bf16[128,1152]{1,0:T(8,128)(2,1)S(1)}, u32[]{:S(2)}, u32[]{:S(2)}) collective-permute-start(bf16[128,1152]{1,0:T(8,128)(2,1)S(1)} %copy-done.37), channel_id=1, source_target_pairs={{0,8},{8,0},{16,24},{24,16},{1,9},{9,1},{17,25},{25,17},{2,10},{10... | collective-permute-start | bytes 884744 | tf_op jit(solution)/shard_map/cond/branch_1_fun/ppermute | solution.py:97
  479.4 22.9 %collective-permute-start.10 = (bf16[128,1152]{1,0:T(8,128)(2,1)}, bf16[128,1152]{1,0:T(8,128)(2,1)S(1)}, u32[]{:S(2)}, u32[]{:S(2)}) collective-permute-start(bf16[128,1152]{1,0:T(8,128)(2,1)} %get-tuple-element.340), channel_id=1, source_target_pairs={{0,8},{8,0},{16,24},{24,16},{1,9},{9,1},{17,25},{25,17},{2,10},{10... | collective-permute-start | bytes 884744 | tf_op jit(solution)/shard_map/cond/branch_1_fun/ppermute | solution.py:97
  502.3 10.2 %collective-permute-start.12 = (bf16[128,1152]{1,0:T(8,128)(2,1)S(1)}, bf16[128,1152]{1,0:T(8,128)(2,1)S(1)}, u32[]{:S(2)}, u32[]{:S(2)}) collective-permute-start(bf16[128,1152]{1,0:T(8,128)(2,1)S(1)} %copy-done.36), channel_id=1, source_target_pairs={{0,8},{8,0},{16,24},{24,16},{1,9},{9,1},{17,25},{25,17},{2,10},{10... | collective-permute-start | bytes 884744 | tf_op jit(solution)/shard_map/cond/branch_1_fun/ppermute | solution.py:97
  (70 other events, 671.9 us)
Sparse Core Ops, SparseCore 0:
  10.2 66.3 all-gather.2
  108.2 112.8 all-gather.4
  295.5 112.5 reduce-scatter.2
  435.8 75.0 reduce-scatter.4

commit v3 on v2

--- a/solution.py
+++ b/solution.py
@@ -78,10 +78,11 @@
 
 class Job:
     def __init__(self, steps):
-        self.steps, self.moves, self.keep, self.value = steps, (), (), None
+        self.steps, self.moves, self.keep, self.held, self.value = steps, (), (), (), None
         self.resume(None)
 
     def resume(self, got):
+        self.held, self.arrived = self.keep, got
         try:
             given = self.steps.send(got)
             self.moves, self.keep = given if isinstance(given, tuple) else (given, ())
@@ -89,8 +90,9 @@
             self.moves, self.keep, self.value = (), (), end.value
 
 
-def beside(*jobs, kernels=()):
+def beside(*jobs, kernels=(), ready=()):
     jobs = [job for job in jobs if job.moves]
+    ready = [job for job in ready if job.moves]
     given = [[move[0] for move in job.moves] for job in jobs], [args for _, args in kernels]
     arrays, args = lax.optimization_barrier(given)
     got = [
@@ -98,7 +100,10 @@
         for held, job in zip(arrays, jobs)
     ]
     results = [kernel[0](*own) for own, kernel in zip(args, kernels)]
-    got, results = lax.optimization_barrier((got, results))
+    later = [[move[0] for move in job.moves] for job in ready]
+    got, results, later = lax.optimization_barrier((got, results, later))
+    for job, arrays in zip(ready, later):
+        job.moves = [(array, *move[1:]) for array, move in zip(arrays, job.moves)]
     for job, arrived in zip(jobs, got):
         job.resume(arrived)
     return results
@@ -200,21 +205,37 @@
     )
 
 
-def plane_scatter(keep, give):
+def fold_end_kernel(position_ref, keep_first_ref, got_first_ref, keep_second_ref, got_second_ref, out_ref):
+    middle = keep_first_ref.shape[-1]
+    out_ref[:, :middle] = low(wide(keep_first_ref[...]) + wide(got_first_ref[...]))
+    out_ref[:, middle:] = low(wide(keep_second_ref[...]) + wide(got_second_ref[...]))
+
+
+def fold_end(keep_first, got_first, keep_second, got_second):
+    rows, width = keep_first.shape
+    (out,) = vmem_call(
+        fold_end_kernel, "fold_end", 16, [(rows, 2 * width)], keep_first, got_first, keep_second, got_second
+    )
+    return out
+
+
+def plane_scatter(keep, give, rounded=False):
     (got,) = yield [(give, "tensor", SWAP)]
     folded = fold_chip(keep, got)
-    return (yield from chip_scatter(*folded))
-
-
-def chip_scatter(give_first, keep_first, give_second, keep_second):
+    return (yield from chip_scatter(*folded, rounded))
+
+
+def chip_scatter(give_first, keep_first, give_second, keep_second, rounded=False):
     held = (give_first, keep_first, give_second, keep_second)
     got = yield [(give_first, "heads", NEAR), (give_second, "heads", FAR)], held
-    return (yield from line_scatter(*fold_line(keep_first, got[0], keep_second, got[1])))
-
-
-def line_scatter(give_first, keep_first, give_second, keep_second):
+    return (yield from line_scatter(*fold_line(keep_first, got[0], keep_second, got[1]), rounded))
+
+
+def line_scatter(give_first, keep_first, give_second, keep_second, rounded=False):
     held = (give_first, keep_first, give_second, keep_second)
     got = yield [(give_first, "heads", FAR), (give_second, "heads", NEAR)], held
+    if rounded:
+        return fold_end(keep_first, got[0], keep_second, got[1])
     first = wide(keep_first) + wide(got[0])
     second = wide(keep_second) + wide(got[1])
     return jnp.concatenate([first, second], axis=-1)
@@ -269,7 +290,7 @@
 
 
 def sum_all(values):
-    for axis in ("tensor", "heads", "fsdp"):
+    for axis in ("fsdp", "tensor", "heads"):
         for stride in bits(axis):
             (got,) = yield [(values, axis, flip(axis, stride))]
             values = values + got
@@ -327,14 +348,11 @@
     key_gain_ref,
     seg_rows_ref,
     seg_keys_ref,
-    position_ref,
     raw_ref,
     query_ref,
     key_ref,
     value_ref,
     mixed_ref,
-    keep_ref,
-    give_ref,
     keys,
     values,
 ):
@@ -343,8 +361,7 @@
     query_cols = kv_cols * group
     count = length // ROWS
     step = pl.program_id(0)
-    split = query_cols + 2 * kv_cols
-    raw = jnp.dot(normed_ref[...], proj_ref[:, :split], preferred_element_type=jnp.float32)
+    raw = jnp.dot(normed_ref[...], proj_ref[...], preferred_element_type=jnp.float32)
     raw_ref[...] = raw[:, : query_cols + kv_cols]
     cosine, sine = cosine_ref[...], sine_ref[...]
     here = pl.ds(pl.multiple_of(step * ROWS, ROWS), ROWS)
@@ -385,12 +402,8 @@
                     jnp.dot(low(probs), values[span, kv], preferred_element_type=jnp.float32)
                 )
 
-    keep_ref[...], give_ref[...] = by_core(
-        position_ref[0], low(contract(mixed_ref[...], proj_ref[:, split:], 1, 1))
-    )
-
-
-def attend(group, normed, proj, cosine, sine, query_gain, key_gain, segment_row):
+
+def attend(group, normed, proj, cosine, sine, query_gain, key_gain, seg_rows, segment_row):
     length, model = normed.shape
     kv_cols = proj.shape[1] // (2 * group + 2)
     query_cols = kv_cols * group
@@ -401,8 +414,8 @@
     def whole(array):
         return pl.BlockSpec(array.shape, lambda i: (0, 0))
 
-    seg_rows, seg_keys = segment_row[:, None], segment_row[None, :]
-    args = (normed, proj, cosine, sine, query_gain[None], key_gain[None], seg_rows, seg_keys, position())
+    seg_keys = segment_row[None, :]
+    args = (normed, proj, cosine, sine, query_gain[None], key_gain[None], seg_rows, seg_keys)
     outs = [
         (query_cols + kv_cols, jnp.float32),
         (query_cols, jnp.bfloat16),
@@ -410,25 +423,21 @@
         (kv_cols, jnp.bfloat16),
         (query_cols, jnp.bfloat16),
     ]
-    halves = (length // 2, model)
     return pl.pallas_call(
         functools.partial(attend_kernel, group),
         grid=(length // ROWS,),
         in_specs=[
             rows(model),
-            whole(proj),
+            pl.BlockSpec((model, query_cols + 2 * kv_cols), lambda i: (0, 0)),
             rows(HD),
             rows(HD),
             whole(args[4]),
             whole(args[5]),
             rows(1),
             whole(seg_keys),
-            pl.BlockSpec(memory_space=pltpu.SMEM),
         ],
-        out_specs=[rows(width) for width, _ in outs]
-        + [pl.BlockSpec((ROWS // 2, model), lambda i: (i, 0))] * 2,
-        out_shape=[jax.ShapeDtypeStruct((length, width), kind) for width, kind in outs]
-        + [jax.ShapeDtypeStruct(halves, jnp.bfloat16)] * 2,
+        out_specs=[rows(width) for width, _ in outs],
+        out_shape=[jax.ShapeDtypeStruct((length, width), kind) for width, kind in outs],
         scratch_shapes=[
             pltpu.VMEM((length, kv_cols), jnp.bfloat16),
             pltpu.VMEM((length, kv_cols), jnp.bfloat16),
@@ -439,11 +448,36 @@
     )(*args)
 
 
+def attend_out_kernel(position_ref, mixed_ref, proj_ref, keep_ref, give_ref):
+    keep_ref[...], give_ref[...] = by_core(
+        position_ref[0], low(contract(mixed_ref[...], proj_ref[...], 1, 1))
+    )
+
+
+def attend_out(mixed, proj):
+    length, cols = mixed.shape
+    model = proj.shape[0]
+    return pl.pallas_call(
+        attend_out_kernel,
+        grid=(length // ROWS,),
+        in_specs=[
+            pl.BlockSpec(memory_space=pltpu.SMEM),
+            pl.BlockSpec((ROWS, cols), lambda i: (i, 0)),
+            pl.BlockSpec((model, cols), lambda i: (0, proj.shape[1] // cols - 1)),
+        ],
+        out_specs=[pl.BlockSpec((ROWS // 2, model), lambda i: (i, 0))] * 2,
+        out_shape=[jax.ShapeDtypeStruct((length // 2, model), jnp.bfloat16)] * 2,
+        compiler_params=call_params(24),
+        cost_estimate=cheap(),
+        name="attend_out",
+    )(position(), mixed, proj)
+
+
 def attend_back_kernel(
     group,
     grad_mine_ref,
     grad_other_ref,
-    proj_ref,
+    out_proj_ref,
     cosine_ref,
     sine_ref,
     query_gain_ref,
@@ -454,18 +488,11 @@
     query_ref,
     key_ref,
     value_ref,
-    tokens_ref,
-    scale_ref,
-    normed_ref,
     mixed_ref,
     position_ref,
-    weight_ref,
-    keep_ref,
-    give_ref,
-    gain_ref,
+    low_ref,
+    mixed_split_ref,
     head_gain_ref,
-    grad_ref,
-    low_ref,
     mixed_grad,
     query_sum,
     key_sum,
@@ -474,14 +501,14 @@
     length, kv_cols = key_sum.shape
     query_cols = kv_cols * group
     count = length // ROWS
-    split = query_cols + 2 * kv_cols
-    for at in range(count):
-        here = slice(at * ROWS, (at + 1) * ROWS)
-        rows = slice(at * ROWS // 2, (at + 1) * ROWS // 2)
-        grad_ref[here, :] = joined(position_ref[0], grad_mine_ref[rows, :], grad_other_ref[rows, :])
-        mixed_grad[here, :] = low(
-            jnp.dot(grad_ref[here, :], proj_ref[:, split:], preferred_element_type=jnp.float32)
-        )
+    share = ROWS // 2
+    core = position_ref[0]
+    for k, ref in enumerate((grad_mine_ref, grad_other_ref)):
+        part = low(jnp.dot(ref[...], out_proj_ref[...], preferred_element_type=jnp.float32))
+        for at in range(count):
+            start = pl.multiple_of(at * ROWS + (core + k - 2 * k * core) * share, share)
+            mixed_grad[pl.ds(start, share), :] = part[at * share : (at + 1) * share]
+            mixed_split_ref[k, at * share : (at + 1) * share, :] = mixed_ref[pl.ds(start, share), :]
     key_sum[...] = jnp.zeros_like(key_sum)
     value_sum[...] = jnp.zeros_like(value_sum)
     for at in range(count):
@@ -510,7 +537,6 @@
             key_sum[span, kv] += contract(score_grad, query, 0, 0)
             value_sum[span, kv] += contract(low(probs), grad, 0, 0)
 
-    gain_ref[...] = jnp.zeros_like(gain_ref)
     head_gain_ref[...] = jnp.zeros_like(head_gain_ref)
     for at in range(count):
         here = slice(at * ROWS, (at + 1) * ROWS)
@@ -527,188 +553,229 @@
             gain = query_gain_ref[...] if is_query else key_gain_ref[...]
             low_ref[here, cols] = low(norm_back(raw, scale, turned * gain))
         low_ref[here, query_cols + kv_cols :] = low(value_sum[here, :])
-        part = contract(low_ref[here, :], proj_ref[:, :split], 1, 1)
-        rows = slice(at * ROWS // 2, (at + 1) * ROWS // 2)
-        keep_ref[rows, :], give_ref[rows, :] = by_core(position_ref[0], low(part))
-        gain_ref[...] += jnp.sum(part * wide(tokens_ref[here, :]) * scale_ref[here, :], axis=0, keepdims=True)
-    cols = 512
-    for at in range(0, normed_ref.shape[1], cols):
-        here = slice(at, at + cols)
-        weight_ref[here, :split] = low(contract(normed_ref[:, here], low_ref[...], 0, 0))
-        weight_ref[here, split:] = low(contract(grad_ref[:, here], mixed_ref[...], 0, 0))
 
 
 def attend_back(
-    group, grad_mine, grad_other, proj, cosine, sine, query_gain, key_gain, segment_row, raw, query, key, value, tokens, scale,
-    normed, mixed,
+    group, grad_mine, grad_other, proj, cosine, sine, query_gain, key_gain, seg_rows, segment_row, raw, query, key, value, mixed
 ):
-    length, model = tokens.shape
-    query_cols, kv_cols = query.shape[1], key.shape[1]
+    length, query_cols, kv_cols = query.shape[0], query.shape[1], key.shape[1]
     args = (
         grad_mine, grad_other, proj, cosine, sine, query_gain[None], key_gain[None],
-        segment_row[:, None], segment_row[None, :], raw, query, key, value, tokens, scale, normed, mixed, position(),
-    )
+        seg_rows, segment_row[None, :], raw, query, key, value, mixed, position(),
+    )
+    out_shape = [
+        jax.ShapeDtypeStruct((length, query_cols + 2 * kv_cols), jnp.bfloat16),
+        jax.ShapeDtypeStruct((2, length // 2, query_cols), jnp.bfloat16),
+        jax.ShapeDtypeStruct((2, HD), jnp.float32),
+    ]
+
+    def whole(array):
+        return pl.BlockSpec(array.shape, lambda i: (0,) * len(array.shape), pipeline_mode=pl.Buffered(1))
+
     return pl.pallas_call(
         functools.partial(attend_back_kernel, group),
-        in_specs=[pl.BlockSpec(memory_space=pltpu.VMEM)] * (len(args) - 1)
+        grid=(1,),
+        in_specs=[whole(grad_mine), whole(grad_other)]
+        + [pl.BlockSpec((proj.shape[0], query_cols), lambda i: (0, proj.shape[1] // query_cols - 1))]
+        + [whole(array) for array in args[3:-1]]
         + [pl.BlockSpec(memory_space=pltpu.SMEM)],
-        out_specs=[pl.BlockSpec(memory_space=pltpu.VMEM)] * 5,
-        out_shape=[
-            jax.ShapeDtypeStruct(proj.shape, jnp.bfloat16),
-            jax.ShapeDtypeStruct((length // 2, model), jnp.bfloat16),
-            jax.ShapeDtypeStruct((length // 2, model), jnp.bfloat16),
-            jax.ShapeDtypeStruct((1, model), jnp.float32),
-            jax.ShapeDtypeStruct((2, HD), jnp.float32),
-        ],
+        out_specs=[whole(out) for out in out_shape],
+        out_shape=out_shape,
         scratch_shapes=[
-            pltpu.VMEM((length, model), jnp.bfloat16),
-            pltpu.VMEM((length, query_cols + 2 * kv_cols), jnp.bfloat16),
             pltpu.VMEM((length, query_cols), jnp.bfloat16),
             pltpu.VMEM((length, query_cols), jnp.float32),
             pltpu.VMEM((length, kv_cols), jnp.float32),
             pltpu.VMEM((length, kv_cols), jnp.float32),
         ],
-        compiler_params=call_params(56),
+        compiler_params=call_params(40),
         cost_estimate=cheap(),
         name="attend_back",
     )(*args)
 
 
-def feed_kernel(own, position_ref, *refs):
-    count = 3 if own else 4
-    proj_ref = refs[count]
-    act_ref, gate_up_grad_ref, keep_ref, give_ref, normed, cotangent = refs[count + 1 :]
-    core = position_ref[0]
-    half = act_ref.shape[-1]
-    middle = normed.shape[0] // 2
-    normed[:middle, :], normed[middle:, :] = refs[0][...], refs[1][...]
-    if own:
-        cotangent[:middle, :], cotangent[middle:, :] = by_core(core, refs[2][...])
-    else:
-        cotangent[:middle, :], cotangent[middle:, :] = refs[2][...], refs[3][...]
-    gate_up = jnp.dot(normed[...], proj_ref[:, : 2 * half], preferred_element_type=jnp.float32)
-    gate, up = gate_up[:, :half], gate_up[:, half:]
-    act_grad = jnp.dot(cotangent[...], proj_ref[:, 2 * half :], preferred_element_type=jnp.float32)
-    sigmoid = jax.nn.sigmoid(gate)
-    silu = gate * sigmoid
-    activated = low(silu * up)
-    gate_grad = low(act_grad * up * sigmoid * (1.0 + gate * (1.0 - sigmoid)))
-    up_grad = low(act_grad * silu)
-    for k in range(2):
-        here = slice(k * middle, (k + 1) * middle)
-        act_ref[k] = activated[here]
-        gate_up_grad_ref[k, :, :half] = gate_grad[here]
-        gate_up_grad_ref[k, :, half:] = up_grad[here]
-    normed_grad = contract(gate_grad, proj_ref[:, :half], 1, 1) + contract(
-        up_grad, proj_ref[:, half : 2 * half], 1, 1
-    )
-    keep_ref[...], give_ref[...] = low(normed_grad[:middle]), low(normed_grad[middle:])
-
-
-def feed(which, mine, other, cotangent, proj):
-    _, rows, model = mine.shape
+def attend_weights_kernel(
+    position_ref, low_ref, mixed_ref, scale_ref, grad_mine_ref, grad_other_ref, proj_ref, tokens_ref, normed_ref,
+    weight_ref, keep_ref, give_ref, gain_ref,
+):
+    split = low_ref.shape[1]
+    share = ROWS // 2
+    gain = jnp.zeros_like(gain_ref)
+    for at in range(low_ref.shape[0] // ROWS):
+        here = slice(at * ROWS, (at + 1) * ROWS)
+        rows = slice(at * share, (at + 1) * share)
+        part = contract(low_ref[here, :], proj_ref[...], 1, 1)
+        keep_ref[rows, :], give_ref[rows, :] = by_core(position_ref[0], low(part))
+        gain += jnp.sum(part * wide(tokens_ref[here, :]) * scale_ref[here, :], axis=0, keepdims=True)
+    gain_ref[...] = gain
+    weight_ref[:, :split] = low(contract(normed_ref[...], low_ref[...], 0, 0))
+    weight_ref[:, split:] = low(
+        contract(grad_mine_ref[...], mixed_ref[0], 0, 0) + contract(grad_other_ref[...], mixed_ref[1], 0, 0)
+    )
+
+
+def attend_weights(low_grad, mixed, scale, grad_mine, grad_other, proj, tokens, normed):
+    length, model = tokens.shape
+    split = low_grad.shape[1]
+    width = split + mixed.shape[-1]
+    cols = min(512, model)
+
+    def whole(array):
+        return pl.BlockSpec(array.shape, lambda i: (0,) * array.ndim, pipeline_mode=pl.Buffered(1))
+
+    def columns(rows):
+        return pl.BlockSpec((rows, cols), lambda i: (0, i))
+
+    return pl.pallas_call(
+        attend_weights_kernel,
+        grid=(model // cols,),
+        in_specs=[
+            pl.BlockSpec(memory_space=pltpu.SMEM),
+            whole(low_grad),
+            whole(mixed),
+            whole(scale),
+            columns(length // 2),
+            columns(length // 2),
+            pl.BlockSpec((cols, split), lambda i: (i, 0)),
+            columns(length),
+            columns(length),
+        ],
+        out_specs=[
+            pl.BlockSpec((cols, width), lambda i: (i, 0)),
+            columns(length // 2),
+            columns(length // 2),
+            columns(1),
+        ],
+        out_shape=[
+            jax.ShapeDtypeStruct((model, width), jnp.bfloat16),
+            jax.ShapeDtypeStruct((length // 2, model), jnp.bfloat16),
+            jax.ShapeDtypeStruct((length // 2, model), jnp.bfloat16),
+            jax.ShapeDtypeStruct((1, model), jnp.float32),
+        ],
+        compiler_params=call_params(40),
+        cost_estimate=cheap(),
+        name="attend_weights",
+    )(position(), low_grad, mixed, scale, grad_mine, grad_other, proj, tokens, normed)
+
+
+def prepare_kernel(tokens_ref, gain_ref, seg_ref, normed_ref, scale_ref, seg_rows_ref):
+    block_in = wide(tokens_ref[...])
+    scale = rms_parts(block_in)
+    scale_ref[...] = scale
+    normed_ref[...] = low(block_in * scale * gain_ref[...])
+    seg_rows_ref[...] = seg_ref[...]
+
+
+def prepare(tokens, gain, seg_rows):
+    length, model = tokens.shape
+
+    def rows(width):
+        return pl.BlockSpec((ROWS, width), lambda i: (i, 0))
+
+    return pl.pallas_call(
+        prepare_kernel,
+        grid=(length // ROWS,),
+        in_specs=[rows(model), pl.BlockSpec((1, model), lambda i: (0, 0)), rows(1)],
+        out_specs=[rows(model), rows(1), rows(1)],
+        out_shape=[
+            jax.ShapeDtypeStruct((length, model), jnp.bfloat16),
+            jax.ShapeDtypeStruct((length, 1), jnp.float32),
+            jax.ShapeDtypeStruct((length, 1), jnp.int32),
+        ],
+        compiler_params=call_params(24),
+        cost_estimate=cheap(),
+        name="prepare",
+    )(tokens, gain[None], seg_rows)
+
+
+def feed_kernel(*refs):
+    normed, cotangent, proj_ref, (act_refs, grad_refs) = refs[:4], refs[4:8], refs[8], (refs[9:11], refs[11:])
+    half = act_refs[0].shape[-1]
+    for k in range(4):
+        act_ref, grad_ref = act_refs[k // 2], grad_refs[k // 2]
+        gate_up = jnp.dot(normed[k][...], proj_ref[:, : 2 * half], preferred_element_type=jnp.float32)
+        gate, up = gate_up[:, :half], gate_up[:, half:]
+        act_grad = jnp.dot(cotangent[k][...], proj_ref[:, 2 * half :], preferred_element_type=jnp.float32)
+        sigmoid = jax.nn.sigmoid(gate)
+        silu = gate * sigmoid
+        act_ref[k % 2] = low(silu * up)
+        grad_ref[k % 2, :, :half] = low(act_grad * up * sigmoid * (1.0 + gate * (1.0 - sigmoid)))
+        grad_ref[k % 2, :, half:] = low(act_grad * silu)
+
+
+def feed(normed, cotangent, proj):
+    rows, model = normed[0].shape
     half = proj.shape[1] // 3
-    own = len(cotangent) == 1
-    tile = ROWS // 2
-
-    def halves(index):
-        return pl.BlockSpec((None, tile, model), lambda i: (index, i, 0))
-
+    tile = min(256, rows)
+    block = pl.BlockSpec((tile, model), lambda i: (i, 0))
+    widths = (half, half, 2 * half, 2 * half)
     return pl.pallas_call(
-        functools.partial(feed_kernel, own),
+        feed_kernel,
         grid=(rows // tile,),
-        in_specs=[pl.BlockSpec(memory_space=pltpu.SMEM), halves(which), halves(which)]
-        + ([pl.BlockSpec((ROWS, model), lambda i: (i, 0))] if own else [halves(0), halves(0)])
-        + [pl.BlockSpec(proj.shape, lambda i: (0, 0), pipeline_mode=pl.Buffered(1))],
-        out_specs=[pl.BlockSpec((2, tile, w), lambda i: (0, i, 0)) for w in (half, 2 * half)]
-        + [pl.BlockSpec((tile, model), lambda i: (i, 0))] * 2,
-        out_shape=[jax.ShapeDtypeStruct((2, rows, w), jnp.bfloat16) for w in (half, 2 * half)]
-        + [jax.ShapeDtypeStruct((rows, model), jnp.bfloat16)] * 2,
-        scratch_shapes=[pltpu.VMEM((ROWS, model), jnp.bfloat16)] * 2,
+        in_specs=[block] * 8 + [pl.BlockSpec(proj.shape, lambda i: (0, 0), pipeline_mode=pl.Buffered(1))],
+        out_specs=[pl.BlockSpec((2, tile, w), lambda i: (0, i, 0)) for w in widths],
+        out_shape=[jax.ShapeDtypeStruct((2, rows, w), jnp.bfloat16) for w in widths],
         compiler_params=call_params(48),
         cost_estimate=cheap(),
         name="feed",
-    )(position(), mine, other, *cotangent, proj)
-
-
-def feed_out_kernel(act_ref, proj_ref, keep_ref, give_ref):
+    )(*normed, *cotangent, proj)
+
+
+def feed_model_kernel(act_ref, grad_ref, proj_ref, keep_ref, give_ref, keep_out_ref, give_out_ref):
     half = act_ref.shape[-1]
-    for k, out_ref in enumerate((keep_ref, give_ref)):
-        out_ref[...] = low(contract(act_ref[k], proj_ref[:, 2 * half :], 1, 1))
-
-
-def feed_out(act, proj):
+    for k, (out_ref, out_out_ref) in enumerate(((keep_ref, keep_out_ref), (give_ref, give_out_ref))):
+        out_ref[...] = low(contract(grad_ref[k], proj_ref[:, : 2 * half], 1, 1))
+        out_out_ref[...] = low(contract(act_ref[k], proj_ref[:, 2 * half :], 1, 1))
+
+
+def feed_model(act, grad, proj):
     _, rows, half = act.shape
     model = proj.shape[0]
-    tile = ROWS
+    tile = min(256, rows)
     return pl.pallas_call(
-        feed_out_kernel,
+        feed_model_kernel,
         grid=(rows // tile,),
         in_specs=[
             pl.BlockSpec((2, tile, half), lambda i: (0, i, 0)),
+            pl.BlockSpec((2, tile, 2 * half), lambda i: (0, i, 0)),
             pl.BlockSpec(proj.shape, lambda i: (0, 0), pipeline_mode=pl.Buffered(1)),
         ],
-        out_specs=[pl.BlockSpec((tile, model), lambda i: (i, 0))] * 2,
-        out_shape=[jax.ShapeDtypeStruct((rows, model), jnp.bfloat16)] * 2,
-        compiler_params=call_params(32),
+        out_specs=[pl.BlockSpec((tile, model), lambda i: (i, 0))] * 4,
+        out_shape=[jax.ShapeDtypeStruct((rows, model), jnp.bfloat16)] * 4,
+        compiler_params=call_params(40),
         cost_estimate=cheap(),
-        name="feed_out",
-    )(act, proj)
-
-
-def feed_weights_kernel(
-    position_ref, mine_own, mine_pair, other_own, other_pair, cot_own, cot_mine, cot_other, grad_own, grad_pair, act_own, act_pair,
-    out_ref,
-):
-    wide_cols = grad_own.shape[-1]
-    core = position_ref[0]
-    rows, cols = mine_own.shape
+        name="feed_model",
+    )(act, grad, proj)
+
+
+def feed_weights_kernel(*refs):
+    normed, cotangent, grad, act, out_ref = refs[:4], refs[4:8], refs[8:10], refs[10:12], refs[12]
+    wide_cols = grad[0].shape[-1]
     out_ref[:, :wide_cols] = low(
-        contract(mine_own[...], grad_own[0], 0, 0)
-        + contract(other_own[...], grad_own[1], 0, 0)
-        + contract(mine_pair[...], grad_pair[0], 0, 0)
-        + contract(other_pair[...], grad_pair[1], 0, 0)
+        sum(contract(normed[k][...], grad[k // 2][k % 2], 0, 0) for k in range(4))
     )
     out_ref[:, wide_cols:] = low(
-        contract(cot_own[:, core].reshape(rows, cols), act_own[0], 0, 0)
-        + contract(cot_own[:, 1 - core].reshape(rows, cols), act_own[1], 0, 0)
-        + contract(cot_mine[...], act_pair[0], 0, 0)
-        + contract(cot_other[...], act_pair[1], 0, 0)
-    )
-
-
-def feed_weights(mine, other, cotangent, cot_mine, cot_other, grad, act):
-    _, rows, model = mine.shape
+        sum(contract(cotangent[k][...], act[k // 2][k % 2], 0, 0) for k in range(4))
+    )
+
+
+def feed_weights(normed, cotangent, grad, act):
+    rows, model = normed[0].shape
     width = grad[0].shape[-1] + act[0].shape[-1]
     cols = min(512, model)
-    cotangent = cotangent.reshape(-1, 2, ROWS // 2, model)
 
     def whole(array):
         return pl.BlockSpec(array.shape, lambda i: (0, 0, 0), pipeline_mode=pl.Buffered(1))
-
-    def part(index):
-        return pl.BlockSpec((None, rows, cols), lambda i: (index, 0, i))
 
     return pl.pallas_call(
         feed_weights_kernel,
         grid=(model // cols,),
-        in_specs=[
-            pl.BlockSpec(memory_space=pltpu.SMEM),
-            part(0),
-            part(1),
-            part(0),
-            part(1),
-            pl.BlockSpec((*cotangent.shape[:3], cols), lambda i: (0, 0, 0, i)),
-            part(0),
-            part(0),
-        ]
-        + [whole(a) for a in (*grad, *act)],
+        in_specs=[pl.BlockSpec((rows, cols), lambda i: (0, i))] * 8 + [whole(a) for a in (*grad, *act)],
         out_specs=pl.BlockSpec((cols, width), lambda i: (i, 0)),
         out_shape=jax.ShapeDtypeStruct((model, width), jnp.bfloat16),
         compiler_params=call_params(48),
         cost_estimate=cheap(),
         name="feed_weights",
-    )(position(), mine, mine, other, other, cotangent, cot_mine, cot_other, *grad, *act)
+    )(*normed, *cotangent, *grad, *act)
 
 
 def feed_sums_kernel(count, side_ref, *refs):
@@ -802,96 +869,96 @@
     key_norm = gains[:, 2 * shard + head_part :].reshape(HD)
 
     cosine, sine = rope_tables(doc_positions(segment_row))
-    block_in = tokens.astype(jnp.float32)
-    scale_one = rms_parts(block_in)
-    normed = (block_in * scale_one * gain_attn.astype(jnp.float32)).astype(jnp.bfloat16)
+    normed, scale_one, seg_rows = prepare(tokens, wide(gain_attn), segment_row[:, None])
     query_gain_wide, key_gain_wide = wide(query_norm), wide(key_norm)
-    raw, query_rot, key_rot, values, mixed_low, out_keep, out_give = attend(
-        group, normed, proj, cosine, sine, query_gain_wide, key_gain_wide, segment_row
-    )
-    out_give, feed_block = lax.optimization_barrier((out_give, feed_block))
+    by_chip = cotangent.reshape(4, 2, share_rows, model)
+    core = lax.axis_index("tensor")
+    own_cot = [pick(by_chip, k, 1).reshape(length // 2, model) for k in (core, 1 - core)]
+    own_cot, normed = lax.optimization_barrier((own_cot, normed))
+    raw, query_rot, key_rot, values, mixed_low = attend(
+        group, normed, proj, cosine, sine, query_gain_wide, key_gain_wide, seg_rows, segment_row
+    )
+    out_keep, out_give = attend_out(mixed_low, proj)
+    out_got = swap(out_give, "tensor", 1)
+    out_got, feed_block = lax.optimization_barrier((out_got, feed_block))
     feed_proj = lax.all_gather(
         feed_block, "fsdp", axis=0, tiled=True, axis_index_groups=alike()
     ).reshape(model, -1)
 
-    def middle(out_keep, out_give, tokens, cotangent):
+    def middle(tokens, cotangent, out_keep, out_got):
         cot = Job(pair_gather(share_of(cotangent), 2))
-        out_sum = Job(plane_scatter(out_keep, out_give))
-        beside(out_sum)
+        out_sum = Job(chip_scatter(*fold_chip(out_keep, out_got)))
         beside(out_sum, cot)
         beside(out_sum, cot)
         hidden_share = wide(share_of(tokens)) + out_sum.value
         scale_share = rms_parts(hidden_share)
         normed_share = low(hidden_share * scale_share * wide(gain_ffn))
-        pair_share = Job(pair_swap(normed_share))
-        beside(pair_share, cot)
-        gather = Job(plane_gather(jnp.stack([normed_share, pair_share.value])))
-        beside(gather, cot)
-        beside(gather, cot)
-        finish(gather)
-        return hidden_share, scale_share, *gather.value, *cot.value
-
-    hidden_share, scale_share, mine, other, cot_mine, cot_other = apart(
-        middle, out_keep, out_give, tokens, cotangent
-    )
-
-    pair_act, pair_grad, *pair_parts = feed(1, mine, other, (cot_mine, cot_other), feed_proj)
-    pair_sum = Job(plane_scatter(*pair_parts))
-    ((act, grad, *own_parts),) = beside(
-        pair_sum, kernels=[(functools.partial(feed, 0), (mine, other, (cotangent,), feed_proj))]
-    )
-    own_sum = Job(plane_scatter(*own_parts))
-    weight_args = (mine, other, cotangent, cot_mine, cot_other, (grad, pair_grad), (act, pair_act))
-    (feed_w_part,) = beside(pair_sum, own_sum, kernels=[(feed_weights, weight_args)])
+        gather = Job(plane_gather(normed_share[None]))
+        pair_share = Job(pair_swap(normed_share, 2))
+        beside(pair_share, gather, cot)
+        beside(pair_share, gather)
+        pair_gather_x = Job(plane_gather(pair_share.value[None]))
+        beside(pair_gather_x, cot, gather)
+        beside(pair_gather_x, cot)
+        finish(pair_gather_x, cot, gather)
+        arrays = (*gather.value, *pair_gather_x.value, *cot.value)
+        return hidden_share, scale_share, *(array[0] for array in arrays)
+
+    hidden_share, scale_share, *parts = apart(middle, tokens, cotangent, out_keep, out_got)
+    own_normed, pair_normed, pair_cot = parts[:2], parts[2:4], parts[4:]
+
+    act, pair_act, grad, pair_grad = feed((*own_normed, *pair_normed), (*own_cot, *pair_cot), feed_proj)
+    pair_parts = feed_model(pair_act, pair_grad, feed_proj)
+    pair_sum = Job(plane_scatter(*pair_parts[:2]))
+    (own_parts,) = beside(pair_sum, kernels=[(feed_model, (act, grad, feed_proj))])
+    weight_args = ((*own_normed, *pair_normed), (*own_cot, *pair_cot), (grad, pair_grad), (act, pair_act))
+    (feed_w_part,) = beside(pair_sum, kernels=[(feed_weights, weight_args)])
     feed_w_sum = lax.psum_scatter(
         feed_w_part, "fsdp", scatter_dimension=0, tiled=True, axis_index_groups=alike()
     ).reshape(2, shard, -1)
-    pair_held, own_held = (tuple(job.keep) for job in (pair_sum, own_sum))
-
-    def back(hidden_share, scale_share, cotangent, act, pair_act, feed_proj, *kept):
-        pair_sum = Job(line_scatter(*pair_held))
-        own_sum = Job(chip_scatter(*own_held))
-        out_parts, pair_out_parts = beside(
-            pair_sum, own_sum, kernels=[(feed_out, (act, feed_proj)), (feed_out, (pair_act, feed_proj))]
-        )
-        out_sum = Job(plane_scatter(*out_parts))
-        pair_out_sum = Job(plane_scatter(*pair_out_parts))
-        pair_share = Job(pair_swap(low(pair_sum.value), 2))
-        beside(pair_share, own_sum, pair_out_sum, out_sum)
-        beside(pair_share, pair_out_sum)
+    pair_held = pair_sum.keep
+
+    def back(hidden_share, scale_share, cotangent, *kept):
+        pair_sum = Job(line_scatter(*pair_held, True))
+        own_sum = Job(plane_scatter(*own_parts[:2]))
+        out_sum = Job(plane_scatter(*own_parts[2:]))
+        pair_out_sum = Job(plane_scatter(*pair_parts[2:], True))
+        beside(pair_sum, own_sum, pair_out_sum, out_sum)
+        pair_share = Job(pair_swap(pair_sum.value, 2))
+        beside(pair_share, own_sum, ready=[pair_out_sum])
+        beside(pair_share, own_sum, pair_out_sum, ready=[out_sum])
         grad_share = own_sum.value + wide(pair_share.value)
         hidden_grad_share = wide(share_of(cotangent)) + norm_back(
             hidden_share, scale_share, grad_share * wide(gain_ffn)
         )
         ffn_gain_part = jnp.sum(grad_share * hidden_share * scale_share, axis=0)
         gather = Job(plane_gather(low(hidden_grad_share)[None]))
-        beside(gather)
+        beside(gather, ready=[pair_out_sum])
         beside(gather)
         beside(gather, pair_out_sum)
-        pair_out = Job(pair_swap(low(pair_out_sum.value)))
-        grad_mine, grad_other = gather.value
-        ((attn_w_part, keep, give, attn_gain_part, head_gain_part),) = beside(
-            pair_out,
-            out_sum,
-            kernels=[(functools.partial(attend_back, group), (grad_mine[0], grad_other[0], *kept))],
-        )
-        out_share = hidden_share + wide(pair_out.value)
-        return (
-            hidden_grad_share, attn_w_part, keep, give, attn_gain_part, head_gain_part, ffn_gain_part, out_share,
-            *out_sum.keep,
-        )
-
-    hidden_grad_share, attn_w_part, keep, give, attn_gain_part, head_gain_part, ffn_gain_part, out_share, *held = apart(
-        back, hidden_share, scale_share, cotangent, act, pair_act, feed_proj,
-        proj, cosine, sine, query_gain_wide, key_gain_wide, segment_row, raw, query_rot, key_rot, values, tokens,
-        scale_one, normed, mixed_low,
-    )
-    attn_w_part, feed_w_sum, give = lax.optimization_barrier((attn_w_part, feed_w_sum, give))
+        grad_mine, grad_other = (array[0] for array in gather.value)
+        pair_out = Job(pair_swap(pair_out_sum.value))
+
+        def attended(*kept):
+            low_grad, mixed_split, head_gain_part = attend_back(group, grad_mine, grad_other, *kept)
+            return *attend_weights(low_grad, mixed_split, scale_one, grad_mine, grad_other, proj, tokens, normed), head_gain_part
+
+        (results,) = beside(pair_out, out_sum, kernels=[(attended, kept)])
+        return hidden_grad_share, ffn_gain_part, *results, pair_out.value, *out_sum.held, *out_sum.arrived
+
+    (
+        hidden_grad_share, ffn_gain_part, attn_w_part, keep, give, attn_gain_part, head_gain_part, pair_out, *held
+    ) = apart(
+        back, hidden_share, scale_share, cotangent, proj, cosine, sine, query_gain_wide, key_gain_wide, seg_rows, segment_row,
+        raw, query_rot, key_rot, values, mixed_low,
+    )
+    feed_w_sum, attn_w_part = lax.optimization_barrier((feed_w_sum, attn_w_part))
+    attn_w_part, give = lax.optimization_barrier((attn_w_part, give))
     attn_w_sum = lax.psum_scatter(attn_w_part, "fsdp", scatter_dimension=0, tiled=True)
 
-    def last(feed_w_sum, keep, give, out_share, hidden_grad_share, tokens, scale_one, *rest):
-        gain_parts, held = rest[:4], rest[4:]
-        out_sum = Job(line_scatter(*held))
+    def last(keep, give, feed_w_sum, hidden_share, pair_out, hidden_grad_share, tokens, scale_one, *rest):
+        gain_parts, (_, keep_first, _, keep_second, got_first, got_second) = rest[:4], rest[4:]
+        out_sum = Job(line_scatter(*fold_line(keep_first, got_first, keep_second, got_second)))
         feed_pair = Job(pair_swap(pick(feed_w_sum, 1 - side, 0), 4))
         normed_sum = Job(plane_scatter(keep, give))
         gains = Job(sum_all(jnp.concatenate([part.reshape(size, -1) for part in gain_parts], axis=1)))
@@ -899,8 +966,10 @@
         beside(normed_sum, feed_pair, gains)
         beside(normed_sum, feed_pair, gains)
         finish(feed_pair, gains)
-        gate_w_grad, up_w_grad, down_w_grad = feed_sums(side[None], [pick(feed_w_sum, side, 0)], [feed_pair.value])
-        block_out = low(out_share + out_sum.value)
+        gate_w_grad, up_w_grad, down_w_grad = feed_sums(
+            side[None], [pick(feed_w_sum, side, 0)], [feed_pair.value]
+        )
+        block_out = low(hidden_share + wide(pair_out) + out_sum.value)
         token_share = wide(share_of(tokens))
         scale_one_share = share_of(scale_one)
         tokens_grad = low(
@@ -910,7 +979,7 @@
         return block_out, tokens_grad, gate_w_grad, up_w_grad, down_w_grad, gain_sums
 
     block_out, tokens_grad, gate_w_grad, up_w_grad, down_w_grad, gain_sums = apart(
-        last, feed_w_sum, keep, give, out_share, hidden_grad_share, tokens, scale_one,
+        last, keep, give, feed_w_sum, hidden_share, pair_out, hidden_grad_share, tokens, scale_one,
         attn_gain_part, ffn_gain_part, head_gain_part[0], head_gain_part[1], *held,
     )
     attn_w_grad, gain_sums = lax.optimization_barrier((attn_w_sum, gain_sums))

time: 540 us -> 513 us (0.950)
  waiting for transfers between devices: 257 us -> 240 us
  other arithmetic: 39.3 us -> 27.7 us
  local copies, waits for them, and re-layouts: 28.6 us -> 19.7 us
  starting transfers between devices: 73.6 us -> 80.9 us
  Pallas kernels: 123 us -> 130 us
    ppermute x60 -> x65, waiting for transfers between devices: 194 us -> 181 us  [beside(): lax.ppermute(array, *move[1:])]
    cond x65 -> x51, local copies, waits for them, and re-layouts: 10.9 us -> 2.19 us
    ppermute x60 -> x65, starting transfers between devices: 57.1 us -> 62.1 us  [beside(): lax.ppermute(array, *move[1:])]
    ppermute x3 -> x4, waiting for transfers between devices: 14.7 us -> 10.1 us  [swap(): return lax.ppermute(array, axis, flip(axis, stride))]
    pallas_call x18 -> x22, Pallas kernels: 30.7 us -> 34.9 us  [vmem_call(): pl.pallas_call(kernel, in_specs=[pl.BlockSpec(memory_space=pltpu.SMEM)] +...]
    pallas_call x5 -> x7, Pallas kernels: 62.1 us -> 66.2 us  [the longest x1 18.9 us: feed(): pl.pallas_call(feed_kernel, grid=(rows // tile,), in_specs=[block] * 8 +...]
  transfers between devices with their start and end apart: 67 -> 73, of which waited for: 36 -> 38; matrix products, arithmetic and copies ran while one was open for 8% -> 7% of each run, Pallas kernels for 20% -> 20%
where the time goes in v3:
time: 513 us
  waiting for transfers between devices  240 us (47%)
  Pallas kernels  130 us (25%)
  starting transfers between devices  80.9 us (16%)
  other arithmetic  27.7 us (5%)
  local copies, waits for them, and re-layouts  19.7 us (4%)
  between operations  14.3 us (3%)
    ppermute x65, waiting for transfers between devices, beside(): lax.ppermute(array, *move[1:])  181 us
    ppermute x65, starting transfers between devices, beside(): lax.ppermute(array, *move[1:])  62.1 us
    all_gather x1, waiting for transfers between devices, per_device(): lax.all_gather(jnp.concatenate([w_query, w_key, w_value, w_out], axis=1),...  48.8 us
    pallas_call x22, Pallas kernels, vmem_call(): pl.pallas_call(kernel, in_specs=[pl.BlockSpec(memory_space=pltpu.SMEM)] +...  34.9 us
    pallas_call x1, Pallas kernels, feed(): pl.pallas_call(feed_kernel, grid=(rows // tile,), in_specs=[block] * 8 +...  18.9 us
    pallas_call x2, Pallas kernels, feed_model(): pl.pallas_call(feed_model_kernel, grid=(rows // tile,), in_specs=[pl.Bloc...  15.2 us
    pallas_call x1, Pallas kernels, feed_weights(): pl.pallas_call(feed_weights_kernel, grid=(model // cols,), in_specs=[pl.B...  15 us
    pallas_call x1, Pallas kernels, attend_back(): pl.pallas_call(functools.partial(attend_back_kernel, group), grid=(1,), i...  13 us
  transfers between devices with their start and end apart: 73, of which 38 were waited for; matrix products, arithmetic and copies ran while one was open for 7% of the time, Pallas kernels for 20%

profile of v3, /device:TPU:0, one launch (start us, length us, event | category | flops | bytes accessed | tf_op | source)
XLA Modules:
  0.0 512.8 jit_solution(15380035214902646049)
XLA Ops:
  9.7 3.1 collective-permute-start.62
  18.9 2.6 constant_dynamic-slice_fusion.9
  21.9 2.7 collective-permute-start.63
  24.9 2.8 collective-permute-done.63
  27.8 48.8 %all-gather.3.cloned.1.call-done.proj_ref = bf16[2048,768]{1,0:T(8,128)(2,1)} async-done(((bf16[512,768]{1,0:T(8,128)(2,1)}), bf16[2048,768]{1,0:T(8,128)(2,1)}) %all-gather.3.cloned.1.call-update) | async-done | bytes 3145744 | tf_op jit(solution)/shard_map/all_gather | solution.py:851
  76.7 5.6 %prepare.1 = (bf16[1024,2048]{1,0:T(8,128)(2,1)}, f32[1024,1]{1,0:T(8,128)}, s32[1024,1]{1,0:T(8,128)S(1)}) custom-call(bf16[1024,2048]{1,0:T(8,128)(2,1)} %tokens_ref.1, f32[1,2048]{1,0:T(1,128)S(1)} %bitcast.130, s32[1024,1]{1,0:T(8,128)S(1)} %copy.36.seg_ref), custom_call_target="tpu_custom_call" | custom-call | flops 1000 | bytes 1000 | tf_op jit(solution)/shard_map/prepare/pallas_call | solution.py:674
  82.5 11.3 %attend.1 = (f32[1024,384]{1,0:T(8,128)}, bf16[1024,256]{1,0:T(8,128)(2,1)}, bf16[1024,128]{1,0:T(8,128)(2,1)}, bf16[1024,128]{1,0:T(8,128)(2,1)}, bf16[1024,256]{1,0:T(8,128)(2,1)S(1)}) custom-call(bf16[1024,2048]{1,0:T(8,128)(2,1)} %get-tuple-element.485.normed_ref, bf16[2048,768]{1,0:T(8,128)(2,1)} %all-gather.3.cloned.1.call-done.proj_ref, ...), custom_call_target="tpu_custom_call" | custom-call | flops 1000 | bytes 1000 | tf_op jit(solution)/shard_map/attend/pallas_call | solution.py:426
  93.8 3.6 attend_out.1
  97.4 7.2 %collective-permute-done.65 = bf16[512,1152]{1,0:T(8,128)(2,1)} collective-permute-done((bf16[512,1152]{1,0:T(8,128)(2,1)}, bf16[512,1152]{1,0:T(8,128)(2,1)}, u32[]{:S(2)}, u32[]{:S(2)}) %collective-permute-start.65) | collective-permute-done | bytes 1179680 | tf_op jit(solution)/shard_map/ppermute | solution.py:123
  108.2 12.6 %reduce-scatter.3.cloned.1.call-start = ((), (), s32[]{:S(2)}) async-start(), calls=%async_computation.4 | async-start | bytes 7077888 | tf_op jit(solution)/shard_map/reduce_scatter | solution.py:916
  120.8 113.8 %conditional.3 = (f32[128,2048]{1,0:T(8,128)S(1)}, f32[128,1]{0,1:T(1,128)S(1)}, bf16[512,2048]{1,0:T(8,128)(2,1)}, bf16[512,2048]{1,0:T(8,128)(2,1)}, bf16[512,...) conditional(s32[]{:T(128)} %convert_element_type.153, () %tuple.81, ...), branch_computations={%region_2.3_spmd, %region_3.5_spmd} | conditional | flops 5777378 | bytes 78160016 | solution.py:74
  122.1 2.7 fold_chip.6
  128.2 11.6 %collective-permute-done.41 = bf16[64,2048]{1,0:T(8,128)(2,1)S(1)} collective-permute-done((bf16[64,2048]{1,0:T(8,128)(2,1)S(1)}, bf16[64,2048]{1,0:T(8,128)(2,1)S(1)}, u32[]{:S(2)}, u32[]{:S(2)}) %collective-permute-start.41) | collective-permute-done | bytes 262176 | tf_op jit(solution)/shard_map/cond/branch_1_fun/ppermute | solution.py:99
  144.3 2.7 collective-permute-done.42
  147.6 7.8 %collective-permute-done.44 = bf16[64,2048]{1,0:T(8,128)(2,1)S(1)} collective-permute-done((bf16[64,2048]{1,0:T(8,128)(2,1)S(1)}, bf16[64,2048]{1,0:T(8,128)(2,1)S(1)}, u32[]{:S(2)}, u32[]{:S(2)}) %collective-permute-start.44) | collective-permute-done | bytes 262176 | tf_op jit(solution)/shard_map/cond/branch_1_fun/ppermute | solution.py:99
  157.5 2.5 collective-permute-start.45
  164.1 6.9 %collective-permute-done.45 = bf16[64,2048]{1,0:T(8,128)(2,1)S(1)} collective-permute-done((bf16[64,2048]{1,0:T(8,128)(2,1)S(1)}, bf16[64,2048]{1,0:T(8,128)(2,1)S(1)}, u32[]{:S(2)}, u32[]{:S(2)}) %collective-permute-start.45) | collective-permute-done | bytes 262176 | tf_op jit(solution)/shard_map/cond/branch_1_fun/ppermute | solution.py:99
  177.7 9.9 %collective-permute-done.50 = bf16[64,2048]{1,0:T(8,128)(2,1)S(1)} collective-permute-done((bf16[64,2048]{1,0:T(8,128)(2,1)S(1)}, bf16[64,2048]{1,0:T(8,128)(2,1)S(1)}, u32[]{:S(2)}, u32[]{:S(2)}) %collective-permute-start.50) | collective-permute-done | bytes 262176 | tf_op jit(solution)/shard_map/cond/branch_1_fun/ppermute | solution.py:99
  193.7 16.2 %collective-permute-done.53.got_first_ref = bf16[1,128,1024]{2,1,0:T(8,128)(2,1)S(1)} collective-permute-done((bf16[1,128,1024]{2,1,0:T(8,128)(2,1)S(1)}, bf16[1,128,1024]{2,1,0:T(8,128)(2,1)S(1)}, u32[]{:S(2)}, u32[]{:S(2)}) %collective-permute-start.53) | collective-permute-done | bytes 262176 | tf_op jit(solution)/shard_map/cond/branch_1_fun/ppermute | solution.py:99
  214.6 12.3 %collective-permute-done.58.got_first_ref = bf16[2,1,128,1024]{3,2,1,0:T(8,128)(2,1)S(1)} collective-permute-done((bf16[2,1,128,1024]{3,2,1,0:T(8,128)(2,1)S(1)}, bf16[2,1,128,1024]{3,2,1,0:T(8,128)(2,1)S(1)}, u32[]{:S(2)}, u32[]{:S(2)}) %collective-permute-start.58) | collective-permute-done | bytes 524320 | tf_op jit(solution)/shard_map/cond/branch_1_fun/ppermute | solution.py:99
  230.1 4.5 collective-permute-done.61
  234.6 18.9 %feed.1 = (bf16[2,512,384]{2,1,0:T(8,128)(2,1)S(1)}, bf16[2,512,384]{2,1,0:T(8,128)(2,1)S(1)}, bf16[2,512,768]{2,1,0:T(8,128)(2,1)S(1)}, bf16[2,512,768]{2,1,0:T(8,128)(2,1)S(1)}) custom-call(bf16[512,2048]{1,0:T(8,128)(2,1)} %get-tuple-element.523.refs_0_, bf16[512,2048]{1,0:T(8,128)(2,1)} %get-tuple-element.524.refs_1_, ...), custom_call_target="tpu_custom_call" | custom-call | flops 1000 | bytes 1000 | tf_op jit(solution)/shard_map/feed/pallas_call | solution.py:711
  253.6 7.2 %feed_model.2 = (bf16[512,2048]{1,0:T(8,128)(2,1)S(1)}, bf16[512,2048]{1,0:T(8,128)(2,1)S(1)}, bf16[512,2048]{1,0:T(8,128)(2,1)}, bf16[512,2048]{1,0:T(8,128)(2,1)}) custom-call(bf16[2,512,384]{2,1,0:T(8,128)(2,1)S(1)} %get-tuple-element.534.act_ref.refs_11_, bf16[2,512,768]{2,1,0:T(8,128)(2,1)S(1)} %get-tuple-element.532.grad_ref.refs_9_, ...), custom_call_target="tpu_custom_call" | custom-call | flops 1000 | bytes 1000 | tf_op jit(solution)/shard_map/feed_model/pallas_call | solution.py:734
  260.9 8.0 %feed_model.3 = (bf16[512,2048]{1,0:T(8,128)(2,1)}, bf16[512,2048]{1,0:T(8,128)(2,1)}, bf16[512,2048]{1,0:T(8,128)(2,1)}, bf16[512,2048]{1,0:T(8,128)(2,1)}) custom-call(bf16[2,512,384]{2,1,0:T(8,128)(2,1)S(1)} %get-tuple-element.533.act_ref.refs_10_, bf16[2,512,768]{2,1,0:T(8,128)(2,1)S(1)} %get-tuple-element.531.grad_ref.refs_8_, ...), custom_call_target="tpu_custom_call" | custom-call | flops 1000 | bytes 1000 | tf_op jit(solution)/shard_map/feed_model/pallas_call | solution.py:734
  271.2 15.0 %feed_weights.1 = bf16[2048,1152]{1,0:T(8,128)(2,1)} custom-call(bf16[512,2048]{1,0:T(8,128)(2,1)} %get-tuple-element.523.refs_0_, bf16[512,2048]{1,0:T(8,128)(2,1)} %get-tuple-element.524.refs_1_, bf16[512,2048]{1,0:T(8,128)(2,1)} %get-tuple-element.525.refs_2_, bf16[512,2048]{1,0:T(8,128)(2,1)} %get-tuple-element.526.refs_3_, bf16[512,2048]{1,0:T(8,128)(2,1)} %bitcast.136, ...), custom_call_target="tpu_custom_call" | custom-call | flops 1000 | bytes 1000 | tf_op jit(solution)/shard_map/feed_weights/pallas_call | solution.py:769
  288.2 120.8 %conditional.4 = (f32[128,2048]{1,0:T(8,128)}, f32[2048]{0:T(1024)S(1)}, bf16[2048,768]{1,0:T(8,128)(2,1)}, bf16[512,2048]{1,0:T(8,128)(2,1)}, bf16[512,2048]{1,...) conditional(s32[]{:T(128)} %convert_element_type.153, () %tuple.80, ...), branch_computations={%region_5.6_spmd, %region_6.9_spmd} | conditional | flops 7613465 | bytes 158409136 | solution.py:74
  291.6 5.8 %collective-permute-done.16.got_first_ref = bf16[128,1024]{1,0:T(8,128)(2,1)S(1)} collective-permute-done((bf16[128,1024]{1,0:T(8,128)(2,1)S(1)}, bf16[128,1024]{1,0:T(8,128)(2,1)S(1)}, u32[]{:S(2)}, u32[]{:S(2)}) %collective-permute-start.16) | collective-permute-done | bytes 262176 | tf_op jit(solution)/shard_map/cond/branch_1_fun/ppermute | solution.py:99
  307.7 3.0 fold_chip.8
  310.7 8.8 %collective-permute-done.21 = bf16[64,2048]{1,0:T(8,128)(2,1)S(1)} collective-permute-done((bf16[64,2048]{1,0:T(8,128)(2,1)S(1)}, bf16[64,2048]{1,0:T(8,128)(2,1)S(1)}, u32[]{:S(2)}, u32[]{:S(2)}) %collective-permute-start.21) | collective-permute-done | bytes 262176 | tf_op jit(solution)/shard_map/cond/branch_1_fun/ppermute | solution.py:99
  329.0 3.0 fold_chip.9
  332.0 4.8 collective-permute-done.24
  336.8 4.5 collective-permute-done.25
  343.9 2.7 convert_bitcast_fusion
  357.4 7.4 %collective-permute-done.31.got_first_ref = bf16[2,1,128,1024]{3,2,1,0:T(8,128)(2,1)S(1)} collective-permute-done((bf16[2,1,128,1024]{3,2,1,0:T(8,128)(2,1)S(1)}, bf16[2,1,128,1024]{3,2,1,0:T(8,128)(2,1)S(1)}, u32[]{:S(2)}, u32[]{:S(2)}) %collective-permute-start.31) | collective-permute-done | bytes 524320 | tf_op jit(solution)/shard_map/cond/branch_1_fun/ppermute | solution.py:99
  368.8 6.5 %collective-permute-done.34.got_first_ref = bf16[128,1024]{1,0:T(8,128)(2,1)S(1)} collective-permute-done((bf16[128,1024]{1,0:T(8,128)(2,1)}, bf16[128,1024]{1,0:T(8,128)(2,1)S(1)}, u32[]{:S(2)}, u32[]{:S(2)}) %collective-permute-start.34) | collective-permute-done | bytes 262176 | tf_op jit(solution)/shard_map/cond/branch_1_fun/ppermute | solution.py:99
  377.3 2.6 collective-permute-start.36
  381.0 13.0 %attend_back.1 = (bf16[1024,512]{1,0:T(8,128)(2,1)S(1)}, bf16[2,512,256]{2,1,0:T(8,128)(2,1)S(1)}, f32[2,128]{1,0:T(2,128)}) custom-call(bf16[512,2048]{1,0:T(8,128)(2,1)S(1)} %bitcast.124, bf16[512,2048]{1,0:T(8,128)(2,1)} %bitcast.33.grad_other_ref, bf16[2048,768]{1,0:T(8,128)(2,1)} %get-tuple-element.278.out_proj_ref.proj_ref, ...), custom_call_target="tpu_custom_call" | custom-call | flops 1000 | bytes 1000 | tf_op jit(solution)/shard_map/cond/branch_1_fun/attend_back/pallas_call | solution.py:575
  394.0 9.8 %attend_weights.1 = (bf16[2048,768]{1,0:T(8,128)(2,1)}, bf16[512,2048]{1,0:T(8,128)(2,1)}, bf16[512,2048]{1,0:T(8,128)(2,1)}, f32[1,2048]{1,0:T(1,128)S(1)}) custom-call(s32[3]{0:T(128)S(1)} %pad_add_fusion.1.position_ref, bf16[1024,512]{1,0:T(8,128)(2,1)S(1)} %get-tuple-element.290.low_ref, bf16[2,512,256]{2,1,0:T(8,128)(2,1)S(1)} %get-tuple-element.291.mixed_ref, ...), custom_call_target="tpu_custom_call" | custom-call | flops 1000 | bytes 1000 | tf_op jit(solution)/shard_map/cond/branch_1_fun/attend_weights/pallas_call | solution.py:628
  403.9 4.3 collective-permute-done.36
  410.0 91.0 %conditional.5 = (bf16[128,2048]{1,0:T(8,128)(2,1)}, bf16[128,2048]{1,0:T(8,128)(2,1)}, f32[512,768]{1,0:T(8,128)}, f32[512,768]{1,0:T(8,128)}, f32[512,768]{1,0:T(8,128)}, /*index=5*/f32[1088]{0:T(1024)S(1)}) conditional(s32[]{:T(128)} %convert_element_type.153, () %tuple.79, (bf16[128,2048]{1,0:T(8,128)(2,1)}, f32[128,2048]{1,0:T(8,128)}, ...), branch_computations={%region_10.11_spmd, %region_11.13_spmd} | conditional | flops 11297041 | bytes 60621348 | solution.py:74
  421.3 3.3 collective-permute-done.1
  425.4 3.2 fold_chip.10
  432.8 13.8 %collective-permute-done.7 = f32[4,1088]{1,0:T(4,128)S(1)} collective-permute-done((f32[4,1088]{1,0:T(4,128)S(1)}, f32[4,1088]{1,0:T(4,128)S(1)}, u32[]{:S(2)}, u32[]{:S(2)}) %collective-permute-start.7) | collective-permute-done | bytes 17440 | tf_op jit(solution)/shard_map/cond/branch_1_fun/ppermute | solution.py:99
  446.6 7.1 %collective-permute-done.6 = bf16[128,1152]{1,0:T(8,128)(2,1)} collective-permute-done((bf16[128,1152]{1,0:T(8,128)(2,1)}, bf16[128,1152]{1,0:T(8,128)(2,1)}, u32[]{:S(2)}, u32[]{:S(2)}) %collective-permute-start.6) | collective-permute-done | bytes 294944 | tf_op jit(solution)/shard_map/cond/branch_1_fun/ppermute | solution.py:99
  463.0 17.6 %collective-permute-done.10 = bf16[128,1152]{1,0:T(8,128)(2,1)S(1)} collective-permute-done((bf16[128,1152]{1,0:T(8,128)(2,1)S(1)}, bf16[128,1152]{1,0:T(8,128)(2,1)S(1)}, u32[]{:S(2)}, u32[]{:S(2)}) %collective-permute-start.10) | collective-permute-done | bytes 294944 | tf_op jit(solution)/shard_map/cond/branch_1_fun/ppermute | solution.py:99
  484.4 5.2 %collective-permute-done.12 = bf16[128,1152]{1,0:T(8,128)(2,1)S(1)} collective-permute-done((bf16[128,1152]{1,0:T(8,128)(2,1)S(1)}, bf16[128,1152]{1,0:T(8,128)(2,1)S(1)}, u32[]{:S(2)}, u32[]{:S(2)}) %collective-permute-start.12) | collective-permute-done | bytes 294944 | tf_op jit(solution)/shard_map/cond/branch_1_fun/ppermute | solution.py:99
  490.8 3.2 fusion.5
  494.0 3.5 collective-permute-done.14
  (315 shorter events, 138.1 us)
Async XLA Ops:
  7.3 69.4 %all-gather.3.cloned.1.call-start = ((), (), s32[]{:S(2)}) async-start(), calls=%async_computation.2 | async-start | bytes 3932160 | tf_op jit(solution)/shard_map/all_gather | solution.py:851
  9.5 225.1 %all-gather.5.cloned.1.call-start = ((), (), s32[]{:S(2)}) async-start(), calls=%async_computation.3 | async-start | bytes 7077888 | tf_op jit(solution)/shard_map/all_gather | solution.py:884
  9.7 12.1 %collective-permute-start.62 = (bf16[1,1088]{1,0:T(2,128)(2,1)S(1)}, bf16[1,1088]{1,0:T(2,128)(2,1)S(1)}, u32[]{:S(2)}, u32[]{:S(2)}) collective-permute-start(bf16[1,1088]{1,0:T(2,128)(2,1)S(1)} %broadcast_in_dim.60), channel_id=1, source_target_pairs={{0,8},{8,0},{16,24},{24,16},{1,9},{9,1},{17,25},{25,17},{2,10},{10... | collective-permute-start | bytes 6536 | tf_op jit(solution)/shard_map/ppermute | solution.py:123
  76.6 28.1 %collective-permute-start.65 = (bf16[512,1152]{1,0:T(8,128)(2,1)}, bf16[512,1152]{1,0:T(8,128)(2,1)}, u32[]{:S(2)}, u32[]{:S(2)}) collective-permute-start(bf16[512,1152]{1,0:T(8,128)(2,1)} %pad_maximum_fusion.3), channel_id=1, source_target_pairs={{0,8},{8,0},{16,24},{24,16},{1,9},{9,1},{17,25},{25,17},{2,10},{10... | collective-permute-start | bytes 3538952 | tf_op jit(solution)/shard_map/ppermute | solution.py:123
  97.4 10.7 %collective-permute-start.64 = (bf16[512,2048]{1,0:T(8,128)(2,1)S(1)}, bf16[512,2048]{1,0:T(8,128)(2,1)}, u32[]{:S(2)}, u32[]{:S(2)}) collective-permute-start(bf16[512,2048]{1,0:T(8,128)(2,1)S(1)} %get-tuple-element.489), channel_id=1, source_target_pairs={{0,1},{1,0},{2,3},{3,2},{4,5},{5,4},{6,7},{7,6},{8,9},{9,8},{10,11... | collective-permute-start | bytes 6291464 | tf_op jit(solution)/shard_map/ppermute | solution.py:123
  108.2 300.8 %reduce-scatter.3.cloned.1.call-start = ((), (), s32[]{:S(2)}) async-start(), calls=%async_computation.4 | async-start | bytes 7077888 | tf_op jit(solution)/shard_map/reduce_scatter | solution.py:916
  124.8 14.9 %collective-permute-start.39 = (bf16[2,128,1024]{2,1,0:T(8,128)(2,1)S(1)}, bf16[2,128,1024]{2,1,0:T(8,128)(2,1)S(1)}, u32[]{:S(2)}, u32[]{:S(2)}) collective-permute-start(bf16[2,128,1024]{2,1,0:T(8,128)(2,1)S(1)} %get-tuple-element.126), channel_id=1, source_target_pairs={{0,2},{2,0},{4,6},{6,4},{1,3},{3,1},{5,7},{7,5},{8,10},{10,8},{12,... | collective-permute-start | bytes 1572872 | tf_op jit(solution)/shard_map/cond/branch_1_fun/ppermute | solution.py:99
  126.4 13.4 %collective-permute-start.40 = (bf16[2,128,1024]{2,1,0:T(8,128)(2,1)S(1)}, bf16[2,128,1024]{2,1,0:T(8,128)(2,1)S(1)}, u32[]{:S(2)}, u32[]{:S(2)}) collective-permute-start(bf16[2,128,1024]{2,1,0:T(8,128)(2,1)S(1)} %get-tuple-element.127), channel_id=1, source_target_pairs={{0,4},{4,0},{2,6},{6,2},{1,5},{5,1},{3,7},{7,3},{8,12},{12,8},{10,... | collective-permute-start | bytes 1572872 | tf_op jit(solution)/shard_map/cond/branch_1_fun/ppermute | solution.py:99
  127.9 11.9 %collective-permute-start.41 = (bf16[64,2048]{1,0:T(8,128)(2,1)S(1)}, bf16[64,2048]{1,0:T(8,128)(2,1)S(1)}, u32[]{:S(2)}, u32[]{:S(2)}) collective-permute-start(bf16[64,2048]{1,0:T(8,128)(2,1)S(1)} %get-tuple-element.128), channel_id=1, source_target_pairs={{0,8},{8,0},{16,24},{24,16},{1,9},{9,1},{17,25},{25,17},{2,10},{10... | collective-permute-start | bytes 786440 | tf_op jit(solution)/shard_map/cond/branch_1_fun/ppermute | solution.py:99
  141.8 13.6 %collective-permute-start.44 = (bf16[64,2048]{1,0:T(8,128)(2,1)S(1)}, bf16[64,2048]{1,0:T(8,128)(2,1)S(1)}, u32[]{:S(2)}, u32[]{:S(2)}) collective-permute-start(bf16[64,2048]{1,0:T(8,128)(2,1)S(1)} %get-tuple-element.137), channel_id=1, source_target_pairs={{0,8},{8,0},{16,24},{24,16},{1,9},{9,1},{17,25},{25,17},{2,10},{10... | collective-permute-start | bytes 786440 | tf_op jit(solution)/shard_map/cond/branch_1_fun/ppermute | solution.py:99
  157.5 13.5 %collective-permute-start.45 = (bf16[64,2048]{1,0:T(8,128)(2,1)S(1)}, bf16[64,2048]{1,0:T(8,128)(2,1)S(1)}, u32[]{:S(2)}, u32[]{:S(2)}) collective-permute-start(bf16[64,2048]{1,0:T(8,128)(2,1)S(1)} %get-tuple-element.144), channel_id=1, source_target_pairs={{0,8},{8,0},{16,24},{24,16},{1,9},{9,1},{17,25},{25,17},{2,10},{10... | collective-permute-start | bytes 786440 | tf_op jit(solution)/shard_map/cond/branch_1_fun/ppermute | solution.py:99
  160.1 10.9 %collective-permute-start.46 = (bf16[1,128,1024]{2,1,0:T(8,128)(2,1)S(1)}, bf16[1,128,1024]{2,1,0:T(8,128)(2,1)S(1)}, u32[]{:S(2)}, u32[]{:S(2)}) collective-permute-start(bf16[1,128,1024]{2,1,0:T(8,128)(2,1)S(1)} %get-tuple-element.145.first_ref), channel_id=1, source_target_pairs={{0,4},{4,0},{2,6},{6,2},{1,5},{5,1},{3,7},{7,3},{8,12},{12,8},{10,... | collective-permute-start | bytes 786440 | tf_op jit(solution)/shard_map/cond/branch_1_fun/ppermute | solution.py:99
  173.4 14.1 %collective-permute-start.51 = (bf16[2,1,128,1024]{3,2,1,0:T(8,128)(2,1)S(1)}, bf16[2,1,128,1024]{3,2,1,0:T(8,128)(2,1)S(1)}, u32[]{:S(2)}, u32[]{:S(2)}) collective-permute-start(bf16[2,1,128,1024]{3,2,1,0:T(8,128)(2,1)S(1)} %get-tuple-element.154.first_ref), channel_id=1, source_target_pairs={{0,2},{2,0},{4,6},{6,4},{1,3},{3,1},{5,7},{7,5},{8,10},{10,8},{12,... | collective-permute-start | bytes 1572872 | tf_op jit(solution)/shard_map/cond/branch_1_fun/ppermute | solution.py:99
  174.9 12.6 %collective-permute-start.52 = (bf16[2,1,128,1024]{3,2,1,0:T(8,128)(2,1)S(1)}, bf16[2,1,128,1024]{3,2,1,0:T(8,128)(2,1)S(1)}, u32[]{:S(2)}, u32[]{:S(2)}) collective-permute-start(bf16[2,1,128,1024]{3,2,1,0:T(8,128)(2,1)S(1)} %get-tuple-element.155.second_ref), channel_id=1, source_target_pairs={{0,4},{4,0},{2,6},{6,2},{1,5},{5,1},{3,7},{7,3},{8,12},{12,8},{10,... | collective-permute-start | bytes 1572872 | tf_op jit(solution)/shard_map/cond/branch_1_fun/ppermute | solution.py:99
  174.9 12.6 %collective-permute-start.50 = (bf16[64,2048]{1,0:T(8,128)(2,1)S(1)}, bf16[64,2048]{1,0:T(8,128)(2,1)S(1)}, u32[]{:S(2)}, u32[]{:S(2)}) collective-permute-start(bf16[64,2048]{1,0:T(8,128)(2,1)S(1)} %get-tuple-element.153), channel_id=1, source_target_pairs={{0,8},{8,0},{16,24},{24,16},{1,9},{9,1},{17,25},{25,17},{2,10},{10... | collective-permute-start | bytes 786440 | tf_op jit(solution)/shard_map/cond/branch_1_fun/ppermute | solution.py:99
  189.7 20.3 %collective-permute-start.57 = (bf16[1,512,2048]{2,1,0:T(8,128)(2,1)}, bf16[1,512,2048]{2,1,0:T(8,128)(2,1)}, u32[]{:S(2)}, u32[]{:S(2)}) collective-permute-start(bf16[1,512,2048]{2,1,0:T(8,128)(2,1)} %bitcast.10), channel_id=1, source_target_pairs={{0,1},{1,0},{2,3},{3,2},{4,5},{5,4},{6,7},{7,6},{8,9},{9,8},{10,11... | collective-permute-start | bytes 6291464 | tf_op jit(solution)/shard_map/cond/branch_1_fun/ppermute | solution.py:99
  189.7 20.3 %collective-permute-start.55 = (bf16[2,1,128,1024]{3,2,1,0:T(8,128)(2,1)S(1)}, bf16[2,1,128,1024]{3,2,1,0:T(8,128)(2,1)S(1)}, u32[]{:S(2)}, u32[]{:S(2)}) collective-permute-start(bf16[2,1,128,1024]{3,2,1,0:T(8,128)(2,1)S(1)} %get-tuple-element.166.first_ref), channel_id=1, source_target_pairs={{0,2},{2,0},{4,6},{6,4},{1,3},{3,1},{5,7},{7,5},{8,10},{10,8},{12,... | collective-permute-start | bytes 1572872 | tf_op jit(solution)/shard_map/cond/branch_1_fun/ppermute | solution.py:99
  190.2 19.7 %collective-permute-start.56 = (bf16[2,1,128,1024]{3,2,1,0:T(8,128)(2,1)S(1)}, bf16[2,1,128,1024]{3,2,1,0:T(8,128)(2,1)S(1)}, u32[]{:S(2)}, u32[]{:S(2)}) collective-permute-start(bf16[2,1,128,1024]{3,2,1,0:T(8,128)(2,1)S(1)} %get-tuple-element.167.second_ref), channel_id=1, source_target_pairs={{0,4},{4,0},{2,6},{6,2},{1,5},{5,1},{3,7},{7,3},{8,12},{12,8},{10,... | collective-permute-start | bytes 1572872 | tf_op jit(solution)/shard_map/cond/branch_1_fun/ppermute | solution.py:99
  190.9 19.1 %collective-permute-start.53 = (bf16[1,128,1024]{2,1,0:T(8,128)(2,1)S(1)}, bf16[1,128,1024]{2,1,0:T(8,128)(2,1)S(1)}, u32[]{:S(2)}, u32[]{:S(2)}) collective-permute-start(bf16[1,128,1024]{2,1,0:T(8,128)(2,1)S(1)} %get-tuple-element.164.first_ref), channel_id=1, source_target_pairs={{0,4},{4,0},{2,6},{6,2},{1,5},{5,1},{3,7},{7,3},{8,12},{12,8},{10,... | collective-permute-start | bytes 786440 | tf_op jit(solution)/shard_map/cond/branch_1_fun/ppermute | solution.py:99
  192.3 17.6 %collective-permute-start.54 = (bf16[1,128,1024]{2,1,0:T(8,128)(2,1)S(1)}, bf16[1,128,1024]{2,1,0:T(8,128)(2,1)S(1)}, u32[]{:S(2)}, u32[]{:S(2)}) collective-permute-start(bf16[1,128,1024]{2,1,0:T(8,128)(2,1)S(1)} %get-tuple-element.165.second_ref), channel_id=1, source_target_pairs={{0,2},{2,0},{4,6},{6,4},{1,3},{3,1},{5,7},{7,5},{8,10},{10,8},{12,... | collective-permute-start | bytes 786440 | tf_op jit(solution)/shard_map/cond/branch_1_fun/ppermute | solution.py:99
  212.6 15.5 %collective-permute-start.60 = (bf16[1,512,2048]{2,1,0:T(8,128)(2,1)}, bf16[1,512,2048]{2,1,0:T(8,128)(2,1)}, u32[]{:S(2)}, u32[]{:S(2)}) collective-permute-start(bf16[1,512,2048]{2,1,0:T(8,128)(2,1)} %bitcast.12), channel_id=1, source_target_pairs={{0,1},{1,0},{2,3},{3,2},{4,5},{5,4},{6,7},{7,6},{8,9},{9,8},{10,11... | collective-permute-start | bytes 6291464 | tf_op jit(solution)/shard_map/cond/branch_1_fun/ppermute | solution.py:99
  212.6 14.3 %collective-permute-start.58 = (bf16[2,1,128,1024]{3,2,1,0:T(8,128)(2,1)S(1)}, bf16[2,1,128,1024]{3,2,1,0:T(8,128)(2,1)S(1)}, u32[]{:S(2)}, u32[]{:S(2)}) collective-permute-start(bf16[2,1,128,1024]{3,2,1,0:T(8,128)(2,1)S(1)} %get-tuple-element.176.first_ref), channel_id=1, source_target_pairs={{0,2},{2,0},{4,6},{6,4},{1,3},{3,1},{5,7},{7,5},{8,10},{10,8},{12,... | collective-permute-start | bytes 1572872 | tf_op jit(solution)/shard_map/cond/branch_1_fun/ppermute | solution.py:99
  214.0 14.1 %collective-permute-start.59 = (bf16[2,1,128,1024]{3,2,1,0:T(8,128)(2,1)S(1)}, bf16[2,1,128,1024]{3,2,1,0:T(8,128)(2,1)S(1)}, u32[]{:S(2)}, u32[]{:S(2)}) collective-permute-start(bf16[2,1,128,1024]{3,2,1,0:T(8,128)(2,1)S(1)} %get-tuple-element.177.second_ref), channel_id=1, source_target_pairs={{0,4},{4,0},{2,6},{6,2},{1,5},{5,1},{3,7},{7,3},{8,12},{12,8},{10,... | collective-permute-start | bytes 1572872 | tf_op jit(solution)/shard_map/cond/branch_1_fun/ppermute | solution.py:99
  270.0 16.3 %collective-permute-start.67 = (bf16[2,128,1024]{2,1,0:T(8,128)(2,1)S(1)}, bf16[2,128,1024]{2,1,0:T(8,128)(2,1)S(1)}, u32[]{:S(2)}, u32[]{:S(2)}) collective-permute-start(bf16[2,128,1024]{2,1,0:T(8,128)(2,1)S(1)} %get-tuple-element.521), channel_id=1, source_target_pairs={{0,2},{2,0},{4,6},{6,4},{1,3},{3,1},{5,7},{7,5},{8,10},{10,8},{12,... | collective-permute-start | bytes 1572872 | tf_op jit(solution)/shard_map/ppermute | solution.py:99
  270.6 15.6 %collective-permute-start.68 = (bf16[2,128,1024]{2,1,0:T(8,128)(2,1)S(1)}, bf16[2,128,1024]{2,1,0:T(8,128)(2,1)S(1)}, u32[]{:S(2)}, u32[]{:S(2)}) collective-permute-start(bf16[2,128,1024]{2,1,0:T(8,128)(2,1)S(1)} %get-tuple-element.522), channel_id=1, source_target_pairs={{0,4},{4,0},{2,6},{6,2},{1,5},{5,1},{3,7},{7,3},{8,12},{12,8},{10,... | collective-permute-start | bytes 1572872 | tf_op jit(solution)/shard_map/ppermute | solution.py:99
  286.3 214.7 %reduce-scatter.5.cloned.1.call-start = ((), (), s32[]{:S(2)}) async-start(), calls=%async_computation.5 | async-start | bytes 3932160 | tf_op jit(solution)/shard_map/reduce_scatter | solution.py:957
  288.2 10.6 %collective-permute-start.18 = (bf16[512,2048]{1,0:T(8,128)(2,1)}, bf16[512,2048]{1,0:T(8,128)(2,1)}, u32[]{:S(2)}, u32[]{:S(2)}) collective-permute-start(bf16[512,2048]{1,0:T(8,128)(2,1)} %get-tuple-element.193), channel_id=1, source_target_pairs={{0,1},{1,0},{2,3},{3,2},{4,5},{5,4},{6,7},{7,6},{8,9},{9,8},{10,11... | collective-permute-start | bytes 6291464 | tf_op jit(solution)/shard_map/cond/branch_1_fun/ppermute | solution.py:99
  288.2 10.6 %collective-permute-start.19 = (bf16[512,2048]{1,0:T(8,128)(2,1)}, bf16[512,2048]{1,0:T(8,128)(2,1)}, u32[]{:S(2)}, u32[]{:S(2)}) collective-permute-start(bf16[512,2048]{1,0:T(8,128)(2,1)} %get-tuple-element.194), channel_id=1, source_target_pairs={{0,1},{1,0},{2,3},{3,2},{4,5},{5,4},{6,7},{7,6},{8,9},{9,8},{10,11... | collective-permute-start | bytes 6291464 | tf_op jit(solution)/shard_map/cond/branch_1_fun/ppermute | solution.py:99
  288.7 10.1 %collective-permute-start.20 = (bf16[512,2048]{1,0:T(8,128)(2,1)}, bf16[512,2048]{1,0:T(8,128)(2,1)S(1)}, u32[]{:S(2)}, u32[]{:S(2)}) collective-permute-start(bf16[512,2048]{1,0:T(8,128)(2,1)} %get-tuple-element.195), channel_id=1, source_target_pairs={{0,1},{1,0},{2,3},{3,2},{4,5},{5,4},{6,7},{7,6},{8,9},{9,8},{10,11... | collective-permute-start | bytes 6291464 | tf_op jit(solution)/shard_map/cond/branch_1_fun/ppermute | solution.py:99
  302.4 17.1 %collective-permute-start.22 = (bf16[2,128,1024]{2,1,0:T(8,128)(2,1)S(1)}, bf16[2,128,1024]{2,1,0:T(8,128)(2,1)S(1)}, u32[]{:S(2)}, u32[]{:S(2)}) collective-permute-start(bf16[2,128,1024]{2,1,0:T(8,128)(2,1)S(1)} %get-tuple-element.205), channel_id=1, source_target_pairs={{0,2},{2,0},{4,6},{6,4},{1,3},{3,1},{5,7},{7,5},{8,10},{10,8},{12,... | collective-permute-start | bytes 1572872 | tf_op jit(solution)/shard_map/cond/branch_1_fun/ppermute | solution.py:99
  303.9 15.6 %collective-permute-start.23 = (bf16[2,128,1024]{2,1,0:T(8,128)(2,1)S(1)}, bf16[2,128,1024]{2,1,0:T(8,128)(2,1)S(1)}, u32[]{:S(2)}, u32[]{:S(2)}) collective-permute-start(bf16[2,128,1024]{2,1,0:T(8,128)(2,1)S(1)} %get-tuple-element.206), channel_id=1, source_target_pairs={{0,4},{4,0},{2,6},{6,2},{1,5},{5,1},{3,7},{7,3},{8,12},{12,8},{10,... | collective-permute-start | bytes 1572872 | tf_op jit(solution)/shard_map/cond/branch_1_fun/ppermute | solution.py:99
  305.3 14.3 %collective-permute-start.21 = (bf16[64,2048]{1,0:T(8,128)(2,1)S(1)}, bf16[64,2048]{1,0:T(8,128)(2,1)S(1)}, u32[]{:S(2)}, u32[]{:S(2)}) collective-permute-start(bf16[64,2048]{1,0:T(8,128)(2,1)S(1)} %get-tuple-element.204), channel_id=1, source_target_pairs={{0,8},{8,0},{16,24},{24,16},{1,9},{9,1},{17,25},{25,17},{2,10},{10... | collective-permute-start | bytes 786440 | tf_op jit(solution)/shard_map/cond/branch_1_fun/ppermute | solution.py:99
  322.5 18.8 %collective-permute-start.27 = (bf16[2,128,1024]{2,1,0:T(8,128)(2,1)}, bf16[2,128,1024]{2,1,0:T(8,128)(2,1)}, u32[]{:S(2)}, u32[]{:S(2)}) collective-permute-start(bf16[2,128,1024]{2,1,0:T(8,128)(2,1)} %get-tuple-element.222), channel_id=1, source_target_pairs={{0,2},{2,0},{4,6},{6,4},{1,3},{3,1},{5,7},{7,5},{8,10},{10,8},{12,... | collective-permute-start | bytes 1572872 | tf_op jit(solution)/shard_map/cond/branch_1_fun/ppermute | solution.py:99
  323.1 18.2 %collective-permute-start.28 = (bf16[2,128,1024]{2,1,0:T(8,128)(2,1)}, bf16[2,128,1024]{2,1,0:T(8,128)(2,1)}, u32[]{:S(2)}, u32[]{:S(2)}) collective-permute-start(bf16[2,128,1024]{2,1,0:T(8,128)(2,1)} %get-tuple-element.223), channel_id=1, source_target_pairs={{0,4},{4,0},{2,6},{6,2},{1,5},{5,1},{3,7},{7,3},{8,12},{12,8},{10,... | collective-permute-start | bytes 1572872 | tf_op jit(solution)/shard_map/cond/branch_1_fun/ppermute | solution.py:99
  323.7 13.1 %collective-permute-start.24 = (bf16[64,2048]{1,0:T(8,128)(2,1)}, bf16[64,2048]{1,0:T(8,128)(2,1)}, u32[]{:S(2)}, u32[]{:S(2)}) collective-permute-start(bf16[64,2048]{1,0:T(8,128)(2,1)} %get-tuple-element.219), channel_id=1, source_target_pairs={{0,8},{8,0},{16,24},{24,16},{1,9},{9,1},{17,25},{25,17},{2,10},{10... | collective-permute-start | bytes 786440 | tf_op jit(solution)/shard_map/cond/branch_1_fun/ppermute | solution.py:99
  326.2 15.1 %collective-permute-start.25 = (bf16[128,1024]{1,0:T(8,128)(2,1)}, bf16[128,1024]{1,0:T(8,128)(2,1)}, u32[]{:S(2)}, u32[]{:S(2)}) collective-permute-start(bf16[128,1024]{1,0:T(8,128)(2,1)} %get-tuple-element.220), channel_id=1, source_target_pairs={{0,4},{4,0},{2,6},{6,2},{1,5},{5,1},{3,7},{7,3},{8,12},{12,8},{10,... | collective-permute-start | bytes 786440 | tf_op jit(solution)/shard_map/cond/branch_1_fun/ppermute | solution.py:99
  327.6 13.7 %collective-permute-start.26 = (bf16[128,1024]{1,0:T(8,128)(2,1)}, bf16[128,1024]{1,0:T(8,128)(2,1)}, u32[]{:S(2)}, u32[]{:S(2)}) collective-permute-start(bf16[128,1024]{1,0:T(8,128)(2,1)} %get-tuple-element.221), channel_id=1, source_target_pairs={{0,2},{2,0},{4,6},{6,4},{1,3},{3,1},{5,7},{7,5},{8,10},{10,8},{12,... | collective-permute-start | bytes 786440 | tf_op jit(solution)/shard_map/cond/branch_1_fun/ppermute | solution.py:99
  354.4 10.4 %collective-permute-start.31 = (bf16[2,1,128,1024]{3,2,1,0:T(8,128)(2,1)S(1)}, bf16[2,1,128,1024]{3,2,1,0:T(8,128)(2,1)S(1)}, u32[]{:S(2)}, u32[]{:S(2)}) collective-permute-start(bf16[2,1,128,1024]{3,2,1,0:T(8,128)(2,1)S(1)} %get-tuple-element.246.first_ref), channel_id=1, source_target_pairs={{0,2},{2,0},{4,6},{6,4},{1,3},{3,1},{5,7},{7,5},{8,10},{10,8},{12,... | collective-permute-start | bytes 1572872 | tf_op jit(solution)/shard_map/cond/branch_1_fun/ppermute | solution.py:99
  366.3 10.3 %collective-permute-start.33 = (bf16[1,512,2048]{2,1,0:T(8,128)(2,1)S(1)}, bf16[1,512,2048]{2,1,0:T(8,128)(2,1)}, u32[]{:S(2)}, u32[]{:S(2)}) collective-permute-start(bf16[1,512,2048]{2,1,0:T(8,128)(2,1)S(1)} %bitcast.123), channel_id=1, source_target_pairs={{0,1},{1,0},{2,3},{3,2},{4,5},{5,4},{6,7},{7,6},{8,9},{9,8},{10,11... | collective-permute-start | bytes 6291464 | tf_op jit(solution)/shard_map/cond/branch_1_fun/ppermute | solution.py:99
  377.3 30.9 %collective-permute-start.36 = (bf16[128,2048]{1,0:T(8,128)(2,1)S(1)}, bf16[128,2048]{1,0:T(8,128)(2,1)}, u32[]{:S(2)}, u32[]{:S(2)}) collective-permute-start(bf16[128,2048]{1,0:T(8,128)(2,1)S(1)} %fold_end.3), channel_id=1, source_target_pairs={{0,8},{8,0},{16,24},{24,16},{1,9},{9,1},{17,25},{25,17},{2,10},{10... | collective-permute-start | bytes 1572872 | tf_op jit(solution)/shard_map/cond/branch_1_fun/ppermute | solution.py:99
  379.9 28.3 %collective-permute-start.37 = (bf16[2,128,1024]{2,1,0:T(8,128)(2,1)}, bf16[2,128,1024]{2,1,0:T(8,128)(2,1)}, u32[]{:S(2)}, u32[]{:S(2)}) collective-permute-start(bf16[2,128,1024]{2,1,0:T(8,128)(2,1)} %copy-done.7), channel_id=1, source_target_pairs={{0,2},{2,0},{4,6},{6,4},{1,3},{3,1},{5,7},{7,5},{8,10},{10,8},{12,... | collective-permute-start | bytes 1572872 | tf_op jit(solution)/shard_map/cond/branch_1_fun/ppermute | solution.py:99
  380.5 27.7 %collective-permute-start.38 = (bf16[2,128,1024]{2,1,0:T(8,128)(2,1)}, bf16[2,128,1024]{2,1,0:T(8,128)(2,1)}, u32[]{:S(2)}, u32[]{:S(2)}) collective-permute-start(bf16[2,128,1024]{2,1,0:T(8,128)(2,1)} %copy-done.6), channel_id=1, source_target_pairs={{0,4},{4,0},{2,6},{6,2},{1,5},{5,1},{3,7},{7,3},{8,12},{12,8},{10,... | collective-permute-start | bytes 1572872 | tf_op jit(solution)/shard_map/cond/branch_1_fun/ppermute | solution.py:99
  415.7 9.7 %collective-permute-start = (bf16[512,2048]{1,0:T(8,128)(2,1)}, bf16[512,2048]{1,0:T(8,128)(2,1)S(1)}, u32[]{:S(2)}, u32[]{:S(2)}) collective-permute-start(bf16[512,2048]{1,0:T(8,128)(2,1)} %get-tuple-element.324), channel_id=1, source_target_pairs={{0,1},{1,0},{2,3},{3,2},{4,5},{5,4},{6,7},{7,6},{8,9},{9,8},{10,11... | collective-permute-start | bytes 6291464 | tf_op jit(solution)/shard_map/cond/branch_1_fun/ppermute | solution.py:99
  428.6 25.1 %collective-permute-start.4 = (bf16[2,128,1024]{2,1,0:T(8,128)(2,1)}, bf16[2,128,1024]{2,1,0:T(8,128)(2,1)S(1)}, u32[]{:S(2)}, u32[]{:S(2)}) collective-permute-start(bf16[2,128,1024]{2,1,0:T(8,128)(2,1)} %get-tuple-element.342), channel_id=1, source_target_pairs={{0,2},{2,0},{4,6},{6,4},{1,3},{3,1},{5,7},{7,5},{8,10},{10,8},{12,... | collective-permute-start | bytes 1572872 | tf_op jit(solution)/shard_map/cond/branch_1_fun/ppermute | solution.py:99
  430.1 23.6 %collective-permute-start.5 = (bf16[2,128,1024]{2,1,0:T(8,128)(2,1)}, bf16[2,128,1024]{2,1,0:T(8,128)(2,1)}, u32[]{:S(2)}, u32[]{:S(2)}) collective-permute-start(bf16[2,128,1024]{2,1,0:T(8,128)(2,1)} %get-tuple-element.343), channel_id=1, source_target_pairs={{0,4},{4,0},{2,6},{6,2},{1,5},{5,1},{3,7},{7,3},{8,12},{12,8},{10,... | collective-permute-start | bytes 1572872 | tf_op jit(solution)/shard_map/cond/branch_1_fun/ppermute | solution.py:99
  430.7 23.0 %collective-permute-start.6 = (bf16[128,1152]{1,0:T(8,128)(2,1)}, bf16[128,1152]{1,0:T(8,128)(2,1)}, u32[]{:S(2)}, u32[]{:S(2)}) collective-permute-start(bf16[128,1152]{1,0:T(8,128)(2,1)} %get-tuple-element.344), channel_id=1, source_target_pairs={{0,8},{8,0},{16,24},{24,16},{1,9},{9,1},{17,25},{25,17},{2,10},{10... | collective-permute-start | bytes 884744 | tf_op jit(solution)/shard_map/cond/branch_1_fun/ppermute | solution.py:99
  432.5 14.1 %collective-permute-start.7 = (f32[4,1088]{1,0:T(4,128)S(1)}, f32[4,1088]{1,0:T(4,128)S(1)}, u32[]{:S(2)}, u32[]{:S(2)}) collective-permute-start(f32[4,1088]{1,0:T(4,128)S(1)} %add.148), channel_id=1, source_target_pairs={{0,16},{8,24},{16,0},{24,8},{1,17},{9,25},{17,1},{25,9},{2,18},{10... | collective-permute-start | bytes 52232 | tf_op jit(solution)/shard_map/cond/branch_1_fun/ppermute | solution.py:99
  457.4 23.3 %collective-permute-start.10 = (bf16[128,1152]{1,0:T(8,128)(2,1)S(1)}, bf16[128,1152]{1,0:T(8,128)(2,1)S(1)}, u32[]{:S(2)}, u32[]{:S(2)}) collective-permute-start(bf16[128,1152]{1,0:T(8,128)(2,1)S(1)} %copy-done.35), channel_id=1, source_target_pairs={{0,8},{8,0},{16,24},{24,16},{1,9},{9,1},{17,25},{25,17},{2,10},{10... | collective-permute-start | bytes 884744 | tf_op jit(solution)/shard_map/cond/branch_1_fun/ppermute | solution.py:99
  (68 other events, 807.6 us)
Sparse Core Ops, SparseCore 0:
  10.2 66.3 all-gather.2
  108.3 112.8 all-gather.4
  286.4 111.9 reduce-scatter.2
  409.1 72.7 reduce-scatter.4

commit v4 on v3

--- a/solution.py
+++ b/solution.py
@@ -263,15 +263,20 @@
 def plane_gather(share):
     lead, rows, width = share.shape
     first, second = share[..., : width // 2], share[..., width // 2 :]
-    got = yield [(first, "heads", FAR), (second, "heads", NEAR)]
+    got = yield [(first, "heads", FAR), (second, "heads", NEAR)], (first, second)
     first, second = vmem_call(
         open_line_kernel, "open_line", 16, [(2, lead, rows, width // 2)] * 2, first, got[0], second, got[1]
     )
-    got = yield [(first, "heads", NEAR), (second, "heads", FAR)]
+    got = yield [(first, "heads", NEAR), (second, "heads", FAR)], (first, second)
+    return (yield from core_gather(first, second, *got))
+
+
+def core_gather(first, second, got_first, got_second):
+    _, lead, rows, middle = first.shape
     (mine,) = vmem_call(
-        open_chip_kernel, "open_chip", 24, [(lead, 2, 2, rows, width)], first, got[0], second, got[1]
-    )
-    mine = mine.reshape(lead, 4 * rows, width)
+        open_chip_kernel, "open_chip", 24, [(lead, 2, 2, rows, 2 * middle)], first, got_first, second, got_second
+    )
+    mine = mine.reshape(lead, 4 * rows, 2 * middle)
     (other,) = yield [(mine, "tensor", SWAP)]
     return mine, other
 
@@ -290,8 +295,11 @@
 
 
 def sum_all(values):
-    for axis in ("fsdp", "tensor", "heads"):
-        for stride in bits(axis):
+    for axis in ("tensor", "heads", "fsdp"):
+        strides = bits(axis)
+        if axis == "fsdp" and len(strides) > 1:
+            strides = [strides[0] + strides[1]] + strides[1:]
+        for stride in strides:
             (got,) = yield [(values, axis, flip(axis, stride))]
             values = values + got
     return values
@@ -682,38 +690,61 @@
             jax.ShapeDtypeStruct((length, 1), jnp.int32),
         ],
         compiler_params=call_params(24),
-        cost_estimate=cheap(),
+        cost_estimate=pl.CostEstimate(flops=20_000_000_000, bytes_accessed=20_000_000, transcendentals=0),
         name="prepare",
     )(tokens, gain[None], seg_rows)
 
 
 def feed_kernel(*refs):
-    normed, cotangent, proj_ref, (act_refs, grad_refs) = refs[:4], refs[4:8], refs[8], (refs[9:11], refs[11:])
-    half = act_refs[0].shape[-1]
+    sources, (proj_hbm, *results, normed, cotangent, proj, arrive) = refs[:8], refs[8:]
+    acts, grads = results[:2], results[2:]
+    half = acts[0].shape[-1]
+    rows = sources[0].shape[0]
+    tile = min(256, rows)
+
+    def fetch(source, target, k):
+        copy = pltpu.make_async_copy(source, target, arrive.at[k])
+        copy.start()
+        return copy
+
+    loads = [fetch(proj_hbm, proj, 8)]
     for k in range(4):
-        act_ref, grad_ref = act_refs[k // 2], grad_refs[k // 2]
-        gate_up = jnp.dot(normed[k][...], proj_ref[:, : 2 * half], preferred_element_type=jnp.float32)
-        gate, up = gate_up[:, :half], gate_up[:, half:]
-        act_grad = jnp.dot(cotangent[k][...], proj_ref[:, 2 * half :], preferred_element_type=jnp.float32)
-        sigmoid = jax.nn.sigmoid(gate)
-        silu = gate * sigmoid
-        act_ref[k % 2] = low(silu * up)
-        grad_ref[k % 2, :, :half] = low(act_grad * up * sigmoid * (1.0 + gate * (1.0 - sigmoid)))
-        grad_ref[k % 2, :, half:] = low(act_grad * silu)
+        loads.append(fetch(sources[k], normed.at[k], 2 * k))
+        loads.append(fetch(sources[4 + k], cotangent.at[k], 2 * k + 1))
+    loads[0].wait()
+    for k in range(4):
+        loads[2 * k + 1].wait()
+        loads[2 * k + 2].wait()
+        act_ref, grad_ref = acts[k // 2], grads[k // 2]
+
+        @pl.loop(0, rows // tile)
+        def _(step):
+            here = pl.ds(pl.multiple_of(step * tile, tile), tile)
+            gate_up = jnp.dot(normed[k, here, :], proj[:, : 2 * half], preferred_element_type=jnp.float32)
+            gate, up = gate_up[:, :half], gate_up[:, half:]
+            act_grad = jnp.dot(cotangent[k, here, :], proj[:, 2 * half :], preferred_element_type=jnp.float32)
+            sigmoid = jax.nn.sigmoid(gate)
+            silu = gate * sigmoid
+            act_ref[k % 2, here, :] = low(silu * up)
+            grad_ref[k % 2, here, :half] = low(act_grad * up * sigmoid * (1.0 + gate * (1.0 - sigmoid)))
+            grad_ref[k % 2, here, half:] = low(act_grad * silu)
 
 
 def feed(normed, cotangent, proj):
     rows, model = normed[0].shape
     half = proj.shape[1] // 3
-    tile = min(256, rows)
-    block = pl.BlockSpec((tile, model), lambda i: (i, 0))
     widths = (half, half, 2 * half, 2 * half)
     return pl.pallas_call(
         feed_kernel,
-        grid=(rows // tile,),
-        in_specs=[block] * 8 + [pl.BlockSpec(proj.shape, lambda i: (0, 0), pipeline_mode=pl.Buffered(1))],
-        out_specs=[pl.BlockSpec((2, tile, w), lambda i: (0, i, 0)) for w in widths],
+        in_specs=[pl.BlockSpec(memory_space=pl.ANY)] * 9,
+        out_specs=[pl.BlockSpec(memory_space=pltpu.VMEM)] * 4,
         out_shape=[jax.ShapeDtypeStruct((2, rows, w), jnp.bfloat16) for w in widths],
+        scratch_shapes=[
+            pltpu.VMEM((4, rows, model), jnp.bfloat16),
+            pltpu.VMEM((4, rows, model), jnp.bfloat16),
+            pltpu.VMEM(proj.shape, jnp.bfloat16),
+            pltpu.SemaphoreType.DMA((9,)),
+        ],
         compiler_params=call_params(48),
         cost_estimate=cheap(),
         name="feed",
@@ -748,19 +779,18 @@
 
 
 def feed_weights_kernel(*refs):
-    normed, cotangent, grad, act, out_ref = refs[:4], refs[4:8], refs[8:10], refs[10:12], refs[12]
-    wide_cols = grad[0].shape[-1]
-    out_ref[:, :wide_cols] = low(
+    normed, cotangent, grad, act, (wide_ref, out_ref) = refs[:4], refs[4:8], refs[8:10], refs[10:12], refs[12:]
+    wide_ref[...] = low(
         sum(contract(normed[k][...], grad[k // 2][k % 2], 0, 0) for k in range(4))
     )
-    out_ref[:, wide_cols:] = low(
+    out_ref[...] = low(
         sum(contract(cotangent[k][...], act[k // 2][k % 2], 0, 0) for k in range(4))
     )
 
 
 def feed_weights(normed, cotangent, grad, act):
     rows, model = normed[0].shape
-    width = grad[0].shape[-1] + act[0].shape[-1]
+    widths = grad[0].shape[-1], act[0].shape[-1]
     cols = min(512, model)
 
     def whole(array):
@@ -770,48 +800,43 @@
         feed_weights_kernel,
         grid=(model // cols,),
         in_specs=[pl.BlockSpec((rows, cols), lambda i: (0, i))] * 8 + [whole(a) for a in (*grad, *act)],
-        out_specs=pl.BlockSpec((cols, width), lambda i: (i, 0)),
-        out_shape=jax.ShapeDtypeStruct((model, width), jnp.bfloat16),
+        out_specs=[pl.BlockSpec((cols, width), lambda i: (i, 0)) for width in widths],
+        out_shape=[jax.ShapeDtypeStruct((model, width), jnp.bfloat16) for width in widths],
         compiler_params=call_params(48),
         cost_estimate=cheap(),
         name="feed_weights",
     )(*normed, *cotangent, *grad, *act)
 
 
-def feed_sums_kernel(count, side_ref, *refs):
-    own, other, outs = refs[:count], refs[count:-3], refs[-3:]
+def feed_sums_kernel(side_ref, *refs):
+    sources, outs = refs[:4], refs[4:]
     half = outs[0].shape[1]
     mine = pl.program_id(0) == side_ref[0]
-    for held, keep in ((own, mine), (other, jnp.logical_not(mine))):
+    for (wide_ref, down_ref), keep in ((sources[:2], mine), (sources[2:], jnp.logical_not(mine))):
 
         @pl.when(keep)
         def _():
-            first = 0
-            for part in held:
-                for k, out in enumerate(outs):
-                    out[first : first + part.shape[0], :] = wide(part[:, k * half : (k + 1) * half])
-                first += part.shape[0]
+            for k in range(2):
+                outs[k][...] = wide(wide_ref[:, k * half : (k + 1) * half])
+            outs[2][...] = wide(down_ref[...])
 
 
 def feed_sums(side, own, other):
-    rows, width = sum(part.shape[0] for part in own), own[0].shape[1]
-    half = width // 3
-    parts = (*own, *other)
+    rows, half = other[1].shape
     return pl.pallas_call(
-        functools.partial(feed_sums_kernel, len(own)),
+        feed_sums_kernel,
         grid_spec=pltpu.PrefetchScalarGridSpec(
             num_scalar_prefetch=1,
             grid=(2,),
-            in_specs=[
-                pl.BlockSpec(p.shape, lambda i, side: (0, 0), pipeline_mode=pl.Buffered(1)) for p in parts
-            ],
+            in_specs=[pl.BlockSpec((None, rows, w), lambda i, side: (side[0], 0, 0)) for w in (2 * half, half)]
+            + [pl.BlockSpec((rows, w), lambda i, side: (0, 0)) for w in (2 * half, half)],
             out_specs=[pl.BlockSpec((rows, half), lambda i, side: (0, i))] * 3,
         ),
         out_shape=[jax.ShapeDtypeStruct((rows, 2 * half), jnp.float32)] * 3,
         compiler_params=call_params(32),
         cost_estimate=cheap(),
         name="feed_sums",
-    )(side, *parts)
+    )(side, *own, *other)
 
 
 def per_device(
@@ -912,13 +937,14 @@
     pair_sum = Job(plane_scatter(*pair_parts[:2]))
     (own_parts,) = beside(pair_sum, kernels=[(feed_model, (act, grad, feed_proj))])
     weight_args = ((*own_normed, *pair_normed), (*own_cot, *pair_cot), (grad, pair_grad), (act, pair_act))
-    (feed_w_part,) = beside(pair_sum, kernels=[(feed_weights, weight_args)])
-    feed_w_sum = lax.psum_scatter(
-        feed_w_part, "fsdp", scatter_dimension=0, tiled=True, axis_index_groups=alike()
-    ).reshape(2, shard, -1)
+    (feed_w_parts,) = beside(pair_sum, kernels=[(feed_weights, weight_args)])
+    feed_w_sums = [
+        lax.psum_scatter(part, "fsdp", scatter_dimension=0, tiled=True, axis_index_groups=alike()).reshape(2, shard, -1)
+        for part in feed_w_parts
+    ]
     pair_held = pair_sum.keep
 
-    def back(hidden_share, scale_share, cotangent, *kept):
+    def back(hidden_share, scale_share, cotangent):
         pair_sum = Job(line_scatter(*pair_held, True))
         own_sum = Job(plane_scatter(*own_parts[:2]))
         out_sum = Job(plane_scatter(*own_parts[2:]))
@@ -931,10 +957,20 @@
         hidden_grad_share = wide(share_of(cotangent)) + norm_back(
             hidden_share, scale_share, grad_share * wide(gain_ffn)
         )
-        ffn_gain_part = jnp.sum(grad_share * hidden_share * scale_share, axis=0)
+        ffn_gain_part = jnp.sum(grad_share * hidden_share * scale_share, axis=0, keepdims=True)
         gather = Job(plane_gather(low(hidden_grad_share)[None]))
         beside(gather, ready=[pair_out_sum])
         beside(gather)
+        return hidden_grad_share, ffn_gain_part, *gather.held, *gather.arrived, *pair_out_sum.keep, *out_sum.keep
+
+    hidden_grad_share, ffn_gain_part, *held = apart(back, hidden_share, scale_share, cotangent)
+    wide_give, held = lax.optimization_barrier((pick(feed_w_sums[0], 1 - side, 0), held))
+    wide_got = swap(wide_give, "fsdp", 1)
+
+    def attention(held, *kept):
+        gather = Job(core_gather(*held[:4]))
+        pair_out_sum = Job(line_scatter(*held[4:8], True))
+        out_sum = Job(chip_scatter(*held[8:]))
         beside(gather, pair_out_sum)
         grad_mine, grad_other = (array[0] for array in gather.value)
         pair_out = Job(pair_swap(pair_out_sum.value))
@@ -944,52 +980,49 @@
             return *attend_weights(low_grad, mixed_split, scale_one, grad_mine, grad_other, proj, tokens, normed), head_gain_part
 
         (results,) = beside(pair_out, out_sum, kernels=[(attended, kept)])
-        return hidden_grad_share, ffn_gain_part, *results, pair_out.value, *out_sum.held, *out_sum.arrived
-
-    (
-        hidden_grad_share, ffn_gain_part, attn_w_part, keep, give, attn_gain_part, head_gain_part, pair_out, *held
-    ) = apart(
-        back, hidden_share, scale_share, cotangent, proj, cosine, sine, query_gain_wide, key_gain_wide, seg_rows, segment_row,
+        return *results, pair_out.value, *out_sum.held, *out_sum.arrived
+
+    attn_w_part, keep, give, attn_gain_part, head_gain_part, pair_out, *held = apart(
+        attention, held, proj, cosine, sine, query_gain_wide, key_gain_wide, seg_rows, segment_row,
         raw, query_rot, key_rot, values, mixed_low,
     )
-    feed_w_sum, attn_w_part = lax.optimization_barrier((feed_w_sum, attn_w_part))
-    attn_w_part, give = lax.optimization_barrier((attn_w_part, give))
+    attn_w_part, give, wide_got, feed_w_sums[1] = lax.optimization_barrier(
+        (attn_w_part, give, wide_got, feed_w_sums[1])
+    )
+    down_got = swap(pick(feed_w_sums[1], 1 - side, 0), "fsdp", 1)
     attn_w_sum = lax.psum_scatter(attn_w_part, "fsdp", scatter_dimension=0, tiled=True)
 
-    def last(keep, give, feed_w_sum, hidden_share, pair_out, hidden_grad_share, tokens, scale_one, *rest):
+    def last(keep, give, hidden_share, pair_out, hidden_grad_share, tokens, scale_one, *rest):
         gain_parts, (_, keep_first, _, keep_second, got_first, got_second) = rest[:4], rest[4:]
         out_sum = Job(line_scatter(*fold_line(keep_first, got_first, keep_second, got_second)))
-        feed_pair = Job(pair_swap(pick(feed_w_sum, 1 - side, 0), 4))
         normed_sum = Job(plane_scatter(keep, give))
-        gains = Job(sum_all(jnp.concatenate([part.reshape(size, -1) for part in gain_parts], axis=1)))
+        gains = Job(sum_all(jnp.concatenate(gain_parts, axis=1)))
         beside(normed_sum, out_sum, gains)
-        beside(normed_sum, feed_pair, gains)
-        beside(normed_sum, feed_pair, gains)
-        finish(feed_pair, gains)
-        gate_w_grad, up_w_grad, down_w_grad = feed_sums(
-            side[None], [pick(feed_w_sum, side, 0)], [feed_pair.value]
-        )
+        beside(normed_sum, gains)
+        beside(normed_sum, gains)
+        finish(gains)
         block_out = low(hidden_share + wide(pair_out) + out_sum.value)
         token_share = wide(share_of(tokens))
         scale_one_share = share_of(scale_one)
         tokens_grad = low(
             hidden_grad_share + norm_back(token_share, scale_one_share, normed_sum.value * wide(gain_attn))
         )
-        gain_sums = pick(gains.value, lax.axis_index("fsdp"), 0)
-        return block_out, tokens_grad, gate_w_grad, up_w_grad, down_w_grad, gain_sums
-
-    block_out, tokens_grad, gate_w_grad, up_w_grad, down_w_grad, gain_sums = apart(
-        last, keep, give, feed_w_sum, hidden_share, pair_out, hidden_grad_share, tokens, scale_one,
-        attn_gain_part, ffn_gain_part, head_gain_part[0], head_gain_part[1], *held,
-    )
-    attn_w_grad, gain_sums = lax.optimization_barrier((attn_w_sum, gain_sums))
+        return block_out, tokens_grad, gains.value
+
+    block_out, tokens_grad, gain_sums = apart(
+        last, keep, give, hidden_share, pair_out, hidden_grad_share, tokens, scale_one,
+        attn_gain_part, ffn_gain_part, head_gain_part[:1], head_gain_part[1:], *held,
+    )
+    gain_sums, down_got = lax.optimization_barrier((gain_sums, down_got))
+    feed_w_grads = feed_sums(side[None], feed_w_sums, (wide_got, down_got))
+    attn_w_grad, (gate_w_grad, up_w_grad, down_w_grad) = lax.optimization_barrier((attn_w_sum, feed_w_grads))
     attn_w_grad = wide(attn_w_grad)
     out_w_grad = attn_w_grad[:, query_cols + 2 * key_cols :]
-    ln1_grad = gain_sums[:shard]
-    ln2_grad = gain_sums[shard : 2 * shard]
-    query_gain_grad = gain_sums[2 * shard : 2 * shard + head_part]
-    key_gain_grad = gain_sums[2 * shard + head_part :]
-
+    ends = [0, model, 2 * model, 2 * model + HD, 2 * model + 2 * HD]
+    ln1_grad, ln2_grad, query_gain_grad, key_gain_grad = (
+        lax.dynamic_slice_in_dim(gain_sums[0, start:end], lax.axis_index("fsdp") * ((end - start) // size), (end - start) // size, 0)
+        for start, end in zip(ends, ends[1:])
+    )
     return (
         block_out,
         tokens_grad,

time: 513 us -> 494 us (0.963)
  waiting for transfers between devices: 240 us -> 211 us
  local copies, waits for them, and re-layouts: 19.7 us -> 32.3 us
    ppermute x65 -> x61, waiting for transfers between devices: 181 us -> 151 us  [beside(): lax.ppermute(array, *move[1:])]
    cond x51 -> x64, local copies, waits for them, and re-layouts: 2.19 us -> 8.99 us
    all_gather x1, waiting for transfers between devices: 48.8 us -> 43.3 us  [per_device(): lax.all_gather(jnp.concatenate([w_query, w_key, w_value, w_out], axis=1),...]
    ppermute x4 -> x6, waiting for transfers between devices: 10.1 us -> 15.6 us  [swap(): return lax.ppermute(array, axis, flip(axis, stride))]
    ppermute x65 -> x61, starting transfers between devices: 62.1 us -> 59.7 us  [beside(): lax.ppermute(array, *move[1:])]
    reduce_scatter x1 -> x2, starting transfers between devices: 12.6 us -> 12.6 us  [per_device(): lax.psum_scatter(part, 'fsdp', scatter_dimension=0, tiled=True, axis_inde...]
  transfers between devices with their start and end apart: 73 -> 72, of which waited for: 38 -> 35; matrix products, arithmetic and copies ran while one was open for 7% -> 8% of each run, Pallas kernels for 20% -> 21%
where the time goes in v4:
time: 494 us; the launch traced here: 493 us
  waiting for transfers between devices  211 us (43%)
  Pallas kernels  129 us (26%)
  starting transfers between devices  81.3 us (16%)
  local copies, waits for them, and re-layouts  32.3 us (7%)
  other arithmetic  24.1 us (5%)
  between operations  14.4 us (3%)
    ppermute x61, waiting for transfers between devices, beside(): lax.ppermute(array, *move[1:])  151 us
    ppermute x61, starting transfers between devices, beside(): lax.ppermute(array, *move[1:])  59.7 us
    all_gather x1, waiting for transfers between devices, per_device(): lax.all_gather(jnp.concatenate([w_query, w_key, w_value, w_out], axis=1),...  43.3 us
    pallas_call x22, Pallas kernels, vmem_call(): pl.pallas_call(kernel, in_specs=[pl.BlockSpec(memory_space=pltpu.SMEM)] +...  36.7 us
    pallas_call x1, Pallas kernels, feed(): pl.pallas_call(feed_kernel, in_specs=[pl.BlockSpec(memory_space=pl.ANY)]...  16.7 us
    ppermute x6, waiting for transfers between devices, swap(): return lax.ppermute(array, axis, flip(axis, stride))  15.6 us
    pallas_call x1, Pallas kernels, feed_weights(): pl.pallas_call(feed_weights_kernel, grid=(model // cols,), in_specs=[pl.B...  15.5 us
    pallas_call x2, Pallas kernels, feed_model(): pl.pallas_call(feed_model_kernel, grid=(rows // tile,), in_specs=[pl.Bloc...  15.3 us
  transfers between devices with their start and end apart: 72, of which 35 were waited for; matrix products, arithmetic and copies ran while one was open for 8% of the time, Pallas kernels for 21%

profile of v4, /device:TPU:0, one launch (start us, length us, event | category | flops | bytes accessed | tf_op | source)
XLA Modules:
  0.0 492.7 jit_solution(9534977307941168356)
XLA Ops:
  7.3 2.9 concatenate.47
  10.2 3.0 collective-permute-start.58
  21.7 2.5 constant_dynamic-slice_fusion.13
  24.6 2.7 collective-permute-start.59
  27.6 2.9 collective-permute-done.59
  30.6 5.5 %prepare.1 = (bf16[1024,2048]{1,0:T(8,128)(2,1)}, f32[1024,1]{1,0:T(8,128)}, s32[1024,1]{1,0:T(8,128)S(1)}) custom-call(bf16[1024,2048]{1,0:T(8,128)(2,1)} %tokens_ref.1, f32[1,2048]{1,0:T(1,128)S(1)} %bitcast.139, s32[1024,1]{1,0:T(8,128)S(1)} %copy.36.seg_ref), custom_call_target="tpu_custom_call" | custom-call | flops 20000000000 | bytes 20000000 | tf_op jit(solution)/shard_map/prepare/pallas_call | solution.py:682
  36.1 43.3 %all-gather.3.cloned.1.call-done.proj_ref = bf16[2048,768]{1,0:T(8,128)(2,1)} async-done(((bf16[512,768]{1,0:T(8,128)(2,1)}), bf16[2048,768]{1,0:T(8,128)(2,1)}) %all-gather.3.cloned.1.call-update) | async-done | bytes 3145744 | tf_op jit(solution)/shard_map/all_gather | solution.py:876
  79.6 11.4 %attend.1 = (f32[1024,384]{1,0:T(8,128)}, bf16[1024,256]{1,0:T(8,128)(2,1)}, bf16[1024,128]{1,0:T(8,128)(2,1)}, bf16[1024,128]{1,0:T(8,128)(2,1)}, bf16[1024,256]{1,0:T(8,128)(2,1)S(1)}) custom-call(bf16[1024,2048]{1,0:T(8,128)(2,1)} %get-tuple-element.528.normed_ref, bf16[2048,768]{1,0:T(8,128)(2,1)} %all-gather.3.cloned.1.call-done.proj_ref, ...), custom_call_target="tpu_custom_call" | custom-call | flops 1000 | bytes 1000 | tf_op jit(solution)/shard_map/attend/pallas_call | solution.py:434
  91.0 3.7 attend_out.1
  94.6 12.7 %collective-permute-done.61 = bf16[512,1152]{1,0:T(8,128)(2,1)} collective-permute-done((bf16[512,1152]{1,0:T(8,128)(2,1)}, bf16[512,1152]{1,0:T(8,128)(2,1)}, u32[]{:S(2)}, u32[]{:S(2)}) %collective-permute-start.61) | collective-permute-done | bytes 1179680 | tf_op jit(solution)/shard_map/ppermute | solution.py:123
  110.9 12.5 %reduce-scatter.4.cloned.1.call-start = ((), (), s32[]{:S(2)}) async-start(), calls=%async_computation.5 | async-start | bytes 4718592 | tf_op jit(solution)/shard_map/reduce_scatter | solution.py:942
  123.4 113.4 %conditional.4 = (f32[128,2048]{1,0:T(8,128)S(1)}, f32[128,1]{0,1:T(1,128)S(1)}, bf16[512,2048]{1,0:T(8,128)(2,1)S(1)}, bf16[512,2048]{1,0:T(8,128)(2,1)}, bf16[...) conditional(s32[]{:T(128)} %convert_element_type.154, () %tuple.86, ...), branch_computations={%region_2.3_spmd, %region_3.5_spmd} | conditional | flops 5777378 | bytes 94937296 | solution.py:74
  124.7 2.7 fold_chip.6
  130.9 11.6 %collective-permute-done.37 = bf16[64,2048]{1,0:T(8,128)(2,1)S(1)} collective-permute-done((bf16[64,2048]{1,0:T(8,128)(2,1)S(1)}, bf16[64,2048]{1,0:T(8,128)(2,1)S(1)}, u32[]{:S(2)}, u32[]{:S(2)}) %collective-permute-start.37) | collective-permute-done | bytes 262176 | tf_op jit(solution)/shard_map/cond/branch_1_fun/ppermute | solution.py:99
  146.9 2.9 collective-permute-done.38
  150.4 7.6 %collective-permute-done.40 = bf16[64,2048]{1,0:T(8,128)(2,1)S(1)} collective-permute-done((bf16[64,2048]{1,0:T(8,128)(2,1)S(1)}, bf16[64,2048]{1,0:T(8,128)(2,1)S(1)}, u32[]{:S(2)}, u32[]{:S(2)}) %collective-permute-start.40) | collective-permute-done | bytes 262176 | tf_op jit(solution)/shard_map/cond/branch_1_fun/ppermute | solution.py:99
  160.7 2.5 collective-permute-start.41
  167.3 6.8 %collective-permute-done.41 = bf16[64,2048]{1,0:T(8,128)(2,1)S(1)} collective-permute-done((bf16[64,2048]{1,0:T(8,128)(2,1)S(1)}, bf16[64,2048]{1,0:T(8,128)(2,1)S(1)}, u32[]{:S(2)}, u32[]{:S(2)}) %collective-permute-start.41) | collective-permute-done | bytes 262176 | tf_op jit(solution)/shard_map/cond/branch_1_fun/ppermute | solution.py:99
  181.1 9.8 %collective-permute-done.46 = bf16[64,2048]{1,0:T(8,128)(2,1)S(1)} collective-permute-done((bf16[64,2048]{1,0:T(8,128)(2,1)S(1)}, bf16[64,2048]{1,0:T(8,128)(2,1)S(1)}, u32[]{:S(2)}, u32[]{:S(2)}) %collective-permute-start.46) | collective-permute-done | bytes 262176 | tf_op jit(solution)/shard_map/cond/branch_1_fun/ppermute | solution.py:99
  195.9 16.0 %collective-permute-done.49.got_first_ref = bf16[1,128,1024]{2,1,0:T(8,128)(2,1)S(1)} collective-permute-done((bf16[1,128,1024]{2,1,0:T(8,128)(2,1)S(1)}, bf16[1,128,1024]{2,1,0:T(8,128)(2,1)S(1)}, u32[]{:S(2)}, u32[]{:S(2)}) %collective-permute-start.49) | collective-permute-done | bytes 262176 | tf_op jit(solution)/shard_map/cond/branch_1_fun/ppermute | solution.py:99
  216.6 12.3 %collective-permute-done.54.got_first_ref = bf16[2,1,128,1024]{3,2,1,0:T(8,128)(2,1)S(1)} collective-permute-done((bf16[2,1,128,1024]{3,2,1,0:T(8,128)(2,1)S(1)}, bf16[2,1,128,1024]{3,2,1,0:T(8,128)(2,1)S(1)}, u32[]{:S(2)}, u32[]{:S(2)}) %collective-permute-start.54) | collective-permute-done | bytes 524320 | tf_op jit(solution)/shard_map/cond/branch_1_fun/ppermute | solution.py:99
  232.2 4.5 collective-permute-done.57
  236.8 16.7 %feed.1 = (bf16[2,512,384]{2,1,0:T(8,128)(2,1)S(1)}, bf16[2,512,384]{2,1,0:T(8,128)(2,1)S(1)}, bf16[2,512,768]{2,1,0:T(8,128)(2,1)S(1)}, bf16[2,512,768]{2,1,0:T(8,128)(2,1)S(1)}) custom-call(bf16[512,2048]{1,0:T(8,128)(2,1)S(1)} %get-tuple-element.563.refs_0_, bf16[512,2048]{1,0:T(8,128)(2,1)} %get-tuple-element.564.refs_1_, ...), custom_call_target="tpu_custom_call" | custom-call | flops 1000 | bytes 1000 | tf_op jit(solution)/shard_map/feed/pallas_call | solution.py:737
  253.5 7.3 %feed_model.2 = (bf16[512,2048]{1,0:T(8,128)(2,1)S(1)}, bf16[512,2048]{1,0:T(8,128)(2,1)S(1)}, bf16[512,2048]{1,0:T(8,128)(2,1)}, bf16[512,2048]{1,0:T(8,128)(2,1)}) custom-call(bf16[2,512,384]{2,1,0:T(8,128)(2,1)S(1)} %get-tuple-element.574.act_ref.refs_11_, bf16[2,512,768]{2,1,0:T(8,128)(2,1)S(1)} %get-tuple-element.572.grad_ref.refs_9_, ...), custom_call_target="tpu_custom_call" | custom-call | flops 1000 | bytes 1000 | tf_op jit(solution)/shard_map/feed_model/pallas_call | solution.py:765
  261.0 7.9 %feed_model.3 = (bf16[512,2048]{1,0:T(8,128)(2,1)}, bf16[512,2048]{1,0:T(8,128)(2,1)}, bf16[512,2048]{1,0:T(8,128)(2,1)}, bf16[512,2048]{1,0:T(8,128)(2,1)}) custom-call(bf16[2,512,384]{2,1,0:T(8,128)(2,1)S(1)} %get-tuple-element.573.act_ref.refs_10_, bf16[2,512,768]{2,1,0:T(8,128)(2,1)S(1)} %get-tuple-element.571.grad_ref.refs_8_, ...), custom_call_target="tpu_custom_call" | custom-call | flops 1000 | bytes 1000 | tf_op jit(solution)/shard_map/feed_model/pallas_call | solution.py:765
  271.0 15.5 %feed_weights.1 = (bf16[2048,768]{1,0:T(8,128)(2,1)}, bf16[2048,384]{1,0:T(8,128)(2,1)}) custom-call(bf16[512,2048]{1,0:T(8,128)(2,1)S(1)} %copy-done.23, bf16[512,2048]{1,0:T(8,128)(2,1)} %get-tuple-element.564.refs_1_, bf16[512,2048]{1,0:T(8,128)(2,1)} %get-tuple-element.565.refs_2_, bf16[512,2048]{1,0:T(8,128)(2,1)} %get-tuple-element.566.refs_3_, ...), custom_call_target="tpu_custom_call" | custom-call | flops 1000 | bytes 1000 | tf_op jit(solution)/shard_map/feed_weights/pallas_call | solution.py:799
  289.0 78.1 %conditional.5 = (f32[128,2048]{1,0:T(8,128)}, f32[1,2048]{1,0:T(1,128)S(1)}, bf16[2,1,128,1024]{3,2,1,0:T(8,128)(2,1)}, bf16[2,1,128,1024]{3,2,1,0:T(8,128)(2,1...) conditional(s32[]{:T(128)} %convert_element_type.154, () %tuple.95, ...), branch_computations={%region_6.7_spmd, %region_7.10_spmd} | conditional | flops 7609465 | bytes 82887264 | solution.py:74
  292.7 5.5 %collective-permute-done.18.got_first_ref = bf16[128,1024]{1,0:T(8,128)(2,1)S(1)} collective-permute-done((bf16[128,1024]{1,0:T(8,128)(2,1)S(1)}, bf16[128,1024]{1,0:T(8,128)(2,1)S(1)}, u32[]{:S(2)}, u32[]{:S(2)}) %collective-permute-start.18) | collective-permute-done | bytes 262176 | tf_op jit(solution)/shard_map/cond/branch_1_fun/ppermute | solution.py:99
  308.8 3.0 fold_chip.8
  311.7 8.8 %collective-permute-done.23 = bf16[64,2048]{1,0:T(8,128)(2,1)S(1)} collective-permute-done((bf16[64,2048]{1,0:T(8,128)(2,1)S(1)}, bf16[64,2048]{1,0:T(8,128)(2,1)S(1)}, u32[]{:S(2)}, u32[]{:S(2)}) %collective-permute-start.23) | collective-permute-done | bytes 262176 | tf_op jit(solution)/shard_map/cond/branch_1_fun/ppermute | solution.py:99
  329.4 3.5 fold_chip.9
  332.8 5.2 %collective-permute-done.26 = bf16[64,2048]{1,0:T(8,128)(2,1)} collective-permute-done((bf16[64,2048]{1,0:T(8,128)(2,1)}, bf16[64,2048]{1,0:T(8,128)(2,1)}, u32[]{:S(2)}, u32[]{:S(2)}) %collective-permute-start.26) | collective-permute-done | bytes 262176 | tf_op jit(solution)/shard_map/cond/branch_1_fun/ppermute | solution.py:99
  338.0 3.5 collective-permute-done.27
  344.1 2.7 convert_bitcast_fusion
  358.4 7.5 %collective-permute-done.33 = bf16[2,1,128,1024]{3,2,1,0:T(8,128)(2,1)} collective-permute-done((bf16[2,1,128,1024]{3,2,1,0:T(8,128)(2,1)}, bf16[2,1,128,1024]{3,2,1,0:T(8,128)(2,1)}, u32[]{:S(2)}, u32[]{:S(2)}) %collective-permute-start.33) | collective-permute-done | bytes 524320 | tf_op jit(solution)/shard_map/cond/branch_1_fun/ppermute | solution.py:99
  369.2 2.5 collective-permute-start.65
  371.7 44.1 %conditional.6 = (bf16[2048,768]{1,0:T(8,128)(2,1)}, bf16[512,2048]{1,0:T(8,128)(2,1)}, bf16[512,2048]{1,0:T(8,128)(2,1)}, f32[1,2048]{1,0:T(1,128)}, f32[2,128]...) conditional(s32[]{:T(128)} %convert_element_type.154, () %tuple.85, ...), branch_computations={%region_10.11_spmd, %region_11.12_spmd} | conditional | flops 4030 | bytes 69230728 | solution.py:74
  376.1 6.7 %collective-permute-done.13.got_first_ref = bf16[128,1024]{1,0:T(8,128)(2,1)S(1)} collective-permute-done((bf16[128,1024]{1,0:T(8,128)(2,1)}, bf16[128,1024]{1,0:T(8,128)(2,1)S(1)}, u32[]{:S(2)}, u32[]{:S(2)}) %collective-permute-start.13) | collective-permute-done | bytes 262176 | tf_op jit(solution)/shard_map/cond/branch_1_fun/ppermute | solution.py:99
  386.2 12.9 %attend_back.1 = (bf16[1024,512]{1,0:T(8,128)(2,1)S(1)}, bf16[2,512,256]{2,1,0:T(8,128)(2,1)S(1)}, f32[2,128]{1,0:T(2,128)}) custom-call(bf16[512,2048]{1,0:T(8,128)(2,1)S(1)} %bitcast.129, bf16[512,2048]{1,0:T(8,128)(2,1)} %bitcast.37.grad_other_ref, bf16[2048,768]{1,0:T(8,128)(2,1)} %get-tuple-element.306.out_proj_ref.proj_ref, ...), custom_call_target="tpu_custom_call" | custom-call | flops 1000 | bytes 1000 | tf_op jit(solution)/shard_map/cond/branch_1_fun/attend_back/pallas_call | solution.py:583
  399.1 9.5 %attend_weights.1 = (bf16[2048,768]{1,0:T(8,128)(2,1)}, bf16[512,2048]{1,0:T(8,128)(2,1)}, bf16[512,2048]{1,0:T(8,128)(2,1)}, f32[1,2048]{1,0:T(1,128)}) custom-call(s32[3]{0:T(128)S(1)} %pad_add_fusion.2.position_ref, bf16[1024,512]{1,0:T(8,128)(2,1)S(1)} %get-tuple-element.318.low_ref, bf16[2,512,256]{2,1,0:T(8,128)(2,1)S(1)} %get-tuple-element.319.mixed_ref, ...), custom_call_target="tpu_custom_call" | custom-call | flops 1000 | bytes 1000 | tf_op jit(solution)/shard_map/cond/branch_1_fun/attend_weights/pallas_call | solution.py:636
  408.7 6.3 %collective-permute-done.15 = bf16[128,2048]{1,0:T(8,128)(2,1)} collective-permute-done((bf16[128,2048]{1,0:T(8,128)(2,1)S(1)}, bf16[128,2048]{1,0:T(8,128)(2,1)}, u32[]{:S(2)}, u32[]{:S(2)}) %collective-permute-start.15) | collective-permute-done | bytes 524320 | tf_op jit(solution)/shard_map/cond/branch_1_fun/ppermute | solution.py:99
  418.0 59.7 %conditional.7 = (bf16[128,2048]{1,0:T(8,128)(2,1)}, bf16[128,2048]{1,0:T(8,128)(2,1)}, f32[1,4352]{1,0:T(1,128)S(1)}) conditional(s32[]{:T(128)} %convert_element_type.154, () %tuple.84, (bf16[128,2048]{1,0:T(8,128)(2,1)}, f32[128,2048]{1,0:T(8,128)}, bf16[2,128,1024]{2,1,0:T(8,128)(2,1)}, bf16[2,128,1024]{2,1,0:T(8,128)(2,1)}, ...), branch_computations={%region_13.14_spmd, %region_14.16_spmd} | conditional | flops 6580697 | bytes 50583148 | solution.py:74
  429.1 4.5 collective-permute-done.1
  435.6 3.0 fold_chip.10
  444.1 10.0 %collective-permute-done.6 = f32[1,4352]{1,0:T(1,128)S(1)} collective-permute-done((f32[1,4352]{1,0:T(1,128)}, f32[1,4352]{1,0:T(1,128)S(1)}, u32[]{:S(2)}, u32[]{:S(2)}) %collective-permute-start.6) | collective-permute-done | bytes 17440 | tf_op jit(solution)/shard_map/cond/branch_1_fun/ppermute | solution.py:99
  462.3 4.1 collective-permute-done.9
  469.9 3.1 collective-permute-done.10
  474.3 3.2 fusion.5
  (332 shorter events, 145.0 us)
Async XLA Ops:
  7.2 72.1 %all-gather.3.cloned.1.call-start = ((), (), s32[]{:S(2)}) async-start(), calls=%async_computation.3 | async-start | bytes 3932160 | tf_op jit(solution)/shard_map/all_gather | solution.py:876
  10.2 14.4 %collective-permute-start.58 = (bf16[1,1088]{1,0:T(2,128)(2,1)S(1)}, bf16[1,1088]{1,0:T(2,128)(2,1)S(1)}, u32[]{:S(2)}, u32[]{:S(2)}) collective-permute-start(bf16[1,1088]{1,0:T(2,128)(2,1)S(1)} %broadcast_in_dim.57), channel_id=1, source_target_pairs={{0,8},{8,0},{16,24},{24,16},{1,9},{9,1},{17,25},{25,17},{2,10},{10... | collective-permute-start | bytes 6536 | tf_op jit(solution)/shard_map/ppermute | solution.py:123
  15.3 221.4 %all-gather.5.cloned.1.call-start = ((), (), s32[]{:S(2)}) async-start(), calls=%async_computation.4 | async-start | bytes 7077888 | tf_op jit(solution)/shard_map/all_gather | solution.py:909
  79.4 28.0 %collective-permute-start.61 = (bf16[512,1152]{1,0:T(8,128)(2,1)}, bf16[512,1152]{1,0:T(8,128)(2,1)}, u32[]{:S(2)}, u32[]{:S(2)}) collective-permute-start(bf16[512,1152]{1,0:T(8,128)(2,1)} %pad_maximum_fusion.2), channel_id=1, source_target_pairs={{0,8},{8,0},{16,24},{24,16},{1,9},{9,1},{17,25},{25,17},{2,10},{10... | collective-permute-start | bytes 3538952 | tf_op jit(solution)/shard_map/ppermute | solution.py:123
  94.6 16.2 %collective-permute-start.60 = (bf16[512,2048]{1,0:T(8,128)(2,1)S(1)}, bf16[512,2048]{1,0:T(8,128)(2,1)}, u32[]{:S(2)}, u32[]{:S(2)}) collective-permute-start(bf16[512,2048]{1,0:T(8,128)(2,1)S(1)} %get-tuple-element.532), channel_id=1, source_target_pairs={{0,1},{1,0},{2,3},{3,2},{4,5},{5,4},{6,7},{7,6},{8,9},{9,8},{10,11... | collective-permute-start | bytes 6291464 | tf_op jit(solution)/shard_map/ppermute | solution.py:123
  110.9 256.3 %reduce-scatter.4.cloned.1.call-start = ((), (), s32[]{:S(2)}) async-start(), calls=%async_computation.5 | async-start | bytes 4718592 | tf_op jit(solution)/shard_map/reduce_scatter | solution.py:942
  127.4 15.1 %collective-permute-start.35 = (bf16[2,128,1024]{2,1,0:T(8,128)(2,1)S(1)}, bf16[2,128,1024]{2,1,0:T(8,128)(2,1)S(1)}, u32[]{:S(2)}, u32[]{:S(2)}) collective-permute-start(bf16[2,128,1024]{2,1,0:T(8,128)(2,1)S(1)} %get-tuple-element.146), channel_id=1, source_target_pairs={{0,2},{2,0},{4,6},{6,4},{1,3},{3,1},{5,7},{7,5},{8,10},{10,8},{12,... | collective-permute-start | bytes 1572872 | tf_op jit(solution)/shard_map/cond/branch_1_fun/ppermute | solution.py:99
  129.0 13.5 %collective-permute-start.36 = (bf16[2,128,1024]{2,1,0:T(8,128)(2,1)S(1)}, bf16[2,128,1024]{2,1,0:T(8,128)(2,1)S(1)}, u32[]{:S(2)}, u32[]{:S(2)}) collective-permute-start(bf16[2,128,1024]{2,1,0:T(8,128)(2,1)S(1)} %get-tuple-element.147), channel_id=1, source_target_pairs={{0,4},{4,0},{2,6},{6,2},{1,5},{5,1},{3,7},{7,3},{8,12},{12,8},{10,... | collective-permute-start | bytes 1572872 | tf_op jit(solution)/shard_map/cond/branch_1_fun/ppermute | solution.py:99
  130.6 11.9 %collective-permute-start.37 = (bf16[64,2048]{1,0:T(8,128)(2,1)S(1)}, bf16[64,2048]{1,0:T(8,128)(2,1)S(1)}, u32[]{:S(2)}, u32[]{:S(2)}) collective-permute-start(bf16[64,2048]{1,0:T(8,128)(2,1)S(1)} %get-tuple-element.148), channel_id=1, source_target_pairs={{0,8},{8,0},{16,24},{24,16},{1,9},{9,1},{17,25},{25,17},{2,10},{10... | collective-permute-start | bytes 786440 | tf_op jit(solution)/shard_map/cond/branch_1_fun/ppermute | solution.py:99
  144.5 13.5 %collective-permute-start.40 = (bf16[64,2048]{1,0:T(8,128)(2,1)S(1)}, bf16[64,2048]{1,0:T(8,128)(2,1)S(1)}, u32[]{:S(2)}, u32[]{:S(2)}) collective-permute-start(bf16[64,2048]{1,0:T(8,128)(2,1)S(1)} %get-tuple-element.157), channel_id=1, source_target_pairs={{0,8},{8,0},{16,24},{24,16},{1,9},{9,1},{17,25},{25,17},{2,10},{10... | collective-permute-start | bytes 786440 | tf_op jit(solution)/shard_map/cond/branch_1_fun/ppermute | solution.py:99
  160.7 13.4 %collective-permute-start.41 = (bf16[64,2048]{1,0:T(8,128)(2,1)S(1)}, bf16[64,2048]{1,0:T(8,128)(2,1)S(1)}, u32[]{:S(2)}, u32[]{:S(2)}) collective-permute-start(bf16[64,2048]{1,0:T(8,128)(2,1)S(1)} %get-tuple-element.164), channel_id=1, source_target_pairs={{0,8},{8,0},{16,24},{24,16},{1,9},{9,1},{17,25},{25,17},{2,10},{10... | collective-permute-start | bytes 786440 | tf_op jit(solution)/shard_map/cond/branch_1_fun/ppermute | solution.py:99
  163.2 10.9 %collective-permute-start.42 = (bf16[1,128,1024]{2,1,0:T(8,128)(2,1)S(1)}, bf16[1,128,1024]{2,1,0:T(8,128)(2,1)S(1)}, u32[]{:S(2)}, u32[]{:S(2)}) collective-permute-start(bf16[1,128,1024]{2,1,0:T(8,128)(2,1)S(1)} %get-tuple-element.165.first_ref), channel_id=1, source_target_pairs={{0,4},{4,0},{2,6},{6,2},{1,5},{5,1},{3,7},{7,3},{8,12},{12,8},{10,... | collective-permute-start | bytes 786440 | tf_op jit(solution)/shard_map/cond/branch_1_fun/ppermute | solution.py:99
  176.7 14.2 %collective-permute-start.47 = (bf16[2,1,128,1024]{3,2,1,0:T(8,128)(2,1)S(1)}, bf16[2,1,128,1024]{3,2,1,0:T(8,128)(2,1)S(1)}, u32[]{:S(2)}, u32[]{:S(2)}) collective-permute-start(bf16[2,1,128,1024]{3,2,1,0:T(8,128)(2,1)S(1)} %get-tuple-element.174.first_ref), channel_id=1, source_target_pairs={{0,2},{2,0},{4,6},{6,4},{1,3},{3,1},{5,7},{7,5},{8,10},{10,8},{12,... | collective-permute-start | bytes 1572872 | tf_op jit(solution)/shard_map/cond/branch_1_fun/ppermute | solution.py:99
  178.3 12.6 %collective-permute-start.48 = (bf16[2,1,128,1024]{3,2,1,0:T(8,128)(2,1)S(1)}, bf16[2,1,128,1024]{3,2,1,0:T(8,128)(2,1)S(1)}, u32[]{:S(2)}, u32[]{:S(2)}) collective-permute-start(bf16[2,1,128,1024]{3,2,1,0:T(8,128)(2,1)S(1)} %get-tuple-element.175.second_ref), channel_id=1, source_target_pairs={{0,4},{4,0},{2,6},{6,2},{1,5},{5,1},{3,7},{7,3},{8,12},{12,8},{10,... | collective-permute-start | bytes 1572872 | tf_op jit(solution)/shard_map/cond/branch_1_fun/ppermute | solution.py:99
  178.3 12.6 %collective-permute-start.46 = (bf16[64,2048]{1,0:T(8,128)(2,1)S(1)}, bf16[64,2048]{1,0:T(8,128)(2,1)S(1)}, u32[]{:S(2)}, u32[]{:S(2)}) collective-permute-start(bf16[64,2048]{1,0:T(8,128)(2,1)S(1)} %get-tuple-element.173), channel_id=1, source_target_pairs={{0,8},{8,0},{16,24},{24,16},{1,9},{9,1},{17,25},{25,17},{2,10},{10... | collective-permute-start | bytes 786440 | tf_op jit(solution)/shard_map/cond/branch_1_fun/ppermute | solution.py:99
  191.7 20.2 %collective-permute-start.53 = (bf16[1,512,2048]{2,1,0:T(8,128)(2,1)S(1)}, bf16[1,512,2048]{2,1,0:T(8,128)(2,1)}, u32[]{:S(2)}, u32[]{:S(2)}) collective-permute-start(bf16[1,512,2048]{2,1,0:T(8,128)(2,1)S(1)} %bitcast.146), channel_id=1, source_target_pairs={{0,1},{1,0},{2,3},{3,2},{4,5},{5,4},{6,7},{7,6},{8,9},{9,8},{10,11... | collective-permute-start | bytes 6291464 | tf_op jit(solution)/shard_map/cond/branch_1_fun/ppermute | solution.py:99
  191.8 20.2 %collective-permute-start.51 = (bf16[2,1,128,1024]{3,2,1,0:T(8,128)(2,1)S(1)}, bf16[2,1,128,1024]{3,2,1,0:T(8,128)(2,1)S(1)}, u32[]{:S(2)}, u32[]{:S(2)}) collective-permute-start(bf16[2,1,128,1024]{3,2,1,0:T(8,128)(2,1)S(1)} %get-tuple-element.186.first_ref), channel_id=1, source_target_pairs={{0,2},{2,0},{4,6},{6,4},{1,3},{3,1},{5,7},{7,5},{8,10},{10,8},{12,... | collective-permute-start | bytes 1572872 | tf_op jit(solution)/shard_map/cond/branch_1_fun/ppermute | solution.py:99
  192.3 19.6 %collective-permute-start.52 = (bf16[2,1,128,1024]{3,2,1,0:T(8,128)(2,1)S(1)}, bf16[2,1,128,1024]{3,2,1,0:T(8,128)(2,1)S(1)}, u32[]{:S(2)}, u32[]{:S(2)}) collective-permute-start(bf16[2,1,128,1024]{3,2,1,0:T(8,128)(2,1)S(1)} %get-tuple-element.187.second_ref), channel_id=1, source_target_pairs={{0,4},{4,0},{2,6},{6,2},{1,5},{5,1},{3,7},{7,3},{8,12},{12,8},{10,... | collective-permute-start | bytes 1572872 | tf_op jit(solution)/shard_map/cond/branch_1_fun/ppermute | solution.py:99
  192.8 19.1 %collective-permute-start.49 = (bf16[1,128,1024]{2,1,0:T(8,128)(2,1)S(1)}, bf16[1,128,1024]{2,1,0:T(8,128)(2,1)S(1)}, u32[]{:S(2)}, u32[]{:S(2)}) collective-permute-start(bf16[1,128,1024]{2,1,0:T(8,128)(2,1)S(1)} %get-tuple-element.184.first_ref), channel_id=1, source_target_pairs={{0,4},{4,0},{2,6},{6,2},{1,5},{5,1},{3,7},{7,3},{8,12},{12,8},{10,... | collective-permute-start | bytes 786440 | tf_op jit(solution)/shard_map/cond/branch_1_fun/ppermute | solution.py:99
  194.4 17.6 %collective-permute-start.50 = (bf16[1,128,1024]{2,1,0:T(8,128)(2,1)S(1)}, bf16[1,128,1024]{2,1,0:T(8,128)(2,1)S(1)}, u32[]{:S(2)}, u32[]{:S(2)}) collective-permute-start(bf16[1,128,1024]{2,1,0:T(8,128)(2,1)S(1)} %get-tuple-element.185.second_ref), channel_id=1, source_target_pairs={{0,2},{2,0},{4,6},{6,4},{1,3},{3,1},{5,7},{7,5},{8,10},{10,8},{12,... | collective-permute-start | bytes 786440 | tf_op jit(solution)/shard_map/cond/branch_1_fun/ppermute | solution.py:99
  214.6 15.6 %collective-permute-start.56 = (bf16[1,512,2048]{2,1,0:T(8,128)(2,1)}, bf16[1,512,2048]{2,1,0:T(8,128)(2,1)}, u32[]{:S(2)}, u32[]{:S(2)}) collective-permute-start(bf16[1,512,2048]{2,1,0:T(8,128)(2,1)} %bitcast.12), channel_id=1, source_target_pairs={{0,1},{1,0},{2,3},{3,2},{4,5},{5,4},{6,7},{7,6},{8,9},{9,8},{10,11... | collective-permute-start | bytes 6291464 | tf_op jit(solution)/shard_map/cond/branch_1_fun/ppermute | solution.py:99
  214.6 14.3 %collective-permute-start.54 = (bf16[2,1,128,1024]{3,2,1,0:T(8,128)(2,1)S(1)}, bf16[2,1,128,1024]{3,2,1,0:T(8,128)(2,1)S(1)}, u32[]{:S(2)}, u32[]{:S(2)}) collective-permute-start(bf16[2,1,128,1024]{3,2,1,0:T(8,128)(2,1)S(1)} %get-tuple-element.196.first_ref), channel_id=1, source_target_pairs={{0,2},{2,0},{4,6},{6,4},{1,3},{3,1},{5,7},{7,5},{8,10},{10,8},{12,... | collective-permute-start | bytes 1572872 | tf_op jit(solution)/shard_map/cond/branch_1_fun/ppermute | solution.py:99
  216.2 14.0 %collective-permute-start.55 = (bf16[2,1,128,1024]{3,2,1,0:T(8,128)(2,1)S(1)}, bf16[2,1,128,1024]{3,2,1,0:T(8,128)(2,1)S(1)}, u32[]{:S(2)}, u32[]{:S(2)}) collective-permute-start(bf16[2,1,128,1024]{3,2,1,0:T(8,128)(2,1)S(1)} %get-tuple-element.197.second_ref), channel_id=1, source_target_pairs={{0,4},{4,0},{2,6},{6,2},{1,5},{5,1},{3,7},{7,3},{8,12},{12,8},{10,... | collective-permute-start | bytes 1572872 | tf_op jit(solution)/shard_map/cond/branch_1_fun/ppermute | solution.py:99
  270.0 16.5 %collective-permute-start.63 = (bf16[2,128,1024]{2,1,0:T(8,128)(2,1)S(1)}, bf16[2,128,1024]{2,1,0:T(8,128)(2,1)S(1)}, u32[]{:S(2)}, u32[]{:S(2)}) collective-permute-start(bf16[2,128,1024]{2,1,0:T(8,128)(2,1)S(1)} %get-tuple-element.561), channel_id=1, source_target_pairs={{0,2},{2,0},{4,6},{6,4},{1,3},{3,1},{5,7},{7,5},{8,10},{10,8},{12,... | collective-permute-start | bytes 1572872 | tf_op jit(solution)/shard_map/ppermute | solution.py:99
  270.5 16.0 %collective-permute-start.64 = (bf16[2,128,1024]{2,1,0:T(8,128)(2,1)S(1)}, bf16[2,128,1024]{2,1,0:T(8,128)(2,1)S(1)}, u32[]{:S(2)}, u32[]{:S(2)}) collective-permute-start(bf16[2,128,1024]{2,1,0:T(8,128)(2,1)S(1)} %get-tuple-element.562), channel_id=1, source_target_pairs={{0,4},{4,0},{2,6},{6,2},{1,5},{5,1},{3,7},{7,3},{8,12},{12,8},{10,... | collective-permute-start | bytes 1572872 | tf_op jit(solution)/shard_map/ppermute | solution.py:99
  286.5 129.3 %reduce-scatter.6.cloned.1.call-start = ((), (), s32[]{:S(2)}) async-start(), calls=%async_computation.6 | async-start | bytes 2359296 | tf_op jit(solution)/shard_map/reduce_scatter | solution.py:942
  287.1 195.9 %reduce-scatter.8.cloned.1.call-start = ((), (), s32[]{:S(2)}) async-start(), calls=%async_computation.7 | async-start | bytes 3932160 | tf_op jit(solution)/shard_map/reduce_scatter | solution.py:993
  289.0 10.7 %collective-permute-start.20 = (bf16[512,2048]{1,0:T(8,128)(2,1)}, bf16[512,2048]{1,0:T(8,128)(2,1)}, u32[]{:S(2)}, u32[]{:S(2)}) collective-permute-start(bf16[512,2048]{1,0:T(8,128)(2,1)} %get-tuple-element.213), channel_id=1, source_target_pairs={{0,1},{1,0},{2,3},{3,2},{4,5},{5,4},{6,7},{7,6},{8,9},{9,8},{10,11... | collective-permute-start | bytes 6291464 | tf_op jit(solution)/shard_map/cond/branch_1_fun/ppermute | solution.py:99
  289.0 10.7 %collective-permute-start.21 = (bf16[512,2048]{1,0:T(8,128)(2,1)}, bf16[512,2048]{1,0:T(8,128)(2,1)}, u32[]{:S(2)}, u32[]{:S(2)}) collective-permute-start(bf16[512,2048]{1,0:T(8,128)(2,1)} %get-tuple-element.214), channel_id=1, source_target_pairs={{0,1},{1,0},{2,3},{3,2},{4,5},{5,4},{6,7},{7,6},{8,9},{9,8},{10,11... | collective-permute-start | bytes 6291464 | tf_op jit(solution)/shard_map/cond/branch_1_fun/ppermute | solution.py:99
  303.3 17.2 %collective-permute-start.24 = (bf16[2,128,1024]{2,1,0:T(8,128)(2,1)S(1)}, bf16[2,128,1024]{2,1,0:T(8,128)(2,1)S(1)}, u32[]{:S(2)}, u32[]{:S(2)}) collective-permute-start(bf16[2,128,1024]{2,1,0:T(8,128)(2,1)S(1)} %get-tuple-element.225), channel_id=1, source_target_pairs={{0,2},{2,0},{4,6},{6,4},{1,3},{3,1},{5,7},{7,5},{8,10},{10,8},{12,... | collective-permute-start | bytes 1572872 | tf_op jit(solution)/shard_map/cond/branch_1_fun/ppermute | solution.py:99
  305.0 15.6 %collective-permute-start.25 = (bf16[2,128,1024]{2,1,0:T(8,128)(2,1)S(1)}, bf16[2,128,1024]{2,1,0:T(8,128)(2,1)S(1)}, u32[]{:S(2)}, u32[]{:S(2)}) collective-permute-start(bf16[2,128,1024]{2,1,0:T(8,128)(2,1)S(1)} %get-tuple-element.226), channel_id=1, source_target_pairs={{0,4},{4,0},{2,6},{6,2},{1,5},{5,1},{3,7},{7,3},{8,12},{12,8},{10,... | collective-permute-start | bytes 1572872 | tf_op jit(solution)/shard_map/cond/branch_1_fun/ppermute | solution.py:99
  306.3 14.3 %collective-permute-start.23 = (bf16[64,2048]{1,0:T(8,128)(2,1)S(1)}, bf16[64,2048]{1,0:T(8,128)(2,1)S(1)}, u32[]{:S(2)}, u32[]{:S(2)}) collective-permute-start(bf16[64,2048]{1,0:T(8,128)(2,1)S(1)} %get-tuple-element.224), channel_id=1, source_target_pairs={{0,8},{8,0},{16,24},{24,16},{1,9},{9,1},{17,25},{25,17},{2,10},{10... | collective-permute-start | bytes 786440 | tf_op jit(solution)/shard_map/cond/branch_1_fun/ppermute | solution.py:99
  322.8 18.7 %collective-permute-start.29 = (bf16[2,128,1024]{2,1,0:T(8,128)(2,1)}, bf16[2,128,1024]{2,1,0:T(8,128)(2,1)}, u32[]{:S(2)}, u32[]{:S(2)}) collective-permute-start(bf16[2,128,1024]{2,1,0:T(8,128)(2,1)} %get-tuple-element.242), channel_id=1, source_target_pairs={{0,2},{2,0},{4,6},{6,4},{1,3},{3,1},{5,7},{7,5},{8,10},{10,8},{12,... | collective-permute-start | bytes 1572872 | tf_op jit(solution)/shard_map/cond/branch_1_fun/ppermute | solution.py:99
  323.3 18.2 %collective-permute-start.30 = (bf16[2,128,1024]{2,1,0:T(8,128)(2,1)}, bf16[2,128,1024]{2,1,0:T(8,128)(2,1)}, u32[]{:S(2)}, u32[]{:S(2)}) collective-permute-start(bf16[2,128,1024]{2,1,0:T(8,128)(2,1)} %get-tuple-element.243), channel_id=1, source_target_pairs={{0,4},{4,0},{2,6},{6,2},{1,5},{5,1},{3,7},{7,3},{8,12},{12,8},{10,... | collective-permute-start | bytes 1572872 | tf_op jit(solution)/shard_map/cond/branch_1_fun/ppermute | solution.py:99
  323.9 14.1 %collective-permute-start.26 = (bf16[64,2048]{1,0:T(8,128)(2,1)}, bf16[64,2048]{1,0:T(8,128)(2,1)}, u32[]{:S(2)}, u32[]{:S(2)}) collective-permute-start(bf16[64,2048]{1,0:T(8,128)(2,1)} %get-tuple-element.239), channel_id=1, source_target_pairs={{0,8},{8,0},{16,24},{24,16},{1,9},{9,1},{17,25},{25,17},{2,10},{10... | collective-permute-start | bytes 786440 | tf_op jit(solution)/shard_map/cond/branch_1_fun/ppermute | solution.py:99
  326.4 15.1 %collective-permute-start.27 = (bf16[128,1024]{1,0:T(8,128)(2,1)}, bf16[128,1024]{1,0:T(8,128)(2,1)}, u32[]{:S(2)}, u32[]{:S(2)}) collective-permute-start(bf16[128,1024]{1,0:T(8,128)(2,1)} %get-tuple-element.240), channel_id=1, source_target_pairs={{0,4},{4,0},{2,6},{6,2},{1,5},{5,1},{3,7},{7,3},{8,12},{12,8},{10,... | collective-permute-start | bytes 786440 | tf_op jit(solution)/shard_map/cond/branch_1_fun/ppermute | solution.py:99
  327.8 13.7 %collective-permute-start.28 = (bf16[128,1024]{1,0:T(8,128)(2,1)}, bf16[128,1024]{1,0:T(8,128)(2,1)}, u32[]{:S(2)}, u32[]{:S(2)}) collective-permute-start(bf16[128,1024]{1,0:T(8,128)(2,1)} %get-tuple-element.241), channel_id=1, source_target_pairs={{0,2},{2,0},{4,6},{6,4},{1,3},{3,1},{5,7},{7,5},{8,10},{10,8},{12,... | collective-permute-start | bytes 786440 | tf_op jit(solution)/shard_map/cond/branch_1_fun/ppermute | solution.py:99
  355.2 10.7 %collective-permute-start.33 = (bf16[2,1,128,1024]{3,2,1,0:T(8,128)(2,1)}, bf16[2,1,128,1024]{3,2,1,0:T(8,128)(2,1)}, u32[]{:S(2)}, u32[]{:S(2)}) collective-permute-start(bf16[2,1,128,1024]{3,2,1,0:T(8,128)(2,1)} %get-tuple-element.267), channel_id=1, source_target_pairs={{0,2},{2,0},{4,6},{6,4},{1,3},{3,1},{5,7},{7,5},{8,10},{10,8},{12,... | collective-permute-start | bytes 1572872 | tf_op jit(solution)/shard_map/cond/branch_1_fun/ppermute | solution.py:99
  356.7 10.4 %collective-permute-start.34 = (bf16[2,1,128,1024]{3,2,1,0:T(8,128)(2,1)}, bf16[2,1,128,1024]{3,2,1,0:T(8,128)(2,1)}, u32[]{:S(2)}, u32[]{:S(2)}) collective-permute-start(bf16[2,1,128,1024]{3,2,1,0:T(8,128)(2,1)} %get-tuple-element.268), channel_id=1, source_target_pairs={{0,4},{4,0},{2,6},{6,2},{1,5},{5,1},{3,7},{7,3},{8,12},{12,8},{10,... | collective-permute-start | bytes 1572872 | tf_op jit(solution)/shard_map/cond/branch_1_fun/ppermute | solution.py:99
  369.2 46.6 %collective-permute-start.65 = (bf16[512,768]{1,0:T(8,128)(2,1)}, bf16[512,768]{1,0:T(8,128)(2,1)S(1)}, u32[]{:S(2)}, u32[]{:S(2)}) collective-permute-start(bf16[512,768]{1,0:T(8,128)(2,1)} %dynamic-slice_bitcast_fusion), channel_id=1, source_target_pairs={{0,8},{8,0},{16,24},{24,16},{1,9},{9,1},{17,25},{25,17},{2,10},{10... | collective-permute-start | bytes 2359304 | tf_op jit(solution)/shard_map/ppermute | solution.py:123
  373.8 10.4 %collective-permute-start.12 = (bf16[1,512,2048]{2,1,0:T(8,128)(2,1)S(1)}, bf16[1,512,2048]{2,1,0:T(8,128)(2,1)}, u32[]{:S(2)}, u32[]{:S(2)}) collective-permute-start(bf16[1,512,2048]{2,1,0:T(8,128)(2,1)S(1)} %bitcast.128), channel_id=1, source_target_pairs={{0,1},{1,0},{2,3},{3,2},{4,5},{5,4},{6,7},{7,6},{8,9},{9,8},{10,11... | collective-permute-start | bytes 6291464 | tf_op jit(solution)/shard_map/cond/branch_1_fun/ppermute | solution.py:99
  385.3 29.7 %collective-permute-start.15 = (bf16[128,2048]{1,0:T(8,128)(2,1)S(1)}, bf16[128,2048]{1,0:T(8,128)(2,1)}, u32[]{:S(2)}, u32[]{:S(2)}) collective-permute-start(bf16[128,2048]{1,0:T(8,128)(2,1)S(1)} %fold_end.3), channel_id=1, source_target_pairs={{0,8},{8,0},{16,24},{24,16},{1,9},{9,1},{17,25},{25,17},{2,10},{10... | collective-permute-start | bytes 1572872 | tf_op jit(solution)/shard_map/cond/branch_1_fun/ppermute | solution.py:99
  385.4 29.6 %collective-permute-start.16 = (bf16[2,128,1024]{2,1,0:T(8,128)(2,1)}, bf16[2,128,1024]{2,1,0:T(8,128)(2,1)}, u32[]{:S(2)}, u32[]{:S(2)}) collective-permute-start(bf16[2,128,1024]{2,1,0:T(8,128)(2,1)} %get-tuple-element.303), channel_id=1, source_target_pairs={{0,2},{2,0},{4,6},{6,4},{1,3},{3,1},{5,7},{7,5},{8,10},{10,8},{12,... | collective-permute-start | bytes 1572872 | tf_op jit(solution)/shard_map/cond/branch_1_fun/ppermute | solution.py:99
  385.8 29.2 %collective-permute-start.17 = (bf16[2,128,1024]{2,1,0:T(8,128)(2,1)}, bf16[2,128,1024]{2,1,0:T(8,128)(2,1)}, u32[]{:S(2)}, u32[]{:S(2)}) collective-permute-start(bf16[2,128,1024]{2,1,0:T(8,128)(2,1)} %get-tuple-element.304), channel_id=1, source_target_pairs={{0,4},{4,0},{2,6},{6,2},{1,5},{5,1},{3,7},{7,3},{8,12},{12,8},{10,... | collective-permute-start | bytes 1572872 | tf_op jit(solution)/shard_map/cond/branch_1_fun/ppermute | solution.py:99
  417.7 60.0 %collective-permute-start.66 = (bf16[512,384]{1,0:T(8,128)(2,1)}, bf16[512,384]{1,0:T(8,128)(2,1)S(1)}, u32[]{:S(2)}, u32[]{:S(2)}) collective-permute-start(bf16[512,384]{1,0:T(8,128)(2,1)} %dynamic-slice_bitcast_fusion.1), channel_id=1, source_target_pairs={{0,8},{8,0},{16,24},{24,16},{1,9},{9,1},{17,25},{25,17},{2,10},{10... | collective-permute-start | bytes 1179656 | tf_op jit(solution)/shard_map/ppermute | solution.py:123
  440.2 13.9 %collective-permute-start.4 = (bf16[2,128,1024]{2,1,0:T(8,128)(2,1)}, bf16[2,128,1024]{2,1,0:T(8,128)(2,1)}, u32[]{:S(2)}, u32[]{:S(2)}) collective-permute-start(bf16[2,128,1024]{2,1,0:T(8,128)(2,1)} %get-tuple-element.368), channel_id=1, source_target_pairs={{0,2},{2,0},{4,6},{6,4},{1,3},{3,1},{5,7},{7,5},{8,10},{10,8},{12,... | collective-permute-start | bytes 1572872 | tf_op jit(solution)/shard_map/cond/branch_1_fun/ppermute | solution.py:99
  441.7 13.4 %collective-permute-start.5 = (bf16[2,128,1024]{2,1,0:T(8,128)(2,1)}, bf16[2,128,1024]{2,1,0:T(8,128)(2,1)}, u32[]{:S(2)}, u32[]{:S(2)}) collective-permute-start(bf16[2,128,1024]{2,1,0:T(8,128)(2,1)} %get-tuple-element.369), channel_id=1, source_target_pairs={{0,4},{4,0},{2,6},{6,2},{1,5},{5,1},{3,7},{7,3},{8,12},{12,8},{10,... | collective-permute-start | bytes 1572872 | tf_op jit(solution)/shard_map/cond/branch_1_fun/ppermute | solution.py:99
  443.5 10.6 %collective-permute-start.6 = (f32[1,4352]{1,0:T(1,128)}, f32[1,4352]{1,0:T(1,128)S(1)}, u32[]{:S(2)}, u32[]{:S(2)}) collective-permute-start(f32[1,4352]{1,0:T(1,128)} %add.155), channel_id=1, source_target_pairs={{0,2},{2,0},{4,6},{6,4},{1,3},{3,1},{5,7},{7,5},{8,10},{10,8},{12,... | collective-permute-start | bytes 52232 | tf_op jit(solution)/shard_map/cond/branch_1_fun/ppermute | solution.py:99
  (76 other events, 767.4 us)
Sparse Core Ops, SparseCore 0:
  15.5 63.8 all-gather.2
  111.0 112.9 all-gather.4
  286.6 78.5 reduce-scatter.3
  368.0 42.8 reduce-scatter.5
  415.9 62.0 reduce-scatter.7

commit v5 on v4

--- a/solution.py
+++ b/solution.py
@@ -145,6 +145,46 @@
     return jnp.stack([lower, upper], axis=axis)
 
 
+def join_kernel(*refs):
+    first = 0
+    for part in refs[:-1]:
+        refs[-1][:, first : first + part.shape[1]] = part[...]
+        first += part.shape[1]
+
+
+def joined_columns(*parts):
+    shape = (parts[0].shape[0], sum(part.shape[1] for part in parts))
+    return pl.pallas_call(
+        join_kernel,
+        in_specs=[pl.BlockSpec(memory_space=pltpu.VMEM)] * len(parts),
+        out_specs=pl.BlockSpec(memory_space=pltpu.VMEM),
+        out_shape=jax.ShapeDtypeStruct(shape, parts[0].dtype),
+        compiler_params=call_params(16),
+        cost_estimate=cheap(),
+        name="join",
+    )(*parts)
+
+
+def widen_kernel(source_ref, *outs):
+    first = 0
+    for out in outs:
+        out[...] = wide(source_ref[:, first : first + out.shape[1]])
+        first += out.shape[1]
+
+
+def widened(source, widths):
+    rows = source.shape[0]
+    return pl.pallas_call(
+        widen_kernel,
+        in_specs=[pl.BlockSpec(memory_space=pltpu.VMEM)],
+        out_specs=[pl.BlockSpec(memory_space=pltpu.VMEM)] * len(widths),
+        out_shape=[jax.ShapeDtypeStruct((rows, width), jnp.float32) for width in widths],
+        compiler_params=call_params(16),
+        cost_estimate=cheap(),
+        name="widen",
+    )(source)
+
+
 def position():
     heads = lax.axis_index("heads")
     return jnp.stack([lax.axis_index("tensor"), heads % 2, heads // 2]).astype(jnp.int32)
@@ -217,6 +257,42 @@
         fold_end_kernel, "fold_end", 16, [(rows, 2 * width)], keep_first, got_first, keep_second, got_second
     )
     return out
+
+
+def share_back_kernel(
+    eps, first_ref, got_first_ref, second_ref, got_second_ref, pair_upper_ref, pair_lower_ref, hidden_ref, cotangent_ref, gain_ref, out_ref, low_ref, part_ref
+):
+    middle = first_ref.shape[-1]
+    hidden = hidden_ref[...]
+    scale = lax.rsqrt(jnp.mean(hidden * hidden, axis=-1, keepdims=True) + eps)
+    grads = []
+    for k, (mine, got) in enumerate(((first_ref, got_first_ref), (second_ref, got_second_ref))):
+        cols = slice(k * middle, (k + 1) * middle)
+        pair = jnp.concatenate([pair_upper_ref[:, cols], pair_lower_ref[:, cols]], axis=0)
+        grads.append(wide(mine[...]) + wide(got[...]) + wide(pair))
+    grad = jnp.concatenate(grads, axis=1)
+    part_ref[...] = jnp.sum(grad * hidden * scale, axis=0, keepdims=True)
+    out = wide(cotangent_ref[...]) + norm_back(hidden, scale, grad * gain_ref[...])
+    out_ref[...] = out
+    low_ref[...] = low(out)
+
+
+def share_back(first, got_first, second, got_second, pair_upper, pair_lower, hidden, cotangent, gain):
+    rows, model = hidden.shape
+    args = (first, got_first, second, got_second, pair_upper, pair_lower, hidden, cotangent, gain)
+    return pl.pallas_call(
+        functools.partial(share_back_kernel, EPSILON),
+        in_specs=[pl.BlockSpec(memory_space=pltpu.VMEM)] * len(args),
+        out_specs=[pl.BlockSpec(memory_space=pltpu.VMEM)] * 3,
+        out_shape=[
+            jax.ShapeDtypeStruct((rows, model), jnp.float32),
+            jax.ShapeDtypeStruct((rows, model), jnp.bfloat16),
+            jax.ShapeDtypeStruct((1, model), jnp.float32),
+        ],
+        compiler_params=call_params(24),
+        cost_estimate=cheap(),
+        name="share_back",
+    )(*args)
 
 
 def plane_scatter(keep, give, rounded=False):
@@ -873,9 +949,8 @@
     def share_of(array):
         return lax.dynamic_slice_in_dim(array, share_start, share_rows, 0)
 
-    proj = lax.all_gather(
-        jnp.concatenate([w_query, w_key, w_value, w_out], axis=1), "fsdp", axis=0, tiled=True
-    )
+    block = joined_columns(w_query, w_key, w_value, w_out)
+    proj = lax.all_gather(block, "fsdp", axis=0, tiled=True)
     side = bit("fsdp", 1)
 
     def half_of(which):
@@ -886,7 +961,7 @@
     got = swap(after(half_of(1 - side), proj), "fsdp", 1)
     feed_block = both(half_of(side), got, side, 0)
 
-    gains = line_gather(jnp.concatenate([ln1_gain, ln2_gain, query_gain, key_gain]), strides)
+    gains = line_gather(after(jnp.concatenate([ln1_gain, ln2_gain, query_gain, key_gain]), block), strides)
     gain_attn = gains[:, :shard].reshape(model)
     gain_ffn = gains[:, shard : 2 * shard].reshape(model)
     head_part = HD // size
@@ -950,15 +1025,18 @@
         out_sum = Job(plane_scatter(*own_parts[2:]))
         pair_out_sum = Job(plane_scatter(*pair_parts[2:], True))
         beside(pair_sum, own_sum, pair_out_sum, out_sum)
-        pair_share = Job(pair_swap(pair_sum.value, 2))
-        beside(pair_share, own_sum, ready=[pair_out_sum])
-        beside(pair_share, own_sum, pair_out_sum, ready=[out_sum])
-        grad_share = own_sum.value + wide(pair_share.value)
-        hidden_grad_share = wide(share_of(cotangent)) + norm_back(
-            hidden_share, scale_share, grad_share * wide(gain_ffn)
+        cut = share_rows // 2
+        upper, lower = (Job(pair_swap(pair_sum.value[k : k + cut])) for k in (0, cut))
+        cot_share = share_of(cotangent)
+        beside(upper, own_sum, ready=[pair_out_sum])
+        beside(lower, own_sum, pair_out_sum, ready=[out_sum])
+        _, keep_first, _, keep_second = own_sum.held
+        got_first, got_second = own_sum.arrived
+        hidden_grad_share, low_share, ffn_gain_part = share_back(
+            keep_first, got_first, keep_second, got_second, upper.value, lower.value, hidden_share, cot_share,
+            wide(gain_ffn)[None],
         )
-        ffn_gain_part = jnp.sum(grad_share * hidden_share * scale_share, axis=0, keepdims=True)
-        gather = Job(plane_gather(low(hidden_grad_share)[None]))
+        gather = Job(plane_gather(low_share[None]))
         beside(gather, ready=[pair_out_sum])
         beside(gather)
         return hidden_grad_share, ffn_gain_part, *gather.held, *gather.arrived, *pair_out_sum.keep, *out_sum.keep
@@ -1016,8 +1094,9 @@
     gain_sums, down_got = lax.optimization_barrier((gain_sums, down_got))
     feed_w_grads = feed_sums(side[None], feed_w_sums, (wide_got, down_got))
     attn_w_grad, (gate_w_grad, up_w_grad, down_w_grad) = lax.optimization_barrier((attn_w_sum, feed_w_grads))
-    attn_w_grad = wide(attn_w_grad)
-    out_w_grad = attn_w_grad[:, query_cols + 2 * key_cols :]
+    query_w_grad, key_w_grad, value_w_grad, out_w_grad = widened(
+        attn_w_grad, (query_cols, key_cols, key_cols, query_cols)
+    )
     ends = [0, model, 2 * model, 2 * model + HD, 2 * model + 2 * HD]
     ln1_grad, ln2_grad, query_gain_grad, key_gain_grad = (
         lax.dynamic_slice_in_dim(gain_sums[0, start:end], lax.axis_index("fsdp") * ((end - start) // size), (end - start) // size, 0)
@@ -1027,9 +1106,9 @@
         block_out,
         tokens_grad,
         ln1_grad,
-        attn_w_grad[:, :query_cols],
-        attn_w_grad[:, query_cols : query_cols + key_cols],
-        attn_w_grad[:, query_cols + key_cols : query_cols + 2 * key_cols],
+        query_w_grad,
+        key_w_grad,
+        value_w_grad,
         query_gain_grad,
         key_gain_grad,
         out_w_grad,

time: 494 us -> 492 us (level)
  other arithmetic: 24.1 us -> 16.7 us
  Pallas kernels: 129 us -> 134 us
    pallas_call x0 -> x3, Pallas kernels: none -> 5.22 us  [the longest x1 3.1 us: share_back(): pl.pallas_call(functools.partial(share_back_kernel, EPSILON), in_specs=[p...]
  transfers between devices with their start and end apart: 72 -> 72, of which waited for: 35 -> 35; matrix products, arithmetic and copies ran while one was open for 8% -> 7% of each run, Pallas kernels for 21% -> 22%
where the time goes in v5:
time: 492 us; the launch traced here: 491 us
  waiting for transfers between devices  211 us (43%)
  Pallas kernels  134 us (27%)
  starting transfers between devices  80.7 us (16%)
  local copies, waits for them, and re-layouts  33.2 us (7%)
  other arithmetic  16.7 us (3%)
  between operations  14.4 us (3%)
    ppermute x61, waiting for transfers between devices, beside(): lax.ppermute(array, *move[1:])  152 us
    ppermute x61, starting transfers between devices, beside(): lax.ppermute(array, *move[1:])  59.1 us
    all_gather x1, waiting for transfers between devices, per_device(): proj = lax.all_gather(block, 'fsdp', axis=0, tiled=True)  43.2 us
    pallas_call x22, Pallas kernels, vmem_call(): pl.pallas_call(kernel, in_specs=[pl.BlockSpec(memory_space=pltpu.SMEM)] +...  36.4 us
    pallas_call x1, Pallas kernels, feed(): pl.pallas_call(feed_kernel, in_specs=[pl.BlockSpec(memory_space=pl.ANY)]...  16.7 us
    pallas_call x1, Pallas kernels, feed_weights(): pl.pallas_call(feed_weights_kernel, grid=(model // cols,), in_specs=[pl.B...  15.5 us
    pallas_call x2, Pallas kernels, feed_model(): pl.pallas_call(feed_model_kernel, grid=(rows // tile,), in_specs=[pl.Bloc...  15.2 us
    ppermute x6, waiting for transfers between devices, swap(): return lax.ppermute(array, axis, flip(axis, stride))  15.1 us
  transfers between devices with their start and end apart: 72, of which 35 were waited for; matrix products, arithmetic and copies ran while one was open for 7% of the time, Pallas kernels for 22%

profile of v5, /device:TPU:0, one launch (start us, length us, event | category | flops | bytes accessed | tf_op | source)
XLA Modules:
  0.0 491.1 jit_solution(18049298553482542498)
XLA Ops:
  12.2 3.1 collective-permute-start.58
  21.4 2.5 constant_dynamic-slice_fusion.14
  24.4 2.7 collective-permute-start.59
  29.8 5.5 %prepare.1 = (bf16[1024,2048]{1,0:T(8,128)(2,1)}, f32[1024,1]{1,0:T(8,128)}, s32[1024,1]{1,0:T(8,128)S(1)}) custom-call(bf16[1024,2048]{1,0:T(8,128)(2,1)} %tokens_ref.1, f32[1,2048]{1,0:T(1,128)S(1)} %bitcast.135, s32[1024,1]{1,0:T(8,128)S(1)} %copy.36.seg_ref), custom_call_target="tpu_custom_call" | custom-call | flops 20000000000 | bytes 20000000 | tf_op jit(solution)/shard_map/prepare/pallas_call | solution.py:758
  35.3 43.2 %all-gather.3.cloned.1.call-done.proj_ref = bf16[2048,768]{1,0:T(8,128)(2,1)} async-done(((bf16[512,768]{1,0:T(8,128)(2,1)}), bf16[2048,768]{1,0:T(8,128)(2,1)}) %all-gather.3.cloned.1.call-update) | async-done | bytes 3145744 | tf_op jit(solution)/shard_map/all_gather | solution.py:953
  78.8 11.4 %attend.1 = (f32[1024,384]{1,0:T(8,128)}, bf16[1024,256]{1,0:T(8,128)(2,1)}, bf16[1024,128]{1,0:T(8,128)(2,1)}, bf16[1024,128]{1,0:T(8,128)(2,1)}, bf16[1024,256]{1,0:T(8,128)(2,1)S(1)}) custom-call(bf16[1024,2048]{1,0:T(8,128)(2,1)} %get-tuple-element.533.normed_ref, bf16[2048,768]{1,0:T(8,128)(2,1)} %all-gather.3.cloned.1.call-done.proj_ref, ...), custom_call_target="tpu_custom_call" | custom-call | flops 1000 | bytes 1000 | tf_op jit(solution)/shard_map/attend/pallas_call | solution.py:510
  90.2 3.6 attend_out.1
  93.8 12.7 %collective-permute-done.61 = bf16[512,1152]{1,0:T(8,128)(2,1)} collective-permute-done((bf16[512,1152]{1,0:T(8,128)(2,1)}, bf16[512,1152]{1,0:T(8,128)(2,1)}, u32[]{:S(2)}, u32[]{:S(2)}) %collective-permute-start.61) | collective-permute-done | bytes 1179680 | tf_op jit(solution)/shard_map/ppermute | solution.py:123
  110.0 12.5 %reduce-scatter.4.cloned.1.call-start = ((), (), s32[]{:S(2)}) async-start(), calls=%async_computation.5 | async-start | bytes 4718592 | tf_op jit(solution)/shard_map/reduce_scatter | solution.py:1017
  122.6 113.2 %conditional.4 = (f32[128,2048]{1,0:T(8,128)S(1)}, bf16[512,2048]{1,0:T(8,128)(2,1)S(1)}, bf16[512,2048]{1,0:T(8,128)(2,1)}, bf16[512,2048]{1,0:T(8,128)(2,1)}, ...) conditional(s32[]{:T(128)} %convert_element_type.128, () %tuple.87, ...), branch_computations={%region_2.3_spmd, %region_3.5_spmd} | conditional | flops 5777378 | bytes 94936776 | solution.py:74
  123.9 2.7 fold_chip.6
  130.0 11.6 %collective-permute-done.37 = bf16[64,2048]{1,0:T(8,128)(2,1)S(1)} collective-permute-done((bf16[64,2048]{1,0:T(8,128)(2,1)S(1)}, bf16[64,2048]{1,0:T(8,128)(2,1)S(1)}, u32[]{:S(2)}, u32[]{:S(2)}) %collective-permute-start.37) | collective-permute-done | bytes 262176 | tf_op jit(solution)/shard_map/cond/branch_1_fun/ppermute | solution.py:99
  146.0 2.8 collective-permute-done.38
  149.4 7.8 %collective-permute-done.40 = bf16[64,2048]{1,0:T(8,128)(2,1)S(1)} collective-permute-done((bf16[64,2048]{1,0:T(8,128)(2,1)S(1)}, bf16[64,2048]{1,0:T(8,128)(2,1)S(1)}, u32[]{:S(2)}, u32[]{:S(2)}) %collective-permute-start.40) | collective-permute-done | bytes 262176 | tf_op jit(solution)/shard_map/cond/branch_1_fun/ppermute | solution.py:99
  159.8 2.5 collective-permute-start.41
  166.4 6.8 %collective-permute-done.41 = bf16[64,2048]{1,0:T(8,128)(2,1)S(1)} collective-permute-done((bf16[64,2048]{1,0:T(8,128)(2,1)S(1)}, bf16[64,2048]{1,0:T(8,128)(2,1)S(1)}, u32[]{:S(2)}, u32[]{:S(2)}) %collective-permute-start.41) | collective-permute-done | bytes 262176 | tf_op jit(solution)/shard_map/cond/branch_1_fun/ppermute | solution.py:99
  180.0 9.8 %collective-permute-done.46 = bf16[64,2048]{1,0:T(8,128)(2,1)S(1)} collective-permute-done((bf16[64,2048]{1,0:T(8,128)(2,1)S(1)}, bf16[64,2048]{1,0:T(8,128)(2,1)S(1)}, u32[]{:S(2)}, u32[]{:S(2)}) %collective-permute-start.46) | collective-permute-done | bytes 262176 | tf_op jit(solution)/shard_map/cond/branch_1_fun/ppermute | solution.py:99
  194.9 16.1 %collective-permute-done.49.got_first_ref = bf16[1,128,1024]{2,1,0:T(8,128)(2,1)S(1)} collective-permute-done((bf16[1,128,1024]{2,1,0:T(8,128)(2,1)S(1)}, bf16[1,128,1024]{2,1,0:T(8,128)(2,1)S(1)}, u32[]{:S(2)}, u32[]{:S(2)}) %collective-permute-start.49) | collective-permute-done | bytes 262176 | tf_op jit(solution)/shard_map/cond/branch_1_fun/ppermute | solution.py:99
  215.7 12.2 %collective-permute-done.54.got_first_ref = bf16[2,1,128,1024]{3,2,1,0:T(8,128)(2,1)S(1)} collective-permute-done((bf16[2,1,128,1024]{3,2,1,0:T(8,128)(2,1)S(1)}, bf16[2,1,128,1024]{3,2,1,0:T(8,128)(2,1)S(1)}, u32[]{:S(2)}, u32[]{:S(2)}) %collective-permute-start.54) | collective-permute-done | bytes 524320 | tf_op jit(solution)/shard_map/cond/branch_1_fun/ppermute | solution.py:99
  231.2 4.5 collective-permute-done.57
  235.8 16.7 %feed.1 = (bf16[2,512,384]{2,1,0:T(8,128)(2,1)S(1)}, bf16[2,512,384]{2,1,0:T(8,128)(2,1)S(1)}, bf16[2,512,768]{2,1,0:T(8,128)(2,1)S(1)}, bf16[2,512,768]{2,1,0:T(8,128)(2,1)S(1)}) custom-call(bf16[512,2048]{1,0:T(8,128)(2,1)S(1)} %get-tuple-element.568.refs_0_, bf16[512,2048]{1,0:T(8,128)(2,1)} %get-tuple-element.569.refs_1_, ...), custom_call_target="tpu_custom_call" | custom-call | flops 1000 | bytes 1000 | tf_op jit(solution)/shard_map/feed/pallas_call | solution.py:813
  252.5 7.3 %feed_model.2 = (bf16[512,2048]{1,0:T(8,128)(2,1)S(1)}, bf16[512,2048]{1,0:T(8,128)(2,1)S(1)}, bf16[512,2048]{1,0:T(8,128)(2,1)}, bf16[512,2048]{1,0:T(8,128)(2,1)}) custom-call(bf16[2,512,384]{2,1,0:T(8,128)(2,1)S(1)} %get-tuple-element.579.act_ref.refs_11_, bf16[2,512,768]{2,1,0:T(8,128)(2,1)S(1)} %get-tuple-element.577.grad_ref.refs_9_, ...), custom_call_target="tpu_custom_call" | custom-call | flops 1000 | bytes 1000 | tf_op jit(solution)/shard_map/feed_model/pallas_call | solution.py:841
  260.0 7.9 %feed_model.3 = (bf16[512,2048]{1,0:T(8,128)(2,1)}, bf16[512,2048]{1,0:T(8,128)(2,1)}, bf16[512,2048]{1,0:T(8,128)(2,1)}, bf16[512,2048]{1,0:T(8,128)(2,1)}) custom-call(bf16[2,512,384]{2,1,0:T(8,128)(2,1)S(1)} %get-tuple-element.578.act_ref.refs_10_, bf16[2,512,768]{2,1,0:T(8,128)(2,1)S(1)} %get-tuple-element.576.grad_ref.refs_8_, ...), custom_call_target="tpu_custom_call" | custom-call | flops 1000 | bytes 1000 | tf_op jit(solution)/shard_map/feed_model/pallas_call | solution.py:841
  270.1 15.5 %feed_weights.1 = (bf16[2048,768]{1,0:T(8,128)(2,1)}, bf16[2048,384]{1,0:T(8,128)(2,1)}) custom-call(bf16[512,2048]{1,0:T(8,128)(2,1)S(1)} %copy-done.30, bf16[512,2048]{1,0:T(8,128)(2,1)} %get-tuple-element.569.refs_1_, bf16[512,2048]{1,0:T(8,128)(2,1)} %get-tuple-element.570.refs_2_, bf16[512,2048]{1,0:T(8,128)(2,1)} %get-tuple-element.571.refs_3_, ...), custom_call_target="tpu_custom_call" | custom-call | flops 1000 | bytes 1000 | tf_op jit(solution)/shard_map/feed_weights/pallas_call | solution.py:875
  288.1 76.5 %conditional.5 = (f32[128,2048]{1,0:T(8,128)}, f32[1,2048]{1,0:T(1,128)S(1)}, bf16[2,1,128,1024]{3,2,1,0:T(8,128)(2,1)}, bf16[2,1,128,1024]{3,2,1,0:T(8,128)(2,1...) conditional(s32[]{:T(128)} %convert_element_type.128, () %tuple.97, ...), branch_computations={%region_6.7_spmd, %region_7.8_spmd} | conditional | flops 10081 | bytes 74470472 | solution.py:74
  291.6 5.7 %collective-permute-done.12.got_first_ref = bf16[128,1024]{1,0:T(8,128)(2,1)S(1)} collective-permute-done((bf16[128,1024]{1,0:T(8,128)(2,1)S(1)}, bf16[128,1024]{1,0:T(8,128)(2,1)S(1)}, u32[]{:S(2)}, u32[]{:S(2)}) %collective-permute-start.12) | collective-permute-done | bytes 262176 | tf_op jit(solution)/shard_map/cond/branch_1_fun/ppermute | solution.py:99
  305.2 2.5 collective-permute-start.17
  307.7 3.0 fold_chip.8
  310.7 8.8 %collective-permute-done.17.pair_upper_ref = bf16[64,2048]{1,0:T(8,128)(2,1)S(1)} collective-permute-done((bf16[64,2048]{1,0:T(8,128)(2,1)S(1)}, bf16[64,2048]{1,0:T(8,128)(2,1)S(1)}, u32[]{:S(2)}, u32[]{:S(2)}) %collective-permute-start.17) | collective-permute-done | bytes 262176 | tf_op jit(solution)/shard_map/cond/branch_1_fun/ppermute | solution.py:99
  323.6 2.5 collective-permute-start.20
  330.2 3.5 fold_chip.9
  333.7 3.6 collective-permute-done.20.pair_lower_ref
  337.3 3.9 collective-permute-done.21.got_first_ref
  341.2 3.1 share_back.1
  355.9 7.5 %collective-permute-done.27 = bf16[2,1,128,1024]{3,2,1,0:T(8,128)(2,1)} collective-permute-done((bf16[2,1,128,1024]{3,2,1,0:T(8,128)(2,1)}, bf16[2,1,128,1024]{3,2,1,0:T(8,128)(2,1)}, u32[]{:S(2)}, u32[]{:S(2)}) %collective-permute-start.27) | collective-permute-done | bytes 524320 | tf_op jit(solution)/shard_map/cond/branch_1_fun/ppermute | solution.py:99
  366.7 2.5 collective-permute-start.65
  369.2 45.8 %conditional.6 = (bf16[2048,768]{1,0:T(8,128)(2,1)}, bf16[512,2048]{1,0:T(8,128)(2,1)}, bf16[512,2048]{1,0:T(8,128)(2,1)}, f32[1,2048]{1,0:T(1,128)}, f32[2,128]...) conditional(s32[]{:T(128)} %convert_element_type.128, () %tuple.86, ...), branch_computations={%region_8.9_spmd, %region_9.10_spmd} | conditional | flops 4030 | bytes 69230728 | solution.py:74
  373.5 6.4 %collective-permute-done.30.got_first_ref = bf16[128,1024]{1,0:T(8,128)(2,1)S(1)} collective-permute-done((bf16[128,1024]{1,0:T(8,128)(2,1)}, bf16[128,1024]{1,0:T(8,128)(2,1)S(1)}, u32[]{:S(2)}, u32[]{:S(2)}) %collective-permute-start.30) | collective-permute-done | bytes 262176 | tf_op jit(solution)/shard_map/cond/branch_1_fun/ppermute | solution.py:99
  383.8 12.9 %attend_back.1 = (bf16[1024,512]{1,0:T(8,128)(2,1)S(1)}, bf16[2,512,256]{2,1,0:T(8,128)(2,1)S(1)}, f32[2,128]{1,0:T(2,128)}) custom-call(bf16[512,2048]{1,0:T(8,128)(2,1)S(1)} %bitcast.123, bf16[512,2048]{1,0:T(8,128)(2,1)} %bitcast.34.grad_other_ref, bf16[2048,768]{1,0:T(8,128)(2,1)} %get-tuple-element.306.out_proj_ref.proj_ref, ...), custom_call_target="tpu_custom_call" | custom-call | flops 1000 | bytes 1000 | tf_op jit(solution)/shard_map/cond/branch_1_fun/attend_back/pallas_call | solution.py:659
  396.7 9.5 %attend_weights.1 = (bf16[2048,768]{1,0:T(8,128)(2,1)}, bf16[512,2048]{1,0:T(8,128)(2,1)}, bf16[512,2048]{1,0:T(8,128)(2,1)}, f32[1,2048]{1,0:T(1,128)}) custom-call(s32[3]{0:T(128)S(1)} %pad_add_fusion.2.position_ref, bf16[1024,512]{1,0:T(8,128)(2,1)S(1)} %get-tuple-element.318.low_ref, bf16[2,512,256]{2,1,0:T(8,128)(2,1)S(1)} %get-tuple-element.319.mixed_ref, ...), custom_call_target="tpu_custom_call" | custom-call | flops 1000 | bytes 1000 | tf_op jit(solution)/shard_map/cond/branch_1_fun/attend_weights/pallas_call | solution.py:712
  406.3 7.9 %collective-permute-done.32 = bf16[128,2048]{1,0:T(8,128)(2,1)} collective-permute-done((bf16[128,2048]{1,0:T(8,128)(2,1)S(1)}, bf16[128,2048]{1,0:T(8,128)(2,1)}, u32[]{:S(2)}, u32[]{:S(2)}) %collective-permute-start.32) | collective-permute-done | bytes 524320 | tf_op jit(solution)/shard_map/cond/branch_1_fun/ppermute | solution.py:99
  417.2 59.7 %conditional.7 = (bf16[128,2048]{1,0:T(8,128)(2,1)}, bf16[128,2048]{1,0:T(8,128)(2,1)}, f32[1,4352]{1,0:T(1,128)S(1)}) conditional(s32[]{:T(128)} %convert_element_type.128, () %tuple.85, (bf16[128,2048]{1,0:T(8,128)(2,1)}, f32[128,2048]{1,0:T(8,128)}, bf16[2,128,1024]{2,1,0:T(8,128)(2,1)}, bf16[2,128,1024]{2,1,0:T(8,128)(2,1)}, ...), branch_computations={%region_11.12_spmd, %region_12.14_spmd} | conditional | flops 6580697 | bytes 50583148 | solution.py:74
  428.3 4.5 collective-permute-done.1
  434.8 3.0 fold_chip.10
  443.3 10.0 %collective-permute-done.6 = f32[1,4352]{1,0:T(1,128)S(1)} collective-permute-done((f32[1,4352]{1,0:T(1,128)}, f32[1,4352]{1,0:T(1,128)S(1)}, u32[]{:S(2)}, u32[]{:S(2)}) %collective-permute-start.6) | collective-permute-done | bytes 17440 | tf_op jit(solution)/shard_map/cond/branch_1_fun/ppermute | solution.py:99
  461.5 4.0 collective-permute-done.9
  469.0 2.9 collective-permute-done.10
  472.1 3.2 fusion.3
  (344 shorter events, 143.8 us)
Async XLA Ops:
  7.2 71.3 %all-gather.3.cloned.1.call-start = ((), (), s32[]{:S(2)}) async-start(), calls=%async_computation.3 | async-start | bytes 3932160 | tf_op jit(solution)/shard_map/all_gather | solution.py:953
  12.0 223.8 %all-gather.5.cloned.1.call-start = ((), (), s32[]{:S(2)}) async-start(), calls=%async_computation.4 | async-start | bytes 7077888 | tf_op jit(solution)/shard_map/all_gather | solution.py:984
  12.2 12.2 %collective-permute-start.58 = (bf16[1,1088]{1,0:T(2,128)(2,1)S(1)}, bf16[1,1088]{1,0:T(2,128)(2,1)S(1)}, u32[]{:S(2)}, u32[]{:S(2)}) collective-permute-start(bf16[1,1088]{1,0:T(2,128)(2,1)S(1)} %broadcast_in_dim.54), channel_id=1, source_target_pairs={{0,8},{8,0},{16,24},{24,16},{1,9},{9,1},{17,25},{25,17},{2,10},{10... | collective-permute-start | bytes 6536 | tf_op jit(solution)/shard_map/ppermute | solution.py:123
  78.5 28.0 %collective-permute-start.61 = (bf16[512,1152]{1,0:T(8,128)(2,1)}, bf16[512,1152]{1,0:T(8,128)(2,1)}, u32[]{:S(2)}, u32[]{:S(2)}) collective-permute-start(bf16[512,1152]{1,0:T(8,128)(2,1)} %pad_maximum_fusion.2), channel_id=1, source_target_pairs={{0,8},{8,0},{16,24},{24,16},{1,9},{9,1},{17,25},{25,17},{2,10},{10... | collective-permute-start | bytes 3538952 | tf_op jit(solution)/shard_map/ppermute | solution.py:123
  93.8 16.2 %collective-permute-start.60 = (bf16[512,2048]{1,0:T(8,128)(2,1)S(1)}, bf16[512,2048]{1,0:T(8,128)(2,1)}, u32[]{:S(2)}, u32[]{:S(2)}) collective-permute-start(bf16[512,2048]{1,0:T(8,128)(2,1)S(1)} %get-tuple-element.537), channel_id=1, source_target_pairs={{0,1},{1,0},{2,3},{3,2},{4,5},{5,4},{6,7},{7,6},{8,9},{9,8},{10,11... | collective-permute-start | bytes 6291464 | tf_op jit(solution)/shard_map/ppermute | solution.py:123
  110.0 254.6 %reduce-scatter.4.cloned.1.call-start = ((), (), s32[]{:S(2)}) async-start(), calls=%async_computation.5 | async-start | bytes 4718592 | tf_op jit(solution)/shard_map/reduce_scatter | solution.py:1017
  126.6 15.0 %collective-permute-start.35 = (bf16[2,128,1024]{2,1,0:T(8,128)(2,1)S(1)}, bf16[2,128,1024]{2,1,0:T(8,128)(2,1)S(1)}, u32[]{:S(2)}, u32[]{:S(2)}) collective-permute-start(bf16[2,128,1024]{2,1,0:T(8,128)(2,1)S(1)} %get-tuple-element.144), channel_id=1, source_target_pairs={{0,2},{2,0},{4,6},{6,4},{1,3},{3,1},{5,7},{7,5},{8,10},{10,8},{12,... | collective-permute-start | bytes 1572872 | tf_op jit(solution)/shard_map/cond/branch_1_fun/ppermute | solution.py:99
  128.2 13.4 %collective-permute-start.36 = (bf16[2,128,1024]{2,1,0:T(8,128)(2,1)S(1)}, bf16[2,128,1024]{2,1,0:T(8,128)(2,1)S(1)}, u32[]{:S(2)}, u32[]{:S(2)}) collective-permute-start(bf16[2,128,1024]{2,1,0:T(8,128)(2,1)S(1)} %get-tuple-element.145), channel_id=1, source_target_pairs={{0,4},{4,0},{2,6},{6,2},{1,5},{5,1},{3,7},{7,3},{8,12},{12,8},{10,... | collective-permute-start | bytes 1572872 | tf_op jit(solution)/shard_map/cond/branch_1_fun/ppermute | solution.py:99
  129.7 11.9 %collective-permute-start.37 = (bf16[64,2048]{1,0:T(8,128)(2,1)S(1)}, bf16[64,2048]{1,0:T(8,128)(2,1)S(1)}, u32[]{:S(2)}, u32[]{:S(2)}) collective-permute-start(bf16[64,2048]{1,0:T(8,128)(2,1)S(1)} %get-tuple-element.146), channel_id=1, source_target_pairs={{0,8},{8,0},{16,24},{24,16},{1,9},{9,1},{17,25},{25,17},{2,10},{10... | collective-permute-start | bytes 786440 | tf_op jit(solution)/shard_map/cond/branch_1_fun/ppermute | solution.py:99
  143.6 13.6 %collective-permute-start.40 = (bf16[64,2048]{1,0:T(8,128)(2,1)S(1)}, bf16[64,2048]{1,0:T(8,128)(2,1)S(1)}, u32[]{:S(2)}, u32[]{:S(2)}) collective-permute-start(bf16[64,2048]{1,0:T(8,128)(2,1)S(1)} %get-tuple-element.155), channel_id=1, source_target_pairs={{0,8},{8,0},{16,24},{24,16},{1,9},{9,1},{17,25},{25,17},{2,10},{10... | collective-permute-start | bytes 786440 | tf_op jit(solution)/shard_map/cond/branch_1_fun/ppermute | solution.py:99
  159.8 13.4 %collective-permute-start.41 = (bf16[64,2048]{1,0:T(8,128)(2,1)S(1)}, bf16[64,2048]{1,0:T(8,128)(2,1)S(1)}, u32[]{:S(2)}, u32[]{:S(2)}) collective-permute-start(bf16[64,2048]{1,0:T(8,128)(2,1)S(1)} %get-tuple-element.162), channel_id=1, source_target_pairs={{0,8},{8,0},{16,24},{24,16},{1,9},{9,1},{17,25},{25,17},{2,10},{10... | collective-permute-start | bytes 786440 | tf_op jit(solution)/shard_map/cond/branch_1_fun/ppermute | solution.py:99
  162.4 10.9 %collective-permute-start.42 = (bf16[1,128,1024]{2,1,0:T(8,128)(2,1)S(1)}, bf16[1,128,1024]{2,1,0:T(8,128)(2,1)S(1)}, u32[]{:S(2)}, u32[]{:S(2)}) collective-permute-start(bf16[1,128,1024]{2,1,0:T(8,128)(2,1)S(1)} %get-tuple-element.163.first_ref), channel_id=1, source_target_pairs={{0,4},{4,0},{2,6},{6,2},{1,5},{5,1},{3,7},{7,3},{8,12},{12,8},{10,... | collective-permute-start | bytes 786440 | tf_op jit(solution)/shard_map/cond/branch_1_fun/ppermute | solution.py:99
  175.8 14.1 %collective-permute-start.47 = (bf16[2,1,128,1024]{3,2,1,0:T(8,128)(2,1)S(1)}, bf16[2,1,128,1024]{3,2,1,0:T(8,128)(2,1)S(1)}, u32[]{:S(2)}, u32[]{:S(2)}) collective-permute-start(bf16[2,1,128,1024]{3,2,1,0:T(8,128)(2,1)S(1)} %get-tuple-element.172.first_ref), channel_id=1, source_target_pairs={{0,2},{2,0},{4,6},{6,4},{1,3},{3,1},{5,7},{7,5},{8,10},{10,8},{12,... | collective-permute-start | bytes 1572872 | tf_op jit(solution)/shard_map/cond/branch_1_fun/ppermute | solution.py:99
  177.3 12.6 %collective-permute-start.48 = (bf16[2,1,128,1024]{3,2,1,0:T(8,128)(2,1)S(1)}, bf16[2,1,128,1024]{3,2,1,0:T(8,128)(2,1)S(1)}, u32[]{:S(2)}, u32[]{:S(2)}) collective-permute-start(bf16[2,1,128,1024]{3,2,1,0:T(8,128)(2,1)S(1)} %get-tuple-element.173.second_ref), channel_id=1, source_target_pairs={{0,4},{4,0},{2,6},{6,2},{1,5},{5,1},{3,7},{7,3},{8,12},{12,8},{10,... | collective-permute-start | bytes 1572872 | tf_op jit(solution)/shard_map/cond/branch_1_fun/ppermute | solution.py:99
  177.3 12.6 %collective-permute-start.46 = (bf16[64,2048]{1,0:T(8,128)(2,1)S(1)}, bf16[64,2048]{1,0:T(8,128)(2,1)S(1)}, u32[]{:S(2)}, u32[]{:S(2)}) collective-permute-start(bf16[64,2048]{1,0:T(8,128)(2,1)S(1)} %get-tuple-element.171), channel_id=1, source_target_pairs={{0,8},{8,0},{16,24},{24,16},{1,9},{9,1},{17,25},{25,17},{2,10},{10... | collective-permute-start | bytes 786440 | tf_op jit(solution)/shard_map/cond/branch_1_fun/ppermute | solution.py:99
  190.7 20.3 %collective-permute-start.53 = (bf16[1,512,2048]{2,1,0:T(8,128)(2,1)S(1)}, bf16[1,512,2048]{2,1,0:T(8,128)(2,1)}, u32[]{:S(2)}, u32[]{:S(2)}) collective-permute-start(bf16[1,512,2048]{2,1,0:T(8,128)(2,1)S(1)} %bitcast.142), channel_id=1, source_target_pairs={{0,1},{1,0},{2,3},{3,2},{4,5},{5,4},{6,7},{7,6},{8,9},{9,8},{10,11... | collective-permute-start | bytes 6291464 | tf_op jit(solution)/shard_map/cond/branch_1_fun/ppermute | solution.py:99
  190.8 20.2 %collective-permute-start.51 = (bf16[2,1,128,1024]{3,2,1,0:T(8,128)(2,1)S(1)}, bf16[2,1,128,1024]{3,2,1,0:T(8,128)(2,1)S(1)}, u32[]{:S(2)}, u32[]{:S(2)}) collective-permute-start(bf16[2,1,128,1024]{3,2,1,0:T(8,128)(2,1)S(1)} %get-tuple-element.184.first_ref), channel_id=1, source_target_pairs={{0,2},{2,0},{4,6},{6,4},{1,3},{3,1},{5,7},{7,5},{8,10},{10,8},{12,... | collective-permute-start | bytes 1572872 | tf_op jit(solution)/shard_map/cond/branch_1_fun/ppermute | solution.py:99
  191.4 19.6 %collective-permute-start.52 = (bf16[2,1,128,1024]{3,2,1,0:T(8,128)(2,1)S(1)}, bf16[2,1,128,1024]{3,2,1,0:T(8,128)(2,1)S(1)}, u32[]{:S(2)}, u32[]{:S(2)}) collective-permute-start(bf16[2,1,128,1024]{3,2,1,0:T(8,128)(2,1)S(1)} %get-tuple-element.185.second_ref), channel_id=1, source_target_pairs={{0,4},{4,0},{2,6},{6,2},{1,5},{5,1},{3,7},{7,3},{8,12},{12,8},{10,... | collective-permute-start | bytes 1572872 | tf_op jit(solution)/shard_map/cond/branch_1_fun/ppermute | solution.py:99
  191.9 19.1 %collective-permute-start.49 = (bf16[1,128,1024]{2,1,0:T(8,128)(2,1)S(1)}, bf16[1,128,1024]{2,1,0:T(8,128)(2,1)S(1)}, u32[]{:S(2)}, u32[]{:S(2)}) collective-permute-start(bf16[1,128,1024]{2,1,0:T(8,128)(2,1)S(1)} %get-tuple-element.182.first_ref), channel_id=1, source_target_pairs={{0,4},{4,0},{2,6},{6,2},{1,5},{5,1},{3,7},{7,3},{8,12},{12,8},{10,... | collective-permute-start | bytes 786440 | tf_op jit(solution)/shard_map/cond/branch_1_fun/ppermute | solution.py:99
  193.4 17.6 %collective-permute-start.50 = (bf16[1,128,1024]{2,1,0:T(8,128)(2,1)S(1)}, bf16[1,128,1024]{2,1,0:T(8,128)(2,1)S(1)}, u32[]{:S(2)}, u32[]{:S(2)}) collective-permute-start(bf16[1,128,1024]{2,1,0:T(8,128)(2,1)S(1)} %get-tuple-element.183.second_ref), channel_id=1, source_target_pairs={{0,2},{2,0},{4,6},{6,4},{1,3},{3,1},{5,7},{7,5},{8,10},{10,8},{12,... | collective-permute-start | bytes 786440 | tf_op jit(solution)/shard_map/cond/branch_1_fun/ppermute | solution.py:99
  213.6 15.5 %collective-permute-start.56 = (bf16[1,512,2048]{2,1,0:T(8,128)(2,1)}, bf16[1,512,2048]{2,1,0:T(8,128)(2,1)}, u32[]{:S(2)}, u32[]{:S(2)}) collective-permute-start(bf16[1,512,2048]{2,1,0:T(8,128)(2,1)} %bitcast.11), channel_id=1, source_target_pairs={{0,1},{1,0},{2,3},{3,2},{4,5},{5,4},{6,7},{7,6},{8,9},{9,8},{10,11... | collective-permute-start | bytes 6291464 | tf_op jit(solution)/shard_map/cond/branch_1_fun/ppermute | solution.py:99
  213.7 14.3 %collective-permute-start.54 = (bf16[2,1,128,1024]{3,2,1,0:T(8,128)(2,1)S(1)}, bf16[2,1,128,1024]{3,2,1,0:T(8,128)(2,1)S(1)}, u32[]{:S(2)}, u32[]{:S(2)}) collective-permute-start(bf16[2,1,128,1024]{3,2,1,0:T(8,128)(2,1)S(1)} %get-tuple-element.194.first_ref), channel_id=1, source_target_pairs={{0,2},{2,0},{4,6},{6,4},{1,3},{3,1},{5,7},{7,5},{8,10},{10,8},{12,... | collective-permute-start | bytes 1572872 | tf_op jit(solution)/shard_map/cond/branch_1_fun/ppermute | solution.py:99
  215.2 14.0 %collective-permute-start.55 = (bf16[2,1,128,1024]{3,2,1,0:T(8,128)(2,1)S(1)}, bf16[2,1,128,1024]{3,2,1,0:T(8,128)(2,1)S(1)}, u32[]{:S(2)}, u32[]{:S(2)}) collective-permute-start(bf16[2,1,128,1024]{3,2,1,0:T(8,128)(2,1)S(1)} %get-tuple-element.195.second_ref), channel_id=1, source_target_pairs={{0,4},{4,0},{2,6},{6,2},{1,5},{5,1},{3,7},{7,3},{8,12},{12,8},{10,... | collective-permute-start | bytes 1572872 | tf_op jit(solution)/shard_map/cond/branch_1_fun/ppermute | solution.py:99
  268.9 16.7 %collective-permute-start.63 = (bf16[2,128,1024]{2,1,0:T(8,128)(2,1)S(1)}, bf16[2,128,1024]{2,1,0:T(8,128)(2,1)S(1)}, u32[]{:S(2)}, u32[]{:S(2)}) collective-permute-start(bf16[2,128,1024]{2,1,0:T(8,128)(2,1)S(1)} %get-tuple-element.566), channel_id=1, source_target_pairs={{0,2},{2,0},{4,6},{6,4},{1,3},{3,1},{5,7},{7,5},{8,10},{10,8},{12,... | collective-permute-start | bytes 1572872 | tf_op jit(solution)/shard_map/ppermute | solution.py:99
  269.5 16.0 %collective-permute-start.64 = (bf16[2,128,1024]{2,1,0:T(8,128)(2,1)S(1)}, bf16[2,128,1024]{2,1,0:T(8,128)(2,1)S(1)}, u32[]{:S(2)}, u32[]{:S(2)}) collective-permute-start(bf16[2,128,1024]{2,1,0:T(8,128)(2,1)S(1)} %get-tuple-element.567), channel_id=1, source_target_pairs={{0,4},{4,0},{2,6},{6,2},{1,5},{5,1},{3,7},{7,3},{8,12},{12,8},{10,... | collective-permute-start | bytes 1572872 | tf_op jit(solution)/shard_map/ppermute | solution.py:99
  285.6 129.4 %reduce-scatter.6.cloned.1.call-start = ((), (), s32[]{:S(2)}) async-start(), calls=%async_computation.6 | async-start | bytes 2359296 | tf_op jit(solution)/shard_map/reduce_scatter | solution.py:1017
  286.2 195.9 %reduce-scatter.8.cloned.1.call-start = ((), (), s32[]{:S(2)}) async-start(), calls=%async_computation.7 | async-start | bytes 3932160 | tf_op jit(solution)/shard_map/reduce_scatter | solution.py:1071
  288.1 10.6 %collective-permute-start.14 = (bf16[512,2048]{1,0:T(8,128)(2,1)}, bf16[512,2048]{1,0:T(8,128)(2,1)}, u32[]{:S(2)}, u32[]{:S(2)}) collective-permute-start(bf16[512,2048]{1,0:T(8,128)(2,1)} %get-tuple-element.208), channel_id=1, source_target_pairs={{0,1},{1,0},{2,3},{3,2},{4,5},{5,4},{6,7},{7,6},{8,9},{9,8},{10,11... | collective-permute-start | bytes 6291464 | tf_op jit(solution)/shard_map/cond/branch_1_fun/ppermute | solution.py:99
  288.1 10.6 %collective-permute-start.15 = (bf16[512,2048]{1,0:T(8,128)(2,1)}, bf16[512,2048]{1,0:T(8,128)(2,1)}, u32[]{:S(2)}, u32[]{:S(2)}) collective-permute-start(bf16[512,2048]{1,0:T(8,128)(2,1)} %get-tuple-element.209), channel_id=1, source_target_pairs={{0,1},{1,0},{2,3},{3,2},{4,5},{5,4},{6,7},{7,6},{8,9},{9,8},{10,11... | collective-permute-start | bytes 6291464 | tf_op jit(solution)/shard_map/cond/branch_1_fun/ppermute | solution.py:99
  302.4 17.2 %collective-permute-start.18 = (bf16[2,128,1024]{2,1,0:T(8,128)(2,1)S(1)}, bf16[2,128,1024]{2,1,0:T(8,128)(2,1)S(1)}, u32[]{:S(2)}, u32[]{:S(2)}) collective-permute-start(bf16[2,128,1024]{2,1,0:T(8,128)(2,1)S(1)} %get-tuple-element.220), channel_id=1, source_target_pairs={{0,2},{2,0},{4,6},{6,4},{1,3},{3,1},{5,7},{7,5},{8,10},{10,8},{12,... | collective-permute-start | bytes 1572872 | tf_op jit(solution)/shard_map/cond/branch_1_fun/ppermute | solution.py:99
  303.9 15.6 %collective-permute-start.19 = (bf16[2,128,1024]{2,1,0:T(8,128)(2,1)S(1)}, bf16[2,128,1024]{2,1,0:T(8,128)(2,1)S(1)}, u32[]{:S(2)}, u32[]{:S(2)}) collective-permute-start(bf16[2,128,1024]{2,1,0:T(8,128)(2,1)S(1)} %get-tuple-element.221), channel_id=1, source_target_pairs={{0,4},{4,0},{2,6},{6,2},{1,5},{5,1},{3,7},{7,3},{8,12},{12,8},{10,... | collective-permute-start | bytes 1572872 | tf_op jit(solution)/shard_map/cond/branch_1_fun/ppermute | solution.py:99
  305.2 14.3 %collective-permute-start.17 = (bf16[64,2048]{1,0:T(8,128)(2,1)S(1)}, bf16[64,2048]{1,0:T(8,128)(2,1)S(1)}, u32[]{:S(2)}, u32[]{:S(2)}) collective-permute-start(bf16[64,2048]{1,0:T(8,128)(2,1)S(1)} %get-tuple-element.219), channel_id=1, source_target_pairs={{0,8},{8,0},{16,24},{24,16},{1,9},{9,1},{17,25},{25,17},{2,10},{10... | collective-permute-start | bytes 786440 | tf_op jit(solution)/shard_map/cond/branch_1_fun/ppermute | solution.py:99
  322.4 18.8 %collective-permute-start.23 = (bf16[2,128,1024]{2,1,0:T(8,128)(2,1)}, bf16[2,128,1024]{2,1,0:T(8,128)(2,1)}, u32[]{:S(2)}, u32[]{:S(2)}) collective-permute-start(bf16[2,128,1024]{2,1,0:T(8,128)(2,1)} %get-tuple-element.237), channel_id=1, source_target_pairs={{0,2},{2,0},{4,6},{6,4},{1,3},{3,1},{5,7},{7,5},{8,10},{10,8},{12,... | collective-permute-start | bytes 1572872 | tf_op jit(solution)/shard_map/cond/branch_1_fun/ppermute | solution.py:99
  323.0 18.2 %collective-permute-start.24 = (bf16[2,128,1024]{2,1,0:T(8,128)(2,1)}, bf16[2,128,1024]{2,1,0:T(8,128)(2,1)}, u32[]{:S(2)}, u32[]{:S(2)}) collective-permute-start(bf16[2,128,1024]{2,1,0:T(8,128)(2,1)} %get-tuple-element.238), channel_id=1, source_target_pairs={{0,4},{4,0},{2,6},{6,2},{1,5},{5,1},{3,7},{7,3},{8,12},{12,8},{10,... | collective-permute-start | bytes 1572872 | tf_op jit(solution)/shard_map/cond/branch_1_fun/ppermute | solution.py:99
  323.6 13.7 %collective-permute-start.20 = (bf16[64,2048]{1,0:T(8,128)(2,1)}, bf16[64,2048]{1,0:T(8,128)(2,1)}, u32[]{:S(2)}, u32[]{:S(2)}) collective-permute-start(bf16[64,2048]{1,0:T(8,128)(2,1)} %get-tuple-element.234), channel_id=1, source_target_pairs={{0,8},{8,0},{16,24},{24,16},{1,9},{9,1},{17,25},{25,17},{2,10},{10... | collective-permute-start | bytes 786440 | tf_op jit(solution)/shard_map/cond/branch_1_fun/ppermute | solution.py:99
  326.1 15.1 %collective-permute-start.21 = (bf16[128,1024]{1,0:T(8,128)(2,1)}, bf16[128,1024]{1,0:T(8,128)(2,1)}, u32[]{:S(2)}, u32[]{:S(2)}) collective-permute-start(bf16[128,1024]{1,0:T(8,128)(2,1)} %get-tuple-element.235), channel_id=1, source_target_pairs={{0,4},{4,0},{2,6},{6,2},{1,5},{5,1},{3,7},{7,3},{8,12},{12,8},{10,... | collective-permute-start | bytes 786440 | tf_op jit(solution)/shard_map/cond/branch_1_fun/ppermute | solution.py:99
  327.5 13.7 %collective-permute-start.22 = (bf16[128,1024]{1,0:T(8,128)(2,1)}, bf16[128,1024]{1,0:T(8,128)(2,1)}, u32[]{:S(2)}, u32[]{:S(2)}) collective-permute-start(bf16[128,1024]{1,0:T(8,128)(2,1)} %get-tuple-element.236), channel_id=1, source_target_pairs={{0,2},{2,0},{4,6},{6,4},{1,3},{3,1},{5,7},{7,5},{8,10},{10,8},{12,... | collective-permute-start | bytes 786440 | tf_op jit(solution)/shard_map/cond/branch_1_fun/ppermute | solution.py:99
  352.9 10.5 %collective-permute-start.27 = (bf16[2,1,128,1024]{3,2,1,0:T(8,128)(2,1)}, bf16[2,1,128,1024]{3,2,1,0:T(8,128)(2,1)}, u32[]{:S(2)}, u32[]{:S(2)}) collective-permute-start(bf16[2,1,128,1024]{3,2,1,0:T(8,128)(2,1)} %get-tuple-element.267), channel_id=1, source_target_pairs={{0,2},{2,0},{4,6},{6,4},{1,3},{3,1},{5,7},{7,5},{8,10},{10,8},{12,... | collective-permute-start | bytes 1572872 | tf_op jit(solution)/shard_map/cond/branch_1_fun/ppermute | solution.py:99
  354.4 10.2 %collective-permute-start.28 = (bf16[2,1,128,1024]{3,2,1,0:T(8,128)(2,1)}, bf16[2,1,128,1024]{3,2,1,0:T(8,128)(2,1)}, u32[]{:S(2)}, u32[]{:S(2)}) collective-permute-start(bf16[2,1,128,1024]{3,2,1,0:T(8,128)(2,1)} %get-tuple-element.268), channel_id=1, source_target_pairs={{0,4},{4,0},{2,6},{6,2},{1,5},{5,1},{3,7},{7,3},{8,12},{12,8},{10,... | collective-permute-start | bytes 1572872 | tf_op jit(solution)/shard_map/cond/branch_1_fun/ppermute | solution.py:99
  366.7 48.3 %collective-permute-start.65 = (bf16[512,768]{1,0:T(8,128)(2,1)}, bf16[512,768]{1,0:T(8,128)(2,1)S(1)}, u32[]{:S(2)}, u32[]{:S(2)}) collective-permute-start(bf16[512,768]{1,0:T(8,128)(2,1)} %dynamic-slice_bitcast_fusion), channel_id=1, source_target_pairs={{0,8},{8,0},{16,24},{24,16},{1,9},{9,1},{17,25},{25,17},{2,10},{10... | collective-permute-start | bytes 2359304 | tf_op jit(solution)/shard_map/ppermute | solution.py:123
  370.9 10.5 %collective-permute-start.29 = (bf16[1,512,2048]{2,1,0:T(8,128)(2,1)S(1)}, bf16[1,512,2048]{2,1,0:T(8,128)(2,1)}, u32[]{:S(2)}, u32[]{:S(2)}) collective-permute-start(bf16[1,512,2048]{2,1,0:T(8,128)(2,1)S(1)} %bitcast.122), channel_id=1, source_target_pairs={{0,1},{1,0},{2,3},{3,2},{4,5},{5,4},{6,7},{7,6},{8,9},{9,8},{10,11... | collective-permute-start | bytes 6291464 | tf_op jit(solution)/shard_map/cond/branch_1_fun/ppermute | solution.py:99
  382.6 31.6 %collective-permute-start.32 = (bf16[128,2048]{1,0:T(8,128)(2,1)S(1)}, bf16[128,2048]{1,0:T(8,128)(2,1)}, u32[]{:S(2)}, u32[]{:S(2)}) collective-permute-start(bf16[128,2048]{1,0:T(8,128)(2,1)S(1)} %fold_end.3), channel_id=1, source_target_pairs={{0,8},{8,0},{16,24},{24,16},{1,9},{9,1},{17,25},{25,17},{2,10},{10... | collective-permute-start | bytes 1572872 | tf_op jit(solution)/shard_map/cond/branch_1_fun/ppermute | solution.py:99
  382.7 31.5 %collective-permute-start.33 = (bf16[2,128,1024]{2,1,0:T(8,128)(2,1)}, bf16[2,128,1024]{2,1,0:T(8,128)(2,1)}, u32[]{:S(2)}, u32[]{:S(2)}) collective-permute-start(bf16[2,128,1024]{2,1,0:T(8,128)(2,1)} %get-tuple-element.303), channel_id=1, source_target_pairs={{0,2},{2,0},{4,6},{6,4},{1,3},{3,1},{5,7},{7,5},{8,10},{10,8},{12,... | collective-permute-start | bytes 1572872 | tf_op jit(solution)/shard_map/cond/branch_1_fun/ppermute | solution.py:99
  383.3 30.9 %collective-permute-start.34 = (bf16[2,128,1024]{2,1,0:T(8,128)(2,1)}, bf16[2,128,1024]{2,1,0:T(8,128)(2,1)}, u32[]{:S(2)}, u32[]{:S(2)}) collective-permute-start(bf16[2,128,1024]{2,1,0:T(8,128)(2,1)} %get-tuple-element.304), channel_id=1, source_target_pairs={{0,4},{4,0},{2,6},{6,2},{1,5},{5,1},{3,7},{7,3},{8,12},{12,8},{10,... | collective-permute-start | bytes 1572872 | tf_op jit(solution)/shard_map/cond/branch_1_fun/ppermute | solution.py:99
  416.9 60.0 %collective-permute-start.66 = (bf16[512,384]{1,0:T(8,128)(2,1)}, bf16[512,384]{1,0:T(8,128)(2,1)S(1)}, u32[]{:S(2)}, u32[]{:S(2)}) collective-permute-start(bf16[512,384]{1,0:T(8,128)(2,1)} %dynamic-slice_bitcast_fusion.1), channel_id=1, source_target_pairs={{0,8},{8,0},{16,24},{24,16},{1,9},{9,1},{17,25},{25,17},{2,10},{10... | collective-permute-start | bytes 1179656 | tf_op jit(solution)/shard_map/ppermute | solution.py:123
  439.3 14.0 %collective-permute-start.4 = (bf16[2,128,1024]{2,1,0:T(8,128)(2,1)}, bf16[2,128,1024]{2,1,0:T(8,128)(2,1)}, u32[]{:S(2)}, u32[]{:S(2)}) collective-permute-start(bf16[2,128,1024]{2,1,0:T(8,128)(2,1)} %get-tuple-element.368), channel_id=1, source_target_pairs={{0,2},{2,0},{4,6},{6,4},{1,3},{3,1},{5,7},{7,5},{8,10},{10,8},{12,... | collective-permute-start | bytes 1572872 | tf_op jit(solution)/shard_map/cond/branch_1_fun/ppermute | solution.py:99
  440.8 13.3 %collective-permute-start.5 = (bf16[2,128,1024]{2,1,0:T(8,128)(2,1)}, bf16[2,128,1024]{2,1,0:T(8,128)(2,1)}, u32[]{:S(2)}, u32[]{:S(2)}) collective-permute-start(bf16[2,128,1024]{2,1,0:T(8,128)(2,1)} %get-tuple-element.369), channel_id=1, source_target_pairs={{0,4},{4,0},{2,6},{6,2},{1,5},{5,1},{3,7},{7,3},{8,12},{12,8},{10,... | collective-permute-start | bytes 1572872 | tf_op jit(solution)/shard_map/cond/branch_1_fun/ppermute | solution.py:99
  442.6 10.7 %collective-permute-start.6 = (f32[1,4352]{1,0:T(1,128)}, f32[1,4352]{1,0:T(1,128)S(1)}, u32[]{:S(2)}, u32[]{:S(2)}) collective-permute-start(f32[1,4352]{1,0:T(1,128)} %add.138), channel_id=1, source_target_pairs={{0,2},{2,0},{4,6},{6,4},{1,3},{3,1},{5,7},{7,5},{8,10},{10,8},{12,... | collective-permute-start | bytes 52232 | tf_op jit(solution)/shard_map/cond/branch_1_fun/ppermute | solution.py:99
  (84 other events, 759.7 us)
Sparse Core Ops, SparseCore 0:
  12.1 66.3 all-gather.2
  110.1 112.8 all-gather.4
  285.7 78.6 reduce-scatter.3
  367.2 41.8 reduce-scatter.5
  415.1 63.7 reduce-scatter.7

commit v6 on v5

--- a/solution.py
+++ b/solution.py
@@ -159,7 +159,7 @@
         in_specs=[pl.BlockSpec(memory_space=pltpu.VMEM)] * len(parts),
         out_specs=pl.BlockSpec(memory_space=pltpu.VMEM),
         out_shape=jax.ShapeDtypeStruct(shape, parts[0].dtype),
-        compiler_params=call_params(16),
+        compiler_params=call_params(60),
         cost_estimate=cheap(),
         name="join",
     )(*parts)

time: 492 us -> 490 us (level)
  no operation moved by 1% of the time
where the time goes in v6:
time: 490 us; the launch traced here: 489 us
  waiting for transfers between devices  212 us (43%)
  Pallas kernels  136 us (28%)
  starting transfers between devices  80.6 us (16%)
  local copies, waits for them, and re-layouts  29.6 us (6%)
  other arithmetic  16.7 us (3%)
  between operations  14.4 us (3%)
    ppermute x61, waiting for transfers between devices, beside(): lax.ppermute(array, *move[1:])  152 us
    ppermute x61, starting transfers between devices, beside(): lax.ppermute(array, *move[1:])  59 us
    all_gather x1, waiting for transfers between devices, per_device(): proj = lax.all_gather(block, 'fsdp', axis=0, tiled=True)  43.3 us
    pallas_call x22, Pallas kernels, vmem_call(): pl.pallas_call(kernel, in_specs=[pl.BlockSpec(memory_space=pltpu.SMEM)] +...  36.4 us
    pallas_call x1, Pallas kernels, feed(): pl.pallas_call(feed_kernel, in_specs=[pl.BlockSpec(memory_space=pl.ANY)]...  16.7 us
    ppermute x6, waiting for transfers between devices, swap(): return lax.ppermute(array, axis, flip(axis, stride))  15.6 us
    pallas_call x1, Pallas kernels, feed_weights(): pl.pallas_call(feed_weights_kernel, grid=(model // cols,), in_specs=[pl.B...  15.5 us
    pallas_call x2, Pallas kernels, feed_model(): pl.pallas_call(feed_model_kernel, grid=(rows // tile,), in_specs=[pl.Bloc...  15.2 us
  transfers between devices with their start and end apart: 72, of which 35 were waited for; matrix products, arithmetic and copies ran while one was open for 7% of the time, Pallas kernels for 22%

profile of v6, /device:TPU:0, one launch (start us, length us, event | category | flops | bytes accessed | tf_op | source)
XLA Modules:
  0.0 489.1 jit_solution(16776816336689674202)
XLA Ops:
  9.7 3.1 collective-permute-start.58
  19.0 2.5 constant_dynamic-slice_fusion.14
  22.0 2.7 collective-permute-start.59
  24.9 2.8 collective-permute-done.59
  27.8 5.5 %prepare.1 = (bf16[1024,2048]{1,0:T(8,128)(2,1)}, f32[1024,1]{1,0:T(8,128)}, s32[1024,1]{1,0:T(8,128)S(1)}) custom-call(bf16[1024,2048]{1,0:T(8,128)(2,1)} %tokens_ref.1, f32[1,2048]{1,0:T(1,128)S(1)} %bitcast.135, s32[1024,1]{1,0:T(8,128)S(1)} %copy.36.seg_ref), custom_call_target="tpu_custom_call" | custom-call | flops 20000000000 | bytes 20000000 | tf_op jit(solution)/shard_map/prepare/pallas_call | solution.py:758
  33.3 43.3 %all-gather.3.cloned.1.call-done.proj_ref = bf16[2048,768]{1,0:T(8,128)(2,1)} async-done(((bf16[512,768]{1,0:T(8,128)(2,1)}), bf16[2048,768]{1,0:T(8,128)(2,1)}) %all-gather.3.cloned.1.call-update) | async-done | bytes 3145744 | tf_op jit(solution)/shard_map/all_gather | solution.py:953
  76.9 11.4 %attend.1 = (f32[1024,384]{1,0:T(8,128)}, bf16[1024,256]{1,0:T(8,128)(2,1)}, bf16[1024,128]{1,0:T(8,128)(2,1)}, bf16[1024,128]{1,0:T(8,128)(2,1)}, bf16[1024,256]{1,0:T(8,128)(2,1)S(1)}) custom-call(bf16[1024,2048]{1,0:T(8,128)(2,1)} %get-tuple-element.533.normed_ref, bf16[2048,768]{1,0:T(8,128)(2,1)} %all-gather.3.cloned.1.call-done.proj_ref, ...), custom_call_target="tpu_custom_call" | custom-call | flops 1000 | bytes 1000 | tf_op jit(solution)/shard_map/attend/pallas_call | solution.py:510
  88.3 3.6 attend_out.1
  91.9 12.8 %collective-permute-done.61 = bf16[512,1152]{1,0:T(8,128)(2,1)} collective-permute-done((bf16[512,1152]{1,0:T(8,128)(2,1)}, bf16[512,1152]{1,0:T(8,128)(2,1)}, u32[]{:S(2)}, u32[]{:S(2)}) %collective-permute-start.61) | collective-permute-done | bytes 1179680 | tf_op jit(solution)/shard_map/ppermute | solution.py:123
  108.2 12.5 %reduce-scatter.4.cloned.1.call-start = ((), (), s32[]{:S(2)}) async-start(), calls=%async_computation.5 | async-start | bytes 4718592 | tf_op jit(solution)/shard_map/reduce_scatter | solution.py:1017
  120.7 113.2 %conditional.4 = (f32[128,2048]{1,0:T(8,128)S(1)}, bf16[512,2048]{1,0:T(8,128)(2,1)S(1)}, bf16[512,2048]{1,0:T(8,128)(2,1)}, bf16[512,2048]{1,0:T(8,128)(2,1)}, ...) conditional(s32[]{:T(128)} %convert_element_type.128, () %tuple.87, ...), branch_computations={%region_2.3_spmd, %region_3.5_spmd} | conditional | flops 5777378 | bytes 94936776 | solution.py:74
  122.0 2.7 fold_chip.6
  128.1 11.6 %collective-permute-done.37 = bf16[64,2048]{1,0:T(8,128)(2,1)S(1)} collective-permute-done((bf16[64,2048]{1,0:T(8,128)(2,1)S(1)}, bf16[64,2048]{1,0:T(8,128)(2,1)S(1)}, u32[]{:S(2)}, u32[]{:S(2)}) %collective-permute-start.37) | collective-permute-done | bytes 262176 | tf_op jit(solution)/shard_map/cond/branch_1_fun/ppermute | solution.py:99
  144.2 2.8 collective-permute-done.38
  147.6 7.7 %collective-permute-done.40 = bf16[64,2048]{1,0:T(8,128)(2,1)S(1)} collective-permute-done((bf16[64,2048]{1,0:T(8,128)(2,1)S(1)}, bf16[64,2048]{1,0:T(8,128)(2,1)S(1)}, u32[]{:S(2)}, u32[]{:S(2)}) %collective-permute-start.40) | collective-permute-done | bytes 262176 | tf_op jit(solution)/shard_map/cond/branch_1_fun/ppermute | solution.py:99
  158.0 2.5 collective-permute-start.41
  164.6 6.9 %collective-permute-done.41 = bf16[64,2048]{1,0:T(8,128)(2,1)S(1)} collective-permute-done((bf16[64,2048]{1,0:T(8,128)(2,1)S(1)}, bf16[64,2048]{1,0:T(8,128)(2,1)S(1)}, u32[]{:S(2)}, u32[]{:S(2)}) %collective-permute-start.41) | collective-permute-done | bytes 262176 | tf_op jit(solution)/shard_map/cond/branch_1_fun/ppermute | solution.py:99
  178.3 9.9 %collective-permute-done.46 = bf16[64,2048]{1,0:T(8,128)(2,1)S(1)} collective-permute-done((bf16[64,2048]{1,0:T(8,128)(2,1)S(1)}, bf16[64,2048]{1,0:T(8,128)(2,1)S(1)}, u32[]{:S(2)}, u32[]{:S(2)}) %collective-permute-start.46) | collective-permute-done | bytes 262176 | tf_op jit(solution)/shard_map/cond/branch_1_fun/ppermute | solution.py:99
  193.1 16.1 %collective-permute-done.49.got_first_ref = bf16[1,128,1024]{2,1,0:T(8,128)(2,1)S(1)} collective-permute-done((bf16[1,128,1024]{2,1,0:T(8,128)(2,1)S(1)}, bf16[1,128,1024]{2,1,0:T(8,128)(2,1)S(1)}, u32[]{:S(2)}, u32[]{:S(2)}) %collective-permute-start.49) | collective-permute-done | bytes 262176 | tf_op jit(solution)/shard_map/cond/branch_1_fun/ppermute | solution.py:99
  213.9 12.2 %collective-permute-done.54.got_first_ref = bf16[2,1,128,1024]{3,2,1,0:T(8,128)(2,1)S(1)} collective-permute-done((bf16[2,1,128,1024]{3,2,1,0:T(8,128)(2,1)S(1)}, bf16[2,1,128,1024]{3,2,1,0:T(8,128)(2,1)S(1)}, u32[]{:S(2)}, u32[]{:S(2)}) %collective-permute-start.54) | collective-permute-done | bytes 524320 | tf_op jit(solution)/shard_map/cond/branch_1_fun/ppermute | solution.py:99
  229.4 4.5 collective-permute-done.57
  234.0 16.7 %feed.1 = (bf16[2,512,384]{2,1,0:T(8,128)(2,1)S(1)}, bf16[2,512,384]{2,1,0:T(8,128)(2,1)S(1)}, bf16[2,512,768]{2,1,0:T(8,128)(2,1)S(1)}, bf16[2,512,768]{2,1,0:T(8,128)(2,1)S(1)}) custom-call(bf16[512,2048]{1,0:T(8,128)(2,1)S(1)} %get-tuple-element.568.refs_0_, bf16[512,2048]{1,0:T(8,128)(2,1)} %get-tuple-element.569.refs_1_, ...), custom_call_target="tpu_custom_call" | custom-call | flops 1000 | bytes 1000 | tf_op jit(solution)/shard_map/feed/pallas_call | solution.py:813
  250.7 7.3 %feed_model.2 = (bf16[512,2048]{1,0:T(8,128)(2,1)S(1)}, bf16[512,2048]{1,0:T(8,128)(2,1)S(1)}, bf16[512,2048]{1,0:T(8,128)(2,1)}, bf16[512,2048]{1,0:T(8,128)(2,1)}) custom-call(bf16[2,512,384]{2,1,0:T(8,128)(2,1)S(1)} %get-tuple-element.579.act_ref.refs_11_, bf16[2,512,768]{2,1,0:T(8,128)(2,1)S(1)} %get-tuple-element.577.grad_ref.refs_9_, ...), custom_call_target="tpu_custom_call" | custom-call | flops 1000 | bytes 1000 | tf_op jit(solution)/shard_map/feed_model/pallas_call | solution.py:841
  258.2 7.9 %feed_model.3 = (bf16[512,2048]{1,0:T(8,128)(2,1)}, bf16[512,2048]{1,0:T(8,128)(2,1)}, bf16[512,2048]{1,0:T(8,128)(2,1)}, bf16[512,2048]{1,0:T(8,128)(2,1)}) custom-call(bf16[2,512,384]{2,1,0:T(8,128)(2,1)S(1)} %get-tuple-element.578.act_ref.refs_10_, bf16[2,512,768]{2,1,0:T(8,128)(2,1)S(1)} %get-tuple-element.576.grad_ref.refs_8_, ...), custom_call_target="tpu_custom_call" | custom-call | flops 1000 | bytes 1000 | tf_op jit(solution)/shard_map/feed_model/pallas_call | solution.py:841
  268.3 15.5 %feed_weights.1 = (bf16[2048,768]{1,0:T(8,128)(2,1)}, bf16[2048,384]{1,0:T(8,128)(2,1)}) custom-call(bf16[512,2048]{1,0:T(8,128)(2,1)S(1)} %copy-done.26, bf16[512,2048]{1,0:T(8,128)(2,1)} %get-tuple-element.569.refs_1_, bf16[512,2048]{1,0:T(8,128)(2,1)} %get-tuple-element.570.refs_2_, bf16[512,2048]{1,0:T(8,128)(2,1)} %get-tuple-element.571.refs_3_, ...), custom_call_target="tpu_custom_call" | custom-call | flops 1000 | bytes 1000 | tf_op jit(solution)/shard_map/feed_weights/pallas_call | solution.py:875
  286.2 76.6 %conditional.5 = (f32[128,2048]{1,0:T(8,128)}, f32[1,2048]{1,0:T(1,128)S(1)}, bf16[2,1,128,1024]{3,2,1,0:T(8,128)(2,1)}, bf16[2,1,128,1024]{3,2,1,0:T(8,128)(2,1...) conditional(s32[]{:T(128)} %convert_element_type.128, () %tuple.97, ...), branch_computations={%region_6.7_spmd, %region_7.8_spmd} | conditional | flops 10081 | bytes 74470472 | solution.py:74
  289.8 5.7 %collective-permute-done.12.got_first_ref = bf16[128,1024]{1,0:T(8,128)(2,1)S(1)} collective-permute-done((bf16[128,1024]{1,0:T(8,128)(2,1)S(1)}, bf16[128,1024]{1,0:T(8,128)(2,1)S(1)}, u32[]{:S(2)}, u32[]{:S(2)}) %collective-permute-start.12) | collective-permute-done | bytes 262176 | tf_op jit(solution)/shard_map/cond/branch_1_fun/ppermute | solution.py:99
  303.5 2.5 collective-permute-start.17
  305.9 3.0 fold_chip.8
  308.9 8.8 %collective-permute-done.17.pair_upper_ref = bf16[64,2048]{1,0:T(8,128)(2,1)S(1)} collective-permute-done((bf16[64,2048]{1,0:T(8,128)(2,1)S(1)}, bf16[64,2048]{1,0:T(8,128)(2,1)S(1)}, u32[]{:S(2)}, u32[]{:S(2)}) %collective-permute-start.17) | collective-permute-done | bytes 262176 | tf_op jit(solution)/shard_map/cond/branch_1_fun/ppermute | solution.py:99
  328.5 3.5 fold_chip.9
  332.0 3.3 collective-permute-done.20.pair_lower_ref
  335.2 4.2 collective-permute-done.21.got_first_ref
  339.5 3.1 share_back.1
  354.2 7.5 %collective-permute-done.27 = bf16[2,1,128,1024]{3,2,1,0:T(8,128)(2,1)} collective-permute-done((bf16[2,1,128,1024]{3,2,1,0:T(8,128)(2,1)}, bf16[2,1,128,1024]{3,2,1,0:T(8,128)(2,1)}, u32[]{:S(2)}, u32[]{:S(2)}) %collective-permute-start.27) | collective-permute-done | bytes 524320 | tf_op jit(solution)/shard_map/cond/branch_1_fun/ppermute | solution.py:99
  364.9 2.5 collective-permute-start.65
  367.5 45.4 %conditional.6 = (bf16[2048,768]{1,0:T(8,128)(2,1)}, bf16[512,2048]{1,0:T(8,128)(2,1)}, bf16[512,2048]{1,0:T(8,128)(2,1)}, f32[1,2048]{1,0:T(1,128)}, f32[2,128]...) conditional(s32[]{:T(128)} %convert_element_type.128, () %tuple.86, ...), branch_computations={%region_8.9_spmd, %region_9.10_spmd} | conditional | flops 4030 | bytes 69230728 | solution.py:74
  371.8 6.4 %collective-permute-done.30.got_first_ref = bf16[128,1024]{1,0:T(8,128)(2,1)S(1)} collective-permute-done((bf16[128,1024]{1,0:T(8,128)(2,1)}, bf16[128,1024]{1,0:T(8,128)(2,1)S(1)}, u32[]{:S(2)}, u32[]{:S(2)}) %collective-permute-start.30) | collective-permute-done | bytes 262176 | tf_op jit(solution)/shard_map/cond/branch_1_fun/ppermute | solution.py:99
  381.9 12.9 %attend_back.1 = (bf16[1024,512]{1,0:T(8,128)(2,1)S(1)}, bf16[2,512,256]{2,1,0:T(8,128)(2,1)S(1)}, f32[2,128]{1,0:T(2,128)}) custom-call(bf16[512,2048]{1,0:T(8,128)(2,1)S(1)} %bitcast.123, bf16[512,2048]{1,0:T(8,128)(2,1)} %bitcast.34.grad_other_ref, bf16[2048,768]{1,0:T(8,128)(2,1)} %get-tuple-element.306.out_proj_ref.proj_ref, ...), custom_call_target="tpu_custom_call" | custom-call | flops 1000 | bytes 1000 | tf_op jit(solution)/shard_map/cond/branch_1_fun/attend_back/pallas_call | solution.py:659
  394.8 9.6 %attend_weights.1 = (bf16[2048,768]{1,0:T(8,128)(2,1)}, bf16[512,2048]{1,0:T(8,128)(2,1)}, bf16[512,2048]{1,0:T(8,128)(2,1)}, f32[1,2048]{1,0:T(1,128)}) custom-call(s32[3]{0:T(128)S(1)} %pad_add_fusion.2.position_ref, bf16[1024,512]{1,0:T(8,128)(2,1)S(1)} %get-tuple-element.318.low_ref, bf16[2,512,256]{2,1,0:T(8,128)(2,1)S(1)} %get-tuple-element.319.mixed_ref, ...), custom_call_target="tpu_custom_call" | custom-call | flops 1000 | bytes 1000 | tf_op jit(solution)/shard_map/cond/branch_1_fun/attend_weights/pallas_call | solution.py:712
  404.4 7.7 %collective-permute-done.32 = bf16[128,2048]{1,0:T(8,128)(2,1)} collective-permute-done((bf16[128,2048]{1,0:T(8,128)(2,1)S(1)}, bf16[128,2048]{1,0:T(8,128)(2,1)}, u32[]{:S(2)}, u32[]{:S(2)}) %collective-permute-start.32) | collective-permute-done | bytes 524320 | tf_op jit(solution)/shard_map/cond/branch_1_fun/ppermute | solution.py:99
  415.1 59.7 %conditional.7 = (bf16[128,2048]{1,0:T(8,128)(2,1)}, bf16[128,2048]{1,0:T(8,128)(2,1)}, f32[1,4352]{1,0:T(1,128)S(1)}) conditional(s32[]{:T(128)} %convert_element_type.128, () %tuple.85, (bf16[128,2048]{1,0:T(8,128)(2,1)}, f32[128,2048]{1,0:T(8,128)}, bf16[2,128,1024]{2,1,0:T(8,128)(2,1)}, bf16[2,128,1024]{2,1,0:T(8,128)(2,1)}, ...), branch_computations={%region_11.12_spmd, %region_12.14_spmd} | conditional | flops 6580697 | bytes 50583148 | solution.py:74
  426.2 4.5 collective-permute-done.1
  432.7 3.0 fold_chip.10
  441.2 10.0 %collective-permute-done.6 = f32[1,4352]{1,0:T(1,128)S(1)} collective-permute-done((f32[1,4352]{1,0:T(1,128)}, f32[1,4352]{1,0:T(1,128)S(1)}, u32[]{:S(2)}, u32[]{:S(2)}) %collective-permute-start.6) | collective-permute-done | bytes 17440 | tf_op jit(solution)/shard_map/cond/branch_1_fun/ppermute | solution.py:99
  459.4 4.0 collective-permute-done.9
  466.9 3.0 collective-permute-done.10
  470.0 3.2 fusion.3
  (336 shorter events, 141.5 us)
Async XLA Ops:
  7.3 69.4 %all-gather.3.cloned.1.call-start = ((), (), s32[]{:S(2)}) async-start(), calls=%async_computation.3 | async-start | bytes 3932160 | tf_op jit(solution)/shard_map/all_gather | solution.py:953
  9.5 224.4 %all-gather.5.cloned.1.call-start = ((), (), s32[]{:S(2)}) async-start(), calls=%async_computation.4 | async-start | bytes 7077888 | tf_op jit(solution)/shard_map/all_gather | solution.py:984
  9.7 12.2 %collective-permute-start.58 = (bf16[1,1088]{1,0:T(2,128)(2,1)S(1)}, bf16[1,1088]{1,0:T(2,128)(2,1)S(1)}, u32[]{:S(2)}, u32[]{:S(2)}) collective-permute-start(bf16[1,1088]{1,0:T(2,128)(2,1)S(1)} %broadcast_in_dim.54), channel_id=1, source_target_pairs={{0,8},{8,0},{16,24},{24,16},{1,9},{9,1},{17,25},{25,17},{2,10},{10... | collective-permute-start | bytes 6536 | tf_op jit(solution)/shard_map/ppermute | solution.py:123
  76.6 28.0 %collective-permute-start.61 = (bf16[512,1152]{1,0:T(8,128)(2,1)}, bf16[512,1152]{1,0:T(8,128)(2,1)}, u32[]{:S(2)}, u32[]{:S(2)}) collective-permute-start(bf16[512,1152]{1,0:T(8,128)(2,1)} %pad_maximum_fusion.2), channel_id=1, source_target_pairs={{0,8},{8,0},{16,24},{24,16},{1,9},{9,1},{17,25},{25,17},{2,10},{10... | collective-permute-start | bytes 3538952 | tf_op jit(solution)/shard_map/ppermute | solution.py:123
  91.9 16.2 %collective-permute-start.60 = (bf16[512,2048]{1,0:T(8,128)(2,1)S(1)}, bf16[512,2048]{1,0:T(8,128)(2,1)}, u32[]{:S(2)}, u32[]{:S(2)}) collective-permute-start(bf16[512,2048]{1,0:T(8,128)(2,1)S(1)} %get-tuple-element.537), channel_id=1, source_target_pairs={{0,1},{1,0},{2,3},{3,2},{4,5},{5,4},{6,7},{7,6},{8,9},{9,8},{10,11... | collective-permute-start | bytes 6291464 | tf_op jit(solution)/shard_map/ppermute | solution.py:123
  108.2 254.7 %reduce-scatter.4.cloned.1.call-start = ((), (), s32[]{:S(2)}) async-start(), calls=%async_computation.5 | async-start | bytes 4718592 | tf_op jit(solution)/shard_map/reduce_scatter | solution.py:1017
  124.7 15.0 %collective-permute-start.35 = (bf16[2,128,1024]{2,1,0:T(8,128)(2,1)S(1)}, bf16[2,128,1024]{2,1,0:T(8,128)(2,1)S(1)}, u32[]{:S(2)}, u32[]{:S(2)}) collective-permute-start(bf16[2,128,1024]{2,1,0:T(8,128)(2,1)S(1)} %get-tuple-element.144), channel_id=1, source_target_pairs={{0,2},{2,0},{4,6},{6,4},{1,3},{3,1},{5,7},{7,5},{8,10},{10,8},{12,... | collective-permute-start | bytes 1572872 | tf_op jit(solution)/shard_map/cond/branch_1_fun/ppermute | solution.py:99
  126.3 13.4 %collective-permute-start.36 = (bf16[2,128,1024]{2,1,0:T(8,128)(2,1)S(1)}, bf16[2,128,1024]{2,1,0:T(8,128)(2,1)S(1)}, u32[]{:S(2)}, u32[]{:S(2)}) collective-permute-start(bf16[2,128,1024]{2,1,0:T(8,128)(2,1)S(1)} %get-tuple-element.145), channel_id=1, source_target_pairs={{0,4},{4,0},{2,6},{6,2},{1,5},{5,1},{3,7},{7,3},{8,12},{12,8},{10,... | collective-permute-start | bytes 1572872 | tf_op jit(solution)/shard_map/cond/branch_1_fun/ppermute | solution.py:99
  127.8 11.9 %collective-permute-start.37 = (bf16[64,2048]{1,0:T(8,128)(2,1)S(1)}, bf16[64,2048]{1,0:T(8,128)(2,1)S(1)}, u32[]{:S(2)}, u32[]{:S(2)}) collective-permute-start(bf16[64,2048]{1,0:T(8,128)(2,1)S(1)} %get-tuple-element.146), channel_id=1, source_target_pairs={{0,8},{8,0},{16,24},{24,16},{1,9},{9,1},{17,25},{25,17},{2,10},{10... | collective-permute-start | bytes 786440 | tf_op jit(solution)/shard_map/cond/branch_1_fun/ppermute | solution.py:99
  141.8 13.6 %collective-permute-start.40 = (bf16[64,2048]{1,0:T(8,128)(2,1)S(1)}, bf16[64,2048]{1,0:T(8,128)(2,1)S(1)}, u32[]{:S(2)}, u32[]{:S(2)}) collective-permute-start(bf16[64,2048]{1,0:T(8,128)(2,1)S(1)} %get-tuple-element.155), channel_id=1, source_target_pairs={{0,8},{8,0},{16,24},{24,16},{1,9},{9,1},{17,25},{25,17},{2,10},{10... | collective-permute-start | bytes 786440 | tf_op jit(solution)/shard_map/cond/branch_1_fun/ppermute | solution.py:99
  158.0 13.5 %collective-permute-start.41 = (bf16[64,2048]{1,0:T(8,128)(2,1)S(1)}, bf16[64,2048]{1,0:T(8,128)(2,1)S(1)}, u32[]{:S(2)}, u32[]{:S(2)}) collective-permute-start(bf16[64,2048]{1,0:T(8,128)(2,1)S(1)} %get-tuple-element.162), channel_id=1, source_target_pairs={{0,8},{8,0},{16,24},{24,16},{1,9},{9,1},{17,25},{25,17},{2,10},{10... | collective-permute-start | bytes 786440 | tf_op jit(solution)/shard_map/cond/branch_1_fun/ppermute | solution.py:99
  160.5 10.9 %collective-permute-start.42 = (bf16[1,128,1024]{2,1,0:T(8,128)(2,1)S(1)}, bf16[1,128,1024]{2,1,0:T(8,128)(2,1)S(1)}, u32[]{:S(2)}, u32[]{:S(2)}) collective-permute-start(bf16[1,128,1024]{2,1,0:T(8,128)(2,1)S(1)} %get-tuple-element.163.first_ref), channel_id=1, source_target_pairs={{0,4},{4,0},{2,6},{6,2},{1,5},{5,1},{3,7},{7,3},{8,12},{12,8},{10,... | collective-permute-start | bytes 786440 | tf_op jit(solution)/shard_map/cond/branch_1_fun/ppermute | solution.py:99
  173.9 14.2 %collective-permute-start.47 = (bf16[2,1,128,1024]{3,2,1,0:T(8,128)(2,1)S(1)}, bf16[2,1,128,1024]{3,2,1,0:T(8,128)(2,1)S(1)}, u32[]{:S(2)}, u32[]{:S(2)}) collective-permute-start(bf16[2,1,128,1024]{3,2,1,0:T(8,128)(2,1)S(1)} %get-tuple-element.172.first_ref), channel_id=1, source_target_pairs={{0,2},{2,0},{4,6},{6,4},{1,3},{3,1},{5,7},{7,5},{8,10},{10,8},{12,... | collective-permute-start | bytes 1572872 | tf_op jit(solution)/shard_map/cond/branch_1_fun/ppermute | solution.py:99
  175.5 12.6 %collective-permute-start.48 = (bf16[2,1,128,1024]{3,2,1,0:T(8,128)(2,1)S(1)}, bf16[2,1,128,1024]{3,2,1,0:T(8,128)(2,1)S(1)}, u32[]{:S(2)}, u32[]{:S(2)}) collective-permute-start(bf16[2,1,128,1024]{3,2,1,0:T(8,128)(2,1)S(1)} %get-tuple-element.173.second_ref), channel_id=1, source_target_pairs={{0,4},{4,0},{2,6},{6,2},{1,5},{5,1},{3,7},{7,3},{8,12},{12,8},{10,... | collective-permute-start | bytes 1572872 | tf_op jit(solution)/shard_map/cond/branch_1_fun/ppermute | solution.py:99
  175.5 12.6 %collective-permute-start.46 = (bf16[64,2048]{1,0:T(8,128)(2,1)S(1)}, bf16[64,2048]{1,0:T(8,128)(2,1)S(1)}, u32[]{:S(2)}, u32[]{:S(2)}) collective-permute-start(bf16[64,2048]{1,0:T(8,128)(2,1)S(1)} %get-tuple-element.171), channel_id=1, source_target_pairs={{0,8},{8,0},{16,24},{24,16},{1,9},{9,1},{17,25},{25,17},{2,10},{10... | collective-permute-start | bytes 786440 | tf_op jit(solution)/shard_map/cond/branch_1_fun/ppermute | solution.py:99
  188.9 20.3 %collective-permute-start.53 = (bf16[1,512,2048]{2,1,0:T(8,128)(2,1)S(1)}, bf16[1,512,2048]{2,1,0:T(8,128)(2,1)}, u32[]{:S(2)}, u32[]{:S(2)}) collective-permute-start(bf16[1,512,2048]{2,1,0:T(8,128)(2,1)S(1)} %bitcast.142), channel_id=1, source_target_pairs={{0,1},{1,0},{2,3},{3,2},{4,5},{5,4},{6,7},{7,6},{8,9},{9,8},{10,11... | collective-permute-start | bytes 6291464 | tf_op jit(solution)/shard_map/cond/branch_1_fun/ppermute | solution.py:99
  189.0 20.2 %collective-permute-start.51 = (bf16[2,1,128,1024]{3,2,1,0:T(8,128)(2,1)S(1)}, bf16[2,1,128,1024]{3,2,1,0:T(8,128)(2,1)S(1)}, u32[]{:S(2)}, u32[]{:S(2)}) collective-permute-start(bf16[2,1,128,1024]{3,2,1,0:T(8,128)(2,1)S(1)} %get-tuple-element.184.first_ref), channel_id=1, source_target_pairs={{0,2},{2,0},{4,6},{6,4},{1,3},{3,1},{5,7},{7,5},{8,10},{10,8},{12,... | collective-permute-start | bytes 1572872 | tf_op jit(solution)/shard_map/cond/branch_1_fun/ppermute | solution.py:99
  189.6 19.6 %collective-permute-start.52 = (bf16[2,1,128,1024]{3,2,1,0:T(8,128)(2,1)S(1)}, bf16[2,1,128,1024]{3,2,1,0:T(8,128)(2,1)S(1)}, u32[]{:S(2)}, u32[]{:S(2)}) collective-permute-start(bf16[2,1,128,1024]{3,2,1,0:T(8,128)(2,1)S(1)} %get-tuple-element.185.second_ref), channel_id=1, source_target_pairs={{0,4},{4,0},{2,6},{6,2},{1,5},{5,1},{3,7},{7,3},{8,12},{12,8},{10,... | collective-permute-start | bytes 1572872 | tf_op jit(solution)/shard_map/cond/branch_1_fun/ppermute | solution.py:99
  190.1 19.1 %collective-permute-start.49 = (bf16[1,128,1024]{2,1,0:T(8,128)(2,1)S(1)}, bf16[1,128,1024]{2,1,0:T(8,128)(2,1)S(1)}, u32[]{:S(2)}, u32[]{:S(2)}) collective-permute-start(bf16[1,128,1024]{2,1,0:T(8,128)(2,1)S(1)} %get-tuple-element.182.first_ref), channel_id=1, source_target_pairs={{0,4},{4,0},{2,6},{6,2},{1,5},{5,1},{3,7},{7,3},{8,12},{12,8},{10,... | collective-permute-start | bytes 786440 | tf_op jit(solution)/shard_map/cond/branch_1_fun/ppermute | solution.py:99
  191.6 17.6 %collective-permute-start.50 = (bf16[1,128,1024]{2,1,0:T(8,128)(2,1)S(1)}, bf16[1,128,1024]{2,1,0:T(8,128)(2,1)S(1)}, u32[]{:S(2)}, u32[]{:S(2)}) collective-permute-start(bf16[1,128,1024]{2,1,0:T(8,128)(2,1)S(1)} %get-tuple-element.183.second_ref), channel_id=1, source_target_pairs={{0,2},{2,0},{4,6},{6,4},{1,3},{3,1},{5,7},{7,5},{8,10},{10,8},{12,... | collective-permute-start | bytes 786440 | tf_op jit(solution)/shard_map/cond/branch_1_fun/ppermute | solution.py:99
  211.8 15.6 %collective-permute-start.56 = (bf16[1,512,2048]{2,1,0:T(8,128)(2,1)}, bf16[1,512,2048]{2,1,0:T(8,128)(2,1)}, u32[]{:S(2)}, u32[]{:S(2)}) collective-permute-start(bf16[1,512,2048]{2,1,0:T(8,128)(2,1)} %bitcast.11), channel_id=1, source_target_pairs={{0,1},{1,0},{2,3},{3,2},{4,5},{5,4},{6,7},{7,6},{8,9},{9,8},{10,11... | collective-permute-start | bytes 6291464 | tf_op jit(solution)/shard_map/cond/branch_1_fun/ppermute | solution.py:99
  211.8 14.3 %collective-permute-start.54 = (bf16[2,1,128,1024]{3,2,1,0:T(8,128)(2,1)S(1)}, bf16[2,1,128,1024]{3,2,1,0:T(8,128)(2,1)S(1)}, u32[]{:S(2)}, u32[]{:S(2)}) collective-permute-start(bf16[2,1,128,1024]{3,2,1,0:T(8,128)(2,1)S(1)} %get-tuple-element.194.first_ref), channel_id=1, source_target_pairs={{0,2},{2,0},{4,6},{6,4},{1,3},{3,1},{5,7},{7,5},{8,10},{10,8},{12,... | collective-permute-start | bytes 1572872 | tf_op jit(solution)/shard_map/cond/branch_1_fun/ppermute | solution.py:99
  213.4 14.0 %collective-permute-start.55 = (bf16[2,1,128,1024]{3,2,1,0:T(8,128)(2,1)S(1)}, bf16[2,1,128,1024]{3,2,1,0:T(8,128)(2,1)S(1)}, u32[]{:S(2)}, u32[]{:S(2)}) collective-permute-start(bf16[2,1,128,1024]{3,2,1,0:T(8,128)(2,1)S(1)} %get-tuple-element.195.second_ref), channel_id=1, source_target_pairs={{0,4},{4,0},{2,6},{6,2},{1,5},{5,1},{3,7},{7,3},{8,12},{12,8},{10,... | collective-permute-start | bytes 1572872 | tf_op jit(solution)/shard_map/cond/branch_1_fun/ppermute | solution.py:99
  267.1 16.6 %collective-permute-start.63 = (bf16[2,128,1024]{2,1,0:T(8,128)(2,1)S(1)}, bf16[2,128,1024]{2,1,0:T(8,128)(2,1)S(1)}, u32[]{:S(2)}, u32[]{:S(2)}) collective-permute-start(bf16[2,128,1024]{2,1,0:T(8,128)(2,1)S(1)} %get-tuple-element.566), channel_id=1, source_target_pairs={{0,2},{2,0},{4,6},{6,4},{1,3},{3,1},{5,7},{7,5},{8,10},{10,8},{12,... | collective-permute-start | bytes 1572872 | tf_op jit(solution)/shard_map/ppermute | solution.py:99
  267.7 16.0 %collective-permute-start.64 = (bf16[2,128,1024]{2,1,0:T(8,128)(2,1)S(1)}, bf16[2,128,1024]{2,1,0:T(8,128)(2,1)S(1)}, u32[]{:S(2)}, u32[]{:S(2)}) collective-permute-start(bf16[2,128,1024]{2,1,0:T(8,128)(2,1)S(1)} %get-tuple-element.567), channel_id=1, source_target_pairs={{0,4},{4,0},{2,6},{6,2},{1,5},{5,1},{3,7},{7,3},{8,12},{12,8},{10,... | collective-permute-start | bytes 1572872 | tf_op jit(solution)/shard_map/ppermute | solution.py:99
  283.8 129.1 %reduce-scatter.6.cloned.1.call-start = ((), (), s32[]{:S(2)}) async-start(), calls=%async_computation.6 | async-start | bytes 2359296 | tf_op jit(solution)/shard_map/reduce_scatter | solution.py:1017
  284.4 195.7 %reduce-scatter.8.cloned.1.call-start = ((), (), s32[]{:S(2)}) async-start(), calls=%async_computation.7 | async-start | bytes 3932160 | tf_op jit(solution)/shard_map/reduce_scatter | solution.py:1071
  286.2 10.6 %collective-permute-start.14 = (bf16[512,2048]{1,0:T(8,128)(2,1)}, bf16[512,2048]{1,0:T(8,128)(2,1)}, u32[]{:S(2)}, u32[]{:S(2)}) collective-permute-start(bf16[512,2048]{1,0:T(8,128)(2,1)} %get-tuple-element.208), channel_id=1, source_target_pairs={{0,1},{1,0},{2,3},{3,2},{4,5},{5,4},{6,7},{7,6},{8,9},{9,8},{10,11... | collective-permute-start | bytes 6291464 | tf_op jit(solution)/shard_map/cond/branch_1_fun/ppermute | solution.py:99
  286.2 10.6 %collective-permute-start.15 = (bf16[512,2048]{1,0:T(8,128)(2,1)}, bf16[512,2048]{1,0:T(8,128)(2,1)}, u32[]{:S(2)}, u32[]{:S(2)}) collective-permute-start(bf16[512,2048]{1,0:T(8,128)(2,1)} %get-tuple-element.209), channel_id=1, source_target_pairs={{0,1},{1,0},{2,3},{3,2},{4,5},{5,4},{6,7},{7,6},{8,9},{9,8},{10,11... | collective-permute-start | bytes 6291464 | tf_op jit(solution)/shard_map/cond/branch_1_fun/ppermute | solution.py:99
  300.6 17.2 %collective-permute-start.18 = (bf16[2,128,1024]{2,1,0:T(8,128)(2,1)S(1)}, bf16[2,128,1024]{2,1,0:T(8,128)(2,1)S(1)}, u32[]{:S(2)}, u32[]{:S(2)}) collective-permute-start(bf16[2,128,1024]{2,1,0:T(8,128)(2,1)S(1)} %get-tuple-element.220), channel_id=1, source_target_pairs={{0,2},{2,0},{4,6},{6,4},{1,3},{3,1},{5,7},{7,5},{8,10},{10,8},{12,... | collective-permute-start | bytes 1572872 | tf_op jit(solution)/shard_map/cond/branch_1_fun/ppermute | solution.py:99
  302.1 15.6 %collective-permute-start.19 = (bf16[2,128,1024]{2,1,0:T(8,128)(2,1)S(1)}, bf16[2,128,1024]{2,1,0:T(8,128)(2,1)S(1)}, u32[]{:S(2)}, u32[]{:S(2)}) collective-permute-start(bf16[2,128,1024]{2,1,0:T(8,128)(2,1)S(1)} %get-tuple-element.221), channel_id=1, source_target_pairs={{0,4},{4,0},{2,6},{6,2},{1,5},{5,1},{3,7},{7,3},{8,12},{12,8},{10,... | collective-permute-start | bytes 1572872 | tf_op jit(solution)/shard_map/cond/branch_1_fun/ppermute | solution.py:99
  303.5 14.3 %collective-permute-start.17 = (bf16[64,2048]{1,0:T(8,128)(2,1)S(1)}, bf16[64,2048]{1,0:T(8,128)(2,1)S(1)}, u32[]{:S(2)}, u32[]{:S(2)}) collective-permute-start(bf16[64,2048]{1,0:T(8,128)(2,1)S(1)} %get-tuple-element.219), channel_id=1, source_target_pairs={{0,8},{8,0},{16,24},{24,16},{1,9},{9,1},{17,25},{25,17},{2,10},{10... | collective-permute-start | bytes 786440 | tf_op jit(solution)/shard_map/cond/branch_1_fun/ppermute | solution.py:99
  320.7 18.7 %collective-permute-start.23 = (bf16[2,128,1024]{2,1,0:T(8,128)(2,1)}, bf16[2,128,1024]{2,1,0:T(8,128)(2,1)}, u32[]{:S(2)}, u32[]{:S(2)}) collective-permute-start(bf16[2,128,1024]{2,1,0:T(8,128)(2,1)} %get-tuple-element.237), channel_id=1, source_target_pairs={{0,2},{2,0},{4,6},{6,4},{1,3},{3,1},{5,7},{7,5},{8,10},{10,8},{12,... | collective-permute-start | bytes 1572872 | tf_op jit(solution)/shard_map/cond/branch_1_fun/ppermute | solution.py:99
  321.2 18.2 %collective-permute-start.24 = (bf16[2,128,1024]{2,1,0:T(8,128)(2,1)}, bf16[2,128,1024]{2,1,0:T(8,128)(2,1)}, u32[]{:S(2)}, u32[]{:S(2)}) collective-permute-start(bf16[2,128,1024]{2,1,0:T(8,128)(2,1)} %get-tuple-element.238), channel_id=1, source_target_pairs={{0,4},{4,0},{2,6},{6,2},{1,5},{5,1},{3,7},{7,3},{8,12},{12,8},{10,... | collective-permute-start | bytes 1572872 | tf_op jit(solution)/shard_map/cond/branch_1_fun/ppermute | solution.py:99
  321.9 13.3 %collective-permute-start.20 = (bf16[64,2048]{1,0:T(8,128)(2,1)}, bf16[64,2048]{1,0:T(8,128)(2,1)}, u32[]{:S(2)}, u32[]{:S(2)}) collective-permute-start(bf16[64,2048]{1,0:T(8,128)(2,1)} %get-tuple-element.234), channel_id=1, source_target_pairs={{0,8},{8,0},{16,24},{24,16},{1,9},{9,1},{17,25},{25,17},{2,10},{10... | collective-permute-start | bytes 786440 | tf_op jit(solution)/shard_map/cond/branch_1_fun/ppermute | solution.py:99
  324.4 15.1 %collective-permute-start.21 = (bf16[128,1024]{1,0:T(8,128)(2,1)}, bf16[128,1024]{1,0:T(8,128)(2,1)}, u32[]{:S(2)}, u32[]{:S(2)}) collective-permute-start(bf16[128,1024]{1,0:T(8,128)(2,1)} %get-tuple-element.235), channel_id=1, source_target_pairs={{0,4},{4,0},{2,6},{6,2},{1,5},{5,1},{3,7},{7,3},{8,12},{12,8},{10,... | collective-permute-start | bytes 786440 | tf_op jit(solution)/shard_map/cond/branch_1_fun/ppermute | solution.py:99
  325.7 13.7 %collective-permute-start.22 = (bf16[128,1024]{1,0:T(8,128)(2,1)}, bf16[128,1024]{1,0:T(8,128)(2,1)}, u32[]{:S(2)}, u32[]{:S(2)}) collective-permute-start(bf16[128,1024]{1,0:T(8,128)(2,1)} %get-tuple-element.236), channel_id=1, source_target_pairs={{0,2},{2,0},{4,6},{6,4},{1,3},{3,1},{5,7},{7,5},{8,10},{10,8},{12,... | collective-permute-start | bytes 786440 | tf_op jit(solution)/shard_map/cond/branch_1_fun/ppermute | solution.py:99
  351.2 10.5 %collective-permute-start.27 = (bf16[2,1,128,1024]{3,2,1,0:T(8,128)(2,1)}, bf16[2,1,128,1024]{3,2,1,0:T(8,128)(2,1)}, u32[]{:S(2)}, u32[]{:S(2)}) collective-permute-start(bf16[2,1,128,1024]{3,2,1,0:T(8,128)(2,1)} %get-tuple-element.267), channel_id=1, source_target_pairs={{0,2},{2,0},{4,6},{6,4},{1,3},{3,1},{5,7},{7,5},{8,10},{10,8},{12,... | collective-permute-start | bytes 1572872 | tf_op jit(solution)/shard_map/cond/branch_1_fun/ppermute | solution.py:99
  352.6 10.3 %collective-permute-start.28 = (bf16[2,1,128,1024]{3,2,1,0:T(8,128)(2,1)}, bf16[2,1,128,1024]{3,2,1,0:T(8,128)(2,1)}, u32[]{:S(2)}, u32[]{:S(2)}) collective-permute-start(bf16[2,1,128,1024]{3,2,1,0:T(8,128)(2,1)} %get-tuple-element.268), channel_id=1, source_target_pairs={{0,4},{4,0},{2,6},{6,2},{1,5},{5,1},{3,7},{7,3},{8,12},{12,8},{10,... | collective-permute-start | bytes 1572872 | tf_op jit(solution)/shard_map/cond/branch_1_fun/ppermute | solution.py:99
  364.9 47.9 %collective-permute-start.65 = (bf16[512,768]{1,0:T(8,128)(2,1)}, bf16[512,768]{1,0:T(8,128)(2,1)S(1)}, u32[]{:S(2)}, u32[]{:S(2)}) collective-permute-start(bf16[512,768]{1,0:T(8,128)(2,1)} %dynamic-slice_bitcast_fusion), channel_id=1, source_target_pairs={{0,8},{8,0},{16,24},{24,16},{1,9},{9,1},{17,25},{25,17},{2,10},{10... | collective-permute-start | bytes 2359304 | tf_op jit(solution)/shard_map/ppermute | solution.py:123
  369.2 10.5 %collective-permute-start.29 = (bf16[1,512,2048]{2,1,0:T(8,128)(2,1)S(1)}, bf16[1,512,2048]{2,1,0:T(8,128)(2,1)}, u32[]{:S(2)}, u32[]{:S(2)}) collective-permute-start(bf16[1,512,2048]{2,1,0:T(8,128)(2,1)S(1)} %bitcast.122), channel_id=1, source_target_pairs={{0,1},{1,0},{2,3},{3,2},{4,5},{5,4},{6,7},{7,6},{8,9},{9,8},{10,11... | collective-permute-start | bytes 6291464 | tf_op jit(solution)/shard_map/cond/branch_1_fun/ppermute | solution.py:99
  380.9 31.3 %collective-permute-start.32 = (bf16[128,2048]{1,0:T(8,128)(2,1)S(1)}, bf16[128,2048]{1,0:T(8,128)(2,1)}, u32[]{:S(2)}, u32[]{:S(2)}) collective-permute-start(bf16[128,2048]{1,0:T(8,128)(2,1)S(1)} %fold_end.3), channel_id=1, source_target_pairs={{0,8},{8,0},{16,24},{24,16},{1,9},{9,1},{17,25},{25,17},{2,10},{10... | collective-permute-start | bytes 1572872 | tf_op jit(solution)/shard_map/cond/branch_1_fun/ppermute | solution.py:99
  380.9 31.2 %collective-permute-start.33 = (bf16[2,128,1024]{2,1,0:T(8,128)(2,1)}, bf16[2,128,1024]{2,1,0:T(8,128)(2,1)}, u32[]{:S(2)}, u32[]{:S(2)}) collective-permute-start(bf16[2,128,1024]{2,1,0:T(8,128)(2,1)} %get-tuple-element.303), channel_id=1, source_target_pairs={{0,2},{2,0},{4,6},{6,4},{1,3},{3,1},{5,7},{7,5},{8,10},{10,8},{12,... | collective-permute-start | bytes 1572872 | tf_op jit(solution)/shard_map/cond/branch_1_fun/ppermute | solution.py:99
  381.5 30.6 %collective-permute-start.34 = (bf16[2,128,1024]{2,1,0:T(8,128)(2,1)}, bf16[2,128,1024]{2,1,0:T(8,128)(2,1)}, u32[]{:S(2)}, u32[]{:S(2)}) collective-permute-start(bf16[2,128,1024]{2,1,0:T(8,128)(2,1)} %get-tuple-element.304), channel_id=1, source_target_pairs={{0,4},{4,0},{2,6},{6,2},{1,5},{5,1},{3,7},{7,3},{8,12},{12,8},{10,... | collective-permute-start | bytes 1572872 | tf_op jit(solution)/shard_map/cond/branch_1_fun/ppermute | solution.py:99
  414.8 60.0 %collective-permute-start.66 = (bf16[512,384]{1,0:T(8,128)(2,1)}, bf16[512,384]{1,0:T(8,128)(2,1)S(1)}, u32[]{:S(2)}, u32[]{:S(2)}) collective-permute-start(bf16[512,384]{1,0:T(8,128)(2,1)} %dynamic-slice_bitcast_fusion.1), channel_id=1, source_target_pairs={{0,8},{8,0},{16,24},{24,16},{1,9},{9,1},{17,25},{25,17},{2,10},{10... | collective-permute-start | bytes 1179656 | tf_op jit(solution)/shard_map/ppermute | solution.py:123
  437.3 14.0 %collective-permute-start.4 = (bf16[2,128,1024]{2,1,0:T(8,128)(2,1)}, bf16[2,128,1024]{2,1,0:T(8,128)(2,1)}, u32[]{:S(2)}, u32[]{:S(2)}) collective-permute-start(bf16[2,128,1024]{2,1,0:T(8,128)(2,1)} %get-tuple-element.368), channel_id=1, source_target_pairs={{0,2},{2,0},{4,6},{6,4},{1,3},{3,1},{5,7},{7,5},{8,10},{10,8},{12,... | collective-permute-start | bytes 1572872 | tf_op jit(solution)/shard_map/cond/branch_1_fun/ppermute | solution.py:99
  438.8 13.3 %collective-permute-start.5 = (bf16[2,128,1024]{2,1,0:T(8,128)(2,1)}, bf16[2,128,1024]{2,1,0:T(8,128)(2,1)}, u32[]{:S(2)}, u32[]{:S(2)}) collective-permute-start(bf16[2,128,1024]{2,1,0:T(8,128)(2,1)} %get-tuple-element.369), channel_id=1, source_target_pairs={{0,4},{4,0},{2,6},{6,2},{1,5},{5,1},{3,7},{7,3},{8,12},{12,8},{10,... | collective-permute-start | bytes 1572872 | tf_op jit(solution)/shard_map/cond/branch_1_fun/ppermute | solution.py:99
  440.5 10.7 %collective-permute-start.6 = (f32[1,4352]{1,0:T(1,128)}, f32[1,4352]{1,0:T(1,128)S(1)}, u32[]{:S(2)}, u32[]{:S(2)}) collective-permute-start(f32[1,4352]{1,0:T(1,128)} %add.138), channel_id=1, source_target_pairs={{0,2},{2,0},{4,6},{6,4},{1,3},{3,1},{5,7},{7,5},{8,10},{10,8},{12,... | collective-permute-start | bytes 52232 | tf_op jit(solution)/shard_map/cond/branch_1_fun/ppermute | solution.py:99
  (80 other events, 766.8 us)
Sparse Core Ops, SparseCore 0:
  10.2 66.3 all-gather.2
  108.3 112.8 all-gather.4
  283.9 78.3 reduce-scatter.3
  365.1 41.9 reduce-scatter.5
  413.0 63.3 reduce-scatter.7
